TPU v7x, 32 devices: a whole 2x2x4 slice. The times are simulated.
32 devices in a mesh: rep: 1, wide: 16 (over z, y, x), narrow: 2 (over core).
Axes of the slice: x: 2, y: 2, z: 4, core: 2. Of those that a mesh axis runs over, the one named last changes fastest.
Arguments:
- hidden_in: bfloat16 [2048, 2048], P(('rep', 'wide', 'narrow')), may hold values from -6 to 6
- queries: bfloat16 [2048, 2048], P(('rep', 'wide'), 'narrow')
- out_gate: bfloat16 [2048, 2048], P(('rep', 'wide'), 'narrow'), may hold values from -6 to 6
- draft_kv: bfloat16 [2, 2048, 256], P(None, ('rep', 'wide')), may hold values from -6 to 6
- cache_keys: bfloat16 [128, 256, 256], P(('rep', 'wide'))
- cache_values: bfloat16 [128, 256, 256], P(('rep', 'wide')), may hold values from -6 to 6
- draft_len: int32 [128], P(('rep', 'wide')), may hold values from 1 to 16, as said below
- cache_len: int32 [128], P(('rep', 'wide')), may hold values from 1 to 256, as said below
- o_weight: bfloat16 [2048, 2048], P('narrow'), may hold values from -0.125 to 0.125
- norm_gain: float32 [2048], replicated, may hold values from 0.5 to 1.5
- route_ids: int32 [2048, 10], P(('rep', 'wide', 'narrow')), may hold values from 0 to 31, all different within a row; in each aligned block of 64 rows (0 to 63, 64 to 127, ...) at most 30 rows name the same one
- route_weights: float32 [2048, 10], P(('rep', 'wide', 'narrow')), may hold values from 0.05 to 0.4
- w_gate: bfloat16 [32, 2048, 512], P(('wide', 'narrow')), may hold values from -0.125 to 0.125
- w_up: bfloat16 [32, 2048, 512], P(('wide', 'narrow')), may hold values from -0.125 to 0.125
- w_down: bfloat16 [32, 512, 2048], P(('wide', 'narrow')), may hold values from -0.25 to 0.25
Outputs:
- mixed: bfloat16 [2048, 2048], P(('rep', 'wide', 'narrow'))
Inputs may be any that keep to these rules, and one draw needn't show every extreme that they name: `route_ids`: in each aligned block of 64 rows (the rows of one device) no expert is named by more than 30 pairs (row, choice), a bound that some block reaches. `draft_len`: some request has all 16 draft rows live. `cache_len`: some request has all 256 cache slots live.
All inputs are finite; a program needn't handle non-finite values.
Results may differ from a plain program's by a relative error of at most 0.0044.
Values may be sent and summed in bfloat16 or wider, within the bound.
No kernel may reach another device: no remote copies, remote signals or barrier semaphores. Data moves between devices by JAX's collectives and lax.ppermute only.
A program may use at most 128 MiB of HBM per device.

v0:
```python
import math

import jax
import jax.numpy as jnp
from jax import lax
from jax.sharding import PartitionSpec as P


def attention_rows(queries, out_gate, draft_kv, cache_keys, cache_values, draft_len, cache_len):
    req_count, context_len, head_size = cache_keys.shape
    row_count = queries.shape[0]
    drafts = row_count // req_count
    head_count = queries.shape[1] // head_size
    query_blocks = queries.reshape(req_count, drafts, head_count, head_size)
    draft_keys = draft_kv[0].reshape(req_count, drafts, head_size)
    draft_values = draft_kv[1].reshape(req_count, drafts, head_size)
    score_scale = 1.0 / math.sqrt(head_size)
    cache_scores = (
        jnp.einsum("rjhd,rcd->rjhc", query_blocks, cache_keys, preferred_element_type=jnp.float32)
        * score_scale
    )
    draft_scores = (
        jnp.einsum("rjhd,rid->rjhi", query_blocks, draft_keys, preferred_element_type=jnp.float32)
        * score_scale
    )
    slots = jnp.arange(context_len, dtype=jnp.int32)
    cache_live = slots[None, :] < cache_len[:, None]
    cache_scores = jnp.where(cache_live[:, None, None, :], cache_scores, -jnp.inf)
    positions = jnp.arange(drafts, dtype=jnp.int32)
    causal = positions[None, :] <= positions[:, None]
    draft_live = causal[None, :, :] & (positions[None, None, :] < draft_len[:, None, None])
    draft_scores = jnp.where(draft_live[:, :, None, :], draft_scores, -jnp.inf)
    row_max = jnp.maximum(jnp.max(cache_scores, axis=-1), jnp.max(draft_scores, axis=-1))
    cache_probs = jnp.exp(cache_scores - row_max[..., None])
    draft_probs = jnp.exp(draft_scores - row_max[..., None])
    denominator = jnp.sum(cache_probs, axis=-1) + jnp.sum(draft_probs, axis=-1)
    context = jnp.einsum(
        "rjhc,rcd->rjhd",
        cache_probs.astype(jnp.bfloat16),
        cache_values,
        preferred_element_type=jnp.float32,
    )
    context = context + jnp.einsum(
        "rjhi,rid->rjhd",
        draft_probs.astype(jnp.bfloat16),
        draft_values,
        preferred_element_type=jnp.float32,
    )
    context = context / denominator[..., None]
    gate_open = jax.nn.sigmoid(out_gate.astype(jnp.float32)).reshape(
        req_count, drafts, head_count, head_size
    )
    row_live = (positions[None, :] < draft_len[:, None]).astype(jnp.float32)
    attended = context * gate_open * row_live[:, :, None, None]
    return attended.reshape(row_count, head_count * head_size).astype(jnp.bfloat16)


def on_device(
    hidden_in,
    queries,
    out_gate,
    draft_kv,
    cache_keys,
    cache_values,
    draft_len,
    cache_len,
    o_weight,
    norm_gain,
    route_ids,
    route_weights,
    w_gate,
    w_up,
    w_down,
):
    attended = attention_rows(
        queries, out_gate, draft_kv, cache_keys, cache_values, draft_len, cache_len
    )
    own_rows = hidden_in.shape[0]
    width = hidden_in.shape[1]
    row_block = attended
    projected = lax.psum_scatter(
        jnp.dot(row_block, o_weight, preferred_element_type=jnp.float32),
        "narrow",
        scatter_dimension=0,
        tiled=True,
    )
    residual = hidden_in.astype(jnp.float32) + projected
    spread = jnp.mean(residual * residual, axis=-1, keepdims=True)
    normed = (residual * lax.rsqrt(spread + 1e-06) * norm_gain).astype(jnp.bfloat16)
    top_count = route_ids.shape[1]
    wide_count = lax.axis_size("wide")
    narrow_count = lax.axis_size("narrow")
    experts = wide_count * narrow_count
    capacity = max(2, min(own_rows, (3 * own_rows * top_count + 2 * experts - 1) // (2 * experts)))
    flat_ids = route_ids.reshape(-1)
    onehot = (flat_ids[:, None] == jnp.arange(experts, dtype=jnp.int32)[None, :]).astype(jnp.int32)
    before = jnp.cumsum(onehot, axis=0) - onehot
    slot_index = jnp.sum(before * onehot, axis=1)
    target = flat_ids * capacity + slot_index
    source_rows = jnp.repeat(normed, top_count, axis=0)
    outgoing = jnp.zeros((experts * capacity, width), jnp.bfloat16).at[target].set(source_rows)
    outgoing = outgoing.reshape(experts, capacity, width)
    slot_block = lax.all_to_all(
        outgoing, ("wide", "narrow"), split_axis=0, concat_axis=0, tiled=True
    )
    row_block = slot_block.reshape(-1, width)
    gate_proj = jnp.dot(row_block, w_gate[0], preferred_element_type=jnp.float32)
    up_proj = jnp.dot(row_block, w_up[0], preferred_element_type=jnp.float32)
    hidden_act = (jax.nn.silu(gate_proj) * up_proj).astype(jnp.bfloat16)
    produced = jnp.dot(hidden_act, w_down[0], preferred_element_type=jnp.float32).astype(
        jnp.bfloat16
    )
    produced = produced.reshape(slot_block.shape)
    returned = lax.all_to_all(produced, ("wide", "narrow"), split_axis=0, concat_axis=0, tiled=True)
    picked = returned.reshape(experts * capacity, width)[target].reshape(own_rows, top_count, width)
    expert_mix = jnp.sum(route_weights[:, :, None] * picked.astype(jnp.float32), axis=1)
    return (residual + expert_mix).astype(jnp.bfloat16)


def solution(mesh):
    placed = (
        P(("rep", "wide", "narrow"), None),
        P(("rep", "wide"), "narrow"),
        P(("rep", "wide"), "narrow"),
        P(None, ("rep", "wide"), None),
        P(("rep", "wide"), None, None),
        P(("rep", "wide"), None, None),
        P(("rep", "wide")),
        P(("rep", "wide")),
        P("narrow", None),
        P(),
        P(("rep", "wide", "narrow"), None),
        P(("rep", "wide", "narrow"), None),
        P(("wide", "narrow"), None, None),
        P(("wide", "narrow"), None, None),
        P(("wide", "narrow"), None, None),
    )
    return jax.shard_map(
        on_device,
        mesh=mesh,
        in_specs=placed,
        out_specs=P(("rep", "wide", "narrow"), None),
        check_vma=False,
    )
```

profile of v0, /device:TPU:0, one launch (start us, length us, event | category | flops | bytes accessed | tf_op | source)
XLA Modules:
  0.0 314.2 jit_solution(11166674125508603859)
XLA Ops:
  6.6 1.3 reshape.165
  10.7 1.8 fusion.38
  12.9 1.1 fusion.27
  15.2 2.0 fusion.13
  18.0 1.7 fusion.40
  20.1 1.5 reduce-window.6
  22.2 8.9 %reduce-scatter.2.cloned.1.call-done = f32[64,2048]{1,0:T(8,128)} async-done(((f32[128,2048]{1,0:T(8,128)}), f32[64,2048]{1,0:T(8,128)}) %reduce-scatter.2.cloned.1.call-update) | async-done | bytes 524304 | tf_op jit(solution)/shard_map/reduce_scatter | solution.py:81
  31.1 1.2 multiply_reduce_fusion.1
  32.4 1.2 multiply_convert_fusion.1
  33.5 2.6 broadcast_in_dim.33
  36.1 5.5 %reshape.186 = bf16[640,2048]{1,0:T(8,128)(2,1)} reshape(bf16[64,10,2048]{2,1,0:T(8,128)(2,1)} %broadcast_in_dim.33) | data formatting | bytes 5242880 | tf_op jit(solution)/shard_map/reshape | solution.py:100
  41.6 10.3 %scatter_custom_fusion = bf16[960,2048]{1,0:T(8,128)(2,1)} fusion(s32[640]{0:T(1024)S(1)} %fusion.34, bf16[640,2048]{1,0:T(8,128)(2,1)} %reshape.186, bf16[]{:T(256)} %constant.14.clone.1), kind=kCustom, calls=%fused_computation.10 | custom fusion | bytes 3932672 | tf_op jit(solution)/shard_map/scatter | solution.py:101
  51.9 5.0 %reshape.169 = bf16[32,30,2048]{2,1,0:T(8,128)(2,1)} reshape(bf16[960,2048]{1,0:T(8,128)(2,1)} %scatter_custom_fusion) | data formatting | bytes 7864320 | tf_op jit(solution)/shard_map/reshape | solution.py:102
  56.9 99.5 %all_to_all.10 = bf16[32,30,2048]{2,1,0:T(8,128)(2,1)} all-to-all(bf16[32,30,2048]{2,1,0:T(8,128)(2,1)} %reshape.169), channel_id=1, replica_groups=mesh['rep'=1,'wide'=16,'narrow'=2] {'wide','narrow'}, dimensions={0} | all-to-all | bytes 7864320 | tf_op jit(solution)/shard_map/all_to_all | solution.py:103
  156.4 5.0 %reshape.170 = bf16[960,2048]{1,0:T(8,128)(2,1)} reshape(bf16[32,30,2048]{2,1,0:T(8,128)(2,1)} %all_to_all.10) | data formatting | bytes 7864320 | tf_op jit(solution)/shard_map/reshape | solution.py:106
  161.5 6.3 %fusion.3 = f32[960,512]{1,0:T(8,128)} fusion(bf16[960,2048]{1,0:T(8,128)(2,1)} %reshape.170, bf16[1,2048,512]{2,1,0:T(8,128)(2,1)} %param.27), kind=kOutput, calls=%fused_computation.7 | convolution fusion | flops 2013265920 | bytes 7995392 | tf_op jit(solution)/shard_map/dot_general | solution.py:107
  167.8 9.5 %convolution_convert_fusion = bf16[960,2048]{1,0:T(8,128)(2,1)} fusion(bf16[1,512,2048]{2,1,0:T(8,128)(2,1)S(1)} %copy-done, f32[960,512]{1,0:T(8,128)} %fusion.3, bf16[960,2048]{1,0:T(8,128)(2,1)} %reshape.170, bf16[1,2048,512]{2,1,0:T(8,128)(2,1)} %param.28), kind=kOutput, calls=%fused_computation.3 | convolution fusion | flops 4031447040 | bytes 14024704 | tf_op jit(solution)/shard_map/dot_general | solution.py:110
  177.3 5.0 %reshape.171 = bf16[32,30,2048]{2,1,0:T(8,128)(2,1)} reshape(bf16[960,2048]{1,0:T(8,128)(2,1)} %convolution_convert_fusion) | data formatting | bytes 7864320 | tf_op jit(solution)/shard_map/reshape | solution.py:113
  182.4 3.8 %all-to-all-start.1 = ((bf16[32,30,2048]{2,1,0:T(8,128)(2,1)}), bf16[32,30,2048]{2,1,0:T(8,128)(2,1)}, u32[]{:S(2)}, u32[]{:S(2)}) async-start(bf16[32,30,2048]{2,1,0:T(8,128)(2,1)} %reshape.171), calls=%async_computation.2 | async-start | bytes 8388608 | tf_op jit(solution)/shard_map/all_to_all | solution.py:114
  186.3 93.8 %all-to-all-done.1 = bf16[32,30,2048]{2,1,0:T(8,128)(2,1)} async-done(((bf16[32,30,2048]{2,1,0:T(8,128)(2,1)}), bf16[32,30,2048]{2,1,0:T(8,128)(2,1)}, u32[]{:S(2)}, u32[]{:S(2)}) %all-to-all-start.1) | async-done | bytes 3932192 | tf_op jit(solution)/shard_map/all_to_all | solution.py:114
  280.1 5.1 %reshape.172 = bf16[960,2048]{1,0:T(8,128)(2,1)} reshape(bf16[32,30,2048]{2,1,0:T(8,128)(2,1)} %all-to-all-done.1) | data formatting | bytes 7864320 | tf_op jit(solution)/shard_map/reshape | solution.py:115
  285.2 9.6 %gather_fusion = bf16[640,2048]{1,0:T(8,128)(2,1)} fusion(bf16[960,2048]{1,0:T(8,128)(2,1)} %reshape.172, s32[1024]{0:T(1024)S(1)} %pad_clamp_fusion), kind=kCustom, calls=%fused_computation | custom fusion | bytes 5245440 | tf_op jit(solution)/shard_map/gather | solution.py:115
  294.7 5.8 %reshape.173 = f32[64,10,2048]{2,1,0:T(8,128)} reshape(bf16[640,2048]{1,0:T(8,128)(2,1)} %gather_fusion) | data formatting | bytes 7864320 | tf_op jit(solution)/shard_map/convert_element_type | solution.py:116
  300.5 6.0 %multiply_reduce_fusion = f32[64,2048]{1,0:T(8,128)S(1)} fusion(f32[64,10,2048]{2,1,0:T(8,128)} %reshape.173, f32[64,10]{1,0:T(8,128)S(1)} %copy.25), kind=kLoop, calls=%fused_computation.2 | loop fusion | flops 2490368 | bytes 5769728 | tf_op jit(solution)/shard_map/reduce_sum | solution.py:116
  (49 shorter events, 7.1 us)
Async XLA Ops:
  6.5 161.3 %copy-start = (bf16[1,512,2048]{2,1,0:T(8,128)(2,1)S(1)}, bf16[1,512,2048]{2,1,0:T(8,128)(2,1)}, u32[]{:S(2)}) copy-start(bf16[1,512,2048]{2,1,0:T(8,128)(2,1)} %param.29) | copy-start | bytes 6291460
  6.5 7.4 %copy-start.5 = (bf16[128,1024]{1,0:T(8,128)(2,1)S(1)}, bf16[128,1024]{1,0:T(8,128)(2,1)}, u32[]{:S(2)}) copy-start(bf16[128,1024]{1,0:T(8,128)(2,1)} %param.17) | copy-start | bytes 786436
  6.5 24.6 %reduce-scatter.2.cloned.1.call-start = ((), (), s32[]{:S(2)}) async-start(), calls=%async_computation.3 | async-start | bytes 1572864 | tf_op jit(solution)/shard_map/reduce_scatter | solution.py:81
  15.2 2.8 copy-start.3
  18.0 1.7 copy-start.6
  18.0 13.1 %copy-start.4 = (bf16[64,2048]{1,0:T(8,128)(2,1)S(1)}, bf16[64,2048]{1,0:T(8,128)(2,1)}, u32[]{:S(2)}) copy-start(bf16[64,2048]{1,0:T(8,128)(2,1)} %param.15) | copy-start | bytes 786436
  18.0 14.4 %copy-start.7 = (f32[2048]{0:T(1024)S(1)}, f32[2048]{0:T(1024)}, u32[]{:S(2)}) copy-start(f32[2048]{0:T(1024)} %param.24) | copy-start | bytes 24580
  182.4 3.9 %copy-start.8 = (f32[64,10]{0,1:T(8,128)S(1)}, f32[64,10]{0,1:T(8,128)}, u32[]{:S(2)}) copy-start(f32[64,10]{0,1:T(8,128)} %param.26) | copy-start | bytes 7684
  182.4 97.7 %all-to-all-start.1 = ((bf16[32,30,2048]{2,1,0:T(8,128)(2,1)}), bf16[32,30,2048]{2,1,0:T(8,128)(2,1)}, u32[]{:S(2)}, u32[]{:S(2)}) async-start(bf16[32,30,2048]{2,1,0:T(8,128)(2,1)} %reshape.171), calls=%async_computation.2 | async-start | bytes 8388608 | tf_op jit(solution)/shard_map/all_to_all | solution.py:114
  300.5 6.0 %copy-start.2 = (f32[64,2048]{1,0:T(8,128)S(1)}, f32[64,2048]{1,0:T(8,128)}, u32[]{:S(2)}) copy-start(f32[64,2048]{1,0:T(8,128)} %reduce-scatter.2.cloned.1.call-done) | copy-start | bytes 1572868
  300.5 6.8 %copy-start.1 = (bf16[1,512,2048]{2,1,0:T(8,128)(2,1)S(1)}, bf16[1,512,2048]{2,1,0:T(8,128)(2,1)}, u32[]{:S(2)}) copy-start(bf16[1,512,2048]{2,1,0:T(8,128)(2,1)} %param.29) | copy-start | bytes 6291460
Sparse Core Ops, SparseCore 0:
  19.8 11.2 reduce-scatter.1
where the time goes:
time: 315 us; the launch traced here: 314 us
  waiting for transfers between devices  103 us (33%)
  blocking collectives  99.5 us (32%)
  local copies, waits for them, and re-layouts  58.9 us (19%)
  matrix products  22.9 us (7%)
  between operations  13.6 us (4%)
  other arithmetic  12.8 us (4%)
  starting transfers between devices  3.84 us (1%)
    all_to_all x1, blocking collectives, on_device(): lax.all_to_all(outgoing, ('wide', 'narrow'), split_axis=0, concat_axis=0,...  99.5 us
    all_to_all x1, waiting for transfers between devices, on_device(): lax.all_to_all(produced, ('wide', 'narrow'), split_axis=0, concat_axis=0,...  93.8 us
    scatter x1, local copies, waits for them, and re-layouts, on_device(): jnp.zeros((experts * capacity, width), jnp.bfloat16).at[target]  10.3 us
    gather x1, local copies, waits for them, and re-layouts, on_device(): returned.reshape(experts * capacity, width)[target]  9.55 us
    dot_general x1, matrix products, on_device(): jnp.dot(hidden_act, w_down[0], preferred_element_type=jnp.float32)  9.54 us
    reduce_scatter x1, waiting for transfers between devices, on_device(): lax.psum_scatter(jnp.dot(row_block, o_weight, preferred_element_type=jnp....  8.89 us
    dot_general x1, matrix products, on_device(): jnp.dot(row_block, w_gate[0], preferred_element_type=jnp.float32)  6.31 us
  transfers between devices with their start and end apart: 2, of which 2 were waited for; matrix products, arithmetic and copies ran while one was open for 1% of the time, Pallas kernels for 0%

commit v1 on v0

v1 whole, which is shorter than its diff:
```python
import functools
import math

import jax
import jax.numpy as jnp
from jax import lax
from jax.experimental import pallas as pl
from jax.experimental.pallas import tpu as pltpu
from jax.sharding import PartitionSpec as P

BF16 = jnp.bfloat16
F32 = jnp.float32
LOWEST = -1e30


def _dot(a, b):
    return jnp.dot(a, b, preferred_element_type=F32)


def _dot_t(a, b):
    return lax.dot_general(a, b, (((1,), (1,)), ((), ())), preferred_element_type=F32)


def attention_kernel(
    half_ref,
    draft_len_ref,
    cache_len_ref,
    queries,
    out_gate,
    draft_kv,
    cache_keys,
    cache_values,
    o_weight,
    out_ref,
    q_buf,
    g_buf,
    d_buf,
    k_buf,
    v_buf,
    w_buf,
    attended,
    sems,
):
    half = half_ref[0]
    reqs, context_len, head_size = k_buf.shape
    rows = q_buf.shape[0]
    drafts = rows // reqs
    heads = q_buf.shape[1] // head_size
    row_span = pl.ds(pl.multiple_of(half * rows, rows), rows)
    req_span = pl.ds(half * reqs, reqs)
    copies = [
        pltpu.make_async_copy(queries.at[row_span], q_buf, sems.at[0]),
        pltpu.make_async_copy(cache_keys.at[req_span], k_buf, sems.at[1]),
        pltpu.make_async_copy(draft_kv.at[:, row_span], d_buf, sems.at[2]),
        pltpu.make_async_copy(cache_values.at[req_span], v_buf, sems.at[3]),
        pltpu.make_async_copy(out_gate.at[row_span], g_buf, sems.at[4]),
        pltpu.make_async_copy(o_weight, w_buf, sems.at[5]),
    ]
    for copy in copies:
        copy.start()
    for copy in copies[:3]:
        copy.wait()
    scale = 1.0 / math.sqrt(head_size)
    stacked = heads * drafts
    slot = lax.broadcasted_iota(jnp.int32, (stacked, context_len), 1)
    draft_slot = lax.broadcasted_iota(jnp.int32, (stacked, drafts), 1)
    draft_row = lax.broadcasted_iota(jnp.int32, (heads, drafts, drafts), 1).reshape(stacked, drafts)
    row_index = lax.broadcasted_iota(jnp.int32, (drafts, head_size), 0)
    probs = []
    for r in range(reqs):
        span = slice(r * drafts, (r + 1) * drafts)
        query = jnp.concatenate(
            [q_buf[span, h * head_size : (h + 1) * head_size] for h in range(heads)], axis=0
        )
        cache_len = cache_len_ref[half * reqs + r]
        draft_len = draft_len_ref[half * reqs + r]
        cache_scores = _dot_t(query, k_buf[r]) * scale
        draft_scores = _dot_t(query, d_buf[0, span]) * scale
        cache_scores = jnp.where(slot < cache_len, cache_scores, LOWEST)
        live = (draft_slot <= draft_row) & (draft_slot < draft_len)
        draft_scores = jnp.where(live, draft_scores, LOWEST)
        row_max = jnp.maximum(
            jnp.max(cache_scores, axis=-1, keepdims=True),
            jnp.max(draft_scores, axis=-1, keepdims=True),
        )
        cache_probs = jnp.exp(cache_scores - row_max)
        draft_probs = jnp.exp(draft_scores - row_max)
        denominator = jnp.sum(cache_probs, axis=-1, keepdims=True) + jnp.sum(
            draft_probs, axis=-1, keepdims=True
        )
        probs.append((cache_probs.astype(BF16), draft_probs.astype(BF16), denominator))
    copies[3].wait()
    copies[4].wait()
    for r in range(reqs):
        span = slice(r * drafts, (r + 1) * drafts)
        cache_probs, draft_probs, denominator = probs[r]
        context = _dot(cache_probs, v_buf[r]) + _dot(draft_probs, d_buf[1, span])
        context = context / denominator
        draft_len = draft_len_ref[half * reqs + r]
        for h in range(heads):
            cols = slice(h * head_size, (h + 1) * head_size)
            gate = jax.nn.sigmoid(g_buf[span, cols].astype(F32))
            piece = context[h * drafts : (h + 1) * drafts] * gate
            piece = jnp.where(row_index < draft_len, piece, 0.0)
            attended[span, cols] = piece.astype(BF16)
    copies[5].wait()
    rows_in = attended[...]
    width = out_ref.shape[1]
    tile = min(512, width)
    for c in range(0, width, tile):
        out_ref[:, c : c + tile] = _dot(rows_in, w_buf[:, c : c + tile]).astype(out_ref.dtype)


def attention(half, own_rows, out_dtype, arrays):
    queries, out_gate, draft_kv, cache_keys, cache_values, draft_len, cache_len, o_weight = arrays
    reqs_all, context_len, head_size = cache_keys.shape
    reqs = reqs_all * own_rows // queries.shape[0]
    width = o_weight.shape[1]
    inner = o_weight.shape[0]
    smem = pl.BlockSpec(memory_space=pltpu.SMEM)
    hbm = pl.BlockSpec(memory_space=pl.ANY)
    return pl.pallas_call(
        attention_kernel,
        out_shape=jax.ShapeDtypeStruct((own_rows, width), out_dtype),
        in_specs=[smem] * 3 + [hbm] * 6,
        out_specs=pl.BlockSpec(memory_space=pltpu.VMEM),
        scratch_shapes=[
            pltpu.VMEM((own_rows, inner), BF16),
            pltpu.VMEM((own_rows, inner), BF16),
            pltpu.VMEM((2, own_rows, head_size), BF16),
            pltpu.VMEM((reqs, context_len, head_size), BF16),
            pltpu.VMEM((reqs, context_len, head_size), BF16),
            pltpu.VMEM((inner, width), BF16),
            pltpu.VMEM((own_rows, inner), BF16),
            pltpu.SemaphoreType.DMA((6,)),
        ],
        compiler_params=pltpu.CompilerParams(vmem_limit_bytes=24 * 1024 * 1024),
        cost_estimate=pl.CostEstimate(
            flops=2 * own_rows * inner * (width + 2 * context_len),
            bytes_accessed=2 * inner * width + 4 * reqs * context_len * head_size,
            transcendentals=0,
        ),
    )(
        half.reshape(1),
        draft_len,
        cache_len,
        queries,
        out_gate,
        draft_kv,
        cache_keys,
        cache_values,
        o_weight,
    )


def norm_kernel(hidden_ref, kept_ref, received_ref, gain_ref, residual_ref, top_ref, bottom_ref):
    residual = hidden_ref[...].astype(F32) + kept_ref[...] + received_ref[...].astype(F32)
    spread = jnp.mean(residual * residual, axis=-1, keepdims=True)
    normed = (residual * lax.rsqrt(spread + 1e-06) * gain_ref[...]).astype(BF16)
    residual_ref[...] = residual
    mid = top_ref.shape[0]
    top_ref[...] = normed[:mid]
    bottom_ref[...] = normed[mid:]


def residual_norm(hidden, kept, received, gain):
    rows, width = hidden.shape
    piece = jax.ShapeDtypeStruct((rows // 2, width), BF16)
    return pl.pallas_call(
        norm_kernel,
        out_shape=(jax.ShapeDtypeStruct((rows, width), F32), piece, piece),
        compiler_params=pltpu.CompilerParams(vmem_limit_bytes=16 * 1024 * 1024),
    )(hidden, kept, received, gain.reshape(1, width))


def experts_kernel(pieces, steps, where_ref, *refs):
    rows_in = refs[:pieces]
    weights = refs[pieces : pieces + 4]
    gates, ups, downs = (refs[pieces + 4 + 2 * i : pieces + 6 + 2 * i] for i in range(3))
    outs = refs[pieces + 10 : 2 * pieces + 10]
    rows, total, weight_buf, sems = refs[2 * pieces + 10 :]
    step = pl.program_id(0)
    size = rows_in[0].shape[0]

    @pl.when(step == 0)
    def _():
        copies = [
            pltpu.make_async_copy(
                rows_in[i], rows.at[pl.ds(i * size, size)], sems.at[i]
            )
            for i in range(pieces)
        ]
        for copy in copies:
            copy.start()
        own = weights[0].shape[1]
        for e in range(2):
            for i in range(4):
                table = weights[i][0]
                column = lax.broadcasted_iota(jnp.int32, table.shape, 1)
                chosen = jnp.where(column == where_ref[4 + e], table, 0.0)
                weight_buf[e, i * own : (i + 1) * own, :] = jnp.sum(
                    chosen, axis=1, keepdims=True
                )
        for copy in copies:
            copy.wait()

    for e in range(2):

        @pl.when(step // steps == e)
        def _():
            block = rows[...]
            gate = _dot(block, gates[e][0])
            up = _dot(block, ups[e][0])
            act = (jax.nn.silu(gate) * up * weight_buf[e]).astype(BF16)
            added = _dot(act, downs[e][0])

            @pl.when(step == 0)
            def _():
                total[...] = added

            @pl.when((step > 0) & (step < 2 * steps - 1))
            def _():
                total[...] += added

            @pl.when(step == 2 * steps - 1)
            def _():
                full = total[...] + added
                for i in range(pieces):
                    outs[i][...] = full[i * size : (i + 1) * size].astype(BF16)


def plane_experts(where, rows_in, table, own_weights, other_weights):
    pieces = len(rows_in)
    size, width = rows_in[0].shape
    hidden = own_weights[0].shape[2]
    tile = min(256, hidden)
    steps = hidden // tile
    own, count = table.shape[1:]
    hbm = pl.BlockSpec(memory_space=pl.ANY)

    def at_step(e):
        return lambda t: jnp.clip(t - e * steps, 0, steps - 1)

    def column_spec(e):
        return pl.BlockSpec((1, width, tile), lambda t, where: (0, 0, at_step(e)(t)))

    def row_spec(e):
        return pl.BlockSpec((1, tile, width), lambda t, where: (0, at_step(e)(t), 0))

    def table_spec(i):
        return pl.BlockSpec((1, own, count), lambda t, where: (where[i], 0, 0))

    piece = jax.ShapeDtypeStruct((size, width), BF16)
    weights = [w for pair in zip(own_weights, other_weights) for w in pair]
    return pl.pallas_call(
        functools.partial(experts_kernel, pieces, steps),
        out_shape=(piece,) * pieces,
        grid_spec=pltpu.PrefetchScalarGridSpec(
            num_scalar_prefetch=1,
            grid=(2 * steps,),
            in_specs=[hbm] * pieces
            + [table_spec(i) for i in range(4)]
            + [column_spec(0), column_spec(1)] * 2
            + [row_spec(0), row_spec(1)],
            out_specs=[pl.BlockSpec((size, width), lambda t, where: (0, 0))] * pieces,
            scratch_shapes=[
                pltpu.VMEM((pieces * size, width), BF16),
                pltpu.VMEM((pieces * size, width), F32),
                pltpu.VMEM((2, pieces * size, 1), F32),
                pltpu.SemaphoreType.DMA((pieces,)),
            ],
        ),
        compiler_params=pltpu.CompilerParams(vmem_limit_bytes=40 * 1024 * 1024),
        cost_estimate=pl.CostEstimate(
            flops=12 * pieces * size * width * hidden,
            bytes_accessed=12 * width * hidden,
            transcendentals=0,
        ),
    )(where, *rows_in, *([table] * 4), *weights)


def final_kernel(count, residual_ref, *refs):
    out_ref = refs[-1]
    mid = residual_ref.shape[0] // 2
    for i in range(2):
        span = slice(i * mid, (i + 1) * mid)
        mix = refs[i][...].astype(F32)
        for ref in refs[2 + i : 2 * count : 2]:
            mix = mix + ref[...].astype(F32)
        out_ref[span] = (residual_ref[span] + mix).astype(BF16)


def final_sum(residual, pieces):
    return pl.pallas_call(
        functools.partial(final_kernel, len(pieces)),
        out_shape=jax.ShapeDtypeStruct(residual.shape, BF16),
        compiler_params=pltpu.CompilerParams(vmem_limit_bytes=16 * 1024 * 1024),
    )(residual, *[half for pair in pieces for half in pair])


def add_bf16(*terms):
    total = terms[0].astype(F32)
    for term in terms[1:]:
        total = total + term.astype(F32)
    return total.astype(BF16)


def on_device(
    hidden_in,
    queries,
    out_gate,
    draft_kv,
    cache_keys,
    cache_values,
    draft_len,
    cache_len,
    o_weight,
    norm_gain,
    route_ids,
    route_weights,
    w_gate,
    w_up,
    w_down,
):
    wide = lax.axis_size("wide")
    narrow = lax.axis_size("narrow")
    chip = lax.axis_index("wide")
    core = lax.axis_index("narrow")
    plane = 4
    planes = wide // plane
    assert narrow == 2 and wide % plane == 0
    experts = wide * narrow
    own_rows = hidden_in.shape[0]

    swap = [(0, 1), (1, 0)]
    own_weights = (w_gate, w_up, w_down)
    other_weights = tuple(lax.ppermute(w, "narrow", swap) for w in own_weights)

    chosen = route_ids[:, :, None] == jnp.arange(experts, dtype=jnp.int32)
    table = jnp.sum(jnp.where(chosen, route_weights[:, :, None], 0.0), axis=1)
    table = lax.all_gather(table, "wide", axis=0, tiled=False)

    arrays = (queries, out_gate, draft_kv, cache_keys, cache_values, draft_len, cache_len, o_weight)
    outgoing = attention(1 - core, own_rows, BF16, arrays)
    received = lax.ppermute(outgoing, "narrow", swap)
    kept = attention(core, own_rows, F32, arrays)
    residual, top, bottom = residual_norm(hidden_in, kept, received, norm_gain)

    def across(flip):
        pairs = [(i, i ^ flip) for i in range(wide)]
        return lambda a: lax.ppermute(a, "wide", pairs)

    def shifted(by):
        pairs = [(i, (i + by * plane) % wide) for i in range(wide)]
        return lambda a: lax.ppermute(a, "wide", pairs)

    over_x, over_y = across(1), across(2)
    order = sorted(range(planes), key=lambda s: min(s, planes - s))

    results = []
    for s in order:
        if s:
            mine_t, mine_b = shifted(s)(top), shifted(s)(bottom)
        else:
            mine_t, mine_b = top, bottom
        x_t, y_b = over_x(mine_t), over_y(mine_b)
        x_b, y_t = over_x(mine_b), over_y(mine_t)
        d_t, d_b = over_y(x_t), over_x(y_b)
        first = (chip + (planes - s) * plane) % wide
        own_expert = chip * narrow + core
        where = jnp.stack(
            [first, first ^ 1, first ^ 2, first ^ 3, own_expert, own_expert ^ 1]
        ).astype(jnp.int32)
        made = plane_experts(
            where, [mine_t, mine_b, x_t, x_b, y_t, y_b, d_t, d_b], table, own_weights, other_weights
        )
        mine_t, mine_b, x_t, x_b, y_t, y_b, d_t, d_b = made
        from_x_t, from_y_b = over_x(x_t), over_y(y_b)
        y_t = add_bf16(y_t, over_x(d_t))
        x_b = add_bf16(x_b, over_y(d_b))
        from_y_t, from_x_b = over_y(y_t), over_x(x_b)
        if s:
            sum_t = add_bf16(mine_t, from_x_t, from_y_t)
            sum_b = add_bf16(mine_b, from_x_b, from_y_b)
            results.append((shifted(planes - s)(sum_t), shifted(planes - s)(sum_b)))
        else:
            results += [(mine_t, mine_b), (from_x_t, from_x_b), (from_y_t, from_y_b)]
    return final_sum(residual, results)


def solution(mesh):
    placed = (
        P(("rep", "wide", "narrow"), None),
        P(("rep", "wide"), "narrow"),
        P(("rep", "wide"), "narrow"),
        P(None, ("rep", "wide"), None),
        P(("rep", "wide"), None, None),
        P(("rep", "wide"), None, None),
        P(("rep", "wide")),
        P(("rep", "wide")),
        P("narrow", None),
        P(),
        P(("rep", "wide", "narrow"), None),
        P(("rep", "wide", "narrow"), None),
        P(("wide", "narrow"), None, None),
        P(("wide", "narrow"), None, None),
        P(("wide", "narrow"), None, None),
    )
    return jax.shard_map(
        on_device,
        mesh=mesh,
        in_specs=placed,
        out_specs=P(("rep", "wide", "narrow"), None),
        check_vma=False,
    )
```

time: 315 us -> 257 us (0.82)
  starting transfers between devices: 3.84 us -> 70.5 us
  blocking collectives: 99.5 us -> 43.2 us
  Pallas kernels: 0 us -> 47.7 us
  local copies, waits for them, and re-layouts: 58.9 us -> 21.8 us
  waiting for transfers between devices: 103 us -> 71.8 us
  matrix products: 22.9 us -> 0 us
  between operations: 13.6 us -> 0.47 us
  other arithmetic: 12.8 us -> 0.6 us
    all_to_all x1 -> x0, blocking collectives: 99.5 us -> none  [on_device(): lax.all_to_all(outgoing, ('wide', 'narrow'), split_axis=0, concat_axis=0,...]
    all_to_all x1 -> x0, waiting for transfers between devices: 93.8 us -> none  [on_device(): lax.all_to_all(produced, ('wide', 'narrow'), split_axis=0, concat_axis=0,...]
    ppermute x0 -> x64, waiting for transfers between devices: none -> 71.8 us  [the longest x48 46.7 us: across(): return lambda a: lax.ppermute(a, 'wide', pairs)]
    ppermute x0 -> x64, starting transfers between devices: none -> 70.5 us  [the longest x48 51 us: across(): return lambda a: lax.ppermute(a, 'wide', pairs)]
    pallas_call x0 -> x8, Pallas kernels: none -> 47.7 us  [the longest x4 40.7 us: plane_experts(): pl.pallas_call(functools.partial(experts_kernel, pieces, steps), out_shap...]
    all_gather x0 -> x1, blocking collectives: none -> 43.2 us  [on_device(): table = lax.all_gather(table, 'wide', axis=0, tiled=False)]
    reshape x7 -> x0, local copies, waits for them, and re-layouts: 28 us -> none  [the longest x1 5.53 us: on_device(): source_rows = jnp.repeat(normed, top_count, axis=0)]
    dot_general x7 -> x0, matrix products: 22.9 us -> none  [the longest x1 9.54 us: on_device(): jnp.dot(hidden_act, w_down[0], preferred_element_type=jnp.float32)]
  transfers between devices with their start and end apart: 2 -> 64, of which waited for: 2 -> 27; matrix products, arithmetic and copies ran while one was open for 1% -> 1% of each run, Pallas kernels for 0% -> 18%
where the time goes in v1:
time: 257 us; the launch traced here: 256 us
  waiting for transfers between devices  71.8 us (28%)
  starting transfers between devices  70.5 us (27%)
  Pallas kernels  47.7 us (19%)
  blocking collectives  43.2 us (17%)
  local copies, waits for them, and re-layouts  21.8 us (8%)
    ppermute x48, starting transfers between devices, across(): return lambda a: lax.ppermute(a, 'wide', pairs)  51 us
    ppermute x48, waiting for transfers between devices, across(): return lambda a: lax.ppermute(a, 'wide', pairs)  46.7 us
    all_gather x1, blocking collectives, on_device(): table = lax.all_gather(table, 'wide', axis=0, tiled=False)  43.2 us
    pallas_call x4, Pallas kernels, plane_experts(): pl.pallas_call(functools.partial(experts_kernel, pieces, steps), out_shap...  40.7 us
    ppermute x12, waiting for transfers between devices, shifted(): return lambda a: lax.ppermute(a, 'wide', pairs)  25.1 us
    unnamed x88, local copies, waits for them, and re-layouts  20.3 us
    ppermute x12, starting transfers between devices, shifted(): return lambda a: lax.ppermute(a, 'wide', pairs)  18.4 us
    pallas_call x2, Pallas kernels, attention(): pl.pallas_call(attention_kernel, out_shape=jax.ShapeDtypeStruct((own_rows...  5.84 us
  transfers between devices with their start and end apart: 64, of which 27 were waited for; matrix products, arithmetic and copies ran while one was open for 1% of the time, Pallas kernels for 18%

profile of v1, /device:TPU:0, one launch (start us, length us, event | category | flops | bytes accessed | tf_op | source)
XLA Modules:
  0.0 255.9 jit_solution(10649900291399341439)
XLA Ops:
  9.7 2.9 %shard_map.146 = bf16[64,2048]{1,0:T(8,128)(2,1)S(1)} custom-call(s32[1]{0:T(128)} %bitcast.1.half_ref, s32[8]{0:T(128)S(1)} %copy-done.38, s32[8]{0:T(128)S(1)} %copy-done.40, bf16[128,1024]{1,0:T(8,128)(2,1)S(1)} %copy-done.10, bf16[128,1024]{1,0:T(8,128)(2,1)S(1)} %copy-done.12, bf16[2,128,256]{2,1,0:T(8,128)(2,1)S(1)} %copy-done.13, ...), custom_call_target="tpu_custom_call" | custom-call | flops 335544320 | bytes 5242880 | tf_op jit(solution)/shard_map/pallas_call | solution.py:122
  12.9 2.9 %shard_map.145.kept_ref = f32[64,2048]{1,0:T(8,128)S(1)} custom-call(s32[1]{0:T(128)} %bitcast.half_ref, s32[8]{0:T(128)S(1)} %copy-done.39, s32[8]{0:T(128)S(1)} %copy-done.41, bf16[128,1024]{1,0:T(8,128)(2,1)S(1)} %copy-done.11, bf16[128,1024]{1,0:T(8,128)(2,1)S(1)} %copy-done.12, bf16[2,128,256]{2,1,0:T(8,128)(2,1)S(1)} %copy-done.13, ...), custom_call_target="tpu_custom_call" | custom-call | flops 335544320 | bytes 5242880 | tf_op jit(solution)/shard_map/pallas_call | solution.py:122
  16.0 4.1 %collective-permute-start.48 = (bf16[32,2048]{1,0:T(8,128)(2,1)S(1)}, bf16[32,2048]{1,0:T(8,128)(2,1)S(1)}, u32[]{:S(2)}, u32[]{:S(2)}) collective-permute-start(bf16[32,2048]{1,0:T(8,128)(2,1)S(1)} %get-tuple-element.41.refs_0_), channel_id=1, source_target_pairs={{0,16},{2,18},{4,20},{6,22},{8,24},{10,26},{12,28},{14,30},{16,0},... | collective-permute-start | bytes 393224 | tf_op jit(solution)/shard_map/ppermute | solution.py:355
  20.2 9.8 %collective-permute-done.48.refs_0_ = bf16[32,2048]{1,0:T(8,128)(2,1)S(1)} collective-permute-done((bf16[32,2048]{1,0:T(8,128)(2,1)S(1)}, bf16[32,2048]{1,0:T(8,128)(2,1)S(1)}, u32[]{:S(2)}, u32[]{:S(2)}) %collective-permute-start.48) | collective-permute-done | bytes 131104 | tf_op jit(solution)/shard_map/ppermute | solution.py:355
  30.1 3.0 %collective-permute-start.32 = (bf16[32,2048]{1,0:T(8,128)(2,1)S(1)}, bf16[32,2048]{1,0:T(8,128)(2,1)S(1)}, u32[]{:S(2)}, u32[]{:S(2)}) collective-permute-start(bf16[32,2048]{1,0:T(8,128)(2,1)S(1)} %get-tuple-element.41.refs_0_), channel_id=1, source_target_pairs={{0,24},{2,26},{4,28},{6,30},{8,0},{10,2},{12,4},{14,6},{16,8},{18,... | collective-permute-start | bytes 393224 | tf_op jit(solution)/shard_map/ppermute | solution.py:355
  36.0 3.8 %collective-permute-done.33.refs_1_ = bf16[32,2048]{1,0:T(8,128)(2,1)S(1)} collective-permute-done((bf16[32,2048]{1,0:T(8,128)(2,1)S(1)}, bf16[32,2048]{1,0:T(8,128)(2,1)S(1)}, u32[]{:S(2)}, u32[]{:S(2)}) %collective-permute-start.33) | collective-permute-done | bytes 131104 | tf_op jit(solution)/shard_map/ppermute | solution.py:355
  39.7 3.5 %collective-permute-done.16.refs_0_ = bf16[32,2048]{1,0:T(8,128)(2,1)S(1)} collective-permute-done((bf16[32,2048]{1,0:T(8,128)(2,1)S(1)}, bf16[32,2048]{1,0:T(8,128)(2,1)S(1)}, u32[]{:S(2)}, u32[]{:S(2)}) %collective-permute-start.16) | collective-permute-done | bytes 131104 | tf_op jit(solution)/shard_map/ppermute | solution.py:355
  68.1 2.8 %collective-permute-done.35.refs_3_ = bf16[32,2048]{1,0:T(8,128)(2,1)S(1)} collective-permute-done((bf16[32,2048]{1,0:T(8,128)(2,1)S(1)}, bf16[32,2048]{1,0:T(8,128)(2,1)S(1)}, u32[]{:S(2)}, u32[]{:S(2)}) %collective-permute-start.35) | collective-permute-done | bytes 131104 | tf_op jit(solution)/shard_map/ppermute | solution.py:351
  72.3 43.2 %all-gather.1 = f32[16,64,32]{1,2,0:T(8,128)} all-gather(f32[1,64,32]{1,2,0:T(8,128)S(1)} %bitcast.23), channel_id=2, replica_groups=mesh['rep'=1,'wide'=16,'narrow'=2] {'wide'}, dimensions={0}, use_global_device_ids=true | all-gather | bytes 139264 | tf_op jit(solution)/shard_map/all_gather | solution.py:341
  128.0 10.1 %shard_map.151 = (bf16[32,2048]{1,0:T(8,128)(2,1)S(1)}, bf16[32,2048]{1,0:T(8,128)(2,1)S(1)}, bf16[32,2048]{1,0:T(8,128)(2,1)S(1)}, bf16[32,2048]{1,0:T(8,128)(2...) custom-call(s32[6]{0:T(128)S(1)} %stack.93.where_ref, ...), custom_call_target="tpu_custom_call" | custom-call | flops 3221225472 | bytes 12582912 | tf_op jit(solution)/shard_map/pallas_call | solution.py:255
  144.2 10.0 %shard_map.150 = (bf16[32,2048]{1,0:T(8,128)(2,1)S(1)}, bf16[32,2048]{1,0:T(8,128)(2,1)S(1)}, bf16[32,2048]{1,0:T(8,128)(2,1)S(1)}, bf16[32,2048]{1,0:T(8,128)(2...) custom-call(s32[6]{0:T(128)S(1)} %stack.88.where_ref, ...), custom_call_target="tpu_custom_call" | custom-call | flops 3221225472 | bytes 12582912 | tf_op jit(solution)/shard_map/pallas_call | solution.py:255
  158.5 10.3 %shard_map.149 = (bf16[32,2048]{1,0:T(8,128)(2,1)S(1)}, bf16[32,2048]{1,0:T(8,128)(2,1)S(1)}, bf16[32,2048]{1,0:T(8,128)(2,1)S(1)}, bf16[32,2048]{1,0:T(8,128)(2...) custom-call(s32[6]{0:T(128)S(1)} %stack.83.where_ref, ...), custom_call_target="tpu_custom_call" | custom-call | flops 3221225472 | bytes 12582912 | tf_op jit(solution)/shard_map/pallas_call | solution.py:255
  173.0 10.2 %shard_map.148 = (bf16[32,2048]{1,0:T(8,128)(2,1)S(1)}, bf16[32,2048]{1,0:T(8,128)(2,1)S(1)}, bf16[32,2048]{1,0:T(8,128)(2,1)S(1)}, bf16[32,2048]{1,0:T(8,128)(2...) custom-call(s32[6]{0:T(128)S(1)} %stack.78.where_ref, ...), custom_call_target="tpu_custom_call" | custom-call | flops 3221225472 | bytes 12582912 | tf_op jit(solution)/shard_map/pallas_call | solution.py:255
  187.2 4.0 %collective-permute-done.41 = bf16[32,2048]{1,0:T(8,128)(2,1)S(1)} collective-permute-done((bf16[32,2048]{1,0:T(8,128)(2,1)S(1)}, bf16[32,2048]{1,0:T(8,128)(2,1)S(1)}, u32[]{:S(2)}, u32[]{:S(2)}) %collective-permute-start.41) | collective-permute-done | bytes 131104 | tf_op jit(solution)/shard_map/ppermute | solution.py:351
  191.7 4.8 %collective-permute-done.28 = bf16[32,2048]{1,0:T(8,128)(2,1)S(1)} collective-permute-done((bf16[32,2048]{1,0:T(8,128)(2,1)S(1)}, bf16[32,2048]{1,0:T(8,128)(2,1)S(1)}, u32[]{:S(2)}, u32[]{:S(2)}) %collective-permute-start.28) | collective-permute-done | bytes 131104 | tf_op jit(solution)/shard_map/ppermute | solution.py:351
  197.4 5.0 %collective-permute-done.25 = bf16[32,2048]{1,0:T(8,128)(2,1)S(1)} collective-permute-done((bf16[32,2048]{1,0:T(8,128)(2,1)S(1)}, bf16[32,2048]{1,0:T(8,128)(2,1)S(1)}, u32[]{:S(2)}, u32[]{:S(2)}) %collective-permute-start.25) | collective-permute-done | bytes 131104 | tf_op jit(solution)/shard_map/ppermute | solution.py:351
  203.8 4.8 %collective-permute-done.13 = bf16[32,2048]{1,0:T(8,128)(2,1)S(1)} collective-permute-done((bf16[32,2048]{1,0:T(8,128)(2,1)S(1)}, bf16[32,2048]{1,0:T(8,128)(2,1)S(1)}, u32[]{:S(2)}, u32[]{:S(2)}) %collective-permute-start.13) | collective-permute-done | bytes 131104 | tf_op jit(solution)/shard_map/ppermute | solution.py:351
  209.0 5.1 %collective-permute-done.11 = bf16[32,2048]{1,0:T(8,128)(2,1)S(1)} collective-permute-done((bf16[32,2048]{1,0:T(8,128)(2,1)S(1)}, bf16[32,2048]{1,0:T(8,128)(2,1)S(1)}, u32[]{:S(2)}, u32[]{:S(2)}) %collective-permute-start.11) | collective-permute-done | bytes 131104 | tf_op jit(solution)/shard_map/ppermute | solution.py:351
  215.9 3.2 %collective-permute-done.61 = bf16[32,2048]{1,0:T(8,128)(2,1)S(1)} collective-permute-done((bf16[32,2048]{1,0:T(8,128)(2,1)S(1)}, bf16[32,2048]{1,0:T(8,128)(2,1)S(1)}, u32[]{:S(2)}, u32[]{:S(2)}) %collective-permute-start.61) | collective-permute-done | bytes 131104 | tf_op jit(solution)/shard_map/ppermute | solution.py:351
  220.8 3.2 %collective-permute-done.58 = bf16[32,2048]{1,0:T(8,128)(2,1)S(1)} collective-permute-done((bf16[32,2048]{1,0:T(8,128)(2,1)S(1)}, bf16[32,2048]{1,0:T(8,128)(2,1)S(1)}, u32[]{:S(2)}, u32[]{:S(2)}) %collective-permute-start.58) | collective-permute-done | bytes 131104 | tf_op jit(solution)/shard_map/ppermute | solution.py:351
  226.2 2.8 %collective-permute-done.45 = bf16[32,2048]{1,0:T(8,128)(2,1)S(1)} collective-permute-done((bf16[32,2048]{1,0:T(8,128)(2,1)S(1)}, bf16[32,2048]{1,0:T(8,128)(2,1)S(1)}, u32[]{:S(2)}, u32[]{:S(2)}) %collective-permute-start.45) | collective-permute-done | bytes 131104 | tf_op jit(solution)/shard_map/ppermute | solution.py:351
  235.7 3.2 %collective-permute-done.29 = bf16[32,2048]{1,0:T(8,128)(2,1)S(1)} collective-permute-done((bf16[32,2048]{1,0:T(8,128)(2,1)S(1)}, bf16[32,2048]{1,0:T(8,128)(2,1)S(1)}, u32[]{:S(2)}, u32[]{:S(2)}) %collective-permute-start.29) | collective-permute-done | bytes 131104 | tf_op jit(solution)/shard_map/ppermute | solution.py:351
  240.8 3.0 %collective-permute-start.59 = (bf16[32,2048]{1,0:T(8,128)(2,1)S(1)}, bf16[32,2048]{1,0:T(8,128)(2,1)S(1)}, u32[]{:S(2)}, u32[]{:S(2)}) collective-permute-start(bf16[32,2048]{1,0:T(8,128)(2,1)S(1)} %add_convert_fusion.2), channel_id=1, source_target_pairs={{0,16},{2,18},{4,20},{6,22},{8,24},{10,26},{12,28},{14,30},{16,0},... | collective-permute-start | bytes 393224 | tf_op jit(solution)/shard_map/ppermute | solution.py:355
  244.5 3.3 %collective-permute-start.31 = (bf16[32,2048]{1,0:T(8,128)(2,1)S(1)}, bf16[32,2048]{1,0:T(8,128)(2,1)S(1)}, u32[]{:S(2)}, u32[]{:S(2)}) collective-permute-start(bf16[32,2048]{1,0:T(8,128)(2,1)S(1)} %add_convert_fusion.8), channel_id=1, source_target_pairs={{0,24},{2,26},{4,28},{6,30},{8,0},{10,2},{12,4},{14,6},{16,8},{18,... | collective-permute-start | bytes 393224 | tf_op jit(solution)/shard_map/ppermute | solution.py:355
  (221 shorter events, 96.3 us)
Async XLA Ops:
  0.0 117.1 %collective-permute-start.7 = (bf16[1,2048,512]{2,1,0:T(8,128)(2,1)}, bf16[1,2048,512]{2,1,0:T(8,128)(2,1)}, u32[]{:S(2)}, u32[]{:S(2)}) collective-permute-start(bf16[1,2048,512]{2,1,0:T(8,128)(2,1)} %refs_12_.7), channel_id=1, source_target_pairs={{0,1},{1,0},{2,3},{3,2},{4,5},{5,4},{6,7},{7,6},{8,9},{9,8},{10,11... | collective-permute-start | bytes 6291464 | tf_op jit(solution)/shard_map/ppermute | solution.py:337
  0.5 118.7 %collective-permute-start.8 = (bf16[1,2048,512]{2,1,0:T(8,128)(2,1)}, bf16[1,2048,512]{2,1,0:T(8,128)(2,1)}, u32[]{:S(2)}, u32[]{:S(2)}) collective-permute-start(bf16[1,2048,512]{2,1,0:T(8,128)(2,1)} %refs_14_.7), channel_id=1, source_target_pairs={{0,1},{1,0},{2,3},{3,2},{4,5},{5,4},{6,7},{7,6},{8,9},{9,8},{10,11... | collective-permute-start | bytes 6291464 | tf_op jit(solution)/shard_map/ppermute | solution.py:337
  0.5 118.7 %collective-permute-start.9 = (bf16[1,512,2048]{2,1,0:T(8,128)(2,1)}, bf16[1,512,2048]{2,1,0:T(8,128)(2,1)}, u32[]{:S(2)}, u32[]{:S(2)}) collective-permute-start(bf16[1,512,2048]{2,1,0:T(8,128)(2,1)} %refs_16_.7), channel_id=1, source_target_pairs={{0,1},{1,0},{2,3},{3,2},{4,5},{5,4},{6,7},{7,6},{8,9},{9,8},{10,11... | collective-permute-start | bytes 6291464 | tf_op jit(solution)/shard_map/ppermute | solution.py:337
  67.1 49.9 %collective-permute-start.54 = (bf16[32,2048]{1,0:T(8,128)(2,1)}, bf16[32,2048]{1,0:T(8,128)(2,1)}, u32[]{:S(2)}, u32[]{:S(2)}) collective-permute-start(bf16[32,2048]{1,0:T(8,128)(2,1)} %collective-permute-done.50.refs_2_), channel_id=1, source_target_pairs={{0,4},{2,6},{4,0},{6,2},{8,12},{10,14},{12,8},{14,10},{16,20},{18,... | collective-permute-start | bytes 393224 | tf_op jit(solution)/shard_map/ppermute | solution.py:351
  71.6 45.4 %collective-permute-start.55 = (bf16[32,2048]{1,0:T(8,128)(2,1)}, bf16[32,2048]{1,0:T(8,128)(2,1)}, u32[]{:S(2)}, u32[]{:S(2)}) collective-permute-start(bf16[32,2048]{1,0:T(8,128)(2,1)} %collective-permute-done.53.refs_5_), channel_id=1, source_target_pairs={{0,2},{2,0},{4,6},{6,4},{8,10},{10,8},{12,14},{14,12},{16,18},{18,... | collective-permute-start | bytes 393224 | tf_op jit(solution)/shard_map/ppermute | solution.py:351
  117.0 21.2 %collective-permute-start.36 = (bf16[32,2048]{1,0:T(8,128)(2,1)}, bf16[32,2048]{1,0:T(8,128)(2,1)S(1)}, u32[]{:S(2)}, u32[]{:S(2)}) collective-permute-start(bf16[32,2048]{1,0:T(8,128)(2,1)} %copy-done.19), channel_id=1, source_target_pairs={{0,4},{2,6},{4,0},{6,2},{8,12},{10,14},{12,8},{14,10},{16,20},{18,... | collective-permute-start | bytes 393224 | tf_op jit(solution)/shard_map/ppermute | solution.py:351
  117.0 23.1 %collective-permute-start.18 = (bf16[32,2048]{1,0:T(8,128)(2,1)}, bf16[32,2048]{1,0:T(8,128)(2,1)S(1)}, u32[]{:S(2)}, u32[]{:S(2)}) collective-permute-start(bf16[32,2048]{1,0:T(8,128)(2,1)} %copy-done.15), channel_id=1, source_target_pairs={{0,2},{2,0},{4,6},{6,4},{8,10},{10,8},{12,14},{14,12},{16,18},{18,... | collective-permute-start | bytes 393224 | tf_op jit(solution)/shard_map/ppermute | solution.py:351
  117.1 23.1 %collective-permute-start.21 = (bf16[32,2048]{1,0:T(8,128)(2,1)}, bf16[32,2048]{1,0:T(8,128)(2,1)S(1)}, u32[]{:S(2)}, u32[]{:S(2)}) collective-permute-start(bf16[32,2048]{1,0:T(8,128)(2,1)} %copy-done.17), channel_id=1, source_target_pairs={{0,4},{2,6},{4,0},{6,2},{8,12},{10,14},{12,8},{14,10},{16,20},{18,... | collective-permute-start | bytes 393224 | tf_op jit(solution)/shard_map/ppermute | solution.py:351
  119.1 21.2 %collective-permute-start.38 = (bf16[32,2048]{1,0:T(8,128)(2,1)}, bf16[32,2048]{1,0:T(8,128)(2,1)S(1)}, u32[]{:S(2)}, u32[]{:S(2)}) collective-permute-start(bf16[32,2048]{1,0:T(8,128)(2,1)} %copy-done.27), channel_id=1, source_target_pairs={{0,4},{2,6},{4,0},{6,2},{8,12},{10,14},{12,8},{14,10},{16,20},{18,... | collective-permute-start | bytes 393224 | tf_op jit(solution)/shard_map/ppermute | solution.py:351
  119.2 23.1 %collective-permute-start.39 = (bf16[32,2048]{1,0:T(8,128)(2,1)}, bf16[32,2048]{1,0:T(8,128)(2,1)S(1)}, u32[]{:S(2)}, u32[]{:S(2)}) collective-permute-start(bf16[32,2048]{1,0:T(8,128)(2,1)} %copy-done.29), channel_id=1, source_target_pairs={{0,2},{2,0},{4,6},{6,4},{8,10},{10,8},{12,14},{14,12},{16,18},{18,... | collective-permute-start | bytes 393224 | tf_op jit(solution)/shard_map/ppermute | solution.py:351
  138.1 16.1 %collective-permute-start.4 = (bf16[32,2048]{1,0:T(8,128)(2,1)S(1)}, bf16[32,2048]{1,0:T(8,128)(2,1)S(1)}, u32[]{:S(2)}, u32[]{:S(2)}) collective-permute-start(bf16[32,2048]{1,0:T(8,128)(2,1)S(1)} %get-tuple-element.42.refs_1_), channel_id=1, source_target_pairs={{0,4},{2,6},{4,0},{6,2},{8,12},{10,14},{12,8},{14,10},{16,20},{18,... | collective-permute-start | bytes 393224 | tf_op jit(solution)/shard_map/ppermute | solution.py:351
  140.4 16.1 %collective-permute-start.22 = (bf16[32,2048]{1,0:T(8,128)(2,1)S(1)}, bf16[32,2048]{1,0:T(8,128)(2,1)S(1)}, u32[]{:S(2)}, u32[]{:S(2)}) collective-permute-start(bf16[32,2048]{1,0:T(8,128)(2,1)S(1)} %collective-permute-done.18.refs_2_), channel_id=1, source_target_pairs={{0,4},{2,6},{4,0},{6,2},{8,12},{10,14},{12,8},{14,10},{16,20},{18,... | collective-permute-start | bytes 393224 | tf_op jit(solution)/shard_map/ppermute | solution.py:351
  142.3 16.1 %collective-permute-start.23 = (bf16[32,2048]{1,0:T(8,128)(2,1)S(1)}, bf16[32,2048]{1,0:T(8,128)(2,1)S(1)}, u32[]{:S(2)}, u32[]{:S(2)}) collective-permute-start(bf16[32,2048]{1,0:T(8,128)(2,1)S(1)} %collective-permute-done.21.refs_5_), channel_id=1, source_target_pairs={{0,2},{2,0},{4,6},{6,4},{8,10},{10,8},{12,14},{14,12},{16,18},{18,... | collective-permute-start | bytes 393224 | tf_op jit(solution)/shard_map/ppermute | solution.py:351
  154.4 16.1 %collective-permute-start.3 = (bf16[32,2048]{1,0:T(8,128)(2,1)S(1)}, bf16[32,2048]{1,0:T(8,128)(2,1)S(1)}, u32[]{:S(2)}, u32[]{:S(2)}) collective-permute-start(bf16[32,2048]{1,0:T(8,128)(2,1)S(1)} %get-tuple-element.41.refs_0_), channel_id=1, source_target_pairs={{0,4},{2,6},{4,0},{6,2},{8,12},{10,14},{12,8},{14,10},{16,20},{18,... | collective-permute-start | bytes 393224 | tf_op jit(solution)/shard_map/ppermute | solution.py:351
  154.5 16.1 %collective-permute-start.5 = (bf16[32,2048]{1,0:T(8,128)(2,1)S(1)}, bf16[32,2048]{1,0:T(8,128)(2,1)S(1)}, u32[]{:S(2)}, u32[]{:S(2)}) collective-permute-start(bf16[32,2048]{1,0:T(8,128)(2,1)S(1)} %collective-permute-done.1.refs_2_), channel_id=1, source_target_pairs={{0,4},{2,6},{4,0},{6,2},{8,12},{10,14},{12,8},{14,10},{16,20},{18,... | collective-permute-start | bytes 393224 | tf_op jit(solution)/shard_map/ppermute | solution.py:351
  156.5 16.1 %collective-permute-start.6 = (bf16[32,2048]{1,0:T(8,128)(2,1)S(1)}, bf16[32,2048]{1,0:T(8,128)(2,1)S(1)}, u32[]{:S(2)}, u32[]{:S(2)}) collective-permute-start(bf16[32,2048]{1,0:T(8,128)(2,1)S(1)} %collective-permute-done.4.refs_5_), channel_id=1, source_target_pairs={{0,2},{2,0},{4,6},{6,4},{8,10},{10,8},{12,14},{14,12},{16,18},{18,... | collective-permute-start | bytes 393224 | tf_op jit(solution)/shard_map/ppermute | solution.py:351
  158.4 24.8 %collective-permute-start.60 = (bf16[32,2048]{1,0:T(8,128)(2,1)S(1)}, bf16[32,2048]{1,0:T(8,128)(2,1)S(1)}, u32[]{:S(2)}, u32[]{:S(2)}) collective-permute-start(bf16[32,2048]{1,0:T(8,128)(2,1)S(1)} %get-tuple-element.73), channel_id=1, source_target_pairs={{0,4},{2,6},{4,0},{6,2},{8,12},{10,14},{12,8},{14,10},{16,20},{18,... | collective-permute-start | bytes 393224 | tf_op jit(solution)/shard_map/ppermute | solution.py:351
  168.9 46.5 %collective-permute-start.62 = (bf16[32,2048]{1,0:T(8,128)(2,1)S(1)}, bf16[32,2048]{1,0:T(8,128)(2,1)S(1)}, u32[]{:S(2)}, u32[]{:S(2)}) collective-permute-start(bf16[32,2048]{1,0:T(8,128)(2,1)S(1)} %get-tuple-element.74), channel_id=1, source_target_pairs={{0,4},{2,6},{4,0},{6,2},{8,12},{10,14},{12,8},{14,10},{16,20},{18,... | collective-permute-start | bytes 393224 | tf_op jit(solution)/shard_map/ppermute | solution.py:351
  170.7 48.9 %collective-permute-start.56 = (bf16[32,2048]{1,0:T(8,128)(2,1)S(1)}, bf16[32,2048]{1,0:T(8,128)(2,1)S(1)}, u32[]{:S(2)}, u32[]{:S(2)}) collective-permute-start(bf16[32,2048]{1,0:T(8,128)(2,1)S(1)} %get-tuple-element.68), channel_id=1, source_target_pairs={{0,2},{2,0},{4,6},{6,4},{8,10},{10,8},{12,14},{14,12},{16,18},{18,... | collective-permute-start | bytes 393224 | tf_op jit(solution)/shard_map/ppermute | solution.py:351
  183.3 42.0 %collective-permute-start.46 = (bf16[32,2048]{1,0:T(8,128)(2,1)S(1)}, bf16[32,2048]{1,0:T(8,128)(2,1)S(1)}, u32[]{:S(2)}, u32[]{:S(2)}) collective-permute-start(bf16[32,2048]{1,0:T(8,128)(2,1)S(1)} %get-tuple-element.66), channel_id=1, source_target_pairs={{0,4},{2,6},{4,0},{6,2},{8,12},{10,14},{12,8},{14,10},{16,20},{18,... | collective-permute-start | bytes 393224 | tf_op jit(solution)/shard_map/ppermute | solution.py:351
  185.2 44.3 %collective-permute-start.40 = (bf16[32,2048]{1,0:T(8,128)(2,1)S(1)}, bf16[32,2048]{1,0:T(8,128)(2,1)S(1)}, u32[]{:S(2)}, u32[]{:S(2)}) collective-permute-start(bf16[32,2048]{1,0:T(8,128)(2,1)S(1)} %get-tuple-element.60), channel_id=1, source_target_pairs={{0,2},{2,0},{4,6},{6,4},{8,10},{10,8},{12,14},{14,12},{16,18},{18,... | collective-permute-start | bytes 393224 | tf_op jit(solution)/shard_map/ppermute | solution.py:351
  215.4 19.9 %collective-permute-start.30 = (bf16[32,2048]{1,0:T(8,128)(2,1)S(1)}, bf16[32,2048]{1,0:T(8,128)(2,1)S(1)}, u32[]{:S(2)}, u32[]{:S(2)}) collective-permute-start(bf16[32,2048]{1,0:T(8,128)(2,1)S(1)} %get-tuple-element.58), channel_id=1, source_target_pairs={{0,4},{2,6},{4,0},{6,2},{8,12},{10,14},{12,8},{14,10},{16,20},{18,... | collective-permute-start | bytes 393224 | tf_op jit(solution)/shard_map/ppermute | solution.py:351
  219.6 19.9 %collective-permute-start.24 = (bf16[32,2048]{1,0:T(8,128)(2,1)S(1)}, bf16[32,2048]{1,0:T(8,128)(2,1)S(1)}, u32[]{:S(2)}, u32[]{:S(2)}) collective-permute-start(bf16[32,2048]{1,0:T(8,128)(2,1)S(1)} %get-tuple-element.52), channel_id=1, source_target_pairs={{0,2},{2,0},{4,6},{6,4},{8,10},{10,8},{12,14},{14,12},{16,18},{18,... | collective-permute-start | bytes 393224 | tf_op jit(solution)/shard_map/ppermute | solution.py:351
  225.3 15.5 %collective-permute-start.10 = (bf16[32,2048]{1,0:T(8,128)(2,1)S(1)}, bf16[32,2048]{1,0:T(8,128)(2,1)S(1)}, u32[]{:S(2)}, u32[]{:S(2)}) collective-permute-start(bf16[32,2048]{1,0:T(8,128)(2,1)S(1)} %get-tuple-element.45), channel_id=1, source_target_pairs={{0,2},{2,0},{4,6},{6,4},{8,10},{10,8},{12,14},{14,12},{16,18},{18,... | collective-permute-start | bytes 393224 | tf_op jit(solution)/shard_map/ppermute | solution.py:351
  (84 other events, 745.7 us)

commit v2 on v1

v2 whole, which is shorter than its diff:
```python
import functools
import math

import jax
import jax.numpy as jnp
from jax import lax
from jax.experimental import pallas as pl
from jax.experimental.pallas import tpu as pltpu
from jax.sharding import PartitionSpec as P

BF16 = jnp.bfloat16
F32 = jnp.float32
LOWEST = -1e30


def _dot(a, b):
    return jnp.dot(a, b, preferred_element_type=F32)


def _dot_t(a, b):
    return lax.dot_general(a, b, (((1,), (1,)), ((), ())), preferred_element_type=F32)


def attention_kernel(
    half_ref,
    draft_len_ref,
    cache_len_ref,
    queries,
    out_gate,
    draft_kv,
    cache_keys,
    cache_values,
    o_weight,
    out_ref,
    q_buf,
    g_buf,
    d_buf,
    k_buf,
    v_buf,
    w_buf,
    attended,
    sems,
):
    half = half_ref[0]
    reqs, context_len, head_size = k_buf.shape
    rows = q_buf.shape[0]
    drafts = rows // reqs
    heads = q_buf.shape[1] // head_size
    row_span = pl.ds(pl.multiple_of(half * rows, rows), rows)
    req_span = pl.ds(half * reqs, reqs)
    copies = [
        pltpu.make_async_copy(queries.at[row_span], q_buf, sems.at[0]),
        pltpu.make_async_copy(cache_keys.at[req_span], k_buf, sems.at[1]),
        pltpu.make_async_copy(draft_kv.at[:, row_span], d_buf, sems.at[2]),
        pltpu.make_async_copy(cache_values.at[req_span], v_buf, sems.at[3]),
        pltpu.make_async_copy(out_gate.at[row_span], g_buf, sems.at[4]),
        pltpu.make_async_copy(o_weight, w_buf, sems.at[5]),
    ]
    for copy in copies:
        copy.start()
    for copy in copies[:3]:
        copy.wait()
    scale = 1.0 / math.sqrt(head_size)
    stacked = heads * drafts
    slot = lax.broadcasted_iota(jnp.int32, (stacked, context_len), 1)
    draft_slot = lax.broadcasted_iota(jnp.int32, (stacked, drafts), 1)
    draft_row = lax.broadcasted_iota(jnp.int32, (heads, drafts, drafts), 1).reshape(stacked, drafts)
    row_index = lax.broadcasted_iota(jnp.int32, (drafts, head_size), 0)
    probs = []
    for r in range(reqs):
        span = slice(r * drafts, (r + 1) * drafts)
        query = jnp.concatenate(
            [q_buf[span, h * head_size : (h + 1) * head_size] for h in range(heads)], axis=0
        )
        cache_len = cache_len_ref[half * reqs + r]
        draft_len = draft_len_ref[half * reqs + r]
        cache_scores = _dot_t(query, k_buf[r]) * scale
        draft_scores = _dot_t(query, d_buf[0, span]) * scale
        cache_scores = jnp.where(slot < cache_len, cache_scores, LOWEST)
        live = (draft_slot <= draft_row) & (draft_slot < draft_len)
        draft_scores = jnp.where(live, draft_scores, LOWEST)
        row_max = jnp.maximum(
            jnp.max(cache_scores, axis=-1, keepdims=True),
            jnp.max(draft_scores, axis=-1, keepdims=True),
        )
        cache_probs = jnp.exp(cache_scores - row_max)
        draft_probs = jnp.exp(draft_scores - row_max)
        denominator = jnp.sum(cache_probs, axis=-1, keepdims=True) + jnp.sum(
            draft_probs, axis=-1, keepdims=True
        )
        probs.append((cache_probs.astype(BF16), draft_probs.astype(BF16), denominator))
    copies[3].wait()
    copies[4].wait()
    for r in range(reqs):
        span = slice(r * drafts, (r + 1) * drafts)
        cache_probs, draft_probs, denominator = probs[r]
        context = _dot(cache_probs, v_buf[r]) + _dot(draft_probs, d_buf[1, span])
        context = context / denominator
        draft_len = draft_len_ref[half * reqs + r]
        for h in range(heads):
            cols = slice(h * head_size, (h + 1) * head_size)
            gate = jax.nn.sigmoid(g_buf[span, cols].astype(F32))
            piece = context[h * drafts : (h + 1) * drafts] * gate
            piece = jnp.where(row_index < draft_len, piece, 0.0)
            attended[span, cols] = piece.astype(BF16)
    copies[5].wait()
    rows_in = attended[...]
    width = out_ref.shape[1]
    tile = min(512, width)
    for c in range(0, width, tile):
        out_ref[:, c : c + tile] = _dot(rows_in, w_buf[:, c : c + tile]).astype(out_ref.dtype)


def attention(half, own_rows, out_dtype, arrays):
    queries, out_gate, draft_kv, cache_keys, cache_values, draft_len, cache_len, o_weight = arrays
    reqs_all, context_len, head_size = cache_keys.shape
    reqs = reqs_all * own_rows // queries.shape[0]
    width = o_weight.shape[1]
    inner = o_weight.shape[0]
    smem = pl.BlockSpec(memory_space=pltpu.SMEM)
    hbm = pl.BlockSpec(memory_space=pl.ANY)
    return pl.pallas_call(
        attention_kernel,
        out_shape=jax.ShapeDtypeStruct((own_rows, width), out_dtype),
        in_specs=[smem] * 3 + [hbm] * 6,
        out_specs=pl.BlockSpec(memory_space=pltpu.VMEM),
        scratch_shapes=[
            pltpu.VMEM((own_rows, inner), BF16),
            pltpu.VMEM((own_rows, inner), BF16),
            pltpu.VMEM((2, own_rows, head_size), BF16),
            pltpu.VMEM((reqs, context_len, head_size), BF16),
            pltpu.VMEM((reqs, context_len, head_size), BF16),
            pltpu.VMEM((inner, width), BF16),
            pltpu.VMEM((own_rows, inner), BF16),
            pltpu.SemaphoreType.DMA((6,)),
        ],
        compiler_params=pltpu.CompilerParams(vmem_limit_bytes=60 * 1024 * 1024),
        cost_estimate=pl.CostEstimate(
            flops=2 * own_rows * inner * (width + 2 * context_len),
            bytes_accessed=2 * inner * width + 4 * reqs * context_len * head_size,
            transcendentals=0,
        ),
    )(
        half.reshape(1),
        draft_len,
        cache_len,
        queries,
        out_gate,
        draft_kv,
        cache_keys,
        cache_values,
        o_weight,
    )


def norm_kernel(
    experts, hidden_ref, kept_ref, received_ref, gain_ref, ids_ref, weights_ref, residual_ref, sent_ref
):
    residual = hidden_ref[...].astype(F32) + kept_ref[...] + received_ref[...].astype(F32)
    width = residual.shape[1]
    spread = jnp.mean(residual * residual, axis=-1, keepdims=True)
    normed = (residual * lax.rsqrt(spread + 1e-06) * gain_ref[...]).astype(BF16)
    residual_ref[...] = residual
    sent_ref[:, :width] = normed
    rows, lanes = sent_ref.shape[0], sent_ref.shape[1] - width
    column = lax.broadcasted_iota(jnp.int32, (rows, lanes), 1)
    table = jnp.zeros((rows, lanes), F32)
    for k in range(ids_ref.shape[1]):
        index = ids_ref[:, k : k + 1]
        weight = weights_ref[:, k : k + 1]
        high = weight.astype(BF16).astype(F32)
        table = jnp.where(column == index, high, table)
        table = jnp.where(column == index + experts, weight - high, table)
    sent_ref[:, width:] = table.astype(BF16)


def residual_norm(hidden, kept, received, gain, ids, weights, experts):
    rows, width = hidden.shape
    lanes = -(-2 * experts // 128) * 128
    return pl.pallas_call(
        functools.partial(norm_kernel, experts),
        out_shape=(
            jax.ShapeDtypeStruct((rows, width), F32),
            jax.ShapeDtypeStruct((rows, width + lanes), BF16),
        ),
        compiler_params=pltpu.CompilerParams(vmem_limit_bytes=16 * 1024 * 1024),
    )(hidden, kept, received, gain.reshape(1, width), ids, weights)


def experts_kernel(spans, experts, where_ref, *refs):
    pieces = len(spans)
    rows_in = refs[:pieces]
    gates, ups, downs = (refs[pieces + 2 * i : pieces + 2 + 2 * i] for i in range(3))
    outs = refs[pieces + 6 : -2]
    rows, total = refs[-2:]
    width = total.shape[1]
    at = 0
    for ref, (start, size) in zip(rows_in, spans):
        rows[at : at + size] = ref[start : start + size]
        at += size
    table = rows[:, width:].astype(F32)
    column = lax.broadcasted_iota(jnp.int32, table.shape, 1)
    block = rows[:, :width]
    hidden = gates[0].shape[2]
    tile = min(256, hidden)
    for e in range(2):
        index = where_ref[e]
        chosen = (column == index) | (column == index + experts)
        weight = jnp.sum(jnp.where(chosen, table, 0.0), axis=1, keepdims=True)
        for c in range(0, hidden, tile):
            span = slice(c, c + tile)
            gate = _dot(block, gates[e][0, :, span])
            up = _dot(block, ups[e][0, :, span])
            act = (jax.nn.silu(gate) * up * weight).astype(BF16)
            added = _dot(act, downs[e][0, span, :])
            if e == 0 and c == 0:
                total[...] = added
            else:
                total[...] += added
    at = 0
    for out in outs:
        size = out.shape[0]
        out[...] = total[at : at + size].astype(BF16)
        at += size


def plane_experts(where, rows_in, experts, own_weights, other_weights):
    arrays = [piece[0] for piece in rows_in]
    spans = tuple(piece[1:] for piece in rows_in)
    sizes = [span[1] for span in spans]
    count = sum(sizes)
    padded = arrays[0].shape[1]
    width, hidden = own_weights[0].shape[1:]
    weights = [w for pair in zip(own_weights, other_weights) for w in pair]
    vmem = pl.BlockSpec(memory_space=pltpu.VMEM)
    return pl.pallas_call(
        functools.partial(experts_kernel, spans, experts),
        out_shape=tuple(jax.ShapeDtypeStruct((size, width), BF16) for size in sizes),
        in_specs=[pl.BlockSpec(memory_space=pltpu.SMEM)] + [vmem] * (len(spans) + 6),
        out_specs=[vmem] * len(spans),
        scratch_shapes=[pltpu.VMEM((count, padded), BF16), pltpu.VMEM((count, width), F32)],
        compiler_params=pltpu.CompilerParams(vmem_limit_bytes=24 * 1024 * 1024),
        cost_estimate=pl.CostEstimate(
            flops=12 * count * width * hidden,
            bytes_accessed=12 * width * hidden,
            transcendentals=0,
        ),
    )(where, *arrays, *weights)


def final_kernel(residual_ref, *refs):
    out_ref = refs[-1]
    mix = refs[0][...].astype(F32)
    for ref in refs[1:-1]:
        mix = mix + ref[...].astype(F32)
    out_ref[...] = (residual_ref[...] + mix).astype(BF16)


def final_sum(residual, pieces):
    return pl.pallas_call(
        final_kernel,
        out_shape=jax.ShapeDtypeStruct(residual.shape, BF16),
        compiler_params=pltpu.CompilerParams(vmem_limit_bytes=16 * 1024 * 1024),
    )(residual, *pieces)


def add_bf16(*terms):
    total = terms[0].astype(F32)
    for term in terms[1:]:
        total = total + term.astype(F32)
    return total.astype(BF16)


def on_device(
    hidden_in,
    queries,
    out_gate,
    draft_kv,
    cache_keys,
    cache_values,
    draft_len,
    cache_len,
    o_weight,
    norm_gain,
    route_ids,
    route_weights,
    w_gate,
    w_up,
    w_down,
):
    wide = lax.axis_size("wide")
    narrow = lax.axis_size("narrow")
    chip = lax.axis_index("wide")
    core = lax.axis_index("narrow")
    plane = 4
    planes = wide // plane
    assert narrow == 2 and wide % plane == 0 and planes > 1
    experts = wide * narrow
    own_rows, width = hidden_in.shape
    mid = own_rows // 2

    swap = [(0, 1), (1, 0)]
    own_weights = (w_gate, w_up, w_down)
    other_weights = tuple(lax.ppermute(w, "narrow", swap) for w in own_weights)

    arrays = (queries, out_gate, draft_kv, cache_keys, cache_values, draft_len, cache_len, o_weight)
    outgoing = attention(1 - core, own_rows, BF16, arrays)
    received = lax.ppermute(outgoing, "narrow", swap)
    kept = attention(core, own_rows, F32, arrays)
    residual, sent = residual_norm(
        hidden_in, kept, received, norm_gain, route_ids, route_weights, experts
    )

    def across(flip):
        pairs = [(i, i ^ flip) for i in range(wide)]
        return lambda a: lax.ppermute(a, "wide", pairs)

    def shifted(by):
        pairs = [(i, (i + by * plane) % wide) for i in range(wide)]
        return lambda a: lax.ppermute(a, "wide", pairs)

    over_x, over_y = across(1), across(2)
    own_expert = chip * narrow + core
    where = jnp.stack([own_expert, own_expert ^ 1]).astype(jnp.int32)

    def run_experts(rows_in):
        return plane_experts(where, rows_in, experts, own_weights, other_weights)

    together = lax.optimization_barrier

    blocks = [sent]
    from_x, from_y = [], []
    made = {}
    for k in range(planes):
        to_x, to_y = blocks[k], blocks[k]
        if k:
            to_x = jnp.concatenate([to_x, from_y[-1][mid:own_rows]])
            to_y = jnp.concatenate([to_y, from_x[-1][:mid]])
        group = [over_x(to_x), over_y(to_y)]
        if k < planes - 1:
            group.append(shifted(1)(blocks[k]))
        if k >= 2:
            s = k - 2
            made[s] = run_experts(
                [
                    (blocks[s], 0, own_rows),
                    (from_x[s], 0, own_rows),
                    (from_y[s], 0, own_rows),
                    (from_y[s + 1], own_rows, mid),
                    (from_x[s + 1], own_rows, mid),
                ]
            )
            group += made[s]
        group = together(tuple(group))
        from_x.append(group[0])
        from_y.append(group[1])
        if k < planes - 1:
            blocks.append(group[2])
        if k >= 2:
            made[k - 2] = group[-5:]

    order = list(range(1, planes)) + [0]
    last_y = over_y(from_x[-1][:mid])
    last_x = over_x(from_y[-1][mid:own_rows])
    results = []
    pending = None

    def experts_of(s):
        end = s == planes - 1
        return run_experts(
            [
                (blocks[s], 0, own_rows),
                (from_x[s], 0, own_rows),
                (from_y[s], 0, own_rows),
                (last_y, 0, mid) if end else (from_y[s + 1], own_rows, mid),
                (last_x, 0, mid) if end else (from_x[s + 1], own_rows, mid),
            ]
        )

    first = order[0]
    if first not in made:
        made[first] = experts_of(first)
    part_x, part_y = over_x(made[first][3]), over_y(made[first][4])
    group = [last_x, last_y, part_x, part_y]
    if planes - 2 not in made:
        made[planes - 2] = experts_of(planes - 2)
        group += made[planes - 2]
        group = together(tuple(group))
        made[planes - 2] = group[-5:]
    else:
        group = together(tuple(group))
    last_x, last_y, part_x, part_y = group[:4]

    for j, s in enumerate(order):
        own, for_x, for_y, _, _ = made[s]
        to_x = jnp.concatenate([for_x[:mid], add_bf16(for_x[mid:], part_y)])
        to_y = jnp.concatenate([add_bf16(for_y[:mid], part_x), for_y[mid:]])
        follows = order[j + 1] if j + 1 < planes else None
        if follows is not None and follows in made:
            to_x = jnp.concatenate([to_x, made[follows][3]])
            to_y = jnp.concatenate([to_y, made[follows][4]])
        group = [over_x(to_x), over_y(to_y)]
        if pending is not None:
            group.append(shifted(planes - pending[0])(pending[1]))
        if planes - 1 not in made:
            made[planes - 1] = experts_of(planes - 1)
            group += made[planes - 1]
            group = together(tuple(group))
            made[planes - 1] = group[-5:]
        else:
            group = together(tuple(group))
        if pending is not None:
            results.append(group[2])
        part_x, part_y = group[0][own_rows:], group[1][own_rows:]
        if s:
            pending = (s, add_bf16(own, group[0][:own_rows], group[1][:own_rows]))
        else:
            pending = None
            results += [own, group[0], group[1]]
        if follows is not None and part_x.shape[0] == 0:
            part_x, part_y = over_x(made[follows][3]), over_y(made[follows][4])
    return final_sum(residual, results)


def solution(mesh):
    placed = (
        P(("rep", "wide", "narrow"), None),
        P(("rep", "wide"), "narrow"),
        P(("rep", "wide"), "narrow"),
        P(None, ("rep", "wide"), None),
        P(("rep", "wide"), None, None),
        P(("rep", "wide"), None, None),
        P(("rep", "wide")),
        P(("rep", "wide")),
        P("narrow", None),
        P(),
        P(("rep", "wide", "narrow"), None),
        P(("rep", "wide", "narrow"), None),
        P(("wide", "narrow"), None, None),
        P(("wide", "narrow"), None, None),
        P(("wide", "narrow"), None, None),
    )
    return jax.shard_map(
        on_device,
        mesh=mesh,
        in_specs=placed,
        out_specs=P(("rep", "wide", "narrow"), None),
        check_vma=False,
    )
```

time: 257 us -> 140 us (0.54)
  blocking collectives: 43.2 us -> 0 us
  starting transfers between devices: 70.5 us -> 32.8 us
  waiting for transfers between devices: 71.8 us -> 55.6 us
  local copies, waits for them, and re-layouts: 21.8 us -> 10 us
  Pallas kernels: 47.7 us -> 38.3 us
    all_gather x1 -> x0, blocking collectives: 43.2 us -> none  [on_device(): table = lax.all_gather(table, 'wide', axis=0, tiled=False)]
    ppermute x48 -> x20, waiting for transfers between devices: 46.7 us -> 19.9 us  [across(): return lambda a: lax.ppermute(a, 'wide', pairs)]
    ppermute x48 -> x20, starting transfers between devices: 51 us -> 25 us  [across(): return lambda a: lax.ppermute(a, 'wide', pairs)]
    pallas_call x6, Pallas kernels: 41.8 us -> 28.1 us  [the longest x4 26.7 us: plane_experts(): pl.pallas_call(functools.partial(experts_kernel, spans, experts), out_sha...]
    ppermute x12 -> x6, starting transfers between devices: 18.4 us -> 6.64 us  [shifted(): return lambda a: lax.ppermute(a, 'wide', pairs)]
    ppermute x12 -> x6, waiting for transfers between devices: 25.1 us -> 35.7 us  [shifted(): return lambda a: lax.ppermute(a, 'wide', pairs)]
    unnamed x88 -> x52, local copies, waits for them, and re-layouts: 20.3 us -> 9.83 us
    pallas_call x2, Pallas kernels: 5.84 us -> 10.2 us  [attention(): pl.pallas_call(attention_kernel, out_shape=jax.ShapeDtypeStruct((own_rows...]
  transfers between devices with their start and end apart: 64 -> 30, of which waited for: 27 -> 13; matrix products, arithmetic and copies ran while one was open for 1% -> 1% of each run, Pallas kernels for 18% -> 27%
where the time goes in v2:
time: 140 us; the launch traced here: 139 us
  waiting for transfers between devices  55.6 us (40%)
  Pallas kernels  38.3 us (27%)
  starting transfers between devices  32.8 us (23%)
  local copies, waits for them, and re-layouts  10 us (7%)
  other arithmetic  2.1 us (2%)
    ppermute x6, waiting for transfers between devices, shifted(): return lambda a: lax.ppermute(a, 'wide', pairs)  35.7 us
    pallas_call x4, Pallas kernels, plane_experts(): pl.pallas_call(functools.partial(experts_kernel, spans, experts), out_sha...  26.7 us
    ppermute x20, starting transfers between devices, across(): return lambda a: lax.ppermute(a, 'wide', pairs)  25 us
    ppermute x20, waiting for transfers between devices, across(): return lambda a: lax.ppermute(a, 'wide', pairs)  19.9 us
    pallas_call x2, Pallas kernels, attention(): pl.pallas_call(attention_kernel, out_shape=jax.ShapeDtypeStruct((own_rows...  10.2 us
    unnamed x52, local copies, waits for them, and re-layouts  9.83 us
    ppermute x6, starting transfers between devices, shifted(): return lambda a: lax.ppermute(a, 'wide', pairs)  6.64 us
  transfers between devices with their start and end apart: 30, of which 13 were waited for; matrix products, arithmetic and copies ran while one was open for 1% of the time, Pallas kernels for 27%

profile of v2, /device:TPU:0, one launch (start us, length us, event | category | flops | bytes accessed | tf_op | source)
XLA Modules:
  0.0 139.3 jit_solution(13454032946247144062)
XLA Ops:
  1.0 5.0 %shard_map.146 = bf16[64,2048]{1,0:T(8,128)(2,1)} custom-call(s32[1]{0:T(128)} %bitcast.1.half_ref, s32[8]{0:T(128)} %draft_len_ref.3, s32[8]{0:T(128)} %cache_len_ref.3, bf16[128,1024]{1,0:T(8,128)(2,1)} %queries.3, bf16[128,1024]{1,0:T(8,128)(2,1)} %out_gate.3, bf16[2,128,256]{2,1,0:T(8,128)(2,1)} %draft_kv.3, bf16[8,256,256]{2,1,0:T(8,128)(2,1)} %cache_keys.3, ...), custom_call_target="tpu_custom_call" | custom-call | flops 335544320 | bytes 5242880 | tf_op jit(solution)/shard_map/pallas_call | solution.py:122
  6.3 5.1 %shard_map.145.kept_ref = f32[64,2048]{1,0:T(8,128)} custom-call(s32[1]{0:T(128)} %bitcast.half_ref, s32[8]{0:T(128)} %draft_len_ref.3, s32[8]{0:T(128)} %cache_len_ref.3, bf16[128,1024]{1,0:T(8,128)(2,1)} %queries.3, bf16[128,1024]{1,0:T(8,128)(2,1)} %out_gate.3, bf16[2,128,256]{2,1,0:T(8,128)(2,1)} %draft_kv.3, bf16[8,256,256]{2,1,0:T(8,128)(2,1)} %cache_keys.3, ...), custom_call_target="tpu_custom_call" | custom-call | flops 335544320 | bytes 5242880 | tf_op jit(solution)/shard_map/pallas_call | solution.py:122
  13.8 2.9 %collective-permute-start.1 = (bf16[64,2176]{1,0:T(8,128)(2,1)S(1)}, bf16[64,2176]{1,0:T(8,128)(2,1)S(1)}, u32[]{:S(2)}, u32[]{:S(2)}) collective-permute-start(bf16[64,2176]{1,0:T(8,128)(2,1)S(1)} %get-tuple-element.74.refs_0_), channel_id=1, source_target_pairs={{0,2},{2,0},{4,6},{6,4},{8,10},{10,8},{12,14},{14,12},{16,18},{18,... | collective-permute-start | bytes 835592 | tf_op jit(solution)/shard_map/ppermute | solution.py:316
  18.3 5.3 %collective-permute-done.1.refs_1_ = bf16[64,2176]{1,0:T(8,128)(2,1)S(1)} collective-permute-done((bf16[64,2176]{1,0:T(8,128)(2,1)S(1)}, bf16[64,2176]{1,0:T(8,128)(2,1)S(1)}, u32[]{:S(2)}, u32[]{:S(2)}) %collective-permute-start.1) | collective-permute-done | bytes 278560 | tf_op jit(solution)/shard_map/ppermute | solution.py:316
  23.6 1.8 %collective-permute-start.3 = (bf16[64,2176]{1,0:T(8,128)(2,1)S(1)}, bf16[64,2176]{1,0:T(8,128)(2,1)S(1)}, u32[]{:S(2)}, u32[]{:S(2)}) collective-permute-start(bf16[64,2176]{1,0:T(8,128)(2,1)S(1)} %get-tuple-element.74.refs_0_), channel_id=1, source_target_pairs={{0,8},{2,10},{4,12},{6,14},{8,16},{10,18},{12,20},{14,22},{16,24},... | collective-permute-start | bytes 835592 | tf_op jit(solution)/shard_map/ppermute | solution.py:320
  26.2 7.3 %collective-permute-done.3.refs_0_ = bf16[64,2176]{1,0:T(8,128)(2,1)S(1)} collective-permute-done((bf16[64,2176]{1,0:T(8,128)(2,1)S(1)}, bf16[64,2176]{1,0:T(8,128)(2,1)S(1)}, u32[]{:S(2)}, u32[]{:S(2)}) %collective-permute-start.3) | collective-permute-done | bytes 278560 | tf_op jit(solution)/shard_map/ppermute | solution.py:320
  33.7 1.5 %collective-permute-start.4 = (bf16[96,2176]{1,0:T(8,128)(2,1)S(1)}, bf16[96,2176]{1,0:T(8,128)(2,1)S(1)}, u32[]{:S(2)}, u32[]{:S(2)}) collective-permute-start(bf16[96,2176]{1,0:T(8,128)(2,1)S(1)} %get-tuple-element.146), channel_id=1, source_target_pairs={{0,2},{2,0},{4,6},{6,4},{8,10},{10,8},{12,14},{14,12},{16,18},{18,... | collective-permute-start | bytes 1253384 | tf_op jit(solution)/shard_map/ppermute | solution.py:316
  35.2 7.3 %collective-permute-done.6.refs_0_ = bf16[64,2176]{1,0:T(8,128)(2,1)S(1)} collective-permute-done((bf16[64,2176]{1,0:T(8,128)(2,1)S(1)}, bf16[64,2176]{1,0:T(8,128)(2,1)S(1)}, u32[]{:S(2)}, u32[]{:S(2)}) %collective-permute-start.6) | collective-permute-done | bytes 278560 | tf_op jit(solution)/shard_map/ppermute | solution.py:320
  43.8 7.8 %collective-permute-done.5.refs_3_.refs_2_ = bf16[96,2176]{1,0:T(8,128)(2,1)S(1)} collective-permute-done((bf16[96,2176]{1,0:T(8,128)(2,1)S(1)}, bf16[96,2176]{1,0:T(8,128)(2,1)S(1)}, u32[]{:S(2)}, u32[]{:S(2)}) %collective-permute-start.5) | collective-permute-done | bytes 417824 | tf_op jit(solution)/shard_map/ppermute | solution.py:316
  53.8 1.5 %collective-permute-start.8 = (bf16[96,2176]{1,0:T(8,128)(2,1)}, bf16[96,2176]{1,0:T(8,128)(2,1)S(1)}, u32[]{:S(2)}, u32[]{:S(2)}) collective-permute-start(bf16[96,2176]{1,0:T(8,128)(2,1)} %get-tuple-element.143), channel_id=1, source_target_pairs={{0,4},{2,6},{4,0},{6,2},{8,12},{10,14},{12,8},{14,10},{16,20},{18,... | collective-permute-start | bytes 1253384 | tf_op jit(solution)/shard_map/ppermute | solution.py:316
  55.7 1.6 %copy-done.1 = bf16[1,2048,512]{2,1,0:T(8,128)(2,1)S(1)} copy-done((bf16[1,2048,512]{2,1,0:T(8,128)(2,1)S(1)}, bf16[1,2048,512]{2,1,0:T(8,128)(2,1)}, u32[]{:S(2)}) %copy-start.1) | copy-done | bytes 2097176
  57.3 1.6 %copy-done.3 = bf16[1,512,2048]{2,1,0:T(8,128)(2,1)S(1)} copy-done((bf16[1,512,2048]{2,1,0:T(8,128)(2,1)S(1)}, bf16[1,512,2048]{2,1,0:T(8,128)(2,1)}, u32[]{:S(2)}) %copy-start.3) | copy-done | bytes 2097176
  62.7 6.8 %shard_map.148 = (bf16[64,2048]{1,0:T(8,128)(2,1)S(1)}, bf16[64,2048]{1,0:T(8,128)(2,1)S(1)}, bf16[64,2048]{1,0:T(8,128)(2,1)S(1)}, bf16[32,2048]{1,0:T(8,128)(2,1)S(1)}, bf16[32,2048]{1,0:T(8,128)(2,1)S(1)}) custom-call(s32[2]{0:T(128)S(1)} %pad_add_fusion.where_ref, bf16[64,2176]{1,0:T(8,128)(2,1)S(1)} %copy-done.20, bf16[64,2176]{1,0:T(8,128)(2,1)S(1)} %copy-done.14, ...), custom_call_target="tpu_custom_call" | custom-call | flops 3221225472 | bytes 12582912 | tf_op jit(solution)/shard_map/pallas_call | solution.py:236
  71.3 6.6 %shard_map.149 = (bf16[64,2048]{1,0:T(8,128)(2,1)S(1)}, bf16[64,2048]{1,0:T(8,128)(2,1)S(1)}, bf16[64,2048]{1,0:T(8,128)(2,1)S(1)}, bf16[32,2048]{1,0:T(8,128)(2,1)S(1)}, bf16[32,2048]{1,0:T(8,128)(2,1)S(1)}) custom-call(s32[2]{0:T(128)S(1)} %pad_add_fusion.where_ref, bf16[64,2176]{1,0:T(8,128)(2,1)S(1)} %copy-done.12, ...), custom_call_target="tpu_custom_call" | custom-call | flops 3221225472 | bytes 12582912 | tf_op jit(solution)/shard_map/pallas_call | solution.py:236
  79.5 2.1 %collective-permute-start.15 = (bf16[32,2176]{1,0:T(8,128)(2,1)S(1)}, bf16[32,2176]{1,0:T(8,128)(2,1)S(1)}, u32[]{:S(2)}, u32[]{:S(2)}) collective-permute-start(bf16[32,2176]{1,0:T(8,128)(2,1)S(1)} %slice.114), channel_id=1, source_target_pairs={{0,2},{2,0},{4,6},{6,4},{8,10},{10,8},{12,14},{14,12},{16,18},{18,... | collective-permute-start | bytes 417800 | tf_op jit(solution)/shard_map/ppermute | solution.py:316
  83.8 6.7 %shard_map.150 = (bf16[64,2048]{1,0:T(8,128)(2,1)S(1)}, bf16[64,2048]{1,0:T(8,128)(2,1)S(1)}, bf16[64,2048]{1,0:T(8,128)(2,1)S(1)}, bf16[32,2048]{1,0:T(8,128)(2,1)S(1)}, bf16[32,2048]{1,0:T(8,128)(2,1)S(1)}) custom-call(s32[2]{0:T(128)S(1)} %pad_add_fusion.where_ref, bf16[64,2176]{1,0:T(8,128)(2,1)S(1)} %copy-done.10, ...), custom_call_target="tpu_custom_call" | custom-call | flops 3221225472 | bytes 12582912 | tf_op jit(solution)/shard_map/pallas_call | solution.py:236
  91.4 1.6 %collective-permute-start.19 = (bf16[96,2048]{1,0:T(8,128)(2,1)S(1)}, bf16[96,2048]{1,0:T(8,128)(2,1)S(1)}, u32[]{:S(2)}, u32[]{:S(2)}) collective-permute-start(bf16[96,2048]{1,0:T(8,128)(2,1)S(1)} %pad_maximum_fusion.6), channel_id=1, source_target_pairs={{0,2},{2,0},{4,6},{6,4},{8,10},{10,8},{12,14},{14,12},{16,18},{18,... | collective-permute-start | bytes 1179656 | tf_op jit(solution)/shard_map/ppermute | solution.py:316
  92.9 6.7 %shard_map.151 = (bf16[64,2048]{1,0:T(8,128)(2,1)S(1)}, bf16[64,2048]{1,0:T(8,128)(2,1)S(1)}, bf16[64,2048]{1,0:T(8,128)(2,1)S(1)}, bf16[32,2048]{1,0:T(8,128)(2,1)S(1)}, bf16[32,2048]{1,0:T(8,128)(2,1)S(1)}) custom-call(s32[2]{0:T(128)S(1)} %pad_add_fusion.where_ref, bf16[64,2176]{1,0:T(8,128)(2,1)S(1)} %collective-permute-done.9.refs_0_, ...), custom_call_target="tpu_custom_call" | custom-call | flops 3221225472 | bytes 12582912 | tf_op jit(solution)/shard_map/pallas_call | solution.py:236
  99.6 2.3 %collective-permute-done.20 = bf16[96,2048]{1,0:T(8,128)(2,1)S(1)} collective-permute-done((bf16[96,2048]{1,0:T(8,128)(2,1)S(1)}, bf16[96,2048]{1,0:T(8,128)(2,1)S(1)}, u32[]{:S(2)}, u32[]{:S(2)}) %collective-permute-start.20) | collective-permute-done | bytes 393248 | tf_op jit(solution)/shard_map/ppermute | solution.py:316
  106.1 4.0 %collective-permute-start.23 = (bf16[64,2048]{1,0:T(8,128)(2,1)S(1)}, bf16[64,2048]{1,0:T(8,128)(2,1)S(1)}, u32[]{:S(2)}, u32[]{:S(2)}) collective-permute-start(bf16[64,2048]{1,0:T(8,128)(2,1)S(1)} %add_convert_fusion.2), channel_id=1, source_target_pairs={{0,24},{2,26},{4,28},{6,30},{8,0},{10,2},{12,4},{14,6},{16,8},{18,... | collective-permute-start | bytes 786440 | tf_op jit(solution)/shard_map/ppermute | solution.py:320
  110.1 3.9 %collective-permute-done.23.refs_0_ = bf16[64,2048]{1,0:T(8,128)(2,1)S(1)} collective-permute-done((bf16[64,2048]{1,0:T(8,128)(2,1)S(1)}, bf16[64,2048]{1,0:T(8,128)(2,1)S(1)}, u32[]{:S(2)}, u32[]{:S(2)}) %collective-permute-start.23) | collective-permute-done | bytes 262176 | tf_op jit(solution)/shard_map/ppermute | solution.py:320
  116.5 1.8 %collective-permute-start.24 = (bf16[96,2048]{1,0:T(8,128)(2,1)S(1)}, bf16[96,2048]{1,0:T(8,128)(2,1)S(1)}, u32[]{:S(2)}, u32[]{:S(2)}) collective-permute-start(bf16[96,2048]{1,0:T(8,128)(2,1)S(1)} %pad_maximum_fusion.10), channel_id=1, source_target_pairs={{0,2},{2,0},{4,6},{6,4},{8,10},{10,8},{12,14},{14,12},{16,18},{18,... | collective-permute-start | bytes 1179656 | tf_op jit(solution)/shard_map/ppermute | solution.py:316
  119.0 10.9 %collective-permute-done.26.refs_1_ = bf16[64,2048]{1,0:T(8,128)(2,1)S(1)} collective-permute-done((bf16[64,2048]{1,0:T(8,128)(2,1)S(1)}, bf16[64,2048]{1,0:T(8,128)(2,1)S(1)}, u32[]{:S(2)}, u32[]{:S(2)}) %collective-permute-start.26) | collective-permute-done | bytes 262176 | tf_op jit(solution)/shard_map/ppermute | solution.py:320
  132.0 6.3 %collective-permute-done.29.refs_2_ = bf16[64,2048]{1,0:T(8,128)(2,1)S(1)} collective-permute-done((bf16[64,2048]{1,0:T(8,128)(2,1)S(1)}, bf16[64,2048]{1,0:T(8,128)(2,1)S(1)}, u32[]{:S(2)}, u32[]{:S(2)}) %collective-permute-start.29) | collective-permute-done | bytes 262176 | tf_op jit(solution)/shard_map/ppermute | solution.py:320
  (135 shorter events, 30.2 us)
Async XLA Ops:
  0.0 55.5 %collective-permute-start.10 = (bf16[1,2048,512]{2,1,0:T(8,128)(2,1)}, bf16[1,2048,512]{2,1,0:T(8,128)(2,1)}, u32[]{:S(2)}, u32[]{:S(2)}) collective-permute-start(bf16[1,2048,512]{2,1,0:T(8,128)(2,1)} %refs_5_.7), channel_id=1, source_target_pairs={{0,1},{1,0},{2,3},{3,2},{4,5},{5,4},{6,7},{7,6},{8,9},{9,8},{10,11... | collective-permute-start | bytes 6291464 | tf_op jit(solution)/shard_map/ppermute | solution.py:304
  0.5 55.2 %collective-permute-start.11 = (bf16[1,2048,512]{2,1,0:T(8,128)(2,1)}, bf16[1,2048,512]{2,1,0:T(8,128)(2,1)}, u32[]{:S(2)}, u32[]{:S(2)}) collective-permute-start(bf16[1,2048,512]{2,1,0:T(8,128)(2,1)} %refs_7_.7), channel_id=1, source_target_pairs={{0,1},{1,0},{2,3},{3,2},{4,5},{5,4},{6,7},{7,6},{8,9},{9,8},{10,11... | collective-permute-start | bytes 6291464 | tf_op jit(solution)/shard_map/ppermute | solution.py:304
  0.5 55.1 %collective-permute-start.12 = (bf16[1,512,2048]{2,1,0:T(8,128)(2,1)}, bf16[1,512,2048]{2,1,0:T(8,128)(2,1)}, u32[]{:S(2)}, u32[]{:S(2)}) collective-permute-start(bf16[1,512,2048]{2,1,0:T(8,128)(2,1)} %refs_9_.7), channel_id=1, source_target_pairs={{0,1},{1,0},{2,3},{3,2},{4,5},{5,4},{6,7},{7,6},{8,9},{9,8},{10,11... | collective-permute-start | bytes 6291464 | tf_op jit(solution)/shard_map/ppermute | solution.py:304
  13.8 9.8 %collective-permute-start.1 = (bf16[64,2176]{1,0:T(8,128)(2,1)S(1)}, bf16[64,2176]{1,0:T(8,128)(2,1)S(1)}, u32[]{:S(2)}, u32[]{:S(2)}) collective-permute-start(bf16[64,2176]{1,0:T(8,128)(2,1)S(1)} %get-tuple-element.74.refs_0_), channel_id=1, source_target_pairs={{0,2},{2,0},{4,6},{6,4},{8,10},{10,8},{12,14},{14,12},{16,18},{18,... | collective-permute-start | bytes 835592 | tf_op jit(solution)/shard_map/ppermute | solution.py:316
  16.8 9.4 %collective-permute-start.2 = (bf16[64,2176]{1,0:T(8,128)(2,1)S(1)}, bf16[64,2176]{1,0:T(8,128)(2,1)S(1)}, u32[]{:S(2)}, u32[]{:S(2)}) collective-permute-start(bf16[64,2176]{1,0:T(8,128)(2,1)S(1)} %get-tuple-element.74.refs_0_), channel_id=1, source_target_pairs={{0,4},{2,6},{4,0},{6,2},{8,12},{10,14},{12,8},{14,10},{16,20},{18,... | collective-permute-start | bytes 835592 | tf_op jit(solution)/shard_map/ppermute | solution.py:316
  23.6 9.9 %collective-permute-start.3 = (bf16[64,2176]{1,0:T(8,128)(2,1)S(1)}, bf16[64,2176]{1,0:T(8,128)(2,1)S(1)}, u32[]{:S(2)}, u32[]{:S(2)}) collective-permute-start(bf16[64,2176]{1,0:T(8,128)(2,1)S(1)} %get-tuple-element.74.refs_0_), channel_id=1, source_target_pairs={{0,8},{2,10},{4,12},{6,14},{8,16},{10,18},{12,20},{14,22},{16,24},... | collective-permute-start | bytes 835592 | tf_op jit(solution)/shard_map/ppermute | solution.py:320
  33.5 9.0 %collective-permute-start.6 = (bf16[64,2176]{1,0:T(8,128)(2,1)S(1)}, bf16[64,2176]{1,0:T(8,128)(2,1)S(1)}, u32[]{:S(2)}, u32[]{:S(2)}) collective-permute-start(bf16[64,2176]{1,0:T(8,128)(2,1)S(1)} %collective-permute-done.3.refs_0_), channel_id=1, source_target_pairs={{0,8},{2,10},{4,12},{6,14},{8,16},{10,18},{12,20},{14,22},{16,24},... | collective-permute-start | bytes 835592 | tf_op jit(solution)/shard_map/ppermute | solution.py:320
  33.7 10.2 %collective-permute-start.4 = (bf16[96,2176]{1,0:T(8,128)(2,1)S(1)}, bf16[96,2176]{1,0:T(8,128)(2,1)S(1)}, u32[]{:S(2)}, u32[]{:S(2)}) collective-permute-start(bf16[96,2176]{1,0:T(8,128)(2,1)S(1)} %get-tuple-element.146), channel_id=1, source_target_pairs={{0,2},{2,0},{4,6},{6,4},{8,10},{10,8},{12,14},{14,12},{16,18},{18,... | collective-permute-start | bytes 1253384 | tf_op jit(solution)/shard_map/ppermute | solution.py:316
  42.5 9.2 %collective-permute-start.5 = (bf16[96,2176]{1,0:T(8,128)(2,1)S(1)}, bf16[96,2176]{1,0:T(8,128)(2,1)S(1)}, u32[]{:S(2)}, u32[]{:S(2)}) collective-permute-start(bf16[96,2176]{1,0:T(8,128)(2,1)S(1)} %get-tuple-element.145), channel_id=1, source_target_pairs={{0,4},{2,6},{4,0},{6,2},{8,12},{10,14},{12,8},{14,10},{16,20},{18,... | collective-permute-start | bytes 1253384 | tf_op jit(solution)/shard_map/ppermute | solution.py:316
  52.8 16.7 %collective-permute-start.7 = (bf16[96,2176]{1,0:T(8,128)(2,1)}, bf16[96,2176]{1,0:T(8,128)(2,1)S(1)}, u32[]{:S(2)}, u32[]{:S(2)}) collective-permute-start(bf16[96,2176]{1,0:T(8,128)(2,1)} %get-tuple-element.144), channel_id=1, source_target_pairs={{0,2},{2,0},{4,6},{6,4},{8,10},{10,8},{12,14},{14,12},{16,18},{18,... | collective-permute-start | bytes 1253384 | tf_op jit(solution)/shard_map/ppermute | solution.py:316
  53.8 15.7 %collective-permute-start.8 = (bf16[96,2176]{1,0:T(8,128)(2,1)}, bf16[96,2176]{1,0:T(8,128)(2,1)S(1)}, u32[]{:S(2)}, u32[]{:S(2)}) collective-permute-start(bf16[96,2176]{1,0:T(8,128)(2,1)} %get-tuple-element.143), channel_id=1, source_target_pairs={{0,4},{2,6},{4,0},{6,2},{8,12},{10,14},{12,8},{14,10},{16,20},{18,... | collective-permute-start | bytes 1253384 | tf_op jit(solution)/shard_map/ppermute | solution.py:316
  55.5 14.1 %collective-permute-start.9 = (bf16[64,2176]{1,0:T(8,128)(2,1)}, bf16[64,2176]{1,0:T(8,128)(2,1)S(1)}, u32[]{:S(2)}, u32[]{:S(2)}) collective-permute-start(bf16[64,2176]{1,0:T(8,128)(2,1)} %copy-done.9), channel_id=1, source_target_pairs={{0,8},{2,10},{4,12},{6,14},{8,16},{10,18},{12,20},{14,22},{16,24},... | collective-permute-start | bytes 835592 | tf_op jit(solution)/shard_map/ppermute | solution.py:320
  69.7 9.6 %collective-permute-start.13 = (bf16[96,2176]{1,0:T(8,128)(2,1)S(1)}, bf16[96,2176]{1,0:T(8,128)(2,1)S(1)}, u32[]{:S(2)}, u32[]{:S(2)}) collective-permute-start(bf16[96,2176]{1,0:T(8,128)(2,1)S(1)} %get-tuple-element.142), channel_id=1, source_target_pairs={{0,2},{2,0},{4,6},{6,4},{8,10},{10,8},{12,14},{14,12},{16,18},{18,... | collective-permute-start | bytes 1253384 | tf_op jit(solution)/shard_map/ppermute | solution.py:316
  70.3 9.2 %collective-permute-start.14 = (bf16[96,2176]{1,0:T(8,128)(2,1)S(1)}, bf16[96,2176]{1,0:T(8,128)(2,1)S(1)}, u32[]{:S(2)}, u32[]{:S(2)}) collective-permute-start(bf16[96,2176]{1,0:T(8,128)(2,1)S(1)} %get-tuple-element.141), channel_id=1, source_target_pairs={{0,4},{2,6},{4,0},{6,2},{8,12},{10,14},{12,8},{14,10},{16,20},{18,... | collective-permute-start | bytes 1253384 | tf_op jit(solution)/shard_map/ppermute | solution.py:316
  79.5 11.0 %collective-permute-start.15 = (bf16[32,2176]{1,0:T(8,128)(2,1)S(1)}, bf16[32,2176]{1,0:T(8,128)(2,1)S(1)}, u32[]{:S(2)}, u32[]{:S(2)}) collective-permute-start(bf16[32,2176]{1,0:T(8,128)(2,1)S(1)} %slice.114), channel_id=1, source_target_pairs={{0,2},{2,0},{4,6},{6,4},{8,10},{10,8},{12,14},{14,12},{16,18},{18,... | collective-permute-start | bytes 417800 | tf_op jit(solution)/shard_map/ppermute | solution.py:316
  81.6 8.8 %collective-permute-start.16 = (bf16[32,2176]{1,0:T(8,128)(2,1)S(1)}, bf16[32,2176]{1,0:T(8,128)(2,1)S(1)}, u32[]{:S(2)}, u32[]{:S(2)}) collective-permute-start(bf16[32,2176]{1,0:T(8,128)(2,1)S(1)} %slice.115), channel_id=1, source_target_pairs={{0,4},{2,6},{4,0},{6,2},{8,12},{10,14},{12,8},{14,10},{16,20},{18,... | collective-permute-start | bytes 417800 | tf_op jit(solution)/shard_map/ppermute | solution.py:316
  81.8 8.6 %collective-permute-start.17 = (bf16[32,2048]{1,0:T(8,128)(2,1)S(1)}, bf16[32,2048]{1,0:T(8,128)(2,1)S(1)}, u32[]{:S(2)}, u32[]{:S(2)}) collective-permute-start(bf16[32,2048]{1,0:T(8,128)(2,1)S(1)} %get-tuple-element.96), channel_id=1, source_target_pairs={{0,2},{2,0},{4,6},{6,4},{8,10},{10,8},{12,14},{14,12},{16,18},{18,... | collective-permute-start | bytes 393224 | tf_op jit(solution)/shard_map/ppermute | solution.py:316
  90.6 11.4 %collective-permute-start.20 = (bf16[96,2048]{1,0:T(8,128)(2,1)S(1)}, bf16[96,2048]{1,0:T(8,128)(2,1)S(1)}, u32[]{:S(2)}, u32[]{:S(2)}) collective-permute-start(bf16[96,2048]{1,0:T(8,128)(2,1)S(1)} %pad_maximum_fusion.7), channel_id=1, source_target_pairs={{0,4},{2,6},{4,0},{6,2},{8,12},{10,14},{12,8},{14,10},{16,20},{18,... | collective-permute-start | bytes 1179656 | tf_op jit(solution)/shard_map/ppermute | solution.py:316
  91.4 11.6 %collective-permute-start.19 = (bf16[96,2048]{1,0:T(8,128)(2,1)S(1)}, bf16[96,2048]{1,0:T(8,128)(2,1)S(1)}, u32[]{:S(2)}, u32[]{:S(2)}) collective-permute-start(bf16[96,2048]{1,0:T(8,128)(2,1)S(1)} %pad_maximum_fusion.6), channel_id=1, source_target_pairs={{0,2},{2,0},{4,6},{6,4},{8,10},{10,8},{12,14},{14,12},{16,18},{18,... | collective-permute-start | bytes 1179656 | tf_op jit(solution)/shard_map/ppermute | solution.py:316
  103.1 11.3 %collective-permute-start.22 = (bf16[96,2048]{1,0:T(8,128)(2,1)S(1)}, bf16[96,2048]{1,0:T(8,128)(2,1)S(1)}, u32[]{:S(2)}, u32[]{:S(2)}) collective-permute-start(bf16[96,2048]{1,0:T(8,128)(2,1)S(1)} %pad_maximum_fusion.9), channel_id=1, source_target_pairs={{0,4},{2,6},{4,0},{6,2},{8,12},{10,14},{12,8},{14,10},{16,20},{18,... | collective-permute-start | bytes 1179656 | tf_op jit(solution)/shard_map/ppermute | solution.py:316
  104.6 11.0 %collective-permute-start.21 = (bf16[96,2048]{1,0:T(8,128)(2,1)S(1)}, bf16[96,2048]{1,0:T(8,128)(2,1)S(1)}, u32[]{:S(2)}, u32[]{:S(2)}) collective-permute-start(bf16[96,2048]{1,0:T(8,128)(2,1)S(1)} %pad_maximum_fusion.8), channel_id=1, source_target_pairs={{0,2},{2,0},{4,6},{6,4},{8,10},{10,8},{12,14},{14,12},{16,18},{18,... | collective-permute-start | bytes 1179656 | tf_op jit(solution)/shard_map/ppermute | solution.py:316
  115.7 14.2 %collective-permute-start.25 = (bf16[96,2048]{1,0:T(8,128)(2,1)S(1)}, bf16[96,2048]{1,0:T(8,128)(2,1)S(1)}, u32[]{:S(2)}, u32[]{:S(2)}) collective-permute-start(bf16[96,2048]{1,0:T(8,128)(2,1)S(1)} %pad_maximum_fusion.11), channel_id=1, source_target_pairs={{0,4},{2,6},{4,0},{6,2},{8,12},{10,14},{12,8},{14,10},{16,20},{18,... | collective-permute-start | bytes 1179656 | tf_op jit(solution)/shard_map/ppermute | solution.py:316
  116.5 13.4 %collective-permute-start.24 = (bf16[96,2048]{1,0:T(8,128)(2,1)S(1)}, bf16[96,2048]{1,0:T(8,128)(2,1)S(1)}, u32[]{:S(2)}, u32[]{:S(2)}) collective-permute-start(bf16[96,2048]{1,0:T(8,128)(2,1)S(1)} %pad_maximum_fusion.10), channel_id=1, source_target_pairs={{0,2},{2,0},{4,6},{6,4},{8,10},{10,8},{12,14},{14,12},{16,18},{18,... | collective-permute-start | bytes 1179656 | tf_op jit(solution)/shard_map/ppermute | solution.py:316
  118.4 11.5 %collective-permute-start.26 = (bf16[64,2048]{1,0:T(8,128)(2,1)S(1)}, bf16[64,2048]{1,0:T(8,128)(2,1)S(1)}, u32[]{:S(2)}, u32[]{:S(2)}) collective-permute-start(bf16[64,2048]{1,0:T(8,128)(2,1)S(1)} %add_convert_fusion.1), channel_id=1, source_target_pairs={{0,16},{2,18},{4,20},{6,22},{8,24},{10,26},{12,28},{14,30},{16,0},... | collective-permute-start | bytes 786440 | tf_op jit(solution)/shard_map/ppermute | solution.py:320
  (31 other events, 211.9 us)

commit v3 on v2

--- a/solution.py
+++ b/solution.py
@@ -22,58 +22,102 @@
 
 
 def attention_kernel(
-    half_ref,
+    experts,
+    core_ref,
     draft_len_ref,
     cache_len_ref,
+    ids_in,
+    weights_in,
+    gain_in,
+    hidden_in,
     queries,
     out_gate,
     draft_kv,
     cache_keys,
     cache_values,
     o_weight,
-    out_ref,
+    sent_ref,
+    kept_ref,
+    table_ref,
+    gain_ref,
     q_buf,
     g_buf,
     d_buf,
     k_buf,
     v_buf,
     w_buf,
+    h_buf,
+    i_buf,
+    r_buf,
     attended,
     sems,
 ):
-    half = half_ref[0]
-    reqs, context_len, head_size = k_buf.shape
-    rows = q_buf.shape[0]
+    core = core_ref[0]
+    reqs_all, context_len, head_size = k_buf.shape
+    rows_all = q_buf.shape[0]
+    rows, reqs = rows_all // 2, reqs_all // 2
     drafts = rows // reqs
     heads = q_buf.shape[1] // head_size
-    row_span = pl.ds(pl.multiple_of(half * rows, rows), rows)
-    req_span = pl.ds(half * reqs, reqs)
-    copies = [
-        pltpu.make_async_copy(queries.at[row_span], q_buf, sems.at[0]),
-        pltpu.make_async_copy(cache_keys.at[req_span], k_buf, sems.at[1]),
-        pltpu.make_async_copy(draft_kv.at[:, row_span], d_buf, sems.at[2]),
-        pltpu.make_async_copy(cache_values.at[req_span], v_buf, sems.at[3]),
-        pltpu.make_async_copy(out_gate.at[row_span], g_buf, sems.at[4]),
-        pltpu.make_async_copy(o_weight, w_buf, sems.at[5]),
-    ]
-    for copy in copies:
+    groups = [[], [], [], []]
+
+    def fetch(group, source, target):
+        at = sum(len(g) for g in groups)
+        copy = pltpu.make_async_copy(source, target, sems.at[at])
         copy.start()
-    for copy in copies[:3]:
+        groups[group].append(copy)
+
+    def half_rows(i):
+        half = 1 - core if i == 0 else core
+        return pl.ds(pl.multiple_of(half * rows, rows), rows)
+
+    def half_reqs(i):
+        half = 1 - core if i == 0 else core
+        return pl.ds(half * reqs, reqs)
+
+    fetch(0, ids_in, i_buf)
+    fetch(0, weights_in, r_buf)
+    for i in range(2):
+        here = pl.ds(i * rows, rows)
+        fetch(0, queries.at[half_rows(i)], q_buf.at[here])
+        fetch(0, cache_keys.at[half_reqs(i)], k_buf.at[pl.ds(i * reqs, reqs)])
+        fetch(0, draft_kv.at[:, half_rows(i)], d_buf.at[:, here])
+    for i in range(2):
+        here = pl.ds(i * rows, rows)
+        fetch(1, cache_values.at[half_reqs(i)], v_buf.at[pl.ds(i * reqs, reqs)])
+        fetch(1, out_gate.at[half_rows(i)], g_buf.at[here])
+    fetch(2, o_weight, w_buf)
+    fetch(3, hidden_in, h_buf)
+    fetch(3, gain_in, gain_ref)
+
+    for copy in groups[0]:
         copy.wait()
+    row = lax.broadcasted_iota(jnp.int32, table_ref.shape[::-1], 0)
+    table = jnp.zeros(row.shape, F32)
+    for k in range(i_buf.shape[0]):
+        index = i_buf[k : k + 1, :]
+        weight = r_buf[k : k + 1, :]
+        high = weight.astype(BF16).astype(F32)
+        table = jnp.where(row == index, high, table)
+        table = jnp.where(row == index + experts, weight - high, table)
+    table_ref[...] = table.T.astype(BF16)
     scale = 1.0 / math.sqrt(head_size)
     stacked = heads * drafts
     slot = lax.broadcasted_iota(jnp.int32, (stacked, context_len), 1)
     draft_slot = lax.broadcasted_iota(jnp.int32, (stacked, drafts), 1)
     draft_row = lax.broadcasted_iota(jnp.int32, (heads, drafts, drafts), 1).reshape(stacked, drafts)
     row_index = lax.broadcasted_iota(jnp.int32, (drafts, head_size), 0)
+    lens = []
+    for r in range(reqs_all):
+        half = 1 - core if r < reqs else core
+        place = half * reqs + r % reqs
+        lens.append((cache_len_ref[place], draft_len_ref[place]))
     probs = []
-    for r in range(reqs):
+    for r in range(reqs_all):
         span = slice(r * drafts, (r + 1) * drafts)
         query = jnp.concatenate(
             [q_buf[span, h * head_size : (h + 1) * head_size] for h in range(heads)], axis=0
         )
-        cache_len = cache_len_ref[half * reqs + r]
-        draft_len = draft_len_ref[half * reqs + r]
+        cache_len, draft_len = lens[r]
         cache_scores = _dot_t(query, k_buf[r]) * scale
         draft_scores = _dot_t(query, d_buf[0, span]) * scale
         cache_scores = jnp.where(slot < cache_len, cache_scores, LOWEST)
@@ -89,102 +133,118 @@
             draft_probs, axis=-1, keepdims=True
         )
         probs.append((cache_probs.astype(BF16), draft_probs.astype(BF16), denominator))
-    copies[3].wait()
-    copies[4].wait()
-    for r in range(reqs):
+    for copy in groups[1]:
+        copy.wait()
+    for r in range(reqs_all):
         span = slice(r * drafts, (r + 1) * drafts)
         cache_probs, draft_probs, denominator = probs[r]
         context = _dot(cache_probs, v_buf[r]) + _dot(draft_probs, d_buf[1, span])
         context = context / denominator
-        draft_len = draft_len_ref[half * reqs + r]
+        draft_len = lens[r][1]
         for h in range(heads):
             cols = slice(h * head_size, (h + 1) * head_size)
             gate = jax.nn.sigmoid(g_buf[span, cols].astype(F32))
             piece = context[h * drafts : (h + 1) * drafts] * gate
             piece = jnp.where(row_index < draft_len, piece, 0.0)
             attended[span, cols] = piece.astype(BF16)
-    copies[5].wait()
+    for copy in groups[2] + groups[3]:
+        copy.wait()
     rows_in = attended[...]
-    width = out_ref.shape[1]
+    width = sent_ref.shape[1]
     tile = min(512, width)
     for c in range(0, width, tile):
-        out_ref[:, c : c + tile] = _dot(rows_in, w_buf[:, c : c + tile]).astype(out_ref.dtype)
-
-
-def attention(half, own_rows, out_dtype, arrays):
+        cols = slice(c, c + tile)
+        projected = _dot(rows_in, w_buf[:, cols])
+        sent_ref[:, cols] = projected[:rows].astype(BF16)
+        kept_ref[:, cols] = h_buf[:, cols].astype(F32) + projected[rows:]
+
+
+def attention(core, experts, hidden, gain, ids, weights, arrays):
     queries, out_gate, draft_kv, cache_keys, cache_values, draft_len, cache_len, o_weight = arrays
     reqs_all, context_len, head_size = cache_keys.shape
-    reqs = reqs_all * own_rows // queries.shape[0]
-    width = o_weight.shape[1]
-    inner = o_weight.shape[0]
+    rows_all = queries.shape[0]
+    own_rows = hidden.shape[0]
+    inner, width = o_weight.shape
+    lanes = -(-2 * experts // 128) * 128
     smem = pl.BlockSpec(memory_space=pltpu.SMEM)
+    vmem = pl.BlockSpec(memory_space=pltpu.VMEM)
     hbm = pl.BlockSpec(memory_space=pl.ANY)
+    ids, weights = ids.T, weights.T
+
+    def in_hbm(a):
+        return pltpu.with_memory_space_constraint(a, pltpu.HBM)
+
     return pl.pallas_call(
-        attention_kernel,
-        out_shape=jax.ShapeDtypeStruct((own_rows, width), out_dtype),
-        in_specs=[smem] * 3 + [hbm] * 6,
-        out_specs=pl.BlockSpec(memory_space=pltpu.VMEM),
+        functools.partial(attention_kernel, experts),
+        out_shape=(
+            jax.ShapeDtypeStruct((own_rows, width), BF16),
+            jax.ShapeDtypeStruct((own_rows, width), F32),
+            jax.ShapeDtypeStruct((own_rows, lanes), BF16),
+            jax.ShapeDtypeStruct((1, width), F32),
+        ),
+        in_specs=[smem] * 3 + [hbm] * 10,
+        out_specs=[vmem] * 4,
         scratch_shapes=[
-            pltpu.VMEM((own_rows, inner), BF16),
-            pltpu.VMEM((own_rows, inner), BF16),
-            pltpu.VMEM((2, own_rows, head_size), BF16),
-            pltpu.VMEM((reqs, context_len, head_size), BF16),
-            pltpu.VMEM((reqs, context_len, head_size), BF16),
+            pltpu.VMEM((rows_all, inner), BF16),
+            pltpu.VMEM((rows_all, inner), BF16),
+            pltpu.VMEM((2, rows_all, head_size), BF16),
+            pltpu.VMEM(cache_keys.shape, BF16),
+            pltpu.VMEM(cache_values.shape, BF16),
             pltpu.VMEM((inner, width), BF16),
-            pltpu.VMEM((own_rows, inner), BF16),
-            pltpu.SemaphoreType.DMA((6,)),
+            pltpu.VMEM((own_rows, width), BF16),
+            pltpu.VMEM(ids.shape, jnp.int32),
+            pltpu.VMEM(weights.shape, F32),
+            pltpu.VMEM((rows_all, inner), BF16),
+            pltpu.SemaphoreType.DMA((15,)),
         ],
-        compiler_params=pltpu.CompilerParams(vmem_limit_bytes=60 * 1024 * 1024),
+        compiler_params=pltpu.CompilerParams(vmem_limit_bytes=24 * 1024 * 1024),
         cost_estimate=pl.CostEstimate(
-            flops=2 * own_rows * inner * (width + 2 * context_len),
-            bytes_accessed=2 * inner * width + 4 * reqs * context_len * head_size,
+            flops=2 * rows_all * inner * (width + 2 * context_len),
+            bytes_accessed=2 * inner * width + 4 * reqs_all * context_len * head_size,
             transcendentals=0,
         ),
     )(
-        half.reshape(1),
-        draft_len,
-        cache_len,
-        queries,
-        out_gate,
-        draft_kv,
-        cache_keys,
-        cache_values,
-        o_weight,
+        core.reshape(1),
+        in_hbm(draft_len),
+        in_hbm(cache_len),
+        *map(
+            in_hbm,
+            (
+                ids,
+                weights,
+                gain.reshape(1, width),
+                hidden,
+                queries,
+                out_gate,
+                draft_kv,
+                cache_keys,
+                cache_values,
+                o_weight,
+            ),
+        ),
     )
 
 
-def norm_kernel(
-    experts, hidden_ref, kept_ref, received_ref, gain_ref, ids_ref, weights_ref, residual_ref, sent_ref
-):
-    residual = hidden_ref[...].astype(F32) + kept_ref[...] + received_ref[...].astype(F32)
+def norm_kernel(kept_ref, received_ref, gain_ref, table_ref, residual_ref, sent_ref):
+    residual = kept_ref[...] + received_ref[...].astype(F32)
     width = residual.shape[1]
     spread = jnp.mean(residual * residual, axis=-1, keepdims=True)
     normed = (residual * lax.rsqrt(spread + 1e-06) * gain_ref[...]).astype(BF16)
     residual_ref[...] = residual
     sent_ref[:, :width] = normed
-    rows, lanes = sent_ref.shape[0], sent_ref.shape[1] - width
-    column = lax.broadcasted_iota(jnp.int32, (rows, lanes), 1)
-    table = jnp.zeros((rows, lanes), F32)
-    for k in range(ids_ref.shape[1]):
-        index = ids_ref[:, k : k + 1]
-        weight = weights_ref[:, k : k + 1]
-        high = weight.astype(BF16).astype(F32)
-        table = jnp.where(column == index, high, table)
-        table = jnp.where(column == index + experts, weight - high, table)
-    sent_ref[:, width:] = table.astype(BF16)
-
-
-def residual_norm(hidden, kept, received, gain, ids, weights, experts):
-    rows, width = hidden.shape
-    lanes = -(-2 * experts // 128) * 128
+    sent_ref[:, width:] = table_ref[...]
+
+
+def residual_norm(kept, received, gain, table):
+    rows, width = kept.shape
     return pl.pallas_call(
-        functools.partial(norm_kernel, experts),
+        norm_kernel,
         out_shape=(
             jax.ShapeDtypeStruct((rows, width), F32),
-            jax.ShapeDtypeStruct((rows, width + lanes), BF16),
+            jax.ShapeDtypeStruct((rows, width + table.shape[1]), BF16),
         ),
         compiler_params=pltpu.CompilerParams(vmem_limit_bytes=16 * 1024 * 1024),
-    )(hidden, kept, received, gain.reshape(1, width), ids, weights)
+    )(kept, received, gain, table)
 
 
 def experts_kernel(spans, experts, where_ref, *refs):
@@ -224,6 +284,25 @@
         at += size
 
 
+def hold_kernel(where_ref, *refs):
+    out_ref = refs[-1]
+    for i in range(out_ref.shape[0]):
+        out_ref[i] = where_ref[i]
+
+
+def hold_weights(where, weights):
+    vmem = pl.BlockSpec(memory_space=pltpu.VMEM)
+    smem = pl.BlockSpec(memory_space=pltpu.SMEM)
+    return pl.pallas_call(
+        hold_kernel,
+        out_shape=jax.ShapeDtypeStruct(where.shape, where.dtype),
+        in_specs=[smem] + [vmem] * len(weights),
+        out_specs=smem,
+        compiler_params=pltpu.CompilerParams(vmem_limit_bytes=16 * 1024 * 1024),
+        cost_estimate=pl.CostEstimate(flops=20_000_000_000, bytes_accessed=0, transcendentals=0),
+    )(where, *weights)
+
+
 def plane_experts(where, rows_in, experts, own_weights, other_weights):
     arrays = [piece[0] for piece in rows_in]
     spans = tuple(piece[1:] for piece in rows_in)
@@ -304,12 +383,11 @@
     other_weights = tuple(lax.ppermute(w, "narrow", swap) for w in own_weights)
 
     arrays = (queries, out_gate, draft_kv, cache_keys, cache_values, draft_len, cache_len, o_weight)
-    outgoing = attention(1 - core, own_rows, BF16, arrays)
+    outgoing, kept, table, gain = attention(
+        core, experts, hidden_in, norm_gain, route_ids, route_weights, arrays
+    )
     received = lax.ppermute(outgoing, "narrow", swap)
-    kept = attention(core, own_rows, F32, arrays)
-    residual, sent = residual_norm(
-        hidden_in, kept, received, norm_gain, route_ids, route_weights, experts
-    )
+    residual, sent = residual_norm(kept, received, gain, table)
 
     def across(flip):
         pairs = [(i, i ^ flip) for i in range(wide)]
@@ -324,9 +402,14 @@
     where = jnp.stack([own_expert, own_expert ^ 1]).astype(jnp.int32)
 
     def run_experts(rows_in):
-        return plane_experts(where, rows_in, experts, own_weights, other_weights)
+        return plane_experts(held[-1], rows_in, experts, own_weights, other_weights)
+
+    held = [where]
 
     together = lax.optimization_barrier
+
+    def pad_rows(a):
+        return jnp.pad(a, ((0, 0), (0, sent.shape[1] - width)))
 
     blocks = [sent]
     from_x, from_y = [], []
@@ -351,7 +434,11 @@
                 ]
             )
             group += made[s]
+        if k < 2:
+            group.append(hold_weights(held[-1], (own_weights + other_weights, ())[k]))
         group = together(tuple(group))
+        if k < 2:
+            held.append(group[-1])
         from_x.append(group[0])
         from_y.append(group[1])
         if k < planes - 1:
@@ -359,66 +446,71 @@
         if k >= 2:
             made[k - 2] = group[-5:]
 
-    order = list(range(1, planes)) + [0]
-    last_y = over_y(from_x[-1][:mid])
-    last_x = over_x(from_y[-1][mid:own_rows])
-    results = []
-    pending = None
-
     def experts_of(s):
-        end = s == planes - 1
         return run_experts(
             [
                 (blocks[s], 0, own_rows),
                 (from_x[s], 0, own_rows),
                 (from_y[s], 0, own_rows),
-                (last_y, 0, mid) if end else (from_y[s + 1], own_rows, mid),
-                (last_x, 0, mid) if end else (from_x[s + 1], own_rows, mid),
+                (from_y[s + 1], own_rows if s < planes - 1 else 0, mid),
+                (from_x[s + 1], own_rows if s < planes - 1 else 0, mid),
             ]
         )
 
+    order = list(range(1, planes)) + [0]
     first = order[0]
     if first not in made:
         made[first] = experts_of(first)
-    part_x, part_y = over_x(made[first][3]), over_y(made[first][4])
-    group = [last_x, last_y, part_x, part_y]
-    if planes - 2 not in made:
-        made[planes - 2] = experts_of(planes - 2)
-        group += made[planes - 2]
-        group = together(tuple(group))
+    to_x = jnp.concatenate([from_y[-1][mid:own_rows], pad_rows(made[first][3])])
+    to_y = jnp.concatenate([from_x[-1][:mid], pad_rows(made[first][4])])
+    group = [over_x(to_x), over_y(to_y)]
+    later = planes - 2 not in made
+    if later:
+        group += experts_of(planes - 2)
+    group = together(tuple(group))
+    if later:
         made[planes - 2] = group[-5:]
-    else:
-        group = together(tuple(group))
-    last_x, last_y, part_x, part_y = group[:4]
-
+    from_x.append(group[0])
+    from_y.append(group[1])
+    part_x, part_y = group[0][mid:, :width], group[1][mid:, :width]
+
+    results = []
+    pending = None
+    carried = None
     for j, s in enumerate(order):
         own, for_x, for_y, _, _ = made[s]
-        to_x = jnp.concatenate([for_x[:mid], add_bf16(for_x[mid:], part_y)])
-        to_y = jnp.concatenate([add_bf16(for_y[:mid], part_x), for_y[mid:]])
+        to_x = [for_x[:mid], add_bf16(for_x[mid:], part_y)]
+        to_y = [add_bf16(for_y[:mid], part_x), for_y[mid:]]
         follows = order[j + 1] if j + 1 < planes else None
-        if follows is not None and follows in made:
-            to_x = jnp.concatenate([to_x, made[follows][3]])
-            to_y = jnp.concatenate([to_y, made[follows][4]])
-        group = [over_x(to_x), over_y(to_y)]
+        if follows is not None:
+            to_x.append(made[follows][3])
+            to_y.append(made[follows][4])
+        group = [over_x(jnp.concatenate(to_x)), over_y(jnp.concatenate(to_y))]
         if pending is not None:
-            group.append(shifted(planes - pending[0])(pending[1]))
-        if planes - 1 not in made:
-            made[planes - 1] = experts_of(planes - 1)
-            group += made[planes - 1]
-            group = together(tuple(group))
+            onward = 2 * pending[0] >= planes
+            group.append(shifted(1 if onward else planes - pending[0])(pending[1]))
+        later = planes - 1 not in made
+        if later:
+            group += experts_of(planes - 1)
+        group = together(tuple(group))
+        if later:
             made[planes - 1] = group[-5:]
+        carried = None
+        if pending is not None:
+            if onward and pending[0] < planes - 1:
+                carried = group[2]
+            else:
+                results.append(group[2])
+        if follows is not None:
+            part_x, part_y = group[0][own_rows:], group[1][own_rows:]
+        arrived_x, arrived_y = group[0][:own_rows], group[1][:own_rows]
+        if s:
+            terms = [own, arrived_x, arrived_y]
+            if carried is not None:
+                terms.append(carried)
+            pending = (s, add_bf16(*terms))
         else:
-            group = together(tuple(group))
-        if pending is not None:
-            results.append(group[2])
-        part_x, part_y = group[0][own_rows:], group[1][own_rows:]
-        if s:
-            pending = (s, add_bf16(own, group[0][:own_rows], group[1][:own_rows]))
-        else:
-            pending = None
-            results += [own, group[0], group[1]]
-        if follows is not None and part_x.shape[0] == 0:
-            part_x, part_y = over_x(made[follows][3]), over_y(made[follows][4])
+            results += [own, arrived_x, arrived_y]
     return final_sum(residual, results)
 
 

time: 140 us -> 111 us (0.79)
  waiting for transfers between devices: 55.6 us -> 34.5 us
  local copies, waits for them, and re-layouts: 10 us -> 3.36 us
  starting transfers between devices: 32.8 us -> 34.3 us
    ppermute x20 -> x18, waiting for transfers between devices: 19.9 us -> 7.6 us  [across(): return lambda a: lax.ppermute(a, 'wide', pairs)]
    ppermute x6, waiting for transfers between devices: 35.7 us -> 24.8 us  [shifted(): return lambda a: lax.ppermute(a, 'wide', pairs)]
    unnamed x52 -> x10, local copies, waits for them, and re-layouts: 9.83 us -> 3.19 us
    ppermute x1, waiting for transfers between devices: 0.01 us -> 2.05 us  [on_device(): received = lax.ppermute(outgoing, 'narrow', swap)]
    pallas_call x3 -> x4, Pallas kernels: 10.7 us -> 9.54 us  [the longest x1 4.77 us: attention(): pl.pallas_call(functools.partial(attention_kernel, experts), out_shape=(j...]
    ppermute x20 -> x18, starting transfers between devices: 25 us -> 25.8 us  [across(): return lambda a: lax.ppermute(a, 'wide', pairs)]
  transfers between devices with their start and end apart: 30 -> 28, of which waited for: 13 -> 15; matrix products, arithmetic and copies ran while one was open for 1% -> 1% of each run, Pallas kernels for 27% -> 33%
where the time goes in v3:
time: 111 us
  Pallas kernels  37.1 us (33%)
  waiting for transfers between devices  34.5 us (31%)
  starting transfers between devices  34.3 us (31%)
  local copies, waits for them, and re-layouts  3.36 us (3%)
  other arithmetic  1.16 us (1%)
    pallas_call x4, Pallas kernels, plane_experts(): pl.pallas_call(functools.partial(experts_kernel, spans, experts), out_sha...  26.6 us
    ppermute x18, starting transfers between devices, across(): return lambda a: lax.ppermute(a, 'wide', pairs)  25.8 us
    ppermute x6, waiting for transfers between devices, shifted(): return lambda a: lax.ppermute(a, 'wide', pairs)  24.8 us
    ppermute x18, waiting for transfers between devices, across(): return lambda a: lax.ppermute(a, 'wide', pairs)  7.6 us
    ppermute x6, starting transfers between devices, shifted(): return lambda a: lax.ppermute(a, 'wide', pairs)  7.39 us
    pallas_call x1, Pallas kernels, attention(): pl.pallas_call(functools.partial(attention_kernel, experts), out_shape=(j...  4.77 us
    pallas_call x2, Pallas kernels, hold_weights(): pl.pallas_call(hold_kernel, out_shape=jax.ShapeDtypeStruct(where.shape, w...  4.6 us
    unnamed x10, local copies, waits for them, and re-layouts  3.19 us
  transfers between devices with their start and end apart: 28, of which 15 were waited for; matrix products, arithmetic and copies ran while one was open for 1% of the time, Pallas kernels for 33%

profile of v3, /device:TPU:0, one launch (start us, length us, event | category | flops | bytes accessed | tf_op | source)
XLA Modules:
  0.0 110.7 jit_solution(6027639288517489030)
XLA Ops:
  1.0 4.8 %shard_map.145 = (bf16[64,2048]{1,0:T(8,128)(2,1)S(1)}, f32[64,2048]{1,0:T(8,128)S(1)}, bf16[64,128]{1,0:T(8,128)(2,1)S(1)}, f32[1,2048]{1,0:T(1,128)S(1)}) custom-call(s32[1]{0:T(128)} %bitcast.core_ref, s32[8]{0:T(128)} %draft_len_ref.1, s32[8]{0:T(128)} %cache_len_ref.1, s32[10,64]{1,0:T(8,128)} %bitcast.6, f32[10,64]{1,0:T(8,128)} %bitcast.7, ...), custom_call_target="tpu_custom_call" | custom-call | flops 671088640 | bytes 6291456 | tf_op jit(solution)/shard_map/pallas_call | solution.py:177
  5.9 2.0 %collective-permute-done.received_ref = bf16[64,2048]{1,0:T(8,128)(2,1)S(1)} collective-permute-done((bf16[64,2048]{1,0:T(8,128)(2,1)S(1)}, bf16[64,2048]{1,0:T(8,128)(2,1)S(1)}, u32[]{:S(2)}, u32[]{:S(2)}) %collective-permute-start) | collective-permute-done | bytes 262176 | tf_op jit(solution)/shard_map/ppermute | solution.py:389
  8.2 2.9 %collective-permute-start.1 = (bf16[64,2176]{1,0:T(8,128)(2,1)S(1)}, bf16[64,2176]{1,0:T(8,128)(2,1)S(1)}, u32[]{:S(2)}, u32[]{:S(2)}) collective-permute-start(bf16[64,2176]{1,0:T(8,128)(2,1)S(1)} %get-tuple-element.82.refs_0_), channel_id=1, source_target_pairs={{0,2},{2,0},{4,6},{6,4},{8,10},{10,8},{12,14},{14,12},{16,18},{18,... | collective-permute-start | bytes 835592 | tf_op jit(solution)/shard_map/ppermute | solution.py:394
  12.6 1.6 %collective-permute-start.3 = (bf16[64,2176]{1,0:T(8,128)(2,1)S(1)}, bf16[64,2176]{1,0:T(8,128)(2,1)S(1)}, u32[]{:S(2)}, u32[]{:S(2)}) collective-permute-start(bf16[64,2176]{1,0:T(8,128)(2,1)S(1)} %get-tuple-element.82.refs_0_), channel_id=1, source_target_pairs={{0,8},{2,10},{4,12},{6,14},{8,16},{10,18},{12,20},{14,22},{16,24},... | collective-permute-start | bytes 835592 | tf_op jit(solution)/shard_map/ppermute | solution.py:398
  14.2 1.6 %copy-done.1 = bf16[1,2048,512]{2,1,0:T(8,128)(2,1)S(1)} copy-done((bf16[1,2048,512]{2,1,0:T(8,128)(2,1)S(1)}, bf16[1,2048,512]{2,1,0:T(8,128)(2,1)}, u32[]{:S(2)}) %copy-start.1) | copy-done | bytes 2097176
  15.8 1.6 %copy-done.3 = bf16[1,512,2048]{2,1,0:T(8,128)(2,1)S(1)} copy-done((bf16[1,512,2048]{2,1,0:T(8,128)(2,1)S(1)}, bf16[1,512,2048]{2,1,0:T(8,128)(2,1)}, u32[]{:S(2)}) %copy-start.3) | copy-done | bytes 2097176
  17.4 3.5 %shard_map.147.where_ref = s32[2]{0:T(128)S(1)} custom-call(s32[2]{0:T(128)S(1)} %pad_add_fusion.where_ref, bf16[1,2048,512]{2,1,0:T(8,128)(2,1)S(1)} %copy-done, bf16[1,2048,512]{2,1,0:T(8,128)(2,1)S(1)} %copy-done.1, bf16[1,512,2048]{2,1,0:T(8,128)(2,1)S(1)} %copy-done.3, bf16[1,2048,512]{2,1,0:T(8,128)(2,1)} %collective-permute-done.4.refs_3_.refs_6_, ...), custom_call_target="tpu_custom_call" | custom-call | flops 20000000000 | tf_op jit(solution)/shard_map/pallas_call | solution.py:296
  20.9 1.7 %collective-permute-done.3.refs_0_ = bf16[64,2176]{1,0:T(8,128)(2,1)S(1)} collective-permute-done((bf16[64,2176]{1,0:T(8,128)(2,1)S(1)}, bf16[64,2176]{1,0:T(8,128)(2,1)S(1)}, u32[]{:S(2)}, u32[]{:S(2)}) %collective-permute-start.3) | collective-permute-done | bytes 278560 | tf_op jit(solution)/shard_map/ppermute | solution.py:398
  25.0 6.8 %collective-permute-done.9.refs_0_ = bf16[64,2176]{1,0:T(8,128)(2,1)S(1)} collective-permute-done((bf16[64,2176]{1,0:T(8,128)(2,1)S(1)}, bf16[64,2176]{1,0:T(8,128)(2,1)S(1)}, u32[]{:S(2)}, u32[]{:S(2)}) %collective-permute-start.9) | collective-permute-done | bytes 278560 | tf_op jit(solution)/shard_map/ppermute | solution.py:398
  35.7 1.6 %collective-permute-start.12 = (bf16[64,2176]{1,0:T(8,128)(2,1)S(1)}, bf16[64,2176]{1,0:T(8,128)(2,1)S(1)}, u32[]{:S(2)}, u32[]{:S(2)}) collective-permute-start(bf16[64,2176]{1,0:T(8,128)(2,1)S(1)} %collective-permute-done.9.refs_0_), channel_id=1, source_target_pairs={{0,8},{2,10},{4,12},{6,14},{8,16},{10,18},{12,20},{14,22},{16,24},... | collective-permute-start | bytes 835592 | tf_op jit(solution)/shard_map/ppermute | solution.py:398
  37.3 6.7 %shard_map.149 = (bf16[64,2048]{1,0:T(8,128)(2,1)S(1)}, bf16[64,2048]{1,0:T(8,128)(2,1)S(1)}, bf16[64,2048]{1,0:T(8,128)(2,1)S(1)}, bf16[32,2048]{1,0:T(8,128)(2,1)S(1)}, bf16[32,2048]{1,0:T(8,128)(2,1)S(1)}) custom-call(s32[2]{0:T(128)S(1)} %shard_map.148.where_ref, bf16[64,2176]{1,0:T(8,128)(2,1)S(1)} %get-tuple-element.82.refs_0_, ...), custom_call_target="tpu_custom_call" | custom-call | flops 3221225472 | bytes 12582912 | tf_op jit(solution)/shard_map/pallas_call | solution.py:315
  47.2 6.7 %shard_map.150 = (bf16[64,2048]{1,0:T(8,128)(2,1)S(1)}, bf16[64,2048]{1,0:T(8,128)(2,1)S(1)}, bf16[64,2048]{1,0:T(8,128)(2,1)S(1)}, bf16[32,2048]{1,0:T(8,128)(2,1)S(1)}, bf16[32,2048]{1,0:T(8,128)(2,1)S(1)}) custom-call(s32[2]{0:T(128)S(1)} %shard_map.148.where_ref, bf16[64,2176]{1,0:T(8,128)(2,1)S(1)} %collective-permute-done.3.refs_0_, ...), custom_call_target="tpu_custom_call" | custom-call | flops 3221225472 | bytes 12582912 | tf_op jit(solution)/shard_map/pallas_call | solution.py:315
  57.7 6.7 %shard_map.151 = (bf16[64,2048]{1,0:T(8,128)(2,1)S(1)}, bf16[64,2048]{1,0:T(8,128)(2,1)S(1)}, bf16[64,2048]{1,0:T(8,128)(2,1)S(1)}, bf16[32,2048]{1,0:T(8,128)(2,1)S(1)}, bf16[32,2048]{1,0:T(8,128)(2,1)S(1)}) custom-call(s32[2]{0:T(128)S(1)} %shard_map.148.where_ref, bf16[64,2176]{1,0:T(8,128)(2,1)S(1)} %collective-permute-done.9.refs_0_, ...), custom_call_target="tpu_custom_call" | custom-call | flops 3221225472 | bytes 12582912 | tf_op jit(solution)/shard_map/pallas_call | solution.py:315
  66.7 6.7 %shard_map.152 = (bf16[64,2048]{1,0:T(8,128)(2,1)S(1)}, bf16[64,2048]{1,0:T(8,128)(2,1)S(1)}, bf16[64,2048]{1,0:T(8,128)(2,1)S(1)}, bf16[32,2048]{1,0:T(8,128)(2,1)S(1)}, bf16[32,2048]{1,0:T(8,128)(2,1)S(1)}) custom-call(s32[2]{0:T(128)S(1)} %shard_map.148.where_ref, bf16[64,2176]{1,0:T(8,128)(2,1)S(1)} %collective-permute-done.12.refs_0_, ...), custom_call_target="tpu_custom_call" | custom-call | flops 3221225472 | bytes 12582912 | tf_op jit(solution)/shard_map/pallas_call | solution.py:315
  74.6 1.8 %collective-permute-start.20 = (bf16[96,2048]{1,0:T(8,128)(2,1)S(1)}, bf16[96,2048]{1,0:T(8,128)(2,1)S(1)}, u32[]{:S(2)}, u32[]{:S(2)}) collective-permute-start(bf16[96,2048]{1,0:T(8,128)(2,1)S(1)} %pad_maximum_fusion.9), channel_id=1, source_target_pairs={{0,4},{2,6},{4,0},{6,2},{8,12},{10,14},{12,8},{14,10},{16,20},{18,... | collective-permute-start | bytes 1179656 | tf_op jit(solution)/shard_map/ppermute | solution.py:394
  76.4 2.3 %collective-permute-start.19 = (bf16[96,2048]{1,0:T(8,128)(2,1)S(1)}, bf16[96,2048]{1,0:T(8,128)(2,1)S(1)}, u32[]{:S(2)}, u32[]{:S(2)}) collective-permute-start(bf16[96,2048]{1,0:T(8,128)(2,1)S(1)} %pad_maximum_fusion.8), channel_id=1, source_target_pairs={{0,2},{2,0},{4,6},{6,4},{8,10},{10,8},{12,14},{14,12},{16,18},{18,... | collective-permute-start | bytes 1179656 | tf_op jit(solution)/shard_map/ppermute | solution.py:394
  79.8 7.2 %collective-permute-done.21.refs_0_ = bf16[64,2048]{1,0:T(8,128)(2,1)S(1)} collective-permute-done((bf16[64,2048]{1,0:T(8,128)(2,1)S(1)}, bf16[64,2048]{1,0:T(8,128)(2,1)S(1)}, u32[]{:S(2)}, u32[]{:S(2)}) %collective-permute-start.21) | collective-permute-done | bytes 262176 | tf_op jit(solution)/shard_map/ppermute | solution.py:398
  88.2 2.5 %collective-permute-start.22 = (bf16[96,2048]{1,0:T(8,128)(2,1)S(1)}, bf16[96,2048]{1,0:T(8,128)(2,1)S(1)}, u32[]{:S(2)}, u32[]{:S(2)}) collective-permute-start(bf16[96,2048]{1,0:T(8,128)(2,1)S(1)} %pad_maximum_fusion.10), channel_id=1, source_target_pairs={{0,2},{2,0},{4,6},{6,4},{8,10},{10,8},{12,14},{14,12},{16,18},{18,... | collective-permute-start | bytes 1179656 | tf_op jit(solution)/shard_map/ppermute | solution.py:394
  90.9 1.7 %collective-permute-start.24 = (bf16[64,2048]{1,0:T(8,128)(2,1)S(1)}, bf16[64,2048]{1,0:T(8,128)(2,1)S(1)}, u32[]{:S(2)}, u32[]{:S(2)}) collective-permute-start(bf16[64,2048]{1,0:T(8,128)(2,1)S(1)} %add_convert_fusion.1), channel_id=1, source_target_pairs={{0,8},{2,10},{4,12},{6,14},{8,16},{10,18},{12,20},{14,22},{16,24},... | collective-permute-start | bytes 786440 | tf_op jit(solution)/shard_map/ppermute | solution.py:398
  92.6 6.6 %collective-permute-done.24 = bf16[64,2048]{1,0:T(8,128)(2,1)S(1)} collective-permute-done((bf16[64,2048]{1,0:T(8,128)(2,1)S(1)}, bf16[64,2048]{1,0:T(8,128)(2,1)S(1)}, u32[]{:S(2)}, u32[]{:S(2)}) %collective-permute-start.24) | collective-permute-done | bytes 262176 | tf_op jit(solution)/shard_map/ppermute | solution.py:398
  101.2 2.2 %collective-permute-start.26 = (bf16[64,2048]{1,0:T(8,128)(2,1)S(1)}, bf16[64,2048]{1,0:T(8,128)(2,1)S(1)}, u32[]{:S(2)}, u32[]{:S(2)}) collective-permute-start(bf16[64,2048]{1,0:T(8,128)(2,1)S(1)} %pad_maximum_fusion.13), channel_id=1, source_target_pairs={{0,4},{2,6},{4,0},{6,2},{8,12},{10,14},{12,8},{14,10},{16,20},{18,... | collective-permute-start | bytes 786440 | tf_op jit(solution)/shard_map/ppermute | solution.py:394
  103.4 2.1 %collective-permute-start.25 = (bf16[64,2048]{1,0:T(8,128)(2,1)S(1)}, bf16[64,2048]{1,0:T(8,128)(2,1)S(1)}, u32[]{:S(2)}, u32[]{:S(2)}) collective-permute-start(bf16[64,2048]{1,0:T(8,128)(2,1)S(1)} %pad_maximum_fusion.12), channel_id=1, source_target_pairs={{0,2},{2,0},{4,6},{6,4},{8,10},{10,8},{12,14},{14,12},{16,18},{18,... | collective-permute-start | bytes 786440 | tf_op jit(solution)/shard_map/ppermute | solution.py:394
  105.5 2.3 %collective-permute-done.27.refs_1_ = bf16[64,2048]{1,0:T(8,128)(2,1)S(1)} collective-permute-done((bf16[64,2048]{1,0:T(8,128)(2,1)S(1)}, bf16[64,2048]{1,0:T(8,128)(2,1)S(1)}, u32[]{:S(2)}, u32[]{:S(2)}) %collective-permute-start.27) | collective-permute-done | bytes 262176 | tf_op jit(solution)/shard_map/ppermute | solution.py:398
  107.8 2.0 %collective-permute-done.25.refs_3_ = bf16[64,2048]{1,0:T(8,128)(2,1)S(1)} collective-permute-done((bf16[64,2048]{1,0:T(8,128)(2,1)S(1)}, bf16[64,2048]{1,0:T(8,128)(2,1)S(1)}, u32[]{:S(2)}, u32[]{:S(2)}) %collective-permute-start.25) | collective-permute-done | bytes 262176 | tf_op jit(solution)/shard_map/ppermute | solution.py:394
  (92 shorter events, 24.9 us)
Async XLA Ops:
  0.0 12.6 %collective-permute-start.4 = (bf16[1,2048,512]{2,1,0:T(8,128)(2,1)}, bf16[1,2048,512]{2,1,0:T(8,128)(2,1)}, u32[]{:S(2)}, u32[]{:S(2)}) collective-permute-start(bf16[1,2048,512]{2,1,0:T(8,128)(2,1)} %refs_5_.7), channel_id=1, source_target_pairs={{0,1},{1,0},{2,3},{3,2},{4,5},{5,4},{6,7},{7,6},{8,9},{9,8},{10,11... | collective-permute-start | bytes 6291464 | tf_op jit(solution)/shard_map/ppermute | solution.py:383
  0.5 13.7 %collective-permute-start.5 = (bf16[1,2048,512]{2,1,0:T(8,128)(2,1)}, bf16[1,2048,512]{2,1,0:T(8,128)(2,1)}, u32[]{:S(2)}, u32[]{:S(2)}) collective-permute-start(bf16[1,2048,512]{2,1,0:T(8,128)(2,1)} %refs_7_.7), channel_id=1, source_target_pairs={{0,1},{1,0},{2,3},{3,2},{4,5},{5,4},{6,7},{7,6},{8,9},{9,8},{10,11... | collective-permute-start | bytes 6291464 | tf_op jit(solution)/shard_map/ppermute | solution.py:383
  0.5 13.7 %collective-permute-start.6 = (bf16[1,512,2048]{2,1,0:T(8,128)(2,1)}, bf16[1,512,2048]{2,1,0:T(8,128)(2,1)}, u32[]{:S(2)}, u32[]{:S(2)}) collective-permute-start(bf16[1,512,2048]{2,1,0:T(8,128)(2,1)} %refs_9_.7), channel_id=1, source_target_pairs={{0,1},{1,0},{2,3},{3,2},{4,5},{5,4},{6,7},{7,6},{8,9},{9,8},{10,11... | collective-permute-start | bytes 6291464 | tf_op jit(solution)/shard_map/ppermute | solution.py:383
  8.2 12.7 %collective-permute-start.1 = (bf16[64,2176]{1,0:T(8,128)(2,1)S(1)}, bf16[64,2176]{1,0:T(8,128)(2,1)S(1)}, u32[]{:S(2)}, u32[]{:S(2)}) collective-permute-start(bf16[64,2176]{1,0:T(8,128)(2,1)S(1)} %get-tuple-element.82.refs_0_), channel_id=1, source_target_pairs={{0,2},{2,0},{4,6},{6,4},{8,10},{10,8},{12,14},{14,12},{16,18},{18,... | collective-permute-start | bytes 835592 | tf_op jit(solution)/shard_map/ppermute | solution.py:394
  11.1 9.8 %collective-permute-start.2 = (bf16[64,2176]{1,0:T(8,128)(2,1)S(1)}, bf16[64,2176]{1,0:T(8,128)(2,1)S(1)}, u32[]{:S(2)}, u32[]{:S(2)}) collective-permute-start(bf16[64,2176]{1,0:T(8,128)(2,1)S(1)} %get-tuple-element.82.refs_0_), channel_id=1, source_target_pairs={{0,4},{2,6},{4,0},{6,2},{8,12},{10,14},{12,8},{14,10},{16,20},{18,... | collective-permute-start | bytes 835592 | tf_op jit(solution)/shard_map/ppermute | solution.py:394
  12.6 10.0 %collective-permute-start.3 = (bf16[64,2176]{1,0:T(8,128)(2,1)S(1)}, bf16[64,2176]{1,0:T(8,128)(2,1)S(1)}, u32[]{:S(2)}, u32[]{:S(2)}) collective-permute-start(bf16[64,2176]{1,0:T(8,128)(2,1)S(1)} %get-tuple-element.82.refs_0_), channel_id=1, source_target_pairs={{0,8},{2,10},{4,12},{6,14},{8,16},{10,18},{12,20},{14,22},{16,24},... | collective-permute-start | bytes 835592 | tf_op jit(solution)/shard_map/ppermute | solution.py:398
  22.6 9.2 %collective-permute-start.9 = (bf16[64,2176]{1,0:T(8,128)(2,1)S(1)}, bf16[64,2176]{1,0:T(8,128)(2,1)S(1)}, u32[]{:S(2)}, u32[]{:S(2)}) collective-permute-start(bf16[64,2176]{1,0:T(8,128)(2,1)S(1)} %collective-permute-done.3.refs_0_), channel_id=1, source_target_pairs={{0,8},{2,10},{4,12},{6,14},{8,16},{10,18},{12,20},{14,22},{16,24},... | collective-permute-start | bytes 835592 | tf_op jit(solution)/shard_map/ppermute | solution.py:398
  22.8 10.5 %collective-permute-start.7 = (bf16[96,2176]{1,0:T(8,128)(2,1)S(1)}, bf16[96,2176]{1,0:T(8,128)(2,1)S(1)}, u32[]{:S(2)}, u32[]{:S(2)}) collective-permute-start(bf16[96,2176]{1,0:T(8,128)(2,1)S(1)} %get-tuple-element.154), channel_id=1, source_target_pairs={{0,2},{2,0},{4,6},{6,4},{8,10},{10,8},{12,14},{14,12},{16,18},{18,... | collective-permute-start | bytes 1253384 | tf_op jit(solution)/shard_map/ppermute | solution.py:394
  23.4 10.1 %collective-permute-start.8 = (bf16[96,2176]{1,0:T(8,128)(2,1)S(1)}, bf16[96,2176]{1,0:T(8,128)(2,1)S(1)}, u32[]{:S(2)}, u32[]{:S(2)}) collective-permute-start(bf16[96,2176]{1,0:T(8,128)(2,1)S(1)} %get-tuple-element.153), channel_id=1, source_target_pairs={{0,4},{2,6},{4,0},{6,2},{8,12},{10,14},{12,8},{14,10},{16,20},{18,... | collective-permute-start | bytes 1253384 | tf_op jit(solution)/shard_map/ppermute | solution.py:394
  33.6 10.5 %collective-permute-start.10 = (bf16[96,2176]{1,0:T(8,128)(2,1)S(1)}, bf16[96,2176]{1,0:T(8,128)(2,1)S(1)}, u32[]{:S(2)}, u32[]{:S(2)}) collective-permute-start(bf16[96,2176]{1,0:T(8,128)(2,1)S(1)} %get-tuple-element.152), channel_id=1, source_target_pairs={{0,2},{2,0},{4,6},{6,4},{8,10},{10,8},{12,14},{14,12},{16,18},{18,... | collective-permute-start | bytes 1253384 | tf_op jit(solution)/shard_map/ppermute | solution.py:394
  35.2 8.9 %collective-permute-start.11 = (bf16[96,2176]{1,0:T(8,128)(2,1)S(1)}, bf16[96,2176]{1,0:T(8,128)(2,1)S(1)}, u32[]{:S(2)}, u32[]{:S(2)}) collective-permute-start(bf16[96,2176]{1,0:T(8,128)(2,1)S(1)} %get-tuple-element.151), channel_id=1, source_target_pairs={{0,4},{2,6},{4,0},{6,2},{8,12},{10,14},{12,8},{14,10},{16,20},{18,... | collective-permute-start | bytes 1253384 | tf_op jit(solution)/shard_map/ppermute | solution.py:394
  35.7 8.4 %collective-permute-start.12 = (bf16[64,2176]{1,0:T(8,128)(2,1)S(1)}, bf16[64,2176]{1,0:T(8,128)(2,1)S(1)}, u32[]{:S(2)}, u32[]{:S(2)}) collective-permute-start(bf16[64,2176]{1,0:T(8,128)(2,1)S(1)} %collective-permute-done.9.refs_0_), channel_id=1, source_target_pairs={{0,8},{2,10},{4,12},{6,14},{8,16},{10,18},{12,20},{14,22},{16,24},... | collective-permute-start | bytes 835592 | tf_op jit(solution)/shard_map/ppermute | solution.py:398
  44.2 9.6 %collective-permute-start.13 = (bf16[96,2176]{1,0:T(8,128)(2,1)S(1)}, bf16[96,2176]{1,0:T(8,128)(2,1)S(1)}, u32[]{:S(2)}, u32[]{:S(2)}) collective-permute-start(bf16[96,2176]{1,0:T(8,128)(2,1)S(1)} %get-tuple-element.150), channel_id=1, source_target_pairs={{0,2},{2,0},{4,6},{6,4},{8,10},{10,8},{12,14},{14,12},{16,18},{18,... | collective-permute-start | bytes 1253384 | tf_op jit(solution)/shard_map/ppermute | solution.py:394
  45.7 9.7 %collective-permute-start.14 = (bf16[96,2176]{1,0:T(8,128)(2,1)S(1)}, bf16[96,2176]{1,0:T(8,128)(2,1)S(1)}, u32[]{:S(2)}, u32[]{:S(2)}) collective-permute-start(bf16[96,2176]{1,0:T(8,128)(2,1)S(1)} %get-tuple-element.149), channel_id=1, source_target_pairs={{0,4},{2,6},{4,0},{6,2},{8,12},{10,14},{12,8},{14,10},{16,20},{18,... | collective-permute-start | bytes 1253384 | tf_op jit(solution)/shard_map/ppermute | solution.py:394
  55.5 8.9 %collective-permute-start.16 = (bf16[64,2176]{1,0:T(8,128)(2,1)S(1)}, bf16[64,2176]{1,0:T(8,128)(2,1)S(1)}, u32[]{:S(2)}, u32[]{:S(2)}) collective-permute-start(bf16[64,2176]{1,0:T(8,128)(2,1)S(1)} %fusion.3), channel_id=1, source_target_pairs={{0,4},{2,6},{4,0},{6,2},{8,12},{10,14},{12,8},{14,10},{16,20},{18,... | collective-permute-start | bytes 835592 | tf_op jit(solution)/shard_map/ppermute | solution.py:394
  64.5 9.3 %collective-permute-start.18 = (bf16[96,2048]{1,0:T(8,128)(2,1)S(1)}, bf16[96,2048]{1,0:T(8,128)(2,1)S(1)}, u32[]{:S(2)}, u32[]{:S(2)}) collective-permute-start(bf16[96,2048]{1,0:T(8,128)(2,1)S(1)} %pad_maximum_fusion.7), channel_id=1, source_target_pairs={{0,4},{2,6},{4,0},{6,2},{8,12},{10,14},{12,8},{14,10},{16,20},{18,... | collective-permute-start | bytes 1179656 | tf_op jit(solution)/shard_map/ppermute | solution.py:394
  65.2 9.3 %collective-permute-start.17 = (bf16[96,2048]{1,0:T(8,128)(2,1)S(1)}, bf16[96,2048]{1,0:T(8,128)(2,1)S(1)}, u32[]{:S(2)}, u32[]{:S(2)}) collective-permute-start(bf16[96,2048]{1,0:T(8,128)(2,1)S(1)} %pad_maximum_fusion.6), channel_id=1, source_target_pairs={{0,2},{2,0},{4,6},{6,4},{8,10},{10,8},{12,14},{14,12},{16,18},{18,... | collective-permute-start | bytes 1179656 | tf_op jit(solution)/shard_map/ppermute | solution.py:394
  74.6 12.4 %collective-permute-start.20 = (bf16[96,2048]{1,0:T(8,128)(2,1)S(1)}, bf16[96,2048]{1,0:T(8,128)(2,1)S(1)}, u32[]{:S(2)}, u32[]{:S(2)}) collective-permute-start(bf16[96,2048]{1,0:T(8,128)(2,1)S(1)} %pad_maximum_fusion.9), channel_id=1, source_target_pairs={{0,4},{2,6},{4,0},{6,2},{8,12},{10,14},{12,8},{14,10},{16,20},{18,... | collective-permute-start | bytes 1179656 | tf_op jit(solution)/shard_map/ppermute | solution.py:394
  76.4 11.6 %collective-permute-start.19 = (bf16[96,2048]{1,0:T(8,128)(2,1)S(1)}, bf16[96,2048]{1,0:T(8,128)(2,1)S(1)}, u32[]{:S(2)}, u32[]{:S(2)}) collective-permute-start(bf16[96,2048]{1,0:T(8,128)(2,1)S(1)} %pad_maximum_fusion.8), channel_id=1, source_target_pairs={{0,2},{2,0},{4,6},{6,4},{8,10},{10,8},{12,14},{14,12},{16,18},{18,... | collective-permute-start | bytes 1179656 | tf_op jit(solution)/shard_map/ppermute | solution.py:394
  78.8 8.2 %collective-permute-start.21 = (bf16[64,2048]{1,0:T(8,128)(2,1)S(1)}, bf16[64,2048]{1,0:T(8,128)(2,1)S(1)}, u32[]{:S(2)}, u32[]{:S(2)}) collective-permute-start(bf16[64,2048]{1,0:T(8,128)(2,1)S(1)} %add_convert_fusion.2), channel_id=1, source_target_pairs={{0,24},{2,26},{4,28},{6,30},{8,0},{10,2},{12,4},{14,6},{16,8},{18,... | collective-permute-start | bytes 786440 | tf_op jit(solution)/shard_map/ppermute | solution.py:398
  88.1 11.1 %collective-permute-start.23 = (bf16[96,2048]{1,0:T(8,128)(2,1)S(1)}, bf16[96,2048]{1,0:T(8,128)(2,1)S(1)}, u32[]{:S(2)}, u32[]{:S(2)}) collective-permute-start(bf16[96,2048]{1,0:T(8,128)(2,1)S(1)} %pad_maximum_fusion.11), channel_id=1, source_target_pairs={{0,4},{2,6},{4,0},{6,2},{8,12},{10,14},{12,8},{14,10},{16,20},{18,... | collective-permute-start | bytes 1179656 | tf_op jit(solution)/shard_map/ppermute | solution.py:394
  88.2 11.1 %collective-permute-start.22 = (bf16[96,2048]{1,0:T(8,128)(2,1)S(1)}, bf16[96,2048]{1,0:T(8,128)(2,1)S(1)}, u32[]{:S(2)}, u32[]{:S(2)}) collective-permute-start(bf16[96,2048]{1,0:T(8,128)(2,1)S(1)} %pad_maximum_fusion.10), channel_id=1, source_target_pairs={{0,2},{2,0},{4,6},{6,4},{8,10},{10,8},{12,14},{14,12},{16,18},{18,... | collective-permute-start | bytes 1179656 | tf_op jit(solution)/shard_map/ppermute | solution.py:394
  90.9 8.3 %collective-permute-start.24 = (bf16[64,2048]{1,0:T(8,128)(2,1)S(1)}, bf16[64,2048]{1,0:T(8,128)(2,1)S(1)}, u32[]{:S(2)}, u32[]{:S(2)}) collective-permute-start(bf16[64,2048]{1,0:T(8,128)(2,1)S(1)} %add_convert_fusion.1), channel_id=1, source_target_pairs={{0,8},{2,10},{4,12},{6,14},{8,16},{10,18},{12,20},{14,22},{16,24},... | collective-permute-start | bytes 786440 | tf_op jit(solution)/shard_map/ppermute | solution.py:398
  99.6 8.2 %collective-permute-start.27 = (bf16[64,2048]{1,0:T(8,128)(2,1)S(1)}, bf16[64,2048]{1,0:T(8,128)(2,1)S(1)}, u32[]{:S(2)}, u32[]{:S(2)}) collective-permute-start(bf16[64,2048]{1,0:T(8,128)(2,1)S(1)} %add_convert_fusion), channel_id=1, source_target_pairs={{0,8},{2,10},{4,12},{6,14},{8,16},{10,18},{12,20},{14,22},{16,24},... | collective-permute-start | bytes 786440 | tf_op jit(solution)/shard_map/ppermute | solution.py:398
  (9 other events, 65.8 us)

commit v4 on v3

--- a/solution.py
+++ b/solution.py
@@ -284,23 +284,34 @@
         at += size
 
 
-def hold_kernel(where_ref, *refs):
-    out_ref = refs[-1]
+def hold_kernel(count, where_ref, *refs):
+    sources, out_ref, held, sems = refs[:count], refs[count], refs[count + 1 : -1], refs[-1]
+    copies = [
+        pltpu.make_async_copy(source, target, sems.at[i])
+        for i, (source, target) in enumerate(zip(sources, held))
+    ]
+    for copy in copies:
+        copy.start()
     for i in range(out_ref.shape[0]):
         out_ref[i] = where_ref[i]
+    for copy in copies:
+        copy.wait()
 
 
 def hold_weights(where, weights):
+    count = len(weights)
     vmem = pl.BlockSpec(memory_space=pltpu.VMEM)
     smem = pl.BlockSpec(memory_space=pltpu.SMEM)
     return pl.pallas_call(
-        hold_kernel,
-        out_shape=jax.ShapeDtypeStruct(where.shape, where.dtype),
-        in_specs=[smem] + [vmem] * len(weights),
-        out_specs=smem,
+        functools.partial(hold_kernel, count),
+        out_shape=[jax.ShapeDtypeStruct(where.shape, where.dtype)]
+        + [jax.ShapeDtypeStruct(w.shape, w.dtype) for w in weights],
+        in_specs=[smem] + [pl.BlockSpec(memory_space=pl.ANY)] * count,
+        out_specs=[smem] + [vmem] * count,
+        scratch_shapes=[pltpu.SemaphoreType.DMA((max(1, count),))],
         compiler_params=pltpu.CompilerParams(vmem_limit_bytes=16 * 1024 * 1024),
         cost_estimate=pl.CostEstimate(flops=20_000_000_000, bytes_accessed=0, transcendentals=0),
-    )(where, *weights)
+    )(where, *[pltpu.with_memory_space_constraint(w, pltpu.HBM) for w in weights])
 
 
 def plane_experts(where, rows_in, experts, own_weights, other_weights):
@@ -389,128 +400,91 @@
     received = lax.ppermute(outgoing, "narrow", swap)
     residual, sent = residual_norm(kept, received, gain, table)
 
-    def across(flip):
-        pairs = [(i, i ^ flip) for i in range(wide)]
-        return lambda a: lax.ppermute(a, "wide", pairs)
+    def across(flips):
+        pairs = [
+            (i * narrow + c, (i ^ flips[c]) * narrow + c) for i in range(wide) for c in range(narrow)
+        ]
+        return lambda a: lax.ppermute(a, ("wide", "narrow"), pairs)
 
     def shifted(by):
         pairs = [(i, (i + by * plane) % wide) for i in range(wide)]
         return lambda a: lax.ppermute(a, "wide", pairs)
 
-    over_x, over_y = across(1), across(2)
+    over_u, over_v = across((1, 2)), across((2, 1))
     own_expert = chip * narrow + core
     where = jnp.stack([own_expert, own_expert ^ 1]).astype(jnp.int32)
 
-    def run_experts(rows_in):
-        return plane_experts(held[-1], rows_in, experts, own_weights, other_weights)
-
-    held = [where]
-
-    together = lax.optimization_barrier
-
-    def pad_rows(a):
-        return jnp.pad(a, ((0, 0), (0, sent.shape[1] - width)))
-
-    blocks = [sent]
-    from_x, from_y = [], []
-    made = {}
-    for k in range(planes):
-        to_x, to_y = blocks[k], blocks[k]
-        if k:
-            to_x = jnp.concatenate([to_x, from_y[-1][mid:own_rows]])
-            to_y = jnp.concatenate([to_y, from_x[-1][:mid]])
-        group = [over_x(to_x), over_y(to_y)]
-        if k < planes - 1:
-            group.append(shifted(1)(blocks[k]))
-        if k >= 2:
-            s = k - 2
-            made[s] = run_experts(
-                [
-                    (blocks[s], 0, own_rows),
-                    (from_x[s], 0, own_rows),
-                    (from_y[s], 0, own_rows),
-                    (from_y[s + 1], own_rows, mid),
-                    (from_x[s + 1], own_rows, mid),
-                ]
-            )
-            group += made[s]
-        if k < 2:
-            group.append(hold_weights(held[-1], (own_weights + other_weights, ())[k]))
-        group = together(tuple(group))
-        if k < 2:
-            held.append(group[-1])
-        from_x.append(group[0])
-        from_y.append(group[1])
-        if k < planes - 1:
-            blocks.append(group[2])
-        if k >= 2:
-            made[k - 2] = group[-5:]
+    def together(kept):
+        names = list(kept)
+        return dict(zip(names, lax.optimization_barrier(tuple(kept[n] for n in names))))
+
+    b, u, v, made = {0: sent}, {}, {}, {}
 
     def experts_of(s):
-        return run_experts(
-            [
-                (blocks[s], 0, own_rows),
-                (from_x[s], 0, own_rows),
-                (from_y[s], 0, own_rows),
-                (from_y[s + 1], own_rows if s < planes - 1 else 0, mid),
-                (from_x[s + 1], own_rows if s < planes - 1 else 0, mid),
-            ]
-        )
-
+        rows_in = [(b[s], 0, own_rows), (u[s], 0, own_rows), (v[s], 0, 2 * own_rows)]
+        return plane_experts(held["where"], rows_in, experts, held["own"], held["other"])
+
+    def phase(starts, experts_for=None, passed=()):
+        kept = {(i, "moved"): start[2] for i, start in enumerate(starts)}
+        if experts_for is not None:
+            kept.update({(i, "made"): a for i, a in enumerate(experts_of(experts_for))})
+        kept.update({(i, "passed"): a for i, a in enumerate(passed)})
+        kept = together(kept)
+        for i, (store, key, _) in enumerate(starts):
+            store[key] = kept[i, "moved"]
+        if experts_for is not None:
+            made[experts_for] = [kept[i, "made"] for i in range(3)]
+        return [kept[i, "passed"] for i in range(len(passed))]
+
+    starts = [(u, 0, over_u(b[0])), (b, 1, shifted(1)(b[0]))]
+    index, *weights = phase(starts, passed=hold_weights(where, own_weights + other_weights))
+    held = {"where": index, "own": weights[:3], "other": weights[3:]}
+    for k in range(1, planes):
+        v[k - 1] = over_v(jnp.concatenate([b[k - 1], u[k - 1]]))
+        starts = [(u, k, over_u(b[k]))]
+        if k + 1 < planes:
+            starts.append((b, k + 1, shifted(1)(b[k])))
+        if k == 1:
+            (held["where"],) = phase(starts, passed=hold_weights(held["where"], ()))
+        else:
+            phase(starts, experts_for=k - 2)
+    v[planes - 1] = over_v(jnp.concatenate([b[planes - 1], u[planes - 1]]))
     order = list(range(1, planes)) + [0]
-    first = order[0]
-    if first not in made:
-        made[first] = experts_of(first)
-    to_x = jnp.concatenate([from_y[-1][mid:own_rows], pad_rows(made[first][3])])
-    to_y = jnp.concatenate([from_x[-1][:mid], pad_rows(made[first][4])])
-    group = [over_x(to_x), over_y(to_y)]
-    later = planes - 2 not in made
-    if later:
-        group += experts_of(planes - 2)
-    group = together(tuple(group))
-    if later:
-        made[planes - 2] = group[-5:]
-    from_x.append(group[0])
-    from_y.append(group[1])
-    part_x, part_y = group[0][mid:, :width], group[1][mid:, :width]
-
+    (*waiting,) = phase([], experts_for=planes - 2, passed=[made[s][2] for s in sorted(made)])
+    for s, array in enumerate(waiting):
+        made[s][2] = array
+    back_v, back_u, back_z, sums = {}, {}, {}, {}
+    first, second = over_v(made[order[0]][2]), None
+    phase([(v, planes - 1, v[planes - 1])])
+    if planes > 3:
+        second = over_v(made[order[1]][2])
+    phase([(back_v, order[0], first)], experts_for=planes - 1)
     results = []
-    pending = None
-    carried = None
     for j, s in enumerate(order):
-        own, for_x, for_y, _, _ = made[s]
-        to_x = [for_x[:mid], add_bf16(for_x[mid:], part_y)]
-        to_y = [add_bf16(for_y[:mid], part_x), for_y[mid:]]
-        follows = order[j + 1] if j + 1 < planes else None
-        if follows is not None:
-            to_x.append(made[follows][3])
-            to_y.append(made[follows][4])
-        group = [over_x(jnp.concatenate(to_x)), over_y(jnp.concatenate(to_y))]
-        if pending is not None:
-            onward = 2 * pending[0] >= planes
-            group.append(shifted(1 if onward else planes - pending[0])(pending[1]))
-        later = planes - 1 not in made
-        if later:
-            group += experts_of(planes - 1)
-        group = together(tuple(group))
-        if later:
-            made[planes - 1] = group[-5:]
-        carried = None
-        if pending is not None:
-            if onward and pending[0] < planes - 1:
-                carried = group[2]
+        own, for_u, _ = made[s]
+        starts = [(back_u, s, over_u(add_bf16(for_u, back_v[s][own_rows:])))]
+        if j + 2 < planes:
+            starts.append((back_v, order[j + 1], second))
+        elif s:
+            starts.append((back_v, 0, over_v(made[0][2])))
+        if j + 3 < planes:
+            second = over_v(made[order[j + 2]][2])
+        if j:
+            last = order[j - 1]
+            onward = 2 * last >= planes
+            moved = shifted(1 if onward else planes - last)(sums[last])
+            if last < planes - 1:
+                starts.append((back_z, last, moved))
             else:
-                results.append(group[2])
-        if follows is not None:
-            part_x, part_y = group[0][own_rows:], group[1][own_rows:]
-        arrived_x, arrived_y = group[0][:own_rows], group[1][:own_rows]
+                back_z[last] = moved
+        (made[0][2],) = phase(starts, passed=(made[0][2],))
+        arrived = [own, back_v[s][:own_rows], back_u[s]]
         if s:
-            terms = [own, arrived_x, arrived_y]
-            if carried is not None:
-                terms.append(carried)
-            pending = (s, add_bf16(*terms))
+            if 2 * (s - 1) >= planes:
+                arrived.append(back_z.pop(s - 1))
+            sums[s] = add_bf16(*arrived)
         else:
-            results += [own, arrived_x, arrived_y]
+            results += arrived + [back_z[last] for last in sorted(back_z)]
     return final_sum(residual, results)
 
 

time: 111 us -> 107 us (0.964)
  waiting for transfers between devices: 34.5 us -> 48.2 us
  starting transfers between devices: 34.3 us -> 25.8 us
  Pallas kernels: 37.1 us -> 30.1 us
  local copies, waits for them, and re-layouts: 3.36 us -> 1.38 us
    ppermute x18 -> x16, waiting for transfers between devices: 7.6 us -> 31.9 us  [across(): return lambda a: lax.ppermute(a, ('wide', 'narrow'), pairs)]
    ppermute x6, waiting for transfers between devices: 24.8 us -> 14.2 us  [shifted(): return lambda a: lax.ppermute(a, 'wide', pairs)]
    ppermute x18 -> x16, starting transfers between devices: 25.8 us -> 16.2 us  [across(): return lambda a: lax.ppermute(a, ('wide', 'narrow'), pairs)]
    pallas_call x4, Pallas kernels: 26.6 us -> 17.4 us  [plane_experts(): pl.pallas_call(functools.partial(experts_kernel, spans, experts), out_sha...]
    pallas_call x2, Pallas kernels: 4.6 us -> 6.99 us  [hold_weights(): pl.pallas_call(functools.partial(hold_kernel, count), out_shape=[jax.Shap...]
    unnamed x10 -> x2, local copies, waits for them, and re-layouts: 3.19 us -> 1.36 us
  transfers between devices with their start and end apart: 28 -> 26, of which waited for: 15 -> 19; matrix products, arithmetic and copies ran while one was open for 1% -> 1% of each run, Pallas kernels for 33% -> 27%
where the time goes in v4:
time: 107 us
  waiting for transfers between devices  48.2 us (45%)
  Pallas kernels  30.1 us (28%)
  starting transfers between devices  25.8 us (24%)
  local copies, waits for them, and re-layouts  1.38 us (1%)
    ppermute x16, waiting for transfers between devices, across(): return lambda a: lax.ppermute(a, ('wide', 'narrow'), pairs)  31.9 us
    pallas_call x4, Pallas kernels, plane_experts(): pl.pallas_call(functools.partial(experts_kernel, spans, experts), out_sha...  17.4 us
    ppermute x16, starting transfers between devices, across(): return lambda a: lax.ppermute(a, ('wide', 'narrow'), pairs)  16.2 us
    ppermute x6, waiting for transfers between devices, shifted(): return lambda a: lax.ppermute(a, 'wide', pairs)  14.2 us
    ppermute x6, starting transfers between devices, shifted(): return lambda a: lax.ppermute(a, 'wide', pairs)  8.49 us
    pallas_call x2, Pallas kernels, hold_weights(): pl.pallas_call(functools.partial(hold_kernel, count), out_shape=[jax.Shap...  6.99 us
    pallas_call x1, Pallas kernels, attention(): pl.pallas_call(functools.partial(attention_kernel, experts), out_shape=(j...  4.64 us
  transfers between devices with their start and end apart: 26, of which 19 were waited for; matrix products, arithmetic and copies ran while one was open for 1% of the time, Pallas kernels for 27%

profile of v4, /device:TPU:0, one launch (start us, length us, event | category | flops | bytes accessed | tf_op | source)
XLA Modules:
  0.0 106.5 jit_solution(210345608574133761)
XLA Ops:
  1.0 4.6 %shard_map.145 = (bf16[64,2048]{1,0:T(8,128)(2,1)S(1)}, f32[64,2048]{1,0:T(8,128)S(1)}, bf16[64,128]{1,0:T(8,128)(2,1)S(1)}, f32[1,2048]{1,0:T(1,128)S(1)}) custom-call(s32[1]{0:T(128)} %bitcast.core_ref, s32[8]{0:T(128)} %draft_len_ref.1, s32[8]{0:T(128)} %cache_len_ref.1, s32[10,64]{1,0:T(8,128)} %bitcast.6, f32[10,64]{1,0:T(8,128)} %bitcast.7, ...), custom_call_target="tpu_custom_call" | custom-call | flops 671088640 | bytes 6291456 | tf_op jit(solution)/shard_map/pallas_call | solution.py:177
  5.8 2.1 %collective-permute-done.received_ref = bf16[64,2048]{1,0:T(8,128)(2,1)S(1)} collective-permute-done((bf16[64,2048]{1,0:T(8,128)(2,1)S(1)}, bf16[64,2048]{1,0:T(8,128)(2,1)S(1)}, u32[]{:S(2)}, u32[]{:S(2)}) %collective-permute-start) | collective-permute-done | bytes 262176 | tf_op jit(solution)/shard_map/ppermute | solution.py:400
  8.1 3.0 %collective-permute-start.2 = (bf16[64,2176]{1,0:T(8,128)(2,1)S(1)}, bf16[64,2176]{1,0:T(8,128)(2,1)S(1)}, u32[]{:S(2)}, u32[]{:S(2)}) collective-permute-start(bf16[64,2176]{1,0:T(8,128)(2,1)S(1)} %get-tuple-element.75.refs_0_), channel_id=1, source_target_pairs={{0,8},{2,10},{4,12},{6,14},{8,16},{10,18},{12,20},{14,22},{16,24},... | collective-permute-start | bytes 835592 | tf_op jit(solution)/shard_map/ppermute | solution.py:411
  14.0 5.8 %shard_map.147 = (s32[2]{0:T(128)S(1)}, bf16[1,2048,512]{2,1,0:T(8,128)(2,1)S(1)}, bf16[1,2048,512]{2,1,0:T(8,128)(2,1)S(1)}, bf16[1,512,2048]{2,1,0:T(8,128)(2,...) custom-call(s32[2]{0:T(128)S(1)} %pad_add_fusion.where_ref, ...), custom_call_target="tpu_custom_call" | custom-call | flops 20000000000 | tf_op jit(solution)/shard_map/pallas_call | solution.py:305
  24.8 5.3 %collective-permute-done.7.refs_0_ = bf16[64,2176]{1,0:T(8,128)(2,1)S(1)} collective-permute-done((bf16[64,2176]{1,0:T(8,128)(2,1)S(1)}, bf16[64,2176]{1,0:T(8,128)(2,1)S(1)}, u32[]{:S(2)}, u32[]{:S(2)}) %collective-permute-start.7) | collective-permute-done | bytes 278560 | tf_op jit(solution)/shard_map/ppermute | solution.py:411
  33.1 1.6 %collective-permute-start.13 = (bf16[128,2176]{1,0:T(8,128)(2,1)S(1)}, bf16[128,2176]{1,0:T(8,128)(2,1)S(1)}, u32[]{:S(2)}, u32[]{:S(2)}) collective-permute-start(bf16[128,2176]{1,0:T(8,128)(2,1)S(1)} %pad_maximum_fusion.2), channel_id=1, source_target_pairs={{0,4},{1,3},{2,6},{3,1},{4,0},{5,7},{6,2},{7,5},{8,12},{9,11},{10,... | collective-permute-start | bytes 1671176 | tf_op jit(solution)/shard_map/ppermute | solution.py:407
  34.7 4.4 %shard_map.149 = (bf16[64,2048]{1,0:T(8,128)(2,1)S(1)}, bf16[64,2048]{1,0:T(8,128)(2,1)S(1)}, bf16[128,2048]{1,0:T(8,128)(2,1)S(1)}) custom-call(s32[2]{0:T(128)S(1)} %shard_map.148.where_ref, bf16[64,2176]{1,0:T(8,128)(2,1)S(1)} %get-tuple-element.75.refs_0_, bf16[64,2176]{1,0:T(8,128)(2,1)S(1)} %collective-permute-done.1.refs_1_, ...), custom_call_target="tpu_custom_call" | custom-call | flops 3221225472 | bytes 12582912 | tf_op jit(solution)/shard_map/pallas_call | solution.py:326
  39.4 2.8 %collective-permute-done.8.refs_1_ = bf16[64,2176]{1,0:T(8,128)(2,1)S(1)} collective-permute-done((bf16[64,2176]{1,0:T(8,128)(2,1)S(1)}, bf16[64,2176]{1,0:T(8,128)(2,1)S(1)}, u32[]{:S(2)}, u32[]{:S(2)}) %collective-permute-start.8) | collective-permute-done | bytes 278560 | tf_op jit(solution)/shard_map/ppermute | solution.py:407
  42.7 1.6 %collective-permute-start.11 = (bf16[128,2176]{1,0:T(8,128)(2,1)S(1)}, bf16[128,2176]{1,0:T(8,128)(2,1)S(1)}, u32[]{:S(2)}, u32[]{:S(2)}) collective-permute-start(bf16[128,2176]{1,0:T(8,128)(2,1)S(1)} %pad_maximum_fusion.1), channel_id=1, source_target_pairs={{0,4},{1,3},{2,6},{3,1},{4,0},{5,7},{6,2},{7,5},{8,12},{9,11},{10,... | collective-permute-start | bytes 1671176 | tf_op jit(solution)/shard_map/ppermute | solution.py:407
  45.5 4.4 %shard_map.151 = (bf16[64,2048]{1,0:T(8,128)(2,1)S(1)}, bf16[64,2048]{1,0:T(8,128)(2,1)S(1)}, bf16[128,2048]{1,0:T(8,128)(2,1)S(1)}) custom-call(s32[2]{0:T(128)S(1)} %shard_map.148.where_ref, bf16[64,2176]{1,0:T(8,128)(2,1)S(1)} %collective-permute-done.2.refs_0_, bf16[64,2176]{1,0:T(8,128)(2,1)S(1)} %collective-permute-done.6.refs_1_, ...), custom_call_target="tpu_custom_call" | custom-call | flops 3221225472 | bytes 12582912 | tf_op jit(solution)/shard_map/pallas_call | solution.py:326
  49.8 2.0 %collective-permute-done.12.refs_1_ = bf16[64,2176]{1,0:T(8,128)(2,1)S(1)} collective-permute-done((bf16[64,2176]{1,0:T(8,128)(2,1)S(1)}, bf16[64,2176]{1,0:T(8,128)(2,1)S(1)}, u32[]{:S(2)}, u32[]{:S(2)}) %collective-permute-start.12) | collective-permute-done | bytes 278560 | tf_op jit(solution)/shard_map/ppermute | solution.py:407
  51.9 1.6 %collective-permute-start.15 = (bf16[128,2176]{1,0:T(8,128)(2,1)S(1)}, bf16[128,2176]{1,0:T(8,128)(2,1)S(1)}, u32[]{:S(2)}, u32[]{:S(2)}) collective-permute-start(bf16[128,2176]{1,0:T(8,128)(2,1)S(1)} %pad_maximum_fusion.3), channel_id=1, source_target_pairs={{0,4},{1,3},{2,6},{3,1},{4,0},{5,7},{6,2},{7,5},{8,12},{9,11},{10,... | collective-permute-start | bytes 1671176 | tf_op jit(solution)/shard_map/ppermute | solution.py:407
  53.5 4.4 %shard_map.150 = (bf16[64,2048]{1,0:T(8,128)(2,1)S(1)}, bf16[64,2048]{1,0:T(8,128)(2,1)S(1)}, bf16[128,2048]{1,0:T(8,128)(2,1)S(1)}) custom-call(s32[2]{0:T(128)S(1)} %shard_map.148.where_ref, bf16[64,2176]{1,0:T(8,128)(2,1)S(1)} %collective-permute-done.7.refs_0_, bf16[64,2176]{1,0:T(8,128)(2,1)S(1)} %collective-permute-done.8.refs_1_, ...), custom_call_target="tpu_custom_call" | custom-call | flops 3221225472 | bytes 12582912 | tf_op jit(solution)/shard_map/pallas_call | solution.py:326
  61.5 4.4 %shard_map.152 = (bf16[64,2048]{1,0:T(8,128)(2,1)S(1)}, bf16[64,2048]{1,0:T(8,128)(2,1)S(1)}, bf16[128,2048]{1,0:T(8,128)(2,1)S(1)}) custom-call(s32[2]{0:T(128)S(1)} %shard_map.148.where_ref, bf16[64,2176]{1,0:T(8,128)(2,1)S(1)} %collective-permute-done.9.refs_0_, bf16[64,2176]{1,0:T(8,128)(2,1)S(1)} %collective-permute-done.12.refs_1_, ...), custom_call_target="tpu_custom_call" | custom-call | flops 3221225472 | bytes 12582912 | tf_op jit(solution)/shard_map/pallas_call | solution.py:326
  65.9 2.5 %collective-permute-done.14 = bf16[128,2048]{1,0:T(8,128)(2,1)S(1)} collective-permute-done((bf16[128,2048]{1,0:T(8,128)(2,1)S(1)}, bf16[128,2048]{1,0:T(8,128)(2,1)S(1)}, u32[]{:S(2)}, u32[]{:S(2)}) %collective-permute-start.14) | collective-permute-done | bytes 524320 | tf_op jit(solution)/shard_map/ppermute | solution.py:407
  68.5 1.6 %collective-permute-start.19 = (bf16[128,2048]{1,0:T(8,128)(2,1)S(1)}, bf16[128,2048]{1,0:T(8,128)(2,1)S(1)}, u32[]{:S(2)}, u32[]{:S(2)}) collective-permute-start(bf16[128,2048]{1,0:T(8,128)(2,1)S(1)} %get-tuple-element.121), channel_id=1, source_target_pairs={{0,4},{1,3},{2,6},{3,1},{4,0},{5,7},{6,2},{7,5},{8,12},{9,11},{10,... | collective-permute-start | bytes 1572872 | tf_op jit(solution)/shard_map/ppermute | solution.py:407
  70.0 5.5 %collective-permute-done.17 = bf16[128,2048]{1,0:T(8,128)(2,1)S(1)} collective-permute-done((bf16[128,2048]{1,0:T(8,128)(2,1)S(1)}, bf16[128,2048]{1,0:T(8,128)(2,1)S(1)}, u32[]{:S(2)}, u32[]{:S(2)}) %collective-permute-start.17) | collective-permute-done | bytes 524320 | tf_op jit(solution)/shard_map/ppermute | solution.py:407
  77.1 2.0 %collective-permute-start.20 = (bf16[64,2048]{1,0:T(8,128)(2,1)S(1)}, bf16[64,2048]{1,0:T(8,128)(2,1)S(1)}, u32[]{:S(2)}, u32[]{:S(2)}) collective-permute-start(bf16[64,2048]{1,0:T(8,128)(2,1)S(1)} %add_convert_fusion.4), channel_id=1, source_target_pairs={{0,24},{2,26},{4,28},{6,30},{8,0},{10,2},{12,4},{14,6},{16,8},{18,... | collective-permute-start | bytes 786440 | tf_op jit(solution)/shard_map/ppermute | solution.py:411
  79.5 4.5 %collective-permute-done.19 = bf16[128,2048]{1,0:T(8,128)(2,1)S(1)} collective-permute-done((bf16[128,2048]{1,0:T(8,128)(2,1)S(1)}, bf16[128,2048]{1,0:T(8,128)(2,1)S(1)}, u32[]{:S(2)}, u32[]{:S(2)}) %collective-permute-start.19) | collective-permute-done | bytes 524320 | tf_op jit(solution)/shard_map/ppermute | solution.py:407
  84.0 1.7 %collective-permute-done.18 = bf16[64,2048]{1,0:T(8,128)(2,1)S(1)} collective-permute-done((bf16[64,2048]{1,0:T(8,128)(2,1)S(1)}, bf16[64,2048]{1,0:T(8,128)(2,1)S(1)}, u32[]{:S(2)}, u32[]{:S(2)}) %collective-permute-start.18) | collective-permute-done | bytes 262176 | tf_op jit(solution)/shard_map/ppermute | solution.py:407
  85.9 2.6 %collective-permute-start.22 = (bf16[128,2048]{1,0:T(8,128)(2,1)S(1)}, bf16[128,2048]{1,0:T(8,128)(2,1)S(1)}, u32[]{:S(2)}, u32[]{:S(2)}) collective-permute-start(bf16[128,2048]{1,0:T(8,128)(2,1)S(1)} %get-tuple-element.126), channel_id=1, source_target_pairs={{0,4},{1,3},{2,6},{3,1},{4,0},{5,7},{6,2},{7,5},{8,12},{9,11},{10,... | collective-permute-start | bytes 1572872 | tf_op jit(solution)/shard_map/ppermute | solution.py:407
  88.6 5.4 %collective-permute-done.23 = bf16[64,2048]{1,0:T(8,128)(2,1)S(1)} collective-permute-done((bf16[64,2048]{1,0:T(8,128)(2,1)S(1)}, bf16[64,2048]{1,0:T(8,128)(2,1)S(1)}, u32[]{:S(2)}, u32[]{:S(2)}) %collective-permute-start.23) | collective-permute-done | bytes 262176 | tf_op jit(solution)/shard_map/ppermute | solution.py:411
  97.2 5.5 %collective-permute-done.24.refs_2_ = bf16[64,2048]{1,0:T(8,128)(2,1)S(1)} collective-permute-done((bf16[64,2048]{1,0:T(8,128)(2,1)S(1)}, bf16[64,2048]{1,0:T(8,128)(2,1)S(1)}, u32[]{:S(2)}, u32[]{:S(2)}) %collective-permute-start.24) | collective-permute-done | bytes 262176 | tf_op jit(solution)/shard_map/ppermute | solution.py:407
  102.7 3.0 %collective-permute-done.25.refs_4_ = bf16[64,2048]{1,0:T(8,128)(2,1)S(1)} collective-permute-done((bf16[64,2048]{1,0:T(8,128)(2,1)S(1)}, bf16[64,2048]{1,0:T(8,128)(2,1)S(1)}, u32[]{:S(2)}, u32[]{:S(2)}) %collective-permute-start.25) | collective-permute-done | bytes 262176 | tf_op jit(solution)/shard_map/ppermute | solution.py:411
  (52 shorter events, 24.3 us)
Async XLA Ops:
  0.0 12.6 %collective-permute-start.3 = (bf16[1,2048,512]{2,1,0:T(8,128)(2,1)}, bf16[1,2048,512]{2,1,0:T(8,128)(2,1)S(1)}, u32[]{:S(2)}, u32[]{:S(2)}) collective-permute-start(bf16[1,2048,512]{2,1,0:T(8,128)(2,1)} %refs_0_.1), channel_id=1, source_target_pairs={{0,1},{1,0},{2,3},{3,2},{4,5},{5,4},{6,7},{7,6},{8,9},{9,8},{10,11... | collective-permute-start | bytes 6291464 | tf_op jit(solution)/shard_map/ppermute | solution.py:394
  0.5 12.2 %collective-permute-start.4 = (bf16[1,2048,512]{2,1,0:T(8,128)(2,1)}, bf16[1,2048,512]{2,1,0:T(8,128)(2,1)}, u32[]{:S(2)}, u32[]{:S(2)}) collective-permute-start(bf16[1,2048,512]{2,1,0:T(8,128)(2,1)} %refs_1_.1), channel_id=1, source_target_pairs={{0,1},{1,0},{2,3},{3,2},{4,5},{5,4},{6,7},{7,6},{8,9},{9,8},{10,11... | collective-permute-start | bytes 6291464 | tf_op jit(solution)/shard_map/ppermute | solution.py:394
  0.5 12.1 %collective-permute-start.5 = (bf16[1,512,2048]{2,1,0:T(8,128)(2,1)}, bf16[1,512,2048]{2,1,0:T(8,128)(2,1)}, u32[]{:S(2)}, u32[]{:S(2)}) collective-permute-start(bf16[1,512,2048]{2,1,0:T(8,128)(2,1)} %refs_2_.1), channel_id=1, source_target_pairs={{0,1},{1,0},{2,3},{3,2},{4,5},{5,4},{6,7},{7,6},{8,9},{9,8},{10,11... | collective-permute-start | bytes 6291464 | tf_op jit(solution)/shard_map/ppermute | solution.py:394
  8.1 12.0 %collective-permute-start.2 = (bf16[64,2176]{1,0:T(8,128)(2,1)S(1)}, bf16[64,2176]{1,0:T(8,128)(2,1)S(1)}, u32[]{:S(2)}, u32[]{:S(2)}) collective-permute-start(bf16[64,2176]{1,0:T(8,128)(2,1)S(1)} %get-tuple-element.75.refs_0_), channel_id=1, source_target_pairs={{0,8},{2,10},{4,12},{6,14},{8,16},{10,18},{12,20},{14,22},{16,24},... | collective-permute-start | bytes 835592 | tf_op jit(solution)/shard_map/ppermute | solution.py:411
  11.1 9.0 %collective-permute-start.1 = (bf16[64,2176]{1,0:T(8,128)(2,1)S(1)}, bf16[64,2176]{1,0:T(8,128)(2,1)S(1)}, u32[]{:S(2)}, u32[]{:S(2)}) collective-permute-start(bf16[64,2176]{1,0:T(8,128)(2,1)S(1)} %get-tuple-element.75.refs_0_), channel_id=1, source_target_pairs={{0,2},{1,5},{2,0},{3,7},{4,6},{5,1},{6,4},{7,3},{8,10},{9,13},{10,... | collective-permute-start | bytes 835592 | tf_op jit(solution)/shard_map/ppermute | solution.py:407
  20.1 10.0 %collective-permute-start.7 = (bf16[64,2176]{1,0:T(8,128)(2,1)S(1)}, bf16[64,2176]{1,0:T(8,128)(2,1)S(1)}, u32[]{:S(2)}, u32[]{:S(2)}) collective-permute-start(bf16[64,2176]{1,0:T(8,128)(2,1)S(1)} %collective-permute-done.2.refs_0_), channel_id=1, source_target_pairs={{0,8},{2,10},{4,12},{6,14},{8,16},{10,18},{12,20},{14,22},{16,24},... | collective-permute-start | bytes 835592 | tf_op jit(solution)/shard_map/ppermute | solution.py:411
  21.5 9.6 %collective-permute-start.6 = (bf16[64,2176]{1,0:T(8,128)(2,1)S(1)}, bf16[64,2176]{1,0:T(8,128)(2,1)S(1)}, u32[]{:S(2)}, u32[]{:S(2)}) collective-permute-start(bf16[64,2176]{1,0:T(8,128)(2,1)S(1)} %collective-permute-done.2.refs_0_), channel_id=1, source_target_pairs={{0,2},{1,5},{2,0},{3,7},{4,6},{5,1},{6,4},{7,3},{8,10},{9,13},{10,... | collective-permute-start | bytes 835592 | tf_op jit(solution)/shard_map/ppermute | solution.py:407
  22.1 12.6 %collective-permute-start.10 = (bf16[128,2176]{1,0:T(8,128)(2,1)S(1)}, bf16[128,2176]{1,0:T(8,128)(2,1)S(1)}, u32[]{:S(2)}, u32[]{:S(2)}) collective-permute-start(bf16[128,2176]{1,0:T(8,128)(2,1)S(1)} %pad_maximum_fusion), channel_id=1, source_target_pairs={{0,4},{1,3},{2,6},{3,1},{4,0},{5,7},{6,2},{7,5},{8,12},{9,11},{10,... | collective-permute-start | bytes 1671176 | tf_op jit(solution)/shard_map/ppermute | solution.py:407
  31.1 8.3 %collective-permute-start.9 = (bf16[64,2176]{1,0:T(8,128)(2,1)S(1)}, bf16[64,2176]{1,0:T(8,128)(2,1)S(1)}, u32[]{:S(2)}, u32[]{:S(2)}) collective-permute-start(bf16[64,2176]{1,0:T(8,128)(2,1)S(1)} %collective-permute-done.7.refs_0_), channel_id=1, source_target_pairs={{0,8},{2,10},{4,12},{6,14},{8,16},{10,18},{12,20},{14,22},{16,24},... | collective-permute-start | bytes 835592 | tf_op jit(solution)/shard_map/ppermute | solution.py:411
  32.7 9.6 %collective-permute-start.8 = (bf16[64,2176]{1,0:T(8,128)(2,1)S(1)}, bf16[64,2176]{1,0:T(8,128)(2,1)S(1)}, u32[]{:S(2)}, u32[]{:S(2)}) collective-permute-start(bf16[64,2176]{1,0:T(8,128)(2,1)S(1)} %collective-permute-done.7.refs_0_), channel_id=1, source_target_pairs={{0,2},{1,5},{2,0},{3,7},{4,6},{5,1},{6,4},{7,3},{8,10},{9,13},{10,... | collective-permute-start | bytes 835592 | tf_op jit(solution)/shard_map/ppermute | solution.py:407
  33.1 12.4 %collective-permute-start.13 = (bf16[128,2176]{1,0:T(8,128)(2,1)S(1)}, bf16[128,2176]{1,0:T(8,128)(2,1)S(1)}, u32[]{:S(2)}, u32[]{:S(2)}) collective-permute-start(bf16[128,2176]{1,0:T(8,128)(2,1)S(1)} %pad_maximum_fusion.2), channel_id=1, source_target_pairs={{0,4},{1,3},{2,6},{3,1},{4,0},{5,7},{6,2},{7,5},{8,12},{9,11},{10,... | collective-permute-start | bytes 1671176 | tf_op jit(solution)/shard_map/ppermute | solution.py:407
  42.3 9.6 %collective-permute-start.12 = (bf16[64,2176]{1,0:T(8,128)(2,1)S(1)}, bf16[64,2176]{1,0:T(8,128)(2,1)S(1)}, u32[]{:S(2)}, u32[]{:S(2)}) collective-permute-start(bf16[64,2176]{1,0:T(8,128)(2,1)S(1)} %collective-permute-done.9.refs_0_), channel_id=1, source_target_pairs={{0,2},{1,5},{2,0},{3,7},{4,6},{5,1},{6,4},{7,3},{8,10},{9,13},{10,... | collective-permute-start | bytes 835592 | tf_op jit(solution)/shard_map/ppermute | solution.py:407
  42.7 10.8 %collective-permute-start.11 = (bf16[128,2176]{1,0:T(8,128)(2,1)S(1)}, bf16[128,2176]{1,0:T(8,128)(2,1)S(1)}, u32[]{:S(2)}, u32[]{:S(2)}) collective-permute-start(bf16[128,2176]{1,0:T(8,128)(2,1)S(1)} %pad_maximum_fusion.1), channel_id=1, source_target_pairs={{0,4},{1,3},{2,6},{3,1},{4,0},{5,7},{6,2},{7,5},{8,12},{9,11},{10,... | collective-permute-start | bytes 1671176 | tf_op jit(solution)/shard_map/ppermute | solution.py:407
  51.9 9.6 %collective-permute-start.15 = (bf16[128,2176]{1,0:T(8,128)(2,1)S(1)}, bf16[128,2176]{1,0:T(8,128)(2,1)S(1)}, u32[]{:S(2)}, u32[]{:S(2)}) collective-permute-start(bf16[128,2176]{1,0:T(8,128)(2,1)S(1)} %pad_maximum_fusion.3), channel_id=1, source_target_pairs={{0,4},{1,3},{2,6},{3,1},{4,0},{5,7},{6,2},{7,5},{8,12},{9,11},{10,... | collective-permute-start | bytes 1671176 | tf_op jit(solution)/shard_map/ppermute | solution.py:407
  57.8 10.5 %collective-permute-start.14 = (bf16[128,2048]{1,0:T(8,128)(2,1)S(1)}, bf16[128,2048]{1,0:T(8,128)(2,1)S(1)}, u32[]{:S(2)}, u32[]{:S(2)}) collective-permute-start(bf16[128,2048]{1,0:T(8,128)(2,1)S(1)} %get-tuple-element.109), channel_id=1, source_target_pairs={{0,4},{1,3},{2,6},{3,1},{4,0},{5,7},{6,2},{7,5},{8,12},{9,11},{10,... | collective-permute-start | bytes 1572872 | tf_op jit(solution)/shard_map/ppermute | solution.py:407
  58.4 17.1 %collective-permute-start.17 = (bf16[128,2048]{1,0:T(8,128)(2,1)S(1)}, bf16[128,2048]{1,0:T(8,128)(2,1)S(1)}, u32[]{:S(2)}, u32[]{:S(2)}) collective-permute-start(bf16[128,2048]{1,0:T(8,128)(2,1)S(1)} %get-tuple-element.118), channel_id=1, source_target_pairs={{0,4},{1,3},{2,6},{3,1},{4,0},{5,7},{6,2},{7,5},{8,12},{9,11},{10,... | collective-permute-start | bytes 1572872 | tf_op jit(solution)/shard_map/ppermute | solution.py:407
  68.4 8.6 %collective-permute-start.16 = (bf16[64,2048]{1,0:T(8,128)(2,1)S(1)}, bf16[64,2048]{1,0:T(8,128)(2,1)S(1)}, u32[]{:S(2)}, u32[]{:S(2)}) collective-permute-start(bf16[64,2048]{1,0:T(8,128)(2,1)S(1)} %add_convert_fusion.6), channel_id=1, source_target_pairs={{0,2},{1,5},{2,0},{3,7},{4,6},{5,1},{6,4},{7,3},{8,10},{9,13},{10,... | collective-permute-start | bytes 786440 | tf_op jit(solution)/shard_map/ppermute | solution.py:407
  68.5 15.5 %collective-permute-start.19 = (bf16[128,2048]{1,0:T(8,128)(2,1)S(1)}, bf16[128,2048]{1,0:T(8,128)(2,1)S(1)}, u32[]{:S(2)}, u32[]{:S(2)}) collective-permute-start(bf16[128,2048]{1,0:T(8,128)(2,1)S(1)} %get-tuple-element.121), channel_id=1, source_target_pairs={{0,4},{1,3},{2,6},{3,1},{4,0},{5,7},{6,2},{7,5},{8,12},{9,11},{10,... | collective-permute-start | bytes 1572872 | tf_op jit(solution)/shard_map/ppermute | solution.py:407
  77.1 6.8 %collective-permute-start.20 = (bf16[64,2048]{1,0:T(8,128)(2,1)S(1)}, bf16[64,2048]{1,0:T(8,128)(2,1)S(1)}, u32[]{:S(2)}, u32[]{:S(2)}) collective-permute-start(bf16[64,2048]{1,0:T(8,128)(2,1)S(1)} %add_convert_fusion.4), channel_id=1, source_target_pairs={{0,24},{2,26},{4,28},{6,30},{8,0},{10,2},{12,4},{14,6},{16,8},{18,... | collective-permute-start | bytes 786440 | tf_op jit(solution)/shard_map/ppermute | solution.py:411
  85.7 8.2 %collective-permute-start.23 = (bf16[64,2048]{1,0:T(8,128)(2,1)S(1)}, bf16[64,2048]{1,0:T(8,128)(2,1)S(1)}, u32[]{:S(2)}, u32[]{:S(2)}) collective-permute-start(bf16[64,2048]{1,0:T(8,128)(2,1)S(1)} %add_convert_fusion.2), channel_id=1, source_target_pairs={{0,8},{2,10},{4,12},{6,14},{8,16},{10,18},{12,20},{14,22},{16,24},... | collective-permute-start | bytes 786440 | tf_op jit(solution)/shard_map/ppermute | solution.py:411
  85.9 10.3 %collective-permute-start.22 = (bf16[128,2048]{1,0:T(8,128)(2,1)S(1)}, bf16[128,2048]{1,0:T(8,128)(2,1)S(1)}, u32[]{:S(2)}, u32[]{:S(2)}) collective-permute-start(bf16[128,2048]{1,0:T(8,128)(2,1)S(1)} %get-tuple-element.126), channel_id=1, source_target_pairs={{0,4},{1,3},{2,6},{3,1},{4,0},{5,7},{6,2},{7,5},{8,12},{9,11},{10,... | collective-permute-start | bytes 1572872 | tf_op jit(solution)/shard_map/ppermute | solution.py:407
  88.5 6.4 %collective-permute-start.21 = (bf16[64,2048]{1,0:T(8,128)(2,1)S(1)}, bf16[64,2048]{1,0:T(8,128)(2,1)S(1)}, u32[]{:S(2)}, u32[]{:S(2)}) collective-permute-start(bf16[64,2048]{1,0:T(8,128)(2,1)S(1)} %add_convert_fusion.3), channel_id=1, source_target_pairs={{0,2},{1,5},{2,0},{3,7},{4,6},{5,1},{6,4},{7,3},{8,10},{9,13},{10,... | collective-permute-start | bytes 786440 | tf_op jit(solution)/shard_map/ppermute | solution.py:407
  96.2 6.4 %collective-permute-start.24 = (bf16[64,2048]{1,0:T(8,128)(2,1)S(1)}, bf16[64,2048]{1,0:T(8,128)(2,1)S(1)}, u32[]{:S(2)}, u32[]{:S(2)}) collective-permute-start(bf16[64,2048]{1,0:T(8,128)(2,1)S(1)} %add_convert_fusion.1), channel_id=1, source_target_pairs={{0,2},{1,5},{2,0},{3,7},{4,6},{5,1},{6,4},{7,3},{8,10},{9,13},{10,... | collective-permute-start | bytes 786440 | tf_op jit(solution)/shard_map/ppermute | solution.py:407
  96.8 8.9 %collective-permute-start.25 = (bf16[64,2048]{1,0:T(8,128)(2,1)S(1)}, bf16[64,2048]{1,0:T(8,128)(2,1)S(1)}, u32[]{:S(2)}, u32[]{:S(2)}) collective-permute-start(bf16[64,2048]{1,0:T(8,128)(2,1)S(1)} %add_convert_fusion), channel_id=1, source_target_pairs={{0,8},{2,10},{4,12},{6,14},{8,16},{10,18},{12,20},{14,22},{16,24},... | collective-permute-start | bytes 786440 | tf_op jit(solution)/shard_map/ppermute | solution.py:411
  (3 other events, 10.1 us)

commit v5 on v4

--- a/solution.py
+++ b/solution.py
@@ -11,6 +11,11 @@
 BF16 = jnp.bfloat16
 F32 = jnp.float32
 LOWEST = -1e30
+STEP_FLOPS = 200_000_000
+
+
+def in_hbm(a):
+    return pltpu.with_memory_space_constraint(a, pltpu.HBM)
 
 
 def _dot(a, b):
@@ -171,9 +176,6 @@
     hbm = pl.BlockSpec(memory_space=pl.ANY)
     ids, weights = ids.T, weights.T
 
-    def in_hbm(a):
-        return pltpu.with_memory_space_constraint(a, pltpu.HBM)
-
     return pl.pallas_call(
         functools.partial(attention_kernel, experts),
         out_shape=(
@@ -310,8 +312,21 @@
         out_specs=[smem] + [vmem] * count,
         scratch_shapes=[pltpu.SemaphoreType.DMA((max(1, count),))],
         compiler_params=pltpu.CompilerParams(vmem_limit_bytes=16 * 1024 * 1024),
-        cost_estimate=pl.CostEstimate(flops=20_000_000_000, bytes_accessed=0, transcendentals=0),
-    )(where, *[pltpu.with_memory_space_constraint(w, pltpu.HBM) for w in weights])
+        cost_estimate=pl.CostEstimate(flops=STEP_FLOPS, bytes_accessed=0, transcendentals=0),
+    )(where, *weights)
+
+
+def step_kernel(token_ref, out_ref):
+    out_ref[...] = token_ref[...]
+
+
+def step(token):
+    return pl.pallas_call(
+        step_kernel,
+        out_shape=jax.ShapeDtypeStruct(token.shape, token.dtype),
+        compiler_params=pltpu.CompilerParams(vmem_limit_bytes=16 * 1024 * 1024),
+        cost_estimate=pl.CostEstimate(flops=STEP_FLOPS, bytes_accessed=0, transcendentals=0),
+    )(token)
 
 
 def plane_experts(where, rows_in, experts, own_weights, other_weights):
@@ -330,15 +345,11 @@
         out_specs=[vmem] * len(spans),
         scratch_shapes=[pltpu.VMEM((count, padded), BF16), pltpu.VMEM((count, width), F32)],
         compiler_params=pltpu.CompilerParams(vmem_limit_bytes=24 * 1024 * 1024),
-        cost_estimate=pl.CostEstimate(
-            flops=12 * count * width * hidden,
-            bytes_accessed=12 * width * hidden,
-            transcendentals=0,
-        ),
+        cost_estimate=pl.CostEstimate(flops=STEP_FLOPS, bytes_accessed=0, transcendentals=0),
     )(where, *arrays, *weights)
 
 
-def final_kernel(residual_ref, *refs):
+def final_kernel(token_ref, residual_ref, *refs):
     out_ref = refs[-1]
     mix = refs[0][...].astype(F32)
     for ref in refs[1:-1]:
@@ -346,12 +357,12 @@
     out_ref[...] = (residual_ref[...] + mix).astype(BF16)
 
 
-def final_sum(residual, pieces):
+def final_sum(token, residual, pieces):
     return pl.pallas_call(
         final_kernel,
         out_shape=jax.ShapeDtypeStruct(residual.shape, BF16),
         compiler_params=pltpu.CompilerParams(vmem_limit_bytes=16 * 1024 * 1024),
-    )(residual, *pieces)
+    )(token, residual, *pieces)
 
 
 def add_bf16(*terms):
@@ -391,7 +402,7 @@
 
     swap = [(0, 1), (1, 0)]
     own_weights = (w_gate, w_up, w_down)
-    other_weights = tuple(lax.ppermute(w, "narrow", swap) for w in own_weights)
+    other_weights = [lax.ppermute(w, "narrow", swap) for w in own_weights]
 
     arrays = (queries, out_gate, draft_kv, cache_keys, cache_values, draft_len, cache_len, o_weight)
     outgoing, kept, table, gain = attention(
@@ -414,78 +425,90 @@
     own_expert = chip * narrow + core
     where = jnp.stack([own_expert, own_expert ^ 1]).astype(jnp.int32)
 
-    def together(kept):
-        names = list(kept)
-        return dict(zip(names, lax.optimization_barrier(tuple(kept[n] for n in names))))
-
     b, u, v, made = {0: sent}, {}, {}, {}
-
-    def experts_of(s):
+    token = jnp.zeros((8, 128), F32)
+
+    def wait(*entries, passed=()):
+        nonlocal token
+        arrays = [store[key] for store, key in entries]
+        token, *rest = lax.optimization_barrier((token, *arrays, *passed))
+        for (store, key), array in zip(entries, rest):
+            store[key] = array
+        return rest[len(entries) :]
+
+    def run_experts(s):
         rows_in = [(b[s], 0, own_rows), (u[s], 0, own_rows), (v[s], 0, 2 * own_rows)]
-        return plane_experts(held["where"], rows_in, experts, held["own"], held["other"])
-
-    def phase(starts, experts_for=None, passed=()):
-        kept = {(i, "moved"): start[2] for i, start in enumerate(starts)}
-        if experts_for is not None:
-            kept.update({(i, "made"): a for i, a in enumerate(experts_of(experts_for))})
-        kept.update({(i, "passed"): a for i, a in enumerate(passed)})
-        kept = together(kept)
-        for i, (store, key, _) in enumerate(starts):
-            store[key] = kept[i, "moved"]
-        if experts_for is not None:
-            made[experts_for] = [kept[i, "made"] for i in range(3)]
-        return [kept[i, "passed"] for i in range(len(passed))]
-
-    starts = [(u, 0, over_u(b[0])), (b, 1, shifted(1)(b[0]))]
-    index, *weights = phase(starts, passed=hold_weights(where, own_weights + other_weights))
-    held = {"where": index, "own": weights[:3], "other": weights[3:]}
+        made[s] = list(plane_experts(index, rows_in, experts, own_held, other_held))
+
+    def made_entries(s):
+        return [(made[s], i) for i in range(3)]
+
+    b[1] = shifted(1)(b[0])
+    u[0] = over_u(b[0])
+    index, *held = hold_weights(where, [in_hbm(w) for w in own_weights] + other_weights)
+    index, *held = wait((b, 1), (u, 0), passed=[index, *held])
+    own_held, other_held = held[:3], held[3:]
     for k in range(1, planes):
+        if k + 1 < planes:
+            b[k + 1] = shifted(1)(b[k])
+        u[k] = over_u(b[k])
         v[k - 1] = over_v(jnp.concatenate([b[k - 1], u[k - 1]]))
-        starts = [(u, k, over_u(b[k]))]
+        token = step(token)
+        entries = [(u, k)]
         if k + 1 < planes:
-            starts.append((b, k + 1, shifted(1)(b[k])))
-        if k == 1:
-            (held["where"],) = phase(starts, passed=hold_weights(held["where"], ()))
-        else:
-            phase(starts, experts_for=k - 2)
+            entries.append((b, k + 1))
+        if k > 1:
+            run_experts(k - 2)
+            entries += made_entries(k - 2)
+        wait(*entries)
     v[planes - 1] = over_v(jnp.concatenate([b[planes - 1], u[planes - 1]]))
-    order = list(range(1, planes)) + [0]
-    (*waiting,) = phase([], experts_for=planes - 2, passed=[made[s][2] for s in sorted(made)])
-    for s, array in enumerate(waiting):
-        made[s][2] = array
+    token = step(token)
+    run_experts(planes - 2)
+    wait(*made_entries(planes - 2), *[(made[s], 2) for s in range(planes - 2)])
+
+    half = (planes + 1) // 2
+    order = list(range(half, planes - 1)) + list(range(1, half)) + [planes - 1, 0]
     back_v, back_u, back_z, sums = {}, {}, {}, {}
-    first, second = over_v(made[order[0]][2]), None
-    phase([(v, planes - 1, v[planes - 1])])
-    if planes > 3:
-        second = over_v(made[order[1]][2])
-    phase([(back_v, order[0], first)], experts_for=planes - 1)
+    for s in order[:2]:
+        if s in made:
+            back_v[s] = over_v(made[s][2])
+    token = step(token)
+    wait((v, planes - 1), (made[0], 2))
+    run_experts(planes - 1)
+    wait(*made_entries(planes - 1), *([(back_v, order[0])] if order[0] in back_v else []))
+    for s in order[:2]:
+        if s not in back_v:
+            back_v[s] = over_v(made[s][2])
     results = []
     for j, s in enumerate(order):
         own, for_u, _ = made[s]
-        starts = [(back_u, s, over_u(add_bf16(for_u, back_v[s][own_rows:])))]
-        if j + 2 < planes:
-            starts.append((back_v, order[j + 1], second))
-        elif s:
-            starts.append((back_v, 0, over_v(made[0][2])))
-        if j + 3 < planes:
-            second = over_v(made[order[j + 2]][2])
         if j:
             last = order[j - 1]
             onward = 2 * last >= planes
-            moved = shifted(1 if onward else planes - last)(sums[last])
-            if last < planes - 1:
-                starts.append((back_z, last, moved))
-            else:
-                back_z[last] = moved
-        (made[0][2],) = phase(starts, passed=(made[0][2],))
-        arrived = [own, back_v[s][:own_rows], back_u[s]]
-        if s:
-            if 2 * (s - 1) >= planes:
-                arrived.append(back_z.pop(s - 1))
-            sums[s] = add_bf16(*arrived)
-        else:
-            results += arrived + [back_z[last] for last in sorted(back_z)]
-    return final_sum(residual, results)
+            back_z[last] = shifted(1 if onward else planes - last)(sums[last])
+        if s == 0:
+            token = step(token)
+            wait((back_v, 0))
+        back_u[s] = over_u(add_bf16(for_u, back_v[s][own_rows:]))
+        if not s:
+            break
+        if j + 2 < planes:
+            back_v[order[j + 2]] = over_v(made[order[j + 2]][2])
+        token = step(token)
+        carried = s - 1 in back_z and 2 * (s - 1) >= planes
+        entries = [(back_u, s)]
+        if order[j + 1]:
+            entries += [(back_v, order[j + 1]), (made[0], 2)]
+        if carried:
+            entries.append((back_z, s - 1))
+        wait(*entries)
+        terms = [own, back_v[s][:own_rows], back_u[s]]
+        if carried:
+            terms.append(back_z.pop(s - 1))
+        sums[s] = add_bf16(*terms)
+    results = [made[0][0], back_v[0][:own_rows], back_u[0]]
+    results += [back_z[s] for s in sorted(back_z)]
+    return final_sum(token, residual, results)
 
 
 def solution(mesh):

time: 107 us -> 102 us (0.953)
  waiting for transfers between devices: 48.2 us -> 43.7 us
  starting transfers between devices: 25.8 us -> 28.5 us
  Pallas kernels: 30.1 us -> 28.4 us
  local copies, waits for them, and re-layouts: 1.38 us -> 0.02 us
    ppermute x16, starting transfers between devices: 16.2 us -> 22.3 us  [across(): return lambda a: lax.ppermute(a, ('wide', 'narrow'), pairs)]
    ppermute x6, starting transfers between devices: 8.49 us -> 5.04 us  [shifted(): return lambda a: lax.ppermute(a, 'wide', pairs)]
    ppermute x6, waiting for transfers between devices: 14.2 us -> 11.6 us  [shifted(): return lambda a: lax.ppermute(a, 'wide', pairs)]
    ppermute x16, waiting for transfers between devices: 31.9 us -> 29.9 us  [across(): return lambda a: lax.ppermute(a, ('wide', 'narrow'), pairs)]
    pallas_call x2 -> x1, Pallas kernels: 6.99 us -> 5.29 us  [hold_weights(): pl.pallas_call(functools.partial(hold_kernel, count), out_shape=[jax.Shap...]
    unnamed x2 -> x0, local copies, waits for them, and re-layouts: 1.36 us -> none
  transfers between devices with their start and end apart: 26 -> 26, of which waited for: 19 -> 17; matrix products, arithmetic and copies ran while one was open for 1% -> 1% of each run, Pallas kernels for 27% -> 27%
where the time goes in v5:
time: 102 us
  waiting for transfers between devices  43.7 us (43%)
  starting transfers between devices  28.5 us (28%)
  Pallas kernels  28.4 us (28%)
    ppermute x16, waiting for transfers between devices, across(): return lambda a: lax.ppermute(a, ('wide', 'narrow'), pairs)  29.9 us
    ppermute x16, starting transfers between devices, across(): return lambda a: lax.ppermute(a, ('wide', 'narrow'), pairs)  22.3 us
    pallas_call x4, Pallas kernels, plane_experts(): pl.pallas_call(functools.partial(experts_kernel, spans, experts), out_sha...  17.4 us
    ppermute x6, waiting for transfers between devices, shifted(): return lambda a: lax.ppermute(a, 'wide', pairs)  11.6 us
    pallas_call x1, Pallas kernels, hold_weights(): pl.pallas_call(functools.partial(hold_kernel, count), out_shape=[jax.Shap...  5.29 us
    ppermute x6, starting transfers between devices, shifted(): return lambda a: lax.ppermute(a, 'wide', pairs)  5.04 us
    pallas_call x1, Pallas kernels, attention(): pl.pallas_call(functools.partial(attention_kernel, experts), out_shape=(j...  4.64 us
    ppermute x1, waiting for transfers between devices, on_device(): received = lax.ppermute(outgoing, 'narrow', swap)  2.18 us
  transfers between devices with their start and end apart: 26, of which 17 were waited for; matrix products, arithmetic and copies ran while one was open for 1% of the time, Pallas kernels for 27%

profile of v5, /device:TPU:0, one launch (start us, length us, event | category | flops | bytes accessed | tf_op | source)
XLA Modules:
  0.0 101.6 jit_solution(17847499601193807610)
XLA Ops:
  1.0 4.6 %shard_map.145 = (bf16[64,2048]{1,0:T(8,128)(2,1)S(1)}, f32[64,2048]{1,0:T(8,128)S(1)}, bf16[64,128]{1,0:T(8,128)(2,1)S(1)}, f32[1,2048]{1,0:T(1,128)S(1)}) custom-call(s32[1]{0:T(128)} %bitcast.core_ref, s32[8]{0:T(128)} %draft_len_ref.1, s32[8]{0:T(128)} %cache_len_ref.1, s32[10,64]{1,0:T(8,128)} %bitcast.6, f32[10,64]{1,0:T(8,128)} %bitcast.7, ...), custom_call_target="tpu_custom_call" | custom-call | flops 671088640 | bytes 6291456 | tf_op jit(solution)/shard_map/pallas_call | solution.py:179
  5.7 2.2 %collective-permute-done.received_ref = bf16[64,2048]{1,0:T(8,128)(2,1)S(1)} collective-permute-done((bf16[64,2048]{1,0:T(8,128)(2,1)S(1)}, bf16[64,2048]{1,0:T(8,128)(2,1)S(1)}, u32[]{:S(2)}, u32[]{:S(2)}) %collective-permute-start) | collective-permute-done | bytes 262176 | tf_op jit(solution)/shard_map/ppermute | solution.py:411
  8.1 3.0 %collective-permute-start.1 = (bf16[64,2176]{1,0:T(8,128)(2,1)S(1)}, bf16[64,2176]{1,0:T(8,128)(2,1)S(1)}, u32[]{:S(2)}, u32[]{:S(2)}) collective-permute-start(bf16[64,2176]{1,0:T(8,128)(2,1)S(1)} %get-tuple-element.84.refs_0_), channel_id=1, source_target_pairs={{0,8},{2,10},{4,12},{6,14},{8,16},{10,18},{12,20},{14,22},{16,24},... | collective-permute-start | bytes 835592 | tf_op jit(solution)/shard_map/ppermute | solution.py:422
  12.7 5.3 %shard_map.147 = (s32[2]{0:T(128)S(1)}, bf16[1,2048,512]{2,1,0:T(8,128)(2,1)S(1)}, bf16[1,2048,512]{2,1,0:T(8,128)(2,1)S(1)}, bf16[1,512,2048]{2,1,0:T(8,128)(2,...) custom-call(s32[2]{0:T(128)S(1)} %pad_add_fusion.where_ref, ...), custom_call_target="tpu_custom_call" | custom-call | flops 200000000 | tf_op jit(solution)/shard_map/pallas_call | solution.py:307
  18.0 2.1 %collective-permute-done.1.refs_0_ = bf16[64,2176]{1,0:T(8,128)(2,1)S(1)} collective-permute-done((bf16[64,2176]{1,0:T(8,128)(2,1)S(1)}, bf16[64,2176]{1,0:T(8,128)(2,1)S(1)}, u32[]{:S(2)}, u32[]{:S(2)}) %collective-permute-start.1) | collective-permute-done | bytes 278560 | tf_op jit(solution)/shard_map/ppermute | solution.py:422
  21.7 1.6 %collective-permute-start.10 = (bf16[128,2176]{1,0:T(8,128)(2,1)S(1)}, bf16[128,2176]{1,0:T(8,128)(2,1)S(1)}, u32[]{:S(2)}, u32[]{:S(2)}) collective-permute-start(bf16[128,2176]{1,0:T(8,128)(2,1)S(1)} %pad_maximum_fusion), channel_id=1, source_target_pairs={{0,4},{1,3},{2,6},{3,1},{4,0},{5,7},{6,2},{7,5},{8,12},{9,11},{10,... | collective-permute-start | bytes 1671176 | tf_op jit(solution)/shard_map/ppermute | solution.py:418
  23.3 6.4 %collective-permute-done.6.refs_1_ = bf16[64,2176]{1,0:T(8,128)(2,1)S(1)} collective-permute-done((bf16[64,2176]{1,0:T(8,128)(2,1)S(1)}, bf16[64,2176]{1,0:T(8,128)(2,1)S(1)}, u32[]{:S(2)}, u32[]{:S(2)}) %collective-permute-start.6) | collective-permute-done | bytes 278560 | tf_op jit(solution)/shard_map/ppermute | solution.py:418
  33.2 4.4 %shard_map.150 = (bf16[64,2048]{1,0:T(8,128)(2,1)S(1)}, bf16[64,2048]{1,0:T(8,128)(2,1)S(1)}, bf16[128,2048]{1,0:T(8,128)(2,1)S(1)}) custom-call(s32[2]{0:T(128)S(1)} %get-tuple-element.96.where_ref, bf16[64,2176]{1,0:T(8,128)(2,1)S(1)} %get-tuple-element.84.refs_0_, bf16[64,2176]{1,0:T(8,128)(2,1)S(1)} %collective-permute-done.2.refs_1_, ...), custom_call_target="tpu_custom_call" | custom-call | flops 200000000 | tf_op jit(solution)/shard_map/pallas_call | solution.py:341
  37.6 3.1 %collective-permute-done.8.refs_1_ = bf16[64,2176]{1,0:T(8,128)(2,1)S(1)} collective-permute-done((bf16[64,2176]{1,0:T(8,128)(2,1)S(1)}, bf16[64,2176]{1,0:T(8,128)(2,1)S(1)}, u32[]{:S(2)}, u32[]{:S(2)}) %collective-permute-start.8) | collective-permute-done | bytes 278560 | tf_op jit(solution)/shard_map/ppermute | solution.py:418
  42.3 1.8 %collective-permute-start.13 = (bf16[128,2176]{1,0:T(8,128)(2,1)S(1)}, bf16[128,2176]{1,0:T(8,128)(2,1)S(1)}, u32[]{:S(2)}, u32[]{:S(2)}) collective-permute-start(bf16[128,2176]{1,0:T(8,128)(2,1)S(1)} %pad_maximum_fusion.2), channel_id=1, source_target_pairs={{0,4},{1,3},{2,6},{3,1},{4,0},{5,7},{6,2},{7,5},{8,12},{9,11},{10,... | collective-permute-start | bytes 1671176 | tf_op jit(solution)/shard_map/ppermute | solution.py:418
  45.1 4.4 %shard_map.152 = (bf16[64,2048]{1,0:T(8,128)(2,1)S(1)}, bf16[64,2048]{1,0:T(8,128)(2,1)S(1)}, bf16[128,2048]{1,0:T(8,128)(2,1)S(1)}) custom-call(s32[2]{0:T(128)S(1)} %get-tuple-element.96.where_ref, bf16[64,2176]{1,0:T(8,128)(2,1)S(1)} %collective-permute-done.1.refs_0_, bf16[64,2176]{1,0:T(8,128)(2,1)S(1)} %collective-permute-done.6.refs_1_, ...), custom_call_target="tpu_custom_call" | custom-call | flops 200000000 | tf_op jit(solution)/shard_map/pallas_call | solution.py:341
  51.9 4.3 %shard_map.154 = (bf16[64,2048]{1,0:T(8,128)(2,1)S(1)}, bf16[64,2048]{1,0:T(8,128)(2,1)S(1)}, bf16[128,2048]{1,0:T(8,128)(2,1)S(1)}) custom-call(s32[2]{0:T(128)S(1)} %get-tuple-element.96.where_ref, bf16[64,2176]{1,0:T(8,128)(2,1)S(1)} %collective-permute-done.7.refs_0_, bf16[64,2176]{1,0:T(8,128)(2,1)S(1)} %collective-permute-done.8.refs_1_, ...), custom_call_target="tpu_custom_call" | custom-call | flops 200000000 | tf_op jit(solution)/shard_map/pallas_call | solution.py:341
  56.2 1.8 %collective-permute-start.15 = (bf16[128,2048]{1,0:T(8,128)(2,1)S(1)}, bf16[128,2048]{1,0:T(8,128)(2,1)S(1)}, u32[]{:S(2)}, u32[]{:S(2)}) collective-permute-start(bf16[128,2048]{1,0:T(8,128)(2,1)S(1)} %get-tuple-element.128), channel_id=1, source_target_pairs={{0,4},{1,3},{2,6},{3,1},{4,0},{5,7},{6,2},{7,5},{8,12},{9,11},{10,... | collective-permute-start | bytes 1572872 | tf_op jit(solution)/shard_map/ppermute | solution.py:418
  58.3 1.8 %collective-permute-done.14.refs_2_ = bf16[128,2176]{1,0:T(8,128)(2,1)S(1)} collective-permute-done((bf16[128,2176]{1,0:T(8,128)(2,1)S(1)}, bf16[128,2176]{1,0:T(8,128)(2,1)S(1)}, u32[]{:S(2)}, u32[]{:S(2)}) %collective-permute-start.14) | collective-permute-done | bytes 557088 | tf_op jit(solution)/shard_map/ppermute | solution.py:418
  60.1 4.3 %shard_map.156 = (bf16[64,2048]{1,0:T(8,128)(2,1)S(1)}, bf16[64,2048]{1,0:T(8,128)(2,1)S(1)}, bf16[128,2048]{1,0:T(8,128)(2,1)S(1)}) custom-call(s32[2]{0:T(128)S(1)} %get-tuple-element.96.where_ref, bf16[64,2176]{1,0:T(8,128)(2,1)S(1)} %collective-permute-done.9.refs_0_, bf16[64,2176]{1,0:T(8,128)(2,1)S(1)} %collective-permute-done.11.refs_1_, ...), custom_call_target="tpu_custom_call" | custom-call | flops 200000000 | tf_op jit(solution)/shard_map/pallas_call | solution.py:341
  68.9 5.2 %collective-permute-done.17 = bf16[128,2048]{1,0:T(8,128)(2,1)S(1)} collective-permute-done((bf16[128,2048]{1,0:T(8,128)(2,1)S(1)}, bf16[128,2048]{1,0:T(8,128)(2,1)S(1)}, u32[]{:S(2)}, u32[]{:S(2)}) %collective-permute-start.17) | collective-permute-done | bytes 524320 | tf_op jit(solution)/shard_map/ppermute | solution.py:418
  75.2 1.6 %collective-permute-start.18 = (bf16[64,2048]{1,0:T(8,128)(2,1)S(1)}, bf16[64,2048]{1,0:T(8,128)(2,1)S(1)}, u32[]{:S(2)}, u32[]{:S(2)}) collective-permute-start(bf16[64,2048]{1,0:T(8,128)(2,1)S(1)} %add_convert_fusion.5), channel_id=1, source_target_pairs={{0,2},{1,5},{2,0},{3,7},{4,6},{5,1},{6,4},{7,3},{8,10},{9,13},{10,... | collective-permute-start | bytes 786440 | tf_op jit(solution)/shard_map/ppermute | solution.py:418
  76.9 1.6 %collective-permute-start.22 = (bf16[128,2048]{1,0:T(8,128)(2,1)S(1)}, bf16[128,2048]{1,0:T(8,128)(2,1)S(1)}, u32[]{:S(2)}, u32[]{:S(2)}) collective-permute-start(bf16[128,2048]{1,0:T(8,128)(2,1)S(1)} %get-tuple-element.138), channel_id=1, source_target_pairs={{0,4},{1,3},{2,6},{3,1},{4,0},{5,7},{6,2},{7,5},{8,12},{9,11},{10,... | collective-permute-start | bytes 1572872 | tf_op jit(solution)/shard_map/ppermute | solution.py:418
  78.5 4.0 %collective-permute-done.19 = bf16[128,2048]{1,0:T(8,128)(2,1)S(1)} collective-permute-done((bf16[128,2048]{1,0:T(8,128)(2,1)S(1)}, bf16[128,2048]{1,0:T(8,128)(2,1)S(1)}, u32[]{:S(2)}, u32[]{:S(2)}) %collective-permute-start.19) | collective-permute-done | bytes 524320 | tf_op jit(solution)/shard_map/ppermute | solution.py:418
  82.6 1.9 %collective-permute-done.18 = bf16[64,2048]{1,0:T(8,128)(2,1)S(1)} collective-permute-done((bf16[64,2048]{1,0:T(8,128)(2,1)S(1)}, bf16[64,2048]{1,0:T(8,128)(2,1)S(1)}, u32[]{:S(2)}, u32[]{:S(2)}) %collective-permute-start.18) | collective-permute-done | bytes 262176 | tf_op jit(solution)/shard_map/ppermute | solution.py:418
  84.6 1.6 %collective-permute-start.20 = (bf16[64,2048]{1,0:T(8,128)(2,1)S(1)}, bf16[64,2048]{1,0:T(8,128)(2,1)S(1)}, u32[]{:S(2)}, u32[]{:S(2)}) collective-permute-start(bf16[64,2048]{1,0:T(8,128)(2,1)S(1)} %add_convert_fusion.4), channel_id=1, source_target_pairs={{0,2},{1,5},{2,0},{3,7},{4,6},{5,1},{6,4},{7,3},{8,10},{9,13},{10,... | collective-permute-start | bytes 786440 | tf_op jit(solution)/shard_map/ppermute | solution.py:418
  86.2 1.9 %collective-permute-start.24 = (bf16[64,2048]{1,0:T(8,128)(2,1)S(1)}, bf16[64,2048]{1,0:T(8,128)(2,1)S(1)}, u32[]{:S(2)}, u32[]{:S(2)}) collective-permute-start(bf16[64,2048]{1,0:T(8,128)(2,1)S(1)} %add_convert_fusion.1), channel_id=1, source_target_pairs={{0,24},{2,26},{4,28},{6,30},{8,0},{10,2},{12,4},{14,6},{16,8},{18,... | collective-permute-start | bytes 786440 | tf_op jit(solution)/shard_map/ppermute | solution.py:422
  88.1 2.9 %collective-permute-done.20 = bf16[64,2048]{1,0:T(8,128)(2,1)S(1)} collective-permute-done((bf16[64,2048]{1,0:T(8,128)(2,1)S(1)}, bf16[64,2048]{1,0:T(8,128)(2,1)S(1)}, u32[]{:S(2)}, u32[]{:S(2)}) %collective-permute-start.20) | collective-permute-done | bytes 262176 | tf_op jit(solution)/shard_map/ppermute | solution.py:418
  92.9 7.8 %collective-permute-done.25.refs_4_ = bf16[64,2048]{1,0:T(8,128)(2,1)S(1)} collective-permute-done((bf16[64,2048]{1,0:T(8,128)(2,1)S(1)}, bf16[64,2048]{1,0:T(8,128)(2,1)S(1)}, u32[]{:S(2)}, u32[]{:S(2)}) %collective-permute-start.25) | collective-permute-done | bytes 262176 | tf_op jit(solution)/shard_map/ppermute | solution.py:422
  (59 shorter events, 21.8 us)
Async XLA Ops:
  0.0 12.7 %collective-permute-start.3 = (bf16[1,2048,512]{2,1,0:T(8,128)(2,1)}, bf16[1,2048,512]{2,1,0:T(8,128)(2,1)S(1)}, u32[]{:S(2)}, u32[]{:S(2)}) collective-permute-start(bf16[1,2048,512]{2,1,0:T(8,128)(2,1)} %refs_0_.1), channel_id=1, source_target_pairs={{0,1},{1,0},{2,3},{3,2},{4,5},{5,4},{6,7},{7,6},{8,9},{9,8},{10,11... | collective-permute-start | bytes 6291464 | tf_op jit(solution)/shard_map/ppermute | solution.py:405
  0.5 12.3 %collective-permute-start.4 = (bf16[1,2048,512]{2,1,0:T(8,128)(2,1)}, bf16[1,2048,512]{2,1,0:T(8,128)(2,1)}, u32[]{:S(2)}, u32[]{:S(2)}) collective-permute-start(bf16[1,2048,512]{2,1,0:T(8,128)(2,1)} %refs_1_.1), channel_id=1, source_target_pairs={{0,1},{1,0},{2,3},{3,2},{4,5},{5,4},{6,7},{7,6},{8,9},{9,8},{10,11... | collective-permute-start | bytes 6291464 | tf_op jit(solution)/shard_map/ppermute | solution.py:405
  0.5 12.2 %collective-permute-start.5 = (bf16[1,512,2048]{2,1,0:T(8,128)(2,1)}, bf16[1,512,2048]{2,1,0:T(8,128)(2,1)}, u32[]{:S(2)}, u32[]{:S(2)}) collective-permute-start(bf16[1,512,2048]{2,1,0:T(8,128)(2,1)} %refs_2_.1), channel_id=1, source_target_pairs={{0,1},{1,0},{2,3},{3,2},{4,5},{5,4},{6,7},{7,6},{8,9},{9,8},{10,11... | collective-permute-start | bytes 6291464 | tf_op jit(solution)/shard_map/ppermute | solution.py:405
  8.1 12.0 %collective-permute-start.1 = (bf16[64,2176]{1,0:T(8,128)(2,1)S(1)}, bf16[64,2176]{1,0:T(8,128)(2,1)S(1)}, u32[]{:S(2)}, u32[]{:S(2)}) collective-permute-start(bf16[64,2176]{1,0:T(8,128)(2,1)S(1)} %get-tuple-element.84.refs_0_), channel_id=1, source_target_pairs={{0,8},{2,10},{4,12},{6,14},{8,16},{10,18},{12,20},{14,22},{16,24},... | collective-permute-start | bytes 835592 | tf_op jit(solution)/shard_map/ppermute | solution.py:422
  11.1 9.0 %collective-permute-start.2 = (bf16[64,2176]{1,0:T(8,128)(2,1)S(1)}, bf16[64,2176]{1,0:T(8,128)(2,1)S(1)}, u32[]{:S(2)}, u32[]{:S(2)}) collective-permute-start(bf16[64,2176]{1,0:T(8,128)(2,1)S(1)} %get-tuple-element.84.refs_0_), channel_id=1, source_target_pairs={{0,2},{1,5},{2,0},{3,7},{4,6},{5,1},{6,4},{7,3},{8,10},{9,13},{10,... | collective-permute-start | bytes 835592 | tf_op jit(solution)/shard_map/ppermute | solution.py:418
  20.1 9.5 %collective-permute-start.6 = (bf16[64,2176]{1,0:T(8,128)(2,1)S(1)}, bf16[64,2176]{1,0:T(8,128)(2,1)S(1)}, u32[]{:S(2)}, u32[]{:S(2)}) collective-permute-start(bf16[64,2176]{1,0:T(8,128)(2,1)S(1)} %collective-permute-done.1.refs_0_), channel_id=1, source_target_pairs={{0,2},{1,5},{2,0},{3,7},{4,6},{5,1},{6,4},{7,3},{8,10},{9,13},{10,... | collective-permute-start | bytes 835592 | tf_op jit(solution)/shard_map/ppermute | solution.py:418
  21.6 9.5 %collective-permute-start.7 = (bf16[64,2176]{1,0:T(8,128)(2,1)S(1)}, bf16[64,2176]{1,0:T(8,128)(2,1)S(1)}, u32[]{:S(2)}, u32[]{:S(2)}) collective-permute-start(bf16[64,2176]{1,0:T(8,128)(2,1)S(1)} %collective-permute-done.1.refs_0_), channel_id=1, source_target_pairs={{0,8},{2,10},{4,12},{6,14},{8,16},{10,18},{12,20},{14,22},{16,24},... | collective-permute-start | bytes 835592 | tf_op jit(solution)/shard_map/ppermute | solution.py:422
  21.7 11.6 %collective-permute-start.10 = (bf16[128,2176]{1,0:T(8,128)(2,1)S(1)}, bf16[128,2176]{1,0:T(8,128)(2,1)S(1)}, u32[]{:S(2)}, u32[]{:S(2)}) collective-permute-start(bf16[128,2176]{1,0:T(8,128)(2,1)S(1)} %pad_maximum_fusion), channel_id=1, source_target_pairs={{0,4},{1,3},{2,6},{3,1},{4,0},{5,7},{6,2},{7,5},{8,12},{9,11},{10,... | collective-permute-start | bytes 1671176 | tf_op jit(solution)/shard_map/ppermute | solution.py:418
  31.1 9.6 %collective-permute-start.8 = (bf16[64,2176]{1,0:T(8,128)(2,1)S(1)}, bf16[64,2176]{1,0:T(8,128)(2,1)S(1)}, u32[]{:S(2)}, u32[]{:S(2)}) collective-permute-start(bf16[64,2176]{1,0:T(8,128)(2,1)S(1)} %collective-permute-done.7.refs_0_), channel_id=1, source_target_pairs={{0,2},{1,5},{2,0},{3,7},{4,6},{5,1},{6,4},{7,3},{8,10},{9,13},{10,... | collective-permute-start | bytes 835592 | tf_op jit(solution)/shard_map/ppermute | solution.py:418
  32.6 8.3 %collective-permute-start.9 = (bf16[64,2176]{1,0:T(8,128)(2,1)S(1)}, bf16[64,2176]{1,0:T(8,128)(2,1)S(1)}, u32[]{:S(2)}, u32[]{:S(2)}) collective-permute-start(bf16[64,2176]{1,0:T(8,128)(2,1)S(1)} %collective-permute-done.7.refs_0_), channel_id=1, source_target_pairs={{0,8},{2,10},{4,12},{6,14},{8,16},{10,18},{12,20},{14,22},{16,24},... | collective-permute-start | bytes 835592 | tf_op jit(solution)/shard_map/ppermute | solution.py:422
  32.6 12.5 %collective-permute-start.12 = (bf16[128,2176]{1,0:T(8,128)(2,1)S(1)}, bf16[128,2176]{1,0:T(8,128)(2,1)S(1)}, u32[]{:S(2)}, u32[]{:S(2)}) collective-permute-start(bf16[128,2176]{1,0:T(8,128)(2,1)S(1)} %pad_maximum_fusion.1), channel_id=1, source_target_pairs={{0,4},{1,3},{2,6},{3,1},{4,0},{5,7},{6,2},{7,5},{8,12},{9,11},{10,... | collective-permute-start | bytes 1671176 | tf_op jit(solution)/shard_map/ppermute | solution.py:418
  40.9 9.5 %collective-permute-start.11 = (bf16[64,2176]{1,0:T(8,128)(2,1)S(1)}, bf16[64,2176]{1,0:T(8,128)(2,1)S(1)}, u32[]{:S(2)}, u32[]{:S(2)}) collective-permute-start(bf16[64,2176]{1,0:T(8,128)(2,1)S(1)} %collective-permute-done.9.refs_0_), channel_id=1, source_target_pairs={{0,2},{1,5},{2,0},{3,7},{4,6},{5,1},{6,4},{7,3},{8,10},{9,13},{10,... | collective-permute-start | bytes 835592 | tf_op jit(solution)/shard_map/ppermute | solution.py:418
  42.3 9.6 %collective-permute-start.13 = (bf16[128,2176]{1,0:T(8,128)(2,1)S(1)}, bf16[128,2176]{1,0:T(8,128)(2,1)S(1)}, u32[]{:S(2)}, u32[]{:S(2)}) collective-permute-start(bf16[128,2176]{1,0:T(8,128)(2,1)S(1)} %pad_maximum_fusion.2), channel_id=1, source_target_pairs={{0,4},{1,3},{2,6},{3,1},{4,0},{5,7},{6,2},{7,5},{8,12},{9,11},{10,... | collective-permute-start | bytes 1671176 | tf_op jit(solution)/shard_map/ppermute | solution.py:418
  50.5 9.6 %collective-permute-start.14 = (bf16[128,2176]{1,0:T(8,128)(2,1)S(1)}, bf16[128,2176]{1,0:T(8,128)(2,1)S(1)}, u32[]{:S(2)}, u32[]{:S(2)}) collective-permute-start(bf16[128,2176]{1,0:T(8,128)(2,1)S(1)} %pad_maximum_fusion.3), channel_id=1, source_target_pairs={{0,4},{1,3},{2,6},{3,1},{4,0},{5,7},{6,2},{7,5},{8,12},{9,11},{10,... | collective-permute-start | bytes 1671176 | tf_op jit(solution)/shard_map/ppermute | solution.py:418
  56.2 9.5 %collective-permute-start.15 = (bf16[128,2048]{1,0:T(8,128)(2,1)S(1)}, bf16[128,2048]{1,0:T(8,128)(2,1)S(1)}, u32[]{:S(2)}, u32[]{:S(2)}) collective-permute-start(bf16[128,2048]{1,0:T(8,128)(2,1)S(1)} %get-tuple-element.128), channel_id=1, source_target_pairs={{0,4},{1,3},{2,6},{3,1},{4,0},{5,7},{6,2},{7,5},{8,12},{9,11},{10,... | collective-permute-start | bytes 1572872 | tf_op jit(solution)/shard_map/ppermute | solution.py:418
  58.0 16.2 %collective-permute-start.17 = (bf16[128,2048]{1,0:T(8,128)(2,1)S(1)}, bf16[128,2048]{1,0:T(8,128)(2,1)S(1)}, u32[]{:S(2)}, u32[]{:S(2)}) collective-permute-start(bf16[128,2048]{1,0:T(8,128)(2,1)S(1)} %get-tuple-element.132), channel_id=1, source_target_pairs={{0,4},{1,3},{2,6},{3,1},{4,0},{5,7},{6,2},{7,5},{8,12},{9,11},{10,... | collective-permute-start | bytes 1572872 | tf_op jit(solution)/shard_map/ppermute | solution.py:418
  65.8 9.3 %collective-permute-start.16 = (bf16[64,2048]{1,0:T(8,128)(2,1)S(1)}, bf16[64,2048]{1,0:T(8,128)(2,1)S(1)}, u32[]{:S(2)}, u32[]{:S(2)}) collective-permute-start(bf16[64,2048]{1,0:T(8,128)(2,1)S(1)} %add_convert_fusion.6), channel_id=1, source_target_pairs={{0,2},{1,5},{2,0},{3,7},{4,6},{5,1},{6,4},{7,3},{8,10},{9,13},{10,... | collective-permute-start | bytes 786440 | tf_op jit(solution)/shard_map/ppermute | solution.py:418
  67.4 15.2 %collective-permute-start.19 = (bf16[128,2048]{1,0:T(8,128)(2,1)S(1)}, bf16[128,2048]{1,0:T(8,128)(2,1)S(1)}, u32[]{:S(2)}, u32[]{:S(2)}) collective-permute-start(bf16[128,2048]{1,0:T(8,128)(2,1)S(1)} %get-tuple-element.137), channel_id=1, source_target_pairs={{0,4},{1,3},{2,6},{3,1},{4,0},{5,7},{6,2},{7,5},{8,12},{9,11},{10,... | collective-permute-start | bytes 1572872 | tf_op jit(solution)/shard_map/ppermute | solution.py:418
  75.2 9.3 %collective-permute-start.18 = (bf16[64,2048]{1,0:T(8,128)(2,1)S(1)}, bf16[64,2048]{1,0:T(8,128)(2,1)S(1)}, u32[]{:S(2)}, u32[]{:S(2)}) collective-permute-start(bf16[64,2048]{1,0:T(8,128)(2,1)S(1)} %add_convert_fusion.5), channel_id=1, source_target_pairs={{0,2},{1,5},{2,0},{3,7},{4,6},{5,1},{6,4},{7,3},{8,10},{9,13},{10,... | collective-permute-start | bytes 786440 | tf_op jit(solution)/shard_map/ppermute | solution.py:418
  76.9 11.3 %collective-permute-start.21 = (bf16[64,2048]{1,0:T(8,128)(2,1)S(1)}, bf16[64,2048]{1,0:T(8,128)(2,1)S(1)}, u32[]{:S(2)}, u32[]{:S(2)}) collective-permute-start(bf16[64,2048]{1,0:T(8,128)(2,1)S(1)} %add_convert_fusion.3), channel_id=1, source_target_pairs={{0,8},{2,10},{4,12},{6,14},{8,16},{10,18},{12,20},{14,22},{16,24},... | collective-permute-start | bytes 786440 | tf_op jit(solution)/shard_map/ppermute | solution.py:422
  76.9 14.3 %collective-permute-start.22 = (bf16[128,2048]{1,0:T(8,128)(2,1)S(1)}, bf16[128,2048]{1,0:T(8,128)(2,1)S(1)}, u32[]{:S(2)}, u32[]{:S(2)}) collective-permute-start(bf16[128,2048]{1,0:T(8,128)(2,1)S(1)} %get-tuple-element.138), channel_id=1, source_target_pairs={{0,4},{1,3},{2,6},{3,1},{4,0},{5,7},{6,2},{7,5},{8,12},{9,11},{10,... | collective-permute-start | bytes 1572872 | tf_op jit(solution)/shard_map/ppermute | solution.py:418
  86.2 6.7 %collective-permute-start.24 = (bf16[64,2048]{1,0:T(8,128)(2,1)S(1)}, bf16[64,2048]{1,0:T(8,128)(2,1)S(1)}, u32[]{:S(2)}, u32[]{:S(2)}) collective-permute-start(bf16[64,2048]{1,0:T(8,128)(2,1)S(1)} %add_convert_fusion.1), channel_id=1, source_target_pairs={{0,24},{2,26},{4,28},{6,30},{8,0},{10,2},{12,4},{14,6},{16,8},{18,... | collective-permute-start | bytes 786440 | tf_op jit(solution)/shard_map/ppermute | solution.py:422
  91.1 9.6 %collective-permute-start.25 = (bf16[64,2048]{1,0:T(8,128)(2,1)S(1)}, bf16[64,2048]{1,0:T(8,128)(2,1)S(1)}, u32[]{:S(2)}, u32[]{:S(2)}) collective-permute-start(bf16[64,2048]{1,0:T(8,128)(2,1)S(1)} %add_convert_fusion), channel_id=1, source_target_pairs={{0,8},{2,10},{4,12},{6,14},{8,16},{10,18},{12,20},{14,22},{16,24},... | collective-permute-start | bytes 786440 | tf_op jit(solution)/shard_map/ppermute | solution.py:422
  91.3 9.4 %collective-permute-start.23 = (bf16[64,2048]{1,0:T(8,128)(2,1)S(1)}, bf16[64,2048]{1,0:T(8,128)(2,1)S(1)}, u32[]{:S(2)}, u32[]{:S(2)}) collective-permute-start(bf16[64,2048]{1,0:T(8,128)(2,1)S(1)} %add_convert_fusion.2), channel_id=1, source_target_pairs={{0,2},{1,5},{2,0},{3,7},{4,6},{5,1},{6,4},{7,3},{8,10},{9,13},{10,... | collective-permute-start | bytes 786440 | tf_op jit(solution)/shard_map/ppermute | solution.py:418
  (2 other events, 8.7 us)

commit v6 on v5

--- a/solution.py
+++ b/solution.py
@@ -329,20 +329,19 @@
     )(token)
 
 
-def plane_experts(where, rows_in, experts, own_weights, other_weights):
+def plane_experts(where, rows_in, out_rows, experts, own_weights, other_weights):
     arrays = [piece[0] for piece in rows_in]
     spans = tuple(piece[1:] for piece in rows_in)
-    sizes = [span[1] for span in spans]
-    count = sum(sizes)
+    count = sum(span[1] for span in spans)
     padded = arrays[0].shape[1]
     width, hidden = own_weights[0].shape[1:]
     weights = [w for pair in zip(own_weights, other_weights) for w in pair]
     vmem = pl.BlockSpec(memory_space=pltpu.VMEM)
     return pl.pallas_call(
         functools.partial(experts_kernel, spans, experts),
-        out_shape=tuple(jax.ShapeDtypeStruct((size, width), BF16) for size in sizes),
+        out_shape=tuple(jax.ShapeDtypeStruct((size, width), BF16) for size in out_rows),
         in_specs=[pl.BlockSpec(memory_space=pltpu.SMEM)] + [vmem] * (len(spans) + 6),
-        out_specs=[vmem] * len(spans),
+        out_specs=[vmem] * len(out_rows),
         scratch_shapes=[pltpu.VMEM((count, padded), BF16), pltpu.VMEM((count, width), F32)],
         compiler_params=pltpu.CompilerParams(vmem_limit_bytes=24 * 1024 * 1024),
         cost_estimate=pl.CostEstimate(flops=STEP_FLOPS, bytes_accessed=0, transcendentals=0),
@@ -395,7 +394,7 @@
     core = lax.axis_index("narrow")
     plane = 4
     planes = wide // plane
-    assert narrow == 2 and wide % plane == 0 and planes > 1
+    assert narrow == 2 and wide % plane == 0 and planes > 2
     experts = wide * narrow
     own_rows, width = hidden_in.shape
     mid = own_rows // 2
@@ -438,10 +437,11 @@
 
     def run_experts(s):
         rows_in = [(b[s], 0, own_rows), (u[s], 0, own_rows), (v[s], 0, 2 * own_rows)]
-        made[s] = list(plane_experts(index, rows_in, experts, own_held, other_held))
+        out_rows = [2 * own_rows] * 2 if s == 1 else [own_rows, own_rows, 2 * own_rows]
+        made[s] = list(plane_experts(index, rows_in, out_rows, experts, own_held, other_held))
 
     def made_entries(s):
-        return [(made[s], i) for i in range(3)]
+        return [(made[s], i) for i in range(len(made[s]))]
 
     b[1] = shifted(1)(b[0])
     u[0] = over_u(b[0])
@@ -462,50 +462,64 @@
             entries += made_entries(k - 2)
         wait(*entries)
     v[planes - 1] = over_v(jnp.concatenate([b[planes - 1], u[planes - 1]]))
+    whole = {}
+    if 1 in made:
+        whole[0] = shifted(planes - 1)(made[1][0])
     token = step(token)
     run_experts(planes - 2)
-    wait(*made_entries(planes - 2), *[(made[s], 2) for s in range(planes - 2)])
-
-    half = (planes + 1) // 2
-    order = list(range(half, planes - 1)) + list(range(1, half)) + [planes - 1, 0]
+    wait(*made_entries(planes - 2), (made[1], 1))
+    if 0 not in whole:
+        whole[0] = shifted(planes - 1)(made[1][0])
+    whole[1] = shifted(planes - 1)(made[1][1])
+
+    half = max(2, (planes + 1) // 2)
+    order = list(range(half, planes - 1)) + list(range(2, half)) + [planes - 1, 0]
     back_v, back_u, back_z, sums = {}, {}, {}, {}
     for s in order[:2]:
-        if s in made:
+        if s in made and s:
             back_v[s] = over_v(made[s][2])
     token = step(token)
-    wait((v, planes - 1), (made[0], 2))
+    wait((v, planes - 1))
     run_experts(planes - 1)
-    wait(*made_entries(planes - 1), *([(back_v, order[0])] if order[0] in back_v else []))
+    wait(
+        *made_entries(planes - 1),
+        *([(back_v, order[0])] if order[0] in back_v else []),
+        (whole, 0),
+    )
     for s in order[:2]:
-        if s not in back_v:
+        if s not in back_v and s:
             back_v[s] = over_v(made[s][2])
-    results = []
-    for j, s in enumerate(order):
+    for j, s in enumerate(order[:-1]):
         own, for_u, _ = made[s]
         if j:
             last = order[j - 1]
             onward = 2 * last >= planes
             back_z[last] = shifted(1 if onward else planes - last)(sums[last])
-        if s == 0:
-            token = step(token)
-            wait((back_v, 0))
         back_u[s] = over_u(add_bf16(for_u, back_v[s][own_rows:]))
-        if not s:
-            break
-        if j + 2 < planes:
+        if order[j + 1] == 0:
+            parts = [whole[0][:own_rows], whole[0][own_rows:], whole[1]]
+            made[0] = [add_bf16(a, part) for a, part in zip(made[0], parts)]
+            back_v[0] = over_v(made[0][2])
+        elif order[j + 2]:
             back_v[order[j + 2]] = over_v(made[order[j + 2]][2])
         token = step(token)
+        if j == 0:
+            wait((whole, 1))
+            token = step(token)
         carried = s - 1 in back_z and 2 * (s - 1) >= planes
-        entries = [(back_u, s)]
-        if order[j + 1]:
-            entries += [(back_v, order[j + 1]), (made[0], 2)]
-        if carried:
-            entries.append((back_z, s - 1))
-        wait(*entries)
+        wait((back_u, s), *([(back_z, s - 1)] if carried else []))
         terms = [own, back_v[s][:own_rows], back_u[s]]
         if carried:
             terms.append(back_z.pop(s - 1))
         sums[s] = add_bf16(*terms)
+        token = step(token)
+        if order[j + 1]:
+            wait((back_v, order[j + 1]), *[(made[0], i) for i in range(3)])
+    last = planes - 1
+    back_z[last] = shifted(1)(sums[last])
+    token = step(token)
+    wait((back_v, 0))
+    back_u[0] = over_u(add_bf16(made[0][1], back_v[0][own_rows:]))
     results = [made[0][0], back_v[0][:own_rows], back_u[0]]
     results += [back_z[s] for s in sorted(back_z)]
     return final_sum(token, residual, results)

time: 102 us -> 99.5 us (0.975)
  the two profiles are of different devices: /device:TPU:0 before, /device:TPU:10 now
where the time goes in v6:
time: 99.5 us; the launch traced here: 99.3 us
  waiting for transfers between devices  43.9 us (44%)
  Pallas kernels  28.4 us (29%)
  starting transfers between devices  25.9 us (26%)
    ppermute x14, waiting for transfers between devices, across(): return lambda a: lax.ppermute(a, ('wide', 'narrow'), pairs)  36.2 us
    pallas_call x4, Pallas kernels, plane_experts(): pl.pallas_call(functools.partial(experts_kernel, spans, experts), out_sha...  17.4 us
    ppermute x14, starting transfers between devices, across(): return lambda a: lax.ppermute(a, ('wide', 'narrow'), pairs)  13.8 us
    ppermute x7, starting transfers between devices, shifted(): return lambda a: lax.ppermute(a, 'wide', pairs)  11 us
    pallas_call x1, Pallas kernels, hold_weights(): pl.pallas_call(functools.partial(hold_kernel, count), out_shape=[jax.Shap...  5.28 us
    ppermute x7, waiting for transfers between devices, shifted(): return lambda a: lax.ppermute(a, 'wide', pairs)  4.99 us
    pallas_call x1, Pallas kernels, attention(): pl.pallas_call(functools.partial(attention_kernel, experts), out_shape=(j...  4.64 us
    ppermute x1, waiting for transfers between devices, on_device(): received = lax.ppermute(outgoing, 'narrow', swap)  2.15 us
  transfers between devices with their start and end apart: 25, of which 15 were waited for; matrix products, arithmetic and copies ran while one was open for 1% of the time, Pallas kernels for 28%

profile of v6, /device:TPU:10, one launch (start us, length us, event | category | flops | bytes accessed | tf_op | source)
XLA Modules:
  0.0 99.3 jit_solution(4233104539410021841)
XLA Ops:
  0.5 4.6 %shard_map.145 = (bf16[64,2048]{1,0:T(8,128)(2,1)S(1)}, f32[64,2048]{1,0:T(8,128)S(1)}, bf16[64,128]{1,0:T(8,128)(2,1)S(1)}, f32[1,2048]{1,0:T(1,128)S(1)}) custom-call(s32[1]{0:T(128)} %bitcast.core_ref, s32[8]{0:T(128)} %draft_len_ref.1, s32[8]{0:T(128)} %cache_len_ref.1, s32[10,64]{1,0:T(8,128)} %bitcast.6, f32[10,64]{1,0:T(8,128)} %bitcast.7, ...), custom_call_target="tpu_custom_call" | custom-call | flops 671088640 | bytes 6291456 | tf_op jit(solution)/shard_map/pallas_call | solution.py:179
  5.7 2.1 %collective-permute-done.received_ref = bf16[64,2048]{1,0:T(8,128)(2,1)S(1)} collective-permute-done((bf16[64,2048]{1,0:T(8,128)(2,1)S(1)}, bf16[64,2048]{1,0:T(8,128)(2,1)S(1)}, u32[]{:S(2)}, u32[]{:S(2)}) %collective-permute-start) | collective-permute-done | bytes 262176 | tf_op jit(solution)/shard_map/ppermute | solution.py:410
  8.1 1.6 %collective-permute-start.1 = (bf16[64,2176]{1,0:T(8,128)(2,1)S(1)}, bf16[64,2176]{1,0:T(8,128)(2,1)S(1)}, u32[]{:S(2)}, u32[]{:S(2)}) collective-permute-start(bf16[64,2176]{1,0:T(8,128)(2,1)S(1)} %get-tuple-element.83.refs_0_), channel_id=1, source_target_pairs={{0,8},{2,10},{4,12},{6,14},{8,16},{10,18},{12,20},{14,22},{16,24},... | collective-permute-start | bytes 835592 | tf_op jit(solution)/shard_map/ppermute | solution.py:421
  10.9 5.3 %shard_map.147 = (s32[2]{0:T(128)S(1)}, bf16[1,2048,512]{2,1,0:T(8,128)(2,1)S(1)}, bf16[1,2048,512]{2,1,0:T(8,128)(2,1)S(1)}, bf16[1,512,2048]{2,1,0:T(8,128)(2,...) custom-call(s32[2]{0:T(128)S(1)} %pad_add_fusion.where_ref, ...), custom_call_target="tpu_custom_call" | custom-call | flops 200000000 | tf_op jit(solution)/shard_map/pallas_call | solution.py:307
  19.0 1.6 %collective-permute-start.10 = (bf16[128,2176]{1,0:T(8,128)(2,1)S(1)}, bf16[128,2176]{1,0:T(8,128)(2,1)S(1)}, u32[]{:S(2)}, u32[]{:S(2)}) collective-permute-start(bf16[128,2176]{1,0:T(8,128)(2,1)S(1)} %pad_maximum_fusion), channel_id=1, source_target_pairs={{0,4},{1,3},{2,6},{3,1},{4,0},{5,7},{6,2},{7,5},{8,12},{9,11},{10,... | collective-permute-start | bytes 1671176 | tf_op jit(solution)/shard_map/ppermute | solution.py:417
  20.6 4.5 %collective-permute-done.6.refs_1_ = bf16[64,2176]{1,0:T(8,128)(2,1)S(1)} collective-permute-done((bf16[64,2176]{1,0:T(8,128)(2,1)S(1)}, bf16[64,2176]{1,0:T(8,128)(2,1)S(1)}, u32[]{:S(2)}, u32[]{:S(2)}) %collective-permute-start.6) | collective-permute-done | bytes 278560 | tf_op jit(solution)/shard_map/ppermute | solution.py:417
  29.9 4.4 %shard_map.150 = (bf16[64,2048]{1,0:T(8,128)(2,1)S(1)}, bf16[64,2048]{1,0:T(8,128)(2,1)S(1)}, bf16[128,2048]{1,0:T(8,128)(2,1)S(1)}) custom-call(s32[2]{0:T(128)S(1)} %get-tuple-element.95.where_ref, bf16[64,2176]{1,0:T(8,128)(2,1)S(1)} %get-tuple-element.83.refs_0_, bf16[64,2176]{1,0:T(8,128)(2,1)S(1)} %collective-permute-done.2.refs_1_, ...), custom_call_target="tpu_custom_call" | custom-call | flops 200000000 | tf_op jit(solution)/shard_map/pallas_call | solution.py:340
  34.2 1.8 %collective-permute-done.8.refs_1_ = bf16[64,2176]{1,0:T(8,128)(2,1)S(1)} collective-permute-done((bf16[64,2176]{1,0:T(8,128)(2,1)S(1)}, bf16[64,2176]{1,0:T(8,128)(2,1)S(1)}, u32[]{:S(2)}, u32[]{:S(2)}) %collective-permute-start.8) | collective-permute-done | bytes 278560 | tf_op jit(solution)/shard_map/ppermute | solution.py:417
  36.7 2.4 %collective-permute-start.13 = (bf16[128,2176]{1,0:T(8,128)(2,1)S(1)}, bf16[128,2176]{1,0:T(8,128)(2,1)S(1)}, u32[]{:S(2)}, u32[]{:S(2)}) collective-permute-start(bf16[128,2176]{1,0:T(8,128)(2,1)S(1)} %pad_maximum_fusion.2), channel_id=1, source_target_pairs={{0,4},{1,3},{2,6},{3,1},{4,0},{5,7},{6,2},{7,5},{8,12},{9,11},{10,... | collective-permute-start | bytes 1671176 | tf_op jit(solution)/shard_map/ppermute | solution.py:417
  39.2 4.3 %shard_map.152 = (bf16[128,2048]{1,0:T(8,128)(2,1)S(1)}, bf16[128,2048]{1,0:T(8,128)(2,1)S(1)}) custom-call(s32[2]{0:T(128)S(1)} %get-tuple-element.95.where_ref, bf16[64,2176]{1,0:T(8,128)(2,1)S(1)} %collective-permute-done.1.refs_0_, bf16[64,2176]{1,0:T(8,128)(2,1)S(1)} %collective-permute-done.6.refs_1_, ...), custom_call_target="tpu_custom_call" | custom-call | flops 200000000 | tf_op jit(solution)/shard_map/pallas_call | solution.py:340
  43.5 2.2 %collective-permute-done.11.refs_1_ = bf16[64,2176]{1,0:T(8,128)(2,1)S(1)} collective-permute-done((bf16[64,2176]{1,0:T(8,128)(2,1)S(1)}, bf16[64,2176]{1,0:T(8,128)(2,1)S(1)}, u32[]{:S(2)}, u32[]{:S(2)}) %collective-permute-start.11) | collective-permute-done | bytes 278560 | tf_op jit(solution)/shard_map/ppermute | solution.py:417
  45.7 1.9 %collective-permute-start.14 = (bf16[128,2176]{1,0:T(8,128)(2,1)S(1)}, bf16[128,2176]{1,0:T(8,128)(2,1)S(1)}, u32[]{:S(2)}, u32[]{:S(2)}) collective-permute-start(bf16[128,2176]{1,0:T(8,128)(2,1)S(1)} %pad_maximum_fusion.3), channel_id=1, source_target_pairs={{0,4},{1,3},{2,6},{3,1},{4,0},{5,7},{6,2},{7,5},{8,12},{9,11},{10,... | collective-permute-start | bytes 1671176 | tf_op jit(solution)/shard_map/ppermute | solution.py:417
  47.6 3.5 %collective-permute-start.16 = (bf16[128,2048]{1,0:T(8,128)(2,1)S(1)}, bf16[128,2048]{1,0:T(8,128)(2,1)S(1)}, u32[]{:S(2)}, u32[]{:S(2)}) collective-permute-start(bf16[128,2048]{1,0:T(8,128)(2,1)S(1)} %get-tuple-element.125), channel_id=1, source_target_pairs={{0,24},{2,26},{4,28},{6,30},{8,0},{10,2},{12,4},{14,6},{16,8},{18,... | collective-permute-start | bytes 1572872 | tf_op jit(solution)/shard_map/ppermute | solution.py:421
  51.2 4.3 %shard_map.154 = (bf16[64,2048]{1,0:T(8,128)(2,1)S(1)}, bf16[64,2048]{1,0:T(8,128)(2,1)S(1)}, bf16[128,2048]{1,0:T(8,128)(2,1)S(1)}) custom-call(s32[2]{0:T(128)S(1)} %get-tuple-element.95.where_ref, bf16[64,2176]{1,0:T(8,128)(2,1)S(1)} %collective-permute-done.7.refs_0_, bf16[64,2176]{1,0:T(8,128)(2,1)S(1)} %collective-permute-done.8.refs_1_, ...), custom_call_target="tpu_custom_call" | custom-call | flops 200000000 | tf_op jit(solution)/shard_map/pallas_call | solution.py:340
  55.7 2.3 %collective-permute-start.17 = (bf16[128,2048]{1,0:T(8,128)(2,1)S(1)}, bf16[128,2048]{1,0:T(8,128)(2,1)S(1)}, u32[]{:S(2)}, u32[]{:S(2)}) collective-permute-start(bf16[128,2048]{1,0:T(8,128)(2,1)S(1)} %get-tuple-element.127), channel_id=1, source_target_pairs={{0,24},{2,26},{4,28},{6,30},{8,0},{10,2},{12,4},{14,6},{16,8},{18,... | collective-permute-start | bytes 1572872 | tf_op jit(solution)/shard_map/ppermute | solution.py:421
  58.0 4.3 %shard_map.156 = (bf16[64,2048]{1,0:T(8,128)(2,1)S(1)}, bf16[64,2048]{1,0:T(8,128)(2,1)S(1)}, bf16[128,2048]{1,0:T(8,128)(2,1)S(1)}) custom-call(s32[2]{0:T(128)S(1)} %get-tuple-element.95.where_ref, bf16[64,2176]{1,0:T(8,128)(2,1)S(1)} %collective-permute-done.9.refs_0_, bf16[64,2176]{1,0:T(8,128)(2,1)S(1)} %collective-permute-done.11.refs_1_, ...), custom_call_target="tpu_custom_call" | custom-call | flops 200000000 | tf_op jit(solution)/shard_map/pallas_call | solution.py:340
  62.4 3.4 %collective-permute-done.15 = bf16[128,2048]{1,0:T(8,128)(2,1)S(1)} collective-permute-done((bf16[128,2048]{1,0:T(8,128)(2,1)S(1)}, bf16[128,2048]{1,0:T(8,128)(2,1)S(1)}, u32[]{:S(2)}, u32[]{:S(2)}) %collective-permute-start.15) | collective-permute-done | bytes 524320 | tf_op jit(solution)/shard_map/ppermute | solution.py:417
  66.4 2.7 %collective-permute-done.17 = bf16[128,2048]{1,0:T(8,128)(2,1)S(1)} collective-permute-done((bf16[128,2048]{1,0:T(8,128)(2,1)S(1)}, bf16[128,2048]{1,0:T(8,128)(2,1)S(1)}, u32[]{:S(2)}, u32[]{:S(2)}) %collective-permute-start.17) | collective-permute-done | bytes 524320 | tf_op jit(solution)/shard_map/ppermute | solution.py:421
  69.1 3.4 %collective-permute-done.18 = bf16[64,2048]{1,0:T(8,128)(2,1)S(1)} collective-permute-done((bf16[64,2048]{1,0:T(8,128)(2,1)S(1)}, bf16[64,2048]{1,0:T(8,128)(2,1)S(1)}, u32[]{:S(2)}, u32[]{:S(2)}) %collective-permute-start.18) | collective-permute-done | bytes 262176 | tf_op jit(solution)/shard_map/ppermute | solution.py:417
  72.7 3.5 %collective-permute-done.19 = bf16[128,2048]{1,0:T(8,128)(2,1)S(1)} collective-permute-done((bf16[128,2048]{1,0:T(8,128)(2,1)S(1)}, bf16[128,2048]{1,0:T(8,128)(2,1)S(1)}, u32[]{:S(2)}, u32[]{:S(2)}) %collective-permute-start.19) | collective-permute-done | bytes 524320 | tf_op jit(solution)/shard_map/ppermute | solution.py:417
  76.3 3.3 %collective-permute-start.20 = (bf16[64,2048]{1,0:T(8,128)(2,1)S(1)}, bf16[64,2048]{1,0:T(8,128)(2,1)S(1)}, u32[]{:S(2)}, u32[]{:S(2)}) collective-permute-start(bf16[64,2048]{1,0:T(8,128)(2,1)S(1)} %add_convert_fusion.6), channel_id=1, source_target_pairs={{0,2},{1,5},{2,0},{3,7},{4,6},{5,1},{6,4},{7,3},{8,10},{9,13},{10,... | collective-permute-start | bytes 786440 | tf_op jit(solution)/shard_map/ppermute | solution.py:417
  79.8 4.3 %collective-permute-done.20 = bf16[64,2048]{1,0:T(8,128)(2,1)S(1)} collective-permute-done((bf16[64,2048]{1,0:T(8,128)(2,1)S(1)}, bf16[64,2048]{1,0:T(8,128)(2,1)S(1)}, u32[]{:S(2)}, u32[]{:S(2)}) %collective-permute-start.20) | collective-permute-done | bytes 262176 | tf_op jit(solution)/shard_map/ppermute | solution.py:417
  85.0 6.8 %collective-permute-done.22 = bf16[128,2048]{1,0:T(8,128)(2,1)S(1)} collective-permute-done((bf16[128,2048]{1,0:T(8,128)(2,1)S(1)}, bf16[128,2048]{1,0:T(8,128)(2,1)S(1)}, u32[]{:S(2)}, u32[]{:S(2)}) %collective-permute-start.22) | collective-permute-done | bytes 524320 | tf_op jit(solution)/shard_map/ppermute | solution.py:417
  92.1 6.3 %collective-permute-done.23.refs_2_ = bf16[64,2048]{1,0:T(8,128)(2,1)S(1)} collective-permute-done((bf16[64,2048]{1,0:T(8,128)(2,1)S(1)}, bf16[64,2048]{1,0:T(8,128)(2,1)S(1)}, u32[]{:S(2)}, u32[]{:S(2)}) %collective-permute-start.23) | collective-permute-done | bytes 262176 | tf_op jit(solution)/shard_map/ppermute | solution.py:417
  (58 shorter events, 14.1 us)
Async XLA Ops:
  0.0 10.3 %collective-permute-start.3 = (bf16[1,2048,512]{2,1,0:T(8,128)(2,1)}, bf16[1,2048,512]{2,1,0:T(8,128)(2,1)S(1)}, u32[]{:S(2)}, u32[]{:S(2)}) collective-permute-start(bf16[1,2048,512]{2,1,0:T(8,128)(2,1)} %refs_0_.1), channel_id=1, source_target_pairs={{0,1},{1,0},{2,3},{3,2},{4,5},{5,4},{6,7},{7,6},{8,9},{9,8},{10,11... | collective-permute-start | bytes 6291464 | tf_op jit(solution)/shard_map/ppermute | solution.py:404
  0.0 10.3 %collective-permute-start.4 = (bf16[1,2048,512]{2,1,0:T(8,128)(2,1)}, bf16[1,2048,512]{2,1,0:T(8,128)(2,1)}, u32[]{:S(2)}, u32[]{:S(2)}) collective-permute-start(bf16[1,2048,512]{2,1,0:T(8,128)(2,1)} %refs_1_.1), channel_id=1, source_target_pairs={{0,1},{1,0},{2,3},{3,2},{4,5},{5,4},{6,7},{7,6},{8,9},{9,8},{10,11... | collective-permute-start | bytes 6291464 | tf_op jit(solution)/shard_map/ppermute | solution.py:404
  0.5 10.4 %collective-permute-start.5 = (bf16[1,512,2048]{2,1,0:T(8,128)(2,1)}, bf16[1,512,2048]{2,1,0:T(8,128)(2,1)}, u32[]{:S(2)}, u32[]{:S(2)}) collective-permute-start(bf16[1,512,2048]{2,1,0:T(8,128)(2,1)} %refs_2_.1), channel_id=1, source_target_pairs={{0,1},{1,0},{2,3},{3,2},{4,5},{5,4},{6,7},{7,6},{8,9},{9,8},{10,11... | collective-permute-start | bytes 6291464 | tf_op jit(solution)/shard_map/ppermute | solution.py:404
  8.1 8.8 %collective-permute-start.1 = (bf16[64,2176]{1,0:T(8,128)(2,1)S(1)}, bf16[64,2176]{1,0:T(8,128)(2,1)S(1)}, u32[]{:S(2)}, u32[]{:S(2)}) collective-permute-start(bf16[64,2176]{1,0:T(8,128)(2,1)S(1)} %get-tuple-element.83.refs_0_), channel_id=1, source_target_pairs={{0,8},{2,10},{4,12},{6,14},{8,16},{10,18},{12,20},{14,22},{16,24},... | collective-permute-start | bytes 835592 | tf_op jit(solution)/shard_map/ppermute | solution.py:421
  9.7 7.1 %collective-permute-start.2 = (bf16[64,2176]{1,0:T(8,128)(2,1)S(1)}, bf16[64,2176]{1,0:T(8,128)(2,1)S(1)}, u32[]{:S(2)}, u32[]{:S(2)}) collective-permute-start(bf16[64,2176]{1,0:T(8,128)(2,1)S(1)} %get-tuple-element.83.refs_0_), channel_id=1, source_target_pairs={{0,2},{1,5},{2,0},{3,7},{4,6},{5,1},{6,4},{7,3},{8,10},{9,13},{10,... | collective-permute-start | bytes 835592 | tf_op jit(solution)/shard_map/ppermute | solution.py:417
  16.8 8.2 %collective-permute-start.6 = (bf16[64,2176]{1,0:T(8,128)(2,1)S(1)}, bf16[64,2176]{1,0:T(8,128)(2,1)S(1)}, u32[]{:S(2)}, u32[]{:S(2)}) collective-permute-start(bf16[64,2176]{1,0:T(8,128)(2,1)S(1)} %collective-permute-done.1.refs_0_), channel_id=1, source_target_pairs={{0,2},{1,5},{2,0},{3,7},{4,6},{5,1},{6,4},{7,3},{8,10},{9,13},{10,... | collective-permute-start | bytes 835592 | tf_op jit(solution)/shard_map/ppermute | solution.py:417
  17.4 9.2 %collective-permute-start.7 = (bf16[64,2176]{1,0:T(8,128)(2,1)S(1)}, bf16[64,2176]{1,0:T(8,128)(2,1)S(1)}, u32[]{:S(2)}, u32[]{:S(2)}) collective-permute-start(bf16[64,2176]{1,0:T(8,128)(2,1)S(1)} %collective-permute-done.1.refs_0_), channel_id=1, source_target_pairs={{0,8},{2,10},{4,12},{6,14},{8,16},{10,18},{12,20},{14,22},{16,24},... | collective-permute-start | bytes 835592 | tf_op jit(solution)/shard_map/ppermute | solution.py:421
  19.0 10.9 %collective-permute-start.10 = (bf16[128,2176]{1,0:T(8,128)(2,1)S(1)}, bf16[128,2176]{1,0:T(8,128)(2,1)S(1)}, u32[]{:S(2)}, u32[]{:S(2)}) collective-permute-start(bf16[128,2176]{1,0:T(8,128)(2,1)S(1)} %pad_maximum_fusion), channel_id=1, source_target_pairs={{0,4},{1,3},{2,6},{3,1},{4,0},{5,7},{6,2},{7,5},{8,12},{9,11},{10,... | collective-permute-start | bytes 1671176 | tf_op jit(solution)/shard_map/ppermute | solution.py:417
  26.6 9.5 %collective-permute-start.8 = (bf16[64,2176]{1,0:T(8,128)(2,1)S(1)}, bf16[64,2176]{1,0:T(8,128)(2,1)S(1)}, u32[]{:S(2)}, u32[]{:S(2)}) collective-permute-start(bf16[64,2176]{1,0:T(8,128)(2,1)S(1)} %collective-permute-done.7.refs_0_), channel_id=1, source_target_pairs={{0,2},{1,5},{2,0},{3,7},{4,6},{5,1},{6,4},{7,3},{8,10},{9,13},{10,... | collective-permute-start | bytes 835592 | tf_op jit(solution)/shard_map/ppermute | solution.py:417
  27.1 9.1 %collective-permute-start.9 = (bf16[64,2176]{1,0:T(8,128)(2,1)S(1)}, bf16[64,2176]{1,0:T(8,128)(2,1)S(1)}, u32[]{:S(2)}, u32[]{:S(2)}) collective-permute-start(bf16[64,2176]{1,0:T(8,128)(2,1)S(1)} %collective-permute-done.7.refs_0_), channel_id=1, source_target_pairs={{0,8},{2,10},{4,12},{6,14},{8,16},{10,18},{12,20},{14,22},{16,24},... | collective-permute-start | bytes 835592 | tf_op jit(solution)/shard_map/ppermute | solution.py:421
  28.3 10.8 %collective-permute-start.12 = (bf16[128,2176]{1,0:T(8,128)(2,1)S(1)}, bf16[128,2176]{1,0:T(8,128)(2,1)S(1)}, u32[]{:S(2)}, u32[]{:S(2)}) collective-permute-start(bf16[128,2176]{1,0:T(8,128)(2,1)S(1)} %pad_maximum_fusion.1), channel_id=1, source_target_pairs={{0,4},{1,3},{2,6},{3,1},{4,0},{5,7},{6,2},{7,5},{8,12},{9,11},{10,... | collective-permute-start | bytes 1671176 | tf_op jit(solution)/shard_map/ppermute | solution.py:417
  36.2 9.5 %collective-permute-start.11 = (bf16[64,2176]{1,0:T(8,128)(2,1)S(1)}, bf16[64,2176]{1,0:T(8,128)(2,1)S(1)}, u32[]{:S(2)}, u32[]{:S(2)}) collective-permute-start(bf16[64,2176]{1,0:T(8,128)(2,1)S(1)} %collective-permute-done.9.refs_0_), channel_id=1, source_target_pairs={{0,2},{1,5},{2,0},{3,7},{4,6},{5,1},{6,4},{7,3},{8,10},{9,13},{10,... | collective-permute-start | bytes 835592 | tf_op jit(solution)/shard_map/ppermute | solution.py:417
  36.7 14.5 %collective-permute-start.13 = (bf16[128,2176]{1,0:T(8,128)(2,1)S(1)}, bf16[128,2176]{1,0:T(8,128)(2,1)S(1)}, u32[]{:S(2)}, u32[]{:S(2)}) collective-permute-start(bf16[128,2176]{1,0:T(8,128)(2,1)S(1)} %pad_maximum_fusion.2), channel_id=1, source_target_pairs={{0,4},{1,3},{2,6},{3,1},{4,0},{5,7},{6,2},{7,5},{8,12},{9,11},{10,... | collective-permute-start | bytes 1671176 | tf_op jit(solution)/shard_map/ppermute | solution.py:417
  45.7 12.3 %collective-permute-start.14 = (bf16[128,2176]{1,0:T(8,128)(2,1)S(1)}, bf16[128,2176]{1,0:T(8,128)(2,1)S(1)}, u32[]{:S(2)}, u32[]{:S(2)}) collective-permute-start(bf16[128,2176]{1,0:T(8,128)(2,1)S(1)} %pad_maximum_fusion.3), channel_id=1, source_target_pairs={{0,4},{1,3},{2,6},{3,1},{4,0},{5,7},{6,2},{7,5},{8,12},{9,11},{10,... | collective-permute-start | bytes 1671176 | tf_op jit(solution)/shard_map/ppermute | solution.py:417
  47.6 14.8 %collective-permute-start.16 = (bf16[128,2048]{1,0:T(8,128)(2,1)S(1)}, bf16[128,2048]{1,0:T(8,128)(2,1)S(1)}, u32[]{:S(2)}, u32[]{:S(2)}) collective-permute-start(bf16[128,2048]{1,0:T(8,128)(2,1)S(1)} %get-tuple-element.125), channel_id=1, source_target_pairs={{0,24},{2,26},{4,28},{6,30},{8,0},{10,2},{12,4},{14,6},{16,8},{18,... | collective-permute-start | bytes 1572872 | tf_op jit(solution)/shard_map/ppermute | solution.py:421
  55.5 10.3 %collective-permute-start.15 = (bf16[128,2048]{1,0:T(8,128)(2,1)S(1)}, bf16[128,2048]{1,0:T(8,128)(2,1)S(1)}, u32[]{:S(2)}, u32[]{:S(2)}) collective-permute-start(bf16[128,2048]{1,0:T(8,128)(2,1)S(1)} %get-tuple-element.124), channel_id=1, source_target_pairs={{0,4},{1,3},{2,6},{3,1},{4,0},{5,7},{6,2},{7,5},{8,12},{9,11},{10,... | collective-permute-start | bytes 1572872 | tf_op jit(solution)/shard_map/ppermute | solution.py:417
  55.7 13.3 %collective-permute-start.17 = (bf16[128,2048]{1,0:T(8,128)(2,1)S(1)}, bf16[128,2048]{1,0:T(8,128)(2,1)S(1)}, u32[]{:S(2)}, u32[]{:S(2)}) collective-permute-start(bf16[128,2048]{1,0:T(8,128)(2,1)S(1)} %get-tuple-element.127), channel_id=1, source_target_pairs={{0,24},{2,26},{4,28},{6,30},{8,0},{10,2},{12,4},{14,6},{16,8},{18,... | collective-permute-start | bytes 1572872 | tf_op jit(solution)/shard_map/ppermute | solution.py:421
  65.8 6.7 %collective-permute-start.18 = (bf16[64,2048]{1,0:T(8,128)(2,1)S(1)}, bf16[64,2048]{1,0:T(8,128)(2,1)S(1)}, u32[]{:S(2)}, u32[]{:S(2)}) collective-permute-start(bf16[64,2048]{1,0:T(8,128)(2,1)S(1)} %add_convert_fusion.7), channel_id=1, source_target_pairs={{0,2},{1,5},{2,0},{3,7},{4,6},{5,1},{6,4},{7,3},{8,10},{9,13},{10,... | collective-permute-start | bytes 786440 | tf_op jit(solution)/shard_map/ppermute | solution.py:417
  65.9 10.3 %collective-permute-start.19 = (bf16[128,2048]{1,0:T(8,128)(2,1)S(1)}, bf16[128,2048]{1,0:T(8,128)(2,1)S(1)}, u32[]{:S(2)}, u32[]{:S(2)}) collective-permute-start(bf16[128,2048]{1,0:T(8,128)(2,1)S(1)} %get-tuple-element.132), channel_id=1, source_target_pairs={{0,4},{1,3},{2,6},{3,1},{4,0},{5,7},{6,2},{7,5},{8,12},{9,11},{10,... | collective-permute-start | bytes 1572872 | tf_op jit(solution)/shard_map/ppermute | solution.py:417
  72.6 7.2 %collective-permute-start.21 = (bf16[64,2048]{1,0:T(8,128)(2,1)S(1)}, bf16[64,2048]{1,0:T(8,128)(2,1)S(1)}, u32[]{:S(2)}, u32[]{:S(2)}) collective-permute-start(bf16[64,2048]{1,0:T(8,128)(2,1)S(1)} %add_convert_fusion.5), channel_id=1, source_target_pairs={{0,8},{2,10},{4,12},{6,14},{8,16},{10,18},{12,20},{14,22},{16,24},... | collective-permute-start | bytes 786440 | tf_op jit(solution)/shard_map/ppermute | solution.py:421
  76.3 7.9 %collective-permute-start.20 = (bf16[64,2048]{1,0:T(8,128)(2,1)S(1)}, bf16[64,2048]{1,0:T(8,128)(2,1)S(1)}, u32[]{:S(2)}, u32[]{:S(2)}) collective-permute-start(bf16[64,2048]{1,0:T(8,128)(2,1)S(1)} %add_convert_fusion.6), channel_id=1, source_target_pairs={{0,2},{1,5},{2,0},{3,7},{4,6},{5,1},{6,4},{7,3},{8,10},{9,13},{10,... | collective-permute-start | bytes 786440 | tf_op jit(solution)/shard_map/ppermute | solution.py:417
  79.7 12.1 %collective-permute-start.22 = (bf16[128,2048]{1,0:T(8,128)(2,1)S(1)}, bf16[128,2048]{1,0:T(8,128)(2,1)S(1)}, u32[]{:S(2)}, u32[]{:S(2)}) collective-permute-start(bf16[128,2048]{1,0:T(8,128)(2,1)S(1)} %add_convert_fusion), channel_id=1, source_target_pairs={{0,4},{1,3},{2,6},{3,1},{4,0},{5,7},{6,2},{7,5},{8,12},{9,11},{10,... | collective-permute-start | bytes 1572872 | tf_op jit(solution)/shard_map/ppermute | solution.py:417
  84.3 7.8 %collective-permute-start.24 = (bf16[64,2048]{1,0:T(8,128)(2,1)S(1)}, bf16[64,2048]{1,0:T(8,128)(2,1)S(1)}, u32[]{:S(2)}, u32[]{:S(2)}) collective-permute-start(bf16[64,2048]{1,0:T(8,128)(2,1)S(1)} %add_convert_fusion.1), channel_id=1, source_target_pairs={{0,8},{2,10},{4,12},{6,14},{8,16},{10,18},{12,20},{14,22},{16,24},... | collective-permute-start | bytes 786440 | tf_op jit(solution)/shard_map/ppermute | solution.py:421
  92.0 6.4 %collective-permute-start.23 = (bf16[64,2048]{1,0:T(8,128)(2,1)S(1)}, bf16[64,2048]{1,0:T(8,128)(2,1)S(1)}, u32[]{:S(2)}, u32[]{:S(2)}) collective-permute-start(bf16[64,2048]{1,0:T(8,128)(2,1)S(1)} %get-tuple-element.153), channel_id=1, source_target_pairs={{0,2},{1,5},{2,0},{3,7},{4,6},{5,1},{6,4},{7,3},{8,10},{9,13},{10,... | collective-permute-start | bytes 786440 | tf_op jit(solution)/shard_map/ppermute | solution.py:417
  (1 other events, 2.7 us)

commit v7 on v6

--- a/solution.py
+++ b/solution.py
@@ -481,14 +481,12 @@
     token = step(token)
     wait((v, planes - 1))
     run_experts(planes - 1)
-    wait(
-        *made_entries(planes - 1),
-        *([(back_v, order[0])] if order[0] in back_v else []),
-        (whole, 0),
-    )
+    wait(*made_entries(planes - 1))
     for s in order[:2]:
         if s not in back_v and s:
             back_v[s] = over_v(made[s][2])
+    token = step(token)
+    wait((back_v, order[0]), (whole, 0))
     for j, s in enumerate(order[:-1]):
         own, for_u, _ = made[s]
         if j:
@@ -496,29 +494,28 @@
             onward = 2 * last >= planes
             back_z[last] = shifted(1 if onward else planes - last)(sums[last])
         back_u[s] = over_u(add_bf16(for_u, back_v[s][own_rows:]))
-        if order[j + 1] == 0:
+        if j + 2 < planes - 1 and order[j + 2]:
+            back_v[order[j + 2]] = over_v(made[order[j + 2]][2])
+        token = step(token)
+        carried = s - 1 in back_z and 2 * (s - 1) >= planes
+        wait(
+            (back_u, s),
+            *([(back_z, s - 1)] if carried else []),
+            *([] if order[j + 1] else [(back_v, 0)]),
+            *([] if j else [(whole, 1)]),
+            *([(back_v, order[j + 1])] if order[j + 1] else []),
+        )
+        if j == 0:
             parts = [whole[0][:own_rows], whole[0][own_rows:], whole[1]]
             made[0] = [add_bf16(a, part) for a, part in zip(made[0], parts)]
             back_v[0] = over_v(made[0][2])
-        elif order[j + 2]:
-            back_v[order[j + 2]] = over_v(made[order[j + 2]][2])
-        token = step(token)
-        if j == 0:
-            wait((whole, 1))
-            token = step(token)
-        carried = s - 1 in back_z and 2 * (s - 1) >= planes
-        wait((back_u, s), *([(back_z, s - 1)] if carried else []))
         terms = [own, back_v[s][:own_rows], back_u[s]]
         if carried:
             terms.append(back_z.pop(s - 1))
         sums[s] = add_bf16(*terms)
         token = step(token)
-        if order[j + 1]:
-            wait((back_v, order[j + 1]), *[(made[0], i) for i in range(3)])
     last = planes - 1
     back_z[last] = shifted(1)(sums[last])
-    token = step(token)
-    wait((back_v, 0))
     back_u[0] = over_u(add_bf16(made[0][1], back_v[0][own_rows:]))
     results = [made[0][0], back_v[0][:own_rows], back_u[0]]
     results += [back_z[s] for s in sorted(back_z)]

time: 99.5 us -> 96.8 us (0.973)
  the two profiles are of different devices: /device:TPU:10 before, /device:TPU:0 now
where the time goes in v7:
time: 96.8 us; the launch traced here: 96.6 us
  waiting for transfers between devices  43.8 us (45%)
  Pallas kernels  28.4 us (29%)
  starting transfers between devices  23.2 us (24%)
    ppermute x7, waiting for transfers between devices, shifted(): return lambda a: lax.ppermute(a, 'wide', pairs)  23.7 us
    ppermute x14, waiting for transfers between devices, across(): return lambda a: lax.ppermute(a, ('wide', 'narrow'), pairs)  17.9 us
    pallas_call x4, Pallas kernels, plane_experts(): pl.pallas_call(functools.partial(experts_kernel, spans, experts), out_sha...  17.4 us
    ppermute x14, starting transfers between devices, across(): return lambda a: lax.ppermute(a, ('wide', 'narrow'), pairs)  16.8 us
    ppermute x7, starting transfers between devices, shifted(): return lambda a: lax.ppermute(a, 'wide', pairs)  5.32 us
    pallas_call x1, Pallas kernels, hold_weights(): pl.pallas_call(functools.partial(hold_kernel, count), out_shape=[jax.Shap...  5.29 us
    pallas_call x1, Pallas kernels, attention(): pl.pallas_call(functools.partial(attention_kernel, experts), out_shape=(j...  4.64 us
    ppermute x1, waiting for transfers between devices, on_device(): received = lax.ppermute(outgoing, 'narrow', swap)  2.18 us
  transfers between devices with their start and end apart: 25, of which 16 were waited for; matrix products, arithmetic and copies ran while one was open for 1% of the time, Pallas kernels for 29%

profile of v7, /device:TPU:0, one launch (start us, length us, event | category | flops | bytes accessed | tf_op | source)
XLA Modules:
  0.0 96.6 jit_solution(14365141572565411758)
XLA Ops:
  1.0 4.6 %shard_map.145 = (bf16[64,2048]{1,0:T(8,128)(2,1)S(1)}, f32[64,2048]{1,0:T(8,128)S(1)}, bf16[64,128]{1,0:T(8,128)(2,1)S(1)}, f32[1,2048]{1,0:T(1,128)S(1)}) custom-call(s32[1]{0:T(128)} %bitcast.core_ref, s32[8]{0:T(128)} %draft_len_ref.1, s32[8]{0:T(128)} %cache_len_ref.1, s32[10,64]{1,0:T(8,128)} %bitcast.6, f32[10,64]{1,0:T(8,128)} %bitcast.7, ...), custom_call_target="tpu_custom_call" | custom-call | flops 671088640 | bytes 6291456 | tf_op jit(solution)/shard_map/pallas_call | solution.py:179
  5.7 2.2 %collective-permute-done.received_ref = bf16[64,2048]{1,0:T(8,128)(2,1)S(1)} collective-permute-done((bf16[64,2048]{1,0:T(8,128)(2,1)S(1)}, bf16[64,2048]{1,0:T(8,128)(2,1)S(1)}, u32[]{:S(2)}, u32[]{:S(2)}) %collective-permute-start) | collective-permute-done | bytes 262176 | tf_op jit(solution)/shard_map/ppermute | solution.py:410
  8.1 3.0 %collective-permute-start.1 = (bf16[64,2176]{1,0:T(8,128)(2,1)S(1)}, bf16[64,2176]{1,0:T(8,128)(2,1)S(1)}, u32[]{:S(2)}, u32[]{:S(2)}) collective-permute-start(bf16[64,2176]{1,0:T(8,128)(2,1)S(1)} %get-tuple-element.78.refs_0_), channel_id=1, source_target_pairs={{0,8},{2,10},{4,12},{6,14},{8,16},{10,18},{12,20},{14,22},{16,24},... | collective-permute-start | bytes 835592 | tf_op jit(solution)/shard_map/ppermute | solution.py:421
  11.1 1.5 %collective-permute-start.2 = (bf16[64,2176]{1,0:T(8,128)(2,1)S(1)}, bf16[64,2176]{1,0:T(8,128)(2,1)S(1)}, u32[]{:S(2)}, u32[]{:S(2)}) collective-permute-start(bf16[64,2176]{1,0:T(8,128)(2,1)S(1)} %get-tuple-element.78.refs_0_), channel_id=1, source_target_pairs={{0,2},{1,5},{2,0},{3,7},{4,6},{5,1},{6,4},{7,3},{8,10},{9,13},{10,... | collective-permute-start | bytes 835592 | tf_op jit(solution)/shard_map/ppermute | solution.py:417
  12.7 5.3 %shard_map.147 = (s32[2]{0:T(128)S(1)}, bf16[1,2048,512]{2,1,0:T(8,128)(2,1)S(1)}, bf16[1,2048,512]{2,1,0:T(8,128)(2,1)S(1)}, bf16[1,512,2048]{2,1,0:T(8,128)(2,...) custom-call(s32[2]{0:T(128)S(1)} %pad_add_fusion.where_ref, ...), custom_call_target="tpu_custom_call" | custom-call | flops 200000000 | tf_op jit(solution)/shard_map/pallas_call | solution.py:307
  18.0 2.1 %collective-permute-done.1.refs_0_ = bf16[64,2176]{1,0:T(8,128)(2,1)S(1)} collective-permute-done((bf16[64,2176]{1,0:T(8,128)(2,1)S(1)}, bf16[64,2176]{1,0:T(8,128)(2,1)S(1)}, u32[]{:S(2)}, u32[]{:S(2)}) %collective-permute-start.1) | collective-permute-done | bytes 278560 | tf_op jit(solution)/shard_map/ppermute | solution.py:421
  20.1 1.5 %collective-permute-start.6 = (bf16[64,2176]{1,0:T(8,128)(2,1)S(1)}, bf16[64,2176]{1,0:T(8,128)(2,1)S(1)}, u32[]{:S(2)}, u32[]{:S(2)}) collective-permute-start(bf16[64,2176]{1,0:T(8,128)(2,1)S(1)} %collective-permute-done.1.refs_0_), channel_id=1, source_target_pairs={{0,2},{1,5},{2,0},{3,7},{4,6},{5,1},{6,4},{7,3},{8,10},{9,13},{10,... | collective-permute-start | bytes 835592 | tf_op jit(solution)/shard_map/ppermute | solution.py:417
  21.7 1.6 %collective-permute-start.10 = (bf16[128,2176]{1,0:T(8,128)(2,1)S(1)}, bf16[128,2176]{1,0:T(8,128)(2,1)S(1)}, u32[]{:S(2)}, u32[]{:S(2)}) collective-permute-start(bf16[128,2176]{1,0:T(8,128)(2,1)S(1)} %pad_maximum_fusion), channel_id=1, source_target_pairs={{0,4},{1,3},{2,6},{3,1},{4,0},{5,7},{6,2},{7,5},{8,12},{9,11},{10,... | collective-permute-start | bytes 1671176 | tf_op jit(solution)/shard_map/ppermute | solution.py:417
  23.3 6.4 %collective-permute-done.6.refs_1_ = bf16[64,2176]{1,0:T(8,128)(2,1)S(1)} collective-permute-done((bf16[64,2176]{1,0:T(8,128)(2,1)S(1)}, bf16[64,2176]{1,0:T(8,128)(2,1)S(1)}, u32[]{:S(2)}, u32[]{:S(2)}) %collective-permute-start.6) | collective-permute-done | bytes 278560 | tf_op jit(solution)/shard_map/ppermute | solution.py:417
  31.1 1.5 %collective-permute-start.8 = (bf16[64,2176]{1,0:T(8,128)(2,1)S(1)}, bf16[64,2176]{1,0:T(8,128)(2,1)S(1)}, u32[]{:S(2)}, u32[]{:S(2)}) collective-permute-start(bf16[64,2176]{1,0:T(8,128)(2,1)S(1)} %collective-permute-done.7.refs_0_), channel_id=1, source_target_pairs={{0,2},{1,5},{2,0},{3,7},{4,6},{5,1},{6,4},{7,3},{8,10},{9,13},{10,... | collective-permute-start | bytes 835592 | tf_op jit(solution)/shard_map/ppermute | solution.py:417
  33.2 4.4 %shard_map.150 = (bf16[64,2048]{1,0:T(8,128)(2,1)S(1)}, bf16[64,2048]{1,0:T(8,128)(2,1)S(1)}, bf16[128,2048]{1,0:T(8,128)(2,1)S(1)}) custom-call(s32[2]{0:T(128)S(1)} %get-tuple-element.90.where_ref, bf16[64,2176]{1,0:T(8,128)(2,1)S(1)} %get-tuple-element.78.refs_0_, bf16[64,2176]{1,0:T(8,128)(2,1)S(1)} %collective-permute-done.2.refs_1_, ...), custom_call_target="tpu_custom_call" | custom-call | flops 200000000 | tf_op jit(solution)/shard_map/pallas_call | solution.py:340
  37.6 3.1 %collective-permute-done.8.refs_1_ = bf16[64,2176]{1,0:T(8,128)(2,1)S(1)} collective-permute-done((bf16[64,2176]{1,0:T(8,128)(2,1)S(1)}, bf16[64,2176]{1,0:T(8,128)(2,1)S(1)}, u32[]{:S(2)}, u32[]{:S(2)}) %collective-permute-start.8) | collective-permute-done | bytes 278560 | tf_op jit(solution)/shard_map/ppermute | solution.py:417
  42.3 1.8 %collective-permute-start.13 = (bf16[128,2176]{1,0:T(8,128)(2,1)S(1)}, bf16[128,2176]{1,0:T(8,128)(2,1)S(1)}, u32[]{:S(2)}, u32[]{:S(2)}) collective-permute-start(bf16[128,2176]{1,0:T(8,128)(2,1)S(1)} %pad_maximum_fusion.2), channel_id=1, source_target_pairs={{0,4},{1,3},{2,6},{3,1},{4,0},{5,7},{6,2},{7,5},{8,12},{9,11},{10,... | collective-permute-start | bytes 1671176 | tf_op jit(solution)/shard_map/ppermute | solution.py:417
  45.1 4.4 %shard_map.152 = (bf16[128,2048]{1,0:T(8,128)(2,1)S(1)}, bf16[128,2048]{1,0:T(8,128)(2,1)S(1)}) custom-call(s32[2]{0:T(128)S(1)} %get-tuple-element.90.where_ref, bf16[64,2176]{1,0:T(8,128)(2,1)S(1)} %collective-permute-done.1.refs_0_, bf16[64,2176]{1,0:T(8,128)(2,1)S(1)} %collective-permute-done.6.refs_1_, ...), custom_call_target="tpu_custom_call" | custom-call | flops 200000000 | tf_op jit(solution)/shard_map/pallas_call | solution.py:340
  51.6 2.1 %collective-permute-start.16 = (bf16[128,2048]{1,0:T(8,128)(2,1)S(1)}, bf16[128,2048]{1,0:T(8,128)(2,1)S(1)}, u32[]{:S(2)}, u32[]{:S(2)}) collective-permute-start(bf16[128,2048]{1,0:T(8,128)(2,1)S(1)} %get-tuple-element.121), channel_id=1, source_target_pairs={{0,24},{2,26},{4,28},{6,30},{8,0},{10,2},{12,4},{14,6},{16,8},{18,... | collective-permute-start | bytes 1572872 | tf_op jit(solution)/shard_map/ppermute | solution.py:421
  53.8 4.3 %shard_map.154 = (bf16[64,2048]{1,0:T(8,128)(2,1)S(1)}, bf16[64,2048]{1,0:T(8,128)(2,1)S(1)}, bf16[128,2048]{1,0:T(8,128)(2,1)S(1)}) custom-call(s32[2]{0:T(128)S(1)} %get-tuple-element.90.where_ref, bf16[64,2176]{1,0:T(8,128)(2,1)S(1)} %collective-permute-done.7.refs_0_, bf16[64,2176]{1,0:T(8,128)(2,1)S(1)} %collective-permute-done.8.refs_1_, ...), custom_call_target="tpu_custom_call" | custom-call | flops 200000000 | tf_op jit(solution)/shard_map/pallas_call | solution.py:340
  58.1 1.9 %collective-permute-start.15 = (bf16[128,2048]{1,0:T(8,128)(2,1)S(1)}, bf16[128,2048]{1,0:T(8,128)(2,1)S(1)}, u32[]{:S(2)}, u32[]{:S(2)}) collective-permute-start(bf16[128,2048]{1,0:T(8,128)(2,1)S(1)} %get-tuple-element.120), channel_id=1, source_target_pairs={{0,4},{1,3},{2,6},{3,1},{4,0},{5,7},{6,2},{7,5},{8,12},{9,11},{10,... | collective-permute-start | bytes 1572872 | tf_op jit(solution)/shard_map/ppermute | solution.py:417
  60.1 4.3 %shard_map.156 = (bf16[64,2048]{1,0:T(8,128)(2,1)S(1)}, bf16[64,2048]{1,0:T(8,128)(2,1)S(1)}, bf16[128,2048]{1,0:T(8,128)(2,1)S(1)}) custom-call(s32[2]{0:T(128)S(1)} %get-tuple-element.90.where_ref, bf16[64,2176]{1,0:T(8,128)(2,1)S(1)} %collective-permute-done.9.refs_0_, bf16[64,2176]{1,0:T(8,128)(2,1)S(1)} %collective-permute-done.11.refs_1_, ...), custom_call_target="tpu_custom_call" | custom-call | flops 200000000 | tf_op jit(solution)/shard_map/pallas_call | solution.py:340
  65.9 1.7 %collective-permute-done.15 = bf16[128,2048]{1,0:T(8,128)(2,1)S(1)} collective-permute-done((bf16[128,2048]{1,0:T(8,128)(2,1)S(1)}, bf16[128,2048]{1,0:T(8,128)(2,1)S(1)}, u32[]{:S(2)}, u32[]{:S(2)}) %collective-permute-start.15) | collective-permute-done | bytes 524320 | tf_op jit(solution)/shard_map/ppermute | solution.py:417
  68.0 4.8 %collective-permute-done.18 = bf16[128,2048]{1,0:T(8,128)(2,1)S(1)} collective-permute-done((bf16[128,2048]{1,0:T(8,128)(2,1)S(1)}, bf16[128,2048]{1,0:T(8,128)(2,1)S(1)}, u32[]{:S(2)}, u32[]{:S(2)}) %collective-permute-start.18) | collective-permute-done | bytes 524320 | tf_op jit(solution)/shard_map/ppermute | solution.py:421
  74.0 2.0 %collective-permute-done.19 = bf16[128,2048]{1,0:T(8,128)(2,1)S(1)} collective-permute-done((bf16[128,2048]{1,0:T(8,128)(2,1)S(1)}, bf16[128,2048]{1,0:T(8,128)(2,1)S(1)}, u32[]{:S(2)}, u32[]{:S(2)}) %collective-permute-start.19) | collective-permute-done | bytes 524320 | tf_op jit(solution)/shard_map/ppermute | solution.py:417
  76.2 1.6 %collective-permute-start.22 = (bf16[128,2048]{1,0:T(8,128)(2,1)S(1)}, bf16[128,2048]{1,0:T(8,128)(2,1)S(1)}, u32[]{:S(2)}, u32[]{:S(2)}) collective-permute-start(bf16[128,2048]{1,0:T(8,128)(2,1)S(1)} %add_convert_fusion), channel_id=1, source_target_pairs={{0,4},{1,3},{2,6},{3,1},{4,0},{5,7},{6,2},{7,5},{8,12},{9,11},{10,... | collective-permute-start | bytes 1572872 | tf_op jit(solution)/shard_map/ppermute | solution.py:417
  78.8 7.3 %collective-permute-done.21 = bf16[64,2048]{1,0:T(8,128)(2,1)S(1)} collective-permute-done((bf16[64,2048]{1,0:T(8,128)(2,1)S(1)}, bf16[64,2048]{1,0:T(8,128)(2,1)S(1)}, u32[]{:S(2)}, u32[]{:S(2)}) %collective-permute-start.21) | collective-permute-done | bytes 262176 | tf_op jit(solution)/shard_map/ppermute | solution.py:421
  87.8 7.9 %collective-permute-done.24.refs_3_ = bf16[64,2048]{1,0:T(8,128)(2,1)S(1)} collective-permute-done((bf16[64,2048]{1,0:T(8,128)(2,1)S(1)}, bf16[64,2048]{1,0:T(8,128)(2,1)S(1)}, u32[]{:S(2)}, u32[]{:S(2)}) %collective-permute-start.24) | collective-permute-done | bytes 262176 | tf_op jit(solution)/shard_map/ppermute | solution.py:421
  (57 shorter events, 15.2 us)
Async XLA Ops:
  0.0 12.7 %collective-permute-start.3 = (bf16[1,2048,512]{2,1,0:T(8,128)(2,1)}, bf16[1,2048,512]{2,1,0:T(8,128)(2,1)S(1)}, u32[]{:S(2)}, u32[]{:S(2)}) collective-permute-start(bf16[1,2048,512]{2,1,0:T(8,128)(2,1)} %refs_0_.1), channel_id=1, source_target_pairs={{0,1},{1,0},{2,3},{3,2},{4,5},{5,4},{6,7},{7,6},{8,9},{9,8},{10,11... | collective-permute-start | bytes 6291464 | tf_op jit(solution)/shard_map/ppermute | solution.py:404
  0.5 12.3 %collective-permute-start.4 = (bf16[1,2048,512]{2,1,0:T(8,128)(2,1)}, bf16[1,2048,512]{2,1,0:T(8,128)(2,1)}, u32[]{:S(2)}, u32[]{:S(2)}) collective-permute-start(bf16[1,2048,512]{2,1,0:T(8,128)(2,1)} %refs_1_.1), channel_id=1, source_target_pairs={{0,1},{1,0},{2,3},{3,2},{4,5},{5,4},{6,7},{7,6},{8,9},{9,8},{10,11... | collective-permute-start | bytes 6291464 | tf_op jit(solution)/shard_map/ppermute | solution.py:404
  0.5 12.2 %collective-permute-start.5 = (bf16[1,512,2048]{2,1,0:T(8,128)(2,1)}, bf16[1,512,2048]{2,1,0:T(8,128)(2,1)}, u32[]{:S(2)}, u32[]{:S(2)}) collective-permute-start(bf16[1,512,2048]{2,1,0:T(8,128)(2,1)} %refs_2_.1), channel_id=1, source_target_pairs={{0,1},{1,0},{2,3},{3,2},{4,5},{5,4},{6,7},{7,6},{8,9},{9,8},{10,11... | collective-permute-start | bytes 6291464 | tf_op jit(solution)/shard_map/ppermute | solution.py:404
  8.1 12.0 %collective-permute-start.1 = (bf16[64,2176]{1,0:T(8,128)(2,1)S(1)}, bf16[64,2176]{1,0:T(8,128)(2,1)S(1)}, u32[]{:S(2)}, u32[]{:S(2)}) collective-permute-start(bf16[64,2176]{1,0:T(8,128)(2,1)S(1)} %get-tuple-element.78.refs_0_), channel_id=1, source_target_pairs={{0,8},{2,10},{4,12},{6,14},{8,16},{10,18},{12,20},{14,22},{16,24},... | collective-permute-start | bytes 835592 | tf_op jit(solution)/shard_map/ppermute | solution.py:421
  11.1 9.0 %collective-permute-start.2 = (bf16[64,2176]{1,0:T(8,128)(2,1)S(1)}, bf16[64,2176]{1,0:T(8,128)(2,1)S(1)}, u32[]{:S(2)}, u32[]{:S(2)}) collective-permute-start(bf16[64,2176]{1,0:T(8,128)(2,1)S(1)} %get-tuple-element.78.refs_0_), channel_id=1, source_target_pairs={{0,2},{1,5},{2,0},{3,7},{4,6},{5,1},{6,4},{7,3},{8,10},{9,13},{10,... | collective-permute-start | bytes 835592 | tf_op jit(solution)/shard_map/ppermute | solution.py:417
  20.1 9.5 %collective-permute-start.6 = (bf16[64,2176]{1,0:T(8,128)(2,1)S(1)}, bf16[64,2176]{1,0:T(8,128)(2,1)S(1)}, u32[]{:S(2)}, u32[]{:S(2)}) collective-permute-start(bf16[64,2176]{1,0:T(8,128)(2,1)S(1)} %collective-permute-done.1.refs_0_), channel_id=1, source_target_pairs={{0,2},{1,5},{2,0},{3,7},{4,6},{5,1},{6,4},{7,3},{8,10},{9,13},{10,... | collective-permute-start | bytes 835592 | tf_op jit(solution)/shard_map/ppermute | solution.py:417
  21.6 9.5 %collective-permute-start.7 = (bf16[64,2176]{1,0:T(8,128)(2,1)S(1)}, bf16[64,2176]{1,0:T(8,128)(2,1)S(1)}, u32[]{:S(2)}, u32[]{:S(2)}) collective-permute-start(bf16[64,2176]{1,0:T(8,128)(2,1)S(1)} %collective-permute-done.1.refs_0_), channel_id=1, source_target_pairs={{0,8},{2,10},{4,12},{6,14},{8,16},{10,18},{12,20},{14,22},{16,24},... | collective-permute-start | bytes 835592 | tf_op jit(solution)/shard_map/ppermute | solution.py:421
  21.7 11.6 %collective-permute-start.10 = (bf16[128,2176]{1,0:T(8,128)(2,1)S(1)}, bf16[128,2176]{1,0:T(8,128)(2,1)S(1)}, u32[]{:S(2)}, u32[]{:S(2)}) collective-permute-start(bf16[128,2176]{1,0:T(8,128)(2,1)S(1)} %pad_maximum_fusion), channel_id=1, source_target_pairs={{0,4},{1,3},{2,6},{3,1},{4,0},{5,7},{6,2},{7,5},{8,12},{9,11},{10,... | collective-permute-start | bytes 1671176 | tf_op jit(solution)/shard_map/ppermute | solution.py:417
  31.1 9.6 %collective-permute-start.8 = (bf16[64,2176]{1,0:T(8,128)(2,1)S(1)}, bf16[64,2176]{1,0:T(8,128)(2,1)S(1)}, u32[]{:S(2)}, u32[]{:S(2)}) collective-permute-start(bf16[64,2176]{1,0:T(8,128)(2,1)S(1)} %collective-permute-done.7.refs_0_), channel_id=1, source_target_pairs={{0,2},{1,5},{2,0},{3,7},{4,6},{5,1},{6,4},{7,3},{8,10},{9,13},{10,... | collective-permute-start | bytes 835592 | tf_op jit(solution)/shard_map/ppermute | solution.py:417
  32.6 8.3 %collective-permute-start.9 = (bf16[64,2176]{1,0:T(8,128)(2,1)S(1)}, bf16[64,2176]{1,0:T(8,128)(2,1)S(1)}, u32[]{:S(2)}, u32[]{:S(2)}) collective-permute-start(bf16[64,2176]{1,0:T(8,128)(2,1)S(1)} %collective-permute-done.7.refs_0_), channel_id=1, source_target_pairs={{0,8},{2,10},{4,12},{6,14},{8,16},{10,18},{12,20},{14,22},{16,24},... | collective-permute-start | bytes 835592 | tf_op jit(solution)/shard_map/ppermute | solution.py:421
  32.6 12.5 %collective-permute-start.12 = (bf16[128,2176]{1,0:T(8,128)(2,1)S(1)}, bf16[128,2176]{1,0:T(8,128)(2,1)S(1)}, u32[]{:S(2)}, u32[]{:S(2)}) collective-permute-start(bf16[128,2176]{1,0:T(8,128)(2,1)S(1)} %pad_maximum_fusion.1), channel_id=1, source_target_pairs={{0,4},{1,3},{2,6},{3,1},{4,0},{5,7},{6,2},{7,5},{8,12},{9,11},{10,... | collective-permute-start | bytes 1671176 | tf_op jit(solution)/shard_map/ppermute | solution.py:417
  40.9 9.5 %collective-permute-start.11 = (bf16[64,2176]{1,0:T(8,128)(2,1)S(1)}, bf16[64,2176]{1,0:T(8,128)(2,1)S(1)}, u32[]{:S(2)}, u32[]{:S(2)}) collective-permute-start(bf16[64,2176]{1,0:T(8,128)(2,1)S(1)} %collective-permute-done.9.refs_0_), channel_id=1, source_target_pairs={{0,2},{1,5},{2,0},{3,7},{4,6},{5,1},{6,4},{7,3},{8,10},{9,13},{10,... | collective-permute-start | bytes 835592 | tf_op jit(solution)/shard_map/ppermute | solution.py:417
  42.3 11.5 %collective-permute-start.13 = (bf16[128,2176]{1,0:T(8,128)(2,1)S(1)}, bf16[128,2176]{1,0:T(8,128)(2,1)S(1)}, u32[]{:S(2)}, u32[]{:S(2)}) collective-permute-start(bf16[128,2176]{1,0:T(8,128)(2,1)S(1)} %pad_maximum_fusion.2), channel_id=1, source_target_pairs={{0,4},{1,3},{2,6},{3,1},{4,0},{5,7},{6,2},{7,5},{8,12},{9,11},{10,... | collective-permute-start | bytes 1671176 | tf_op jit(solution)/shard_map/ppermute | solution.py:417
  50.5 9.6 %collective-permute-start.14 = (bf16[128,2176]{1,0:T(8,128)(2,1)S(1)}, bf16[128,2176]{1,0:T(8,128)(2,1)S(1)}, u32[]{:S(2)}, u32[]{:S(2)}) collective-permute-start(bf16[128,2176]{1,0:T(8,128)(2,1)S(1)} %pad_maximum_fusion.3), channel_id=1, source_target_pairs={{0,4},{1,3},{2,6},{3,1},{4,0},{5,7},{6,2},{7,5},{8,12},{9,11},{10,... | collective-permute-start | bytes 1671176 | tf_op jit(solution)/shard_map/ppermute | solution.py:417
  51.6 14.3 %collective-permute-start.16 = (bf16[128,2048]{1,0:T(8,128)(2,1)S(1)}, bf16[128,2048]{1,0:T(8,128)(2,1)S(1)}, u32[]{:S(2)}, u32[]{:S(2)}) collective-permute-start(bf16[128,2048]{1,0:T(8,128)(2,1)S(1)} %get-tuple-element.121), channel_id=1, source_target_pairs={{0,24},{2,26},{4,28},{6,30},{8,0},{10,2},{12,4},{14,6},{16,8},{18,... | collective-permute-start | bytes 1572872 | tf_op jit(solution)/shard_map/ppermute | solution.py:421
  58.1 9.4 %collective-permute-start.15 = (bf16[128,2048]{1,0:T(8,128)(2,1)S(1)}, bf16[128,2048]{1,0:T(8,128)(2,1)S(1)}, u32[]{:S(2)}, u32[]{:S(2)}) collective-permute-start(bf16[128,2048]{1,0:T(8,128)(2,1)S(1)} %get-tuple-element.120), channel_id=1, source_target_pairs={{0,4},{1,3},{2,6},{3,1},{4,0},{5,7},{6,2},{7,5},{8,12},{9,11},{10,... | collective-permute-start | bytes 1572872 | tf_op jit(solution)/shard_map/ppermute | solution.py:417
  60.0 12.8 %collective-permute-start.18 = (bf16[128,2048]{1,0:T(8,128)(2,1)S(1)}, bf16[128,2048]{1,0:T(8,128)(2,1)S(1)}, u32[]{:S(2)}, u32[]{:S(2)}) collective-permute-start(bf16[128,2048]{1,0:T(8,128)(2,1)S(1)} %get-tuple-element.125), channel_id=1, source_target_pairs={{0,24},{2,26},{4,28},{6,30},{8,0},{10,2},{12,4},{14,6},{16,8},{18,... | collective-permute-start | bytes 1572872 | tf_op jit(solution)/shard_map/ppermute | solution.py:421
  64.5 11.6 %collective-permute-start.19 = (bf16[128,2048]{1,0:T(8,128)(2,1)S(1)}, bf16[128,2048]{1,0:T(8,128)(2,1)S(1)}, u32[]{:S(2)}, u32[]{:S(2)}) collective-permute-start(bf16[128,2048]{1,0:T(8,128)(2,1)S(1)} %get-tuple-element.126), channel_id=1, source_target_pairs={{0,4},{1,3},{2,6},{3,1},{4,0},{5,7},{6,2},{7,5},{8,12},{9,11},{10,... | collective-permute-start | bytes 1572872 | tf_op jit(solution)/shard_map/ppermute | solution.py:417
  67.6 6.4 %collective-permute-start.17 = (bf16[64,2048]{1,0:T(8,128)(2,1)S(1)}, bf16[64,2048]{1,0:T(8,128)(2,1)S(1)}, u32[]{:S(2)}, u32[]{:S(2)}) collective-permute-start(bf16[64,2048]{1,0:T(8,128)(2,1)S(1)} %add_convert_fusion.7), channel_id=1, source_target_pairs={{0,2},{1,5},{2,0},{3,7},{4,6},{5,1},{6,4},{7,3},{8,10},{9,13},{10,... | collective-permute-start | bytes 786440 | tf_op jit(solution)/shard_map/ppermute | solution.py:417
  76.2 11.1 %collective-permute-start.22 = (bf16[128,2048]{1,0:T(8,128)(2,1)S(1)}, bf16[128,2048]{1,0:T(8,128)(2,1)S(1)}, u32[]{:S(2)}, u32[]{:S(2)}) collective-permute-start(bf16[128,2048]{1,0:T(8,128)(2,1)S(1)} %add_convert_fusion), channel_id=1, source_target_pairs={{0,4},{1,3},{2,6},{3,1},{4,0},{5,7},{6,2},{7,5},{8,12},{9,11},{10,... | collective-permute-start | bytes 1572872 | tf_op jit(solution)/shard_map/ppermute | solution.py:417
  77.9 8.2 %collective-permute-start.21 = (bf16[64,2048]{1,0:T(8,128)(2,1)S(1)}, bf16[64,2048]{1,0:T(8,128)(2,1)S(1)}, u32[]{:S(2)}, u32[]{:S(2)}) collective-permute-start(bf16[64,2048]{1,0:T(8,128)(2,1)S(1)} %add_convert_fusion.5), channel_id=1, source_target_pairs={{0,8},{2,10},{4,12},{6,14},{8,16},{10,18},{12,20},{14,22},{16,24},... | collective-permute-start | bytes 786440 | tf_op jit(solution)/shard_map/ppermute | solution.py:421
  78.0 8.1 %collective-permute-start.20 = (bf16[64,2048]{1,0:T(8,128)(2,1)S(1)}, bf16[64,2048]{1,0:T(8,128)(2,1)S(1)}, u32[]{:S(2)}, u32[]{:S(2)}) collective-permute-start(bf16[64,2048]{1,0:T(8,128)(2,1)S(1)} %add_convert_fusion.6), channel_id=1, source_target_pairs={{0,2},{1,5},{2,0},{3,7},{4,6},{5,1},{6,4},{7,3},{8,10},{9,13},{10,... | collective-permute-start | bytes 786440 | tf_op jit(solution)/shard_map/ppermute | solution.py:417
  87.5 8.2 %collective-permute-start.24 = (bf16[64,2048]{1,0:T(8,128)(2,1)S(1)}, bf16[64,2048]{1,0:T(8,128)(2,1)S(1)}, u32[]{:S(2)}, u32[]{:S(2)}) collective-permute-start(bf16[64,2048]{1,0:T(8,128)(2,1)S(1)} %add_convert_fusion.1), channel_id=1, source_target_pairs={{0,8},{2,10},{4,12},{6,14},{8,16},{10,18},{12,20},{14,22},{16,24},... | collective-permute-start | bytes 786440 | tf_op jit(solution)/shard_map/ppermute | solution.py:421
  87.7 8.0 %collective-permute-start.23 = (bf16[64,2048]{1,0:T(8,128)(2,1)S(1)}, bf16[64,2048]{1,0:T(8,128)(2,1)S(1)}, u32[]{:S(2)}, u32[]{:S(2)}) collective-permute-start(bf16[64,2048]{1,0:T(8,128)(2,1)S(1)} %get-tuple-element.143), channel_id=1, source_target_pairs={{0,2},{1,5},{2,0},{3,7},{4,6},{5,1},{6,4},{7,3},{8,10},{9,13},{10,... | collective-permute-start | bytes 786440 | tf_op jit(solution)/shard_map/ppermute | solution.py:417
  (1 other events, 2.3 us)

commit v8 on v7

--- a/solution.py
+++ b/solution.py
@@ -437,7 +437,7 @@
 
     def run_experts(s):
         rows_in = [(b[s], 0, own_rows), (u[s], 0, own_rows), (v[s], 0, 2 * own_rows)]
-        out_rows = [2 * own_rows] * 2 if s == 1 else [own_rows, own_rows, 2 * own_rows]
+        out_rows = [2 * own_rows] * 2 if s == 1 else [own_rows] * 4
         made[s] = list(plane_experts(index, rows_in, out_rows, experts, own_held, other_held))
 
     def made_entries(s):
@@ -474,50 +474,56 @@
 
     half = max(2, (planes + 1) // 2)
     order = list(range(half, planes - 1)) + list(range(2, half)) + [planes - 1, 0]
-    back_v, back_u, back_z, sums = {}, {}, {}, {}
+    back_d, back_v, back_u, back_z, sums = {}, {}, {}, {}, {}
     for s in order[:2]:
         if s in made and s:
-            back_v[s] = over_v(made[s][2])
+            back_d[s] = over_v(made[s][3])
     token = step(token)
     wait((v, planes - 1))
     run_experts(planes - 1)
     wait(*made_entries(planes - 1))
     for s in order[:2]:
-        if s not in back_v and s:
-            back_v[s] = over_v(made[s][2])
+        if s not in back_d and s:
+            back_d[s] = over_v(made[s][3])
     token = step(token)
-    wait((back_v, order[0]), (whole, 0))
+    wait((back_d, order[0]), (whole, 0))
     for j, s in enumerate(order[:-1]):
-        own, for_u, _ = made[s]
+        own, for_u, for_v, _ = made[s]
+        follows = order[j + 1]
         if j:
             last = order[j - 1]
             onward = 2 * last >= planes
             back_z[last] = shifted(1 if onward else planes - last)(sums[last])
-        back_u[s] = over_u(add_bf16(for_u, back_v[s][own_rows:]))
-        if j + 2 < planes - 1 and order[j + 2]:
-            back_v[order[j + 2]] = over_v(made[order[j + 2]][2])
+        back_u[s] = over_u(add_bf16(for_u, back_d[s]))
+        back_v[s] = over_v(for_v)
+        if follows and order[j + 2]:
+            back_d[order[j + 2]] = over_v(made[order[j + 2]][3])
         token = step(token)
         carried = s - 1 in back_z and 2 * (s - 1) >= planes
         wait(
             (back_u, s),
+            (back_v, s),
             *([(back_z, s - 1)] if carried else []),
-            *([] if order[j + 1] else [(back_v, 0)]),
             *([] if j else [(whole, 1)]),
-            *([(back_v, order[j + 1])] if order[j + 1] else []),
+            *([(back_d, follows)] if follows else []),
         )
         if j == 0:
-            parts = [whole[0][:own_rows], whole[0][own_rows:], whole[1]]
-            made[0] = [add_bf16(a, part) for a, part in zip(made[0], parts)]
-            back_v[0] = over_v(made[0][2])
-        terms = [own, back_v[s][:own_rows], back_u[s]]
+            own_0, for_u_0, for_v_0, for_d_0 = made[0]
+            own_0 = add_bf16(own_0, whole[0][:own_rows])
+            for_u_0 = add_bf16(for_u_0, whole[0][own_rows:])
+            back_d[0] = over_v(add_bf16(for_d_0, whole[1][own_rows:]))
+            back_v[0] = over_v(add_bf16(for_v_0, whole[1][:own_rows]))
+        terms = [own, back_v[s], back_u[s]]
         if carried:
             terms.append(back_z.pop(s - 1))
         sums[s] = add_bf16(*terms)
         token = step(token)
     last = planes - 1
     back_z[last] = shifted(1)(sums[last])
-    back_u[0] = over_u(add_bf16(made[0][1], back_v[0][own_rows:]))
-    results = [made[0][0], back_v[0][:own_rows], back_u[0]]
+    token = step(token)
+    wait((back_d, 0))
+    back_u[0] = over_u(add_bf16(for_u_0, back_d[0]))
+    results = [own_0, back_v[0], back_u[0]]
     results += [back_z[s] for s in sorted(back_z)]
     return final_sum(token, residual, results)
 

time: 96.8 us -> 93.2 us (0.963)
  waiting for transfers between devices: 43.8 us -> 34.6 us
  starting transfers between devices: 23.2 us -> 28.9 us
    ppermute x7, waiting for transfers between devices: 23.7 us -> 14.9 us  [shifted(): return lambda a: lax.ppermute(a, 'wide', pairs)]
    ppermute x14 -> x17, starting transfers between devices: 16.8 us -> 21.2 us  [across(): return lambda a: lax.ppermute(a, ('wide', 'narrow'), pairs)]
    ppermute x7, starting transfers between devices: 5.32 us -> 6.66 us  [shifted(): return lambda a: lax.ppermute(a, 'wide', pairs)]
    ppermute x14 -> x17, waiting for transfers between devices: 17.9 us -> 17.5 us  [across(): return lambda a: lax.ppermute(a, ('wide', 'narrow'), pairs)]
  transfers between devices with their start and end apart: 25 -> 28, of which waited for: 16 -> 15; matrix products, arithmetic and copies ran while one was open for 1% -> 1% of each run, Pallas kernels for 29% -> 30%
where the time goes in v8:
time: 93.2 us; the launch traced here: 93 us
  waiting for transfers between devices  34.6 us (37%)
  starting transfers between devices  28.9 us (31%)
  Pallas kernels  28.4 us (30%)
    ppermute x17, starting transfers between devices, across(): return lambda a: lax.ppermute(a, ('wide', 'narrow'), pairs)  21.2 us
    ppermute x17, waiting for transfers between devices, across(): return lambda a: lax.ppermute(a, ('wide', 'narrow'), pairs)  17.5 us
    pallas_call x4, Pallas kernels, plane_experts(): pl.pallas_call(functools.partial(experts_kernel, spans, experts), out_sha...  17.4 us
    ppermute x7, waiting for transfers between devices, shifted(): return lambda a: lax.ppermute(a, 'wide', pairs)  14.9 us
    ppermute x7, starting transfers between devices, shifted(): return lambda a: lax.ppermute(a, 'wide', pairs)  6.66 us
    pallas_call x1, Pallas kernels, hold_weights(): pl.pallas_call(functools.partial(hold_kernel, count), out_shape=[jax.Shap...  5.29 us
    pallas_call x1, Pallas kernels, attention(): pl.pallas_call(functools.partial(attention_kernel, experts), out_shape=(j...  4.64 us
    ppermute x1, waiting for transfers between devices, on_device(): received = lax.ppermute(outgoing, 'narrow', swap)  2.18 us
  transfers between devices with their start and end apart: 28, of which 15 were waited for; matrix products, arithmetic and copies ran while one was open for 1% of the time, Pallas kernels for 30%

profile of v8, /device:TPU:0, one launch (start us, length us, event | category | flops | bytes accessed | tf_op | source)
XLA Modules:
  0.0 93.0 jit_solution(5986205884651628873)
XLA Ops:
  1.0 4.6 %shard_map.145 = (bf16[64,2048]{1,0:T(8,128)(2,1)S(1)}, f32[64,2048]{1,0:T(8,128)S(1)}, bf16[64,128]{1,0:T(8,128)(2,1)S(1)}, f32[1,2048]{1,0:T(1,128)S(1)}) custom-call(s32[1]{0:T(128)} %bitcast.core_ref, s32[8]{0:T(128)} %draft_len_ref.1, s32[8]{0:T(128)} %cache_len_ref.1, s32[10,64]{1,0:T(8,128)} %bitcast.6, f32[10,64]{1,0:T(8,128)} %bitcast.7, ...), custom_call_target="tpu_custom_call" | custom-call | flops 671088640 | bytes 6291456 | tf_op jit(solution)/shard_map/pallas_call | solution.py:179
  5.7 2.2 %collective-permute-done.received_ref = bf16[64,2048]{1,0:T(8,128)(2,1)S(1)} collective-permute-done((bf16[64,2048]{1,0:T(8,128)(2,1)S(1)}, bf16[64,2048]{1,0:T(8,128)(2,1)S(1)}, u32[]{:S(2)}, u32[]{:S(2)}) %collective-permute-start) | collective-permute-done | bytes 262176 | tf_op jit(solution)/shard_map/ppermute | solution.py:410
  8.1 3.0 %collective-permute-start.1 = (bf16[64,2176]{1,0:T(8,128)(2,1)S(1)}, bf16[64,2176]{1,0:T(8,128)(2,1)S(1)}, u32[]{:S(2)}, u32[]{:S(2)}) collective-permute-start(bf16[64,2176]{1,0:T(8,128)(2,1)S(1)} %get-tuple-element.87.refs_0_), channel_id=1, source_target_pairs={{0,8},{2,10},{4,12},{6,14},{8,16},{10,18},{12,20},{14,22},{16,24},... | collective-permute-start | bytes 835592 | tf_op jit(solution)/shard_map/ppermute | solution.py:421
  11.1 1.5 %collective-permute-start.2 = (bf16[64,2176]{1,0:T(8,128)(2,1)S(1)}, bf16[64,2176]{1,0:T(8,128)(2,1)S(1)}, u32[]{:S(2)}, u32[]{:S(2)}) collective-permute-start(bf16[64,2176]{1,0:T(8,128)(2,1)S(1)} %get-tuple-element.87.refs_0_), channel_id=1, source_target_pairs={{0,2},{1,5},{2,0},{3,7},{4,6},{5,1},{6,4},{7,3},{8,10},{9,13},{10,... | collective-permute-start | bytes 835592 | tf_op jit(solution)/shard_map/ppermute | solution.py:417
  12.7 5.3 %shard_map.147 = (s32[2]{0:T(128)S(1)}, bf16[1,2048,512]{2,1,0:T(8,128)(2,1)S(1)}, bf16[1,2048,512]{2,1,0:T(8,128)(2,1)S(1)}, bf16[1,512,2048]{2,1,0:T(8,128)(2,...) custom-call(s32[2]{0:T(128)S(1)} %pad_add_fusion.where_ref, ...), custom_call_target="tpu_custom_call" | custom-call | flops 200000000 | tf_op jit(solution)/shard_map/pallas_call | solution.py:307
  18.0 2.1 %collective-permute-done.1.refs_0_ = bf16[64,2176]{1,0:T(8,128)(2,1)S(1)} collective-permute-done((bf16[64,2176]{1,0:T(8,128)(2,1)S(1)}, bf16[64,2176]{1,0:T(8,128)(2,1)S(1)}, u32[]{:S(2)}, u32[]{:S(2)}) %collective-permute-start.1) | collective-permute-done | bytes 278560 | tf_op jit(solution)/shard_map/ppermute | solution.py:421
  20.1 1.5 %collective-permute-start.6 = (bf16[64,2176]{1,0:T(8,128)(2,1)S(1)}, bf16[64,2176]{1,0:T(8,128)(2,1)S(1)}, u32[]{:S(2)}, u32[]{:S(2)}) collective-permute-start(bf16[64,2176]{1,0:T(8,128)(2,1)S(1)} %collective-permute-done.1.refs_0_), channel_id=1, source_target_pairs={{0,2},{1,5},{2,0},{3,7},{4,6},{5,1},{6,4},{7,3},{8,10},{9,13},{10,... | collective-permute-start | bytes 835592 | tf_op jit(solution)/shard_map/ppermute | solution.py:417
  21.7 1.6 %collective-permute-start.10 = (bf16[128,2176]{1,0:T(8,128)(2,1)S(1)}, bf16[128,2176]{1,0:T(8,128)(2,1)S(1)}, u32[]{:S(2)}, u32[]{:S(2)}) collective-permute-start(bf16[128,2176]{1,0:T(8,128)(2,1)S(1)} %pad_maximum_fusion), channel_id=1, source_target_pairs={{0,4},{1,3},{2,6},{3,1},{4,0},{5,7},{6,2},{7,5},{8,12},{9,11},{10,... | collective-permute-start | bytes 1671176 | tf_op jit(solution)/shard_map/ppermute | solution.py:417
  23.3 6.4 %collective-permute-done.6.refs_1_ = bf16[64,2176]{1,0:T(8,128)(2,1)S(1)} collective-permute-done((bf16[64,2176]{1,0:T(8,128)(2,1)S(1)}, bf16[64,2176]{1,0:T(8,128)(2,1)S(1)}, u32[]{:S(2)}, u32[]{:S(2)}) %collective-permute-start.6) | collective-permute-done | bytes 278560 | tf_op jit(solution)/shard_map/ppermute | solution.py:417
  33.2 4.4 %shard_map.150 = (bf16[64,2048]{1,0:T(8,128)(2,1)S(1)}, bf16[64,2048]{1,0:T(8,128)(2,1)S(1)}, bf16[64,2048]{1,0:T(8,128)(2,1)S(1)}, bf16[64,2048]{1,0:T(8,128)(2,1)S(1)}) custom-call(s32[2]{0:T(128)S(1)} %get-tuple-element.99.where_ref, bf16[64,2176]{1,0:T(8,128)(2,1)S(1)} %get-tuple-element.87.refs_0_, bf16[64,2176]{1,0:T(8,128)(2,1)S(1)} %collective-permute-done.2.refs_1_, ...), custom_call_target="tpu_custom_call" | custom-call | flops 200000000 | tf_op jit(solution)/shard_map/pallas_call | solution.py:340
  37.6 3.1 %collective-permute-done.8.refs_1_ = bf16[64,2176]{1,0:T(8,128)(2,1)S(1)} collective-permute-done((bf16[64,2176]{1,0:T(8,128)(2,1)S(1)}, bf16[64,2176]{1,0:T(8,128)(2,1)S(1)}, u32[]{:S(2)}, u32[]{:S(2)}) %collective-permute-start.8) | collective-permute-done | bytes 278560 | tf_op jit(solution)/shard_map/ppermute | solution.py:417
  42.3 1.8 %collective-permute-start.13 = (bf16[128,2176]{1,0:T(8,128)(2,1)S(1)}, bf16[128,2176]{1,0:T(8,128)(2,1)S(1)}, u32[]{:S(2)}, u32[]{:S(2)}) collective-permute-start(bf16[128,2176]{1,0:T(8,128)(2,1)S(1)} %pad_maximum_fusion.2), channel_id=1, source_target_pairs={{0,4},{1,3},{2,6},{3,1},{4,0},{5,7},{6,2},{7,5},{8,12},{9,11},{10,... | collective-permute-start | bytes 1671176 | tf_op jit(solution)/shard_map/ppermute | solution.py:417
  45.1 4.4 %shard_map.152 = (bf16[128,2048]{1,0:T(8,128)(2,1)S(1)}, bf16[128,2048]{1,0:T(8,128)(2,1)S(1)}) custom-call(s32[2]{0:T(128)S(1)} %get-tuple-element.99.where_ref, bf16[64,2176]{1,0:T(8,128)(2,1)S(1)} %collective-permute-done.1.refs_0_, bf16[64,2176]{1,0:T(8,128)(2,1)S(1)} %collective-permute-done.6.refs_1_, ...), custom_call_target="tpu_custom_call" | custom-call | flops 200000000 | tf_op jit(solution)/shard_map/pallas_call | solution.py:340
  51.6 2.1 %collective-permute-start.16 = (bf16[128,2048]{1,0:T(8,128)(2,1)S(1)}, bf16[128,2048]{1,0:T(8,128)(2,1)S(1)}, u32[]{:S(2)}, u32[]{:S(2)}) collective-permute-start(bf16[128,2048]{1,0:T(8,128)(2,1)S(1)} %get-tuple-element.133), channel_id=1, source_target_pairs={{0,24},{2,26},{4,28},{6,30},{8,0},{10,2},{12,4},{14,6},{16,8},{18,... | collective-permute-start | bytes 1572872 | tf_op jit(solution)/shard_map/ppermute | solution.py:421
  53.8 4.3 %shard_map.154 = (bf16[64,2048]{1,0:T(8,128)(2,1)S(1)}, bf16[64,2048]{1,0:T(8,128)(2,1)S(1)}, bf16[64,2048]{1,0:T(8,128)(2,1)S(1)}, bf16[64,2048]{1,0:T(8,128)(2,1)S(1)}) custom-call(s32[2]{0:T(128)S(1)} %get-tuple-element.99.where_ref, bf16[64,2176]{1,0:T(8,128)(2,1)S(1)} %collective-permute-done.7.refs_0_, ...), custom_call_target="tpu_custom_call" | custom-call | flops 200000000 | tf_op jit(solution)/shard_map/pallas_call | solution.py:340
  58.1 1.9 %collective-permute-start.15 = (bf16[64,2048]{1,0:T(8,128)(2,1)S(1)}, bf16[64,2048]{1,0:T(8,128)(2,1)S(1)}, u32[]{:S(2)}, u32[]{:S(2)}) collective-permute-start(bf16[64,2048]{1,0:T(8,128)(2,1)S(1)} %get-tuple-element.132), channel_id=1, source_target_pairs={{0,4},{1,3},{2,6},{3,1},{4,0},{5,7},{6,2},{7,5},{8,12},{9,11},{10,... | collective-permute-start | bytes 786440 | tf_op jit(solution)/shard_map/ppermute | solution.py:417
  61.5 4.3 %shard_map.156 = (bf16[64,2048]{1,0:T(8,128)(2,1)S(1)}, bf16[64,2048]{1,0:T(8,128)(2,1)S(1)}, bf16[64,2048]{1,0:T(8,128)(2,1)S(1)}, bf16[64,2048]{1,0:T(8,128)(2,1)S(1)}) custom-call(s32[2]{0:T(128)S(1)} %get-tuple-element.99.where_ref, bf16[64,2176]{1,0:T(8,128)(2,1)S(1)} %collective-permute-done.9.refs_0_, ...), custom_call_target="tpu_custom_call" | custom-call | flops 200000000 | tf_op jit(solution)/shard_map/pallas_call | solution.py:340
  69.0 3.7 %collective-permute-done.19 = bf16[128,2048]{1,0:T(8,128)(2,1)S(1)} collective-permute-done((bf16[128,2048]{1,0:T(8,128)(2,1)S(1)}, bf16[128,2048]{1,0:T(8,128)(2,1)S(1)}, u32[]{:S(2)}, u32[]{:S(2)}) %collective-permute-start.19) | collective-permute-done | bytes 524320 | tf_op jit(solution)/shard_map/ppermute | solution.py:421
  72.8 2.1 %collective-permute-done.17 = bf16[64,2048]{1,0:T(8,128)(2,1)S(1)} collective-permute-done((bf16[64,2048]{1,0:T(8,128)(2,1)S(1)}, bf16[64,2048]{1,0:T(8,128)(2,1)S(1)}, u32[]{:S(2)}, u32[]{:S(2)}) %collective-permute-start.17) | collective-permute-done | bytes 262176 | tf_op jit(solution)/shard_map/ppermute | solution.py:417
  77.0 1.8 %collective-permute-start.24 = (bf16[64,2048]{1,0:T(8,128)(2,1)S(1)}, bf16[64,2048]{1,0:T(8,128)(2,1)S(1)}, u32[]{:S(2)}, u32[]{:S(2)}) collective-permute-start(bf16[64,2048]{1,0:T(8,128)(2,1)S(1)} %get-tuple-element.164), channel_id=1, source_target_pairs={{0,4},{1,3},{2,6},{3,1},{4,0},{5,7},{6,2},{7,5},{8,12},{9,11},{10,... | collective-permute-start | bytes 786440 | tf_op jit(solution)/shard_map/ppermute | solution.py:417
  79.1 4.3 %collective-permute-done.23 = bf16[64,2048]{1,0:T(8,128)(2,1)S(1)} collective-permute-done((bf16[64,2048]{1,0:T(8,128)(2,1)S(1)}, bf16[64,2048]{1,0:T(8,128)(2,1)S(1)}, u32[]{:S(2)}, u32[]{:S(2)}) %collective-permute-start.23) | collective-permute-done | bytes 262176 | tf_op jit(solution)/shard_map/ppermute | solution.py:421
  84.6 1.6 %collective-permute-start.26 = (bf16[64,2048]{1,0:T(8,128)(2,1)S(1)}, bf16[64,2048]{1,0:T(8,128)(2,1)S(1)}, u32[]{:S(2)}, u32[]{:S(2)}) collective-permute-start(bf16[64,2048]{1,0:T(8,128)(2,1)S(1)} %get-tuple-element.161), channel_id=1, source_target_pairs={{0,2},{1,5},{2,0},{3,7},{4,6},{5,1},{6,4},{7,3},{8,10},{9,13},{10,... | collective-permute-start | bytes 786440 | tf_op jit(solution)/shard_map/ppermute | solution.py:417
  86.1 2.9 %collective-permute-done.25.refs_1_ = bf16[64,2048]{1,0:T(8,128)(2,1)S(1)} collective-permute-done((bf16[64,2048]{1,0:T(8,128)(2,1)S(1)}, bf16[64,2048]{1,0:T(8,128)(2,1)S(1)}, u32[]{:S(2)}, u32[]{:S(2)}) %collective-permute-start.25) | collective-permute-done | bytes 262176 | tf_op jit(solution)/shard_map/ppermute | solution.py:417
  89.0 3.1 %collective-permute-done.27.refs_3_ = bf16[64,2048]{1,0:T(8,128)(2,1)S(1)} collective-permute-done((bf16[64,2048]{1,0:T(8,128)(2,1)S(1)}, bf16[64,2048]{1,0:T(8,128)(2,1)S(1)}, u32[]{:S(2)}, u32[]{:S(2)}) %collective-permute-start.27) | collective-permute-done | bytes 262176 | tf_op jit(solution)/shard_map/ppermute | solution.py:421
  (63 shorter events, 18.8 us)
Async XLA Ops:
  0.0 12.7 %collective-permute-start.3 = (bf16[1,2048,512]{2,1,0:T(8,128)(2,1)}, bf16[1,2048,512]{2,1,0:T(8,128)(2,1)S(1)}, u32[]{:S(2)}, u32[]{:S(2)}) collective-permute-start(bf16[1,2048,512]{2,1,0:T(8,128)(2,1)} %refs_0_.1), channel_id=1, source_target_pairs={{0,1},{1,0},{2,3},{3,2},{4,5},{5,4},{6,7},{7,6},{8,9},{9,8},{10,11... | collective-permute-start | bytes 6291464 | tf_op jit(solution)/shard_map/ppermute | solution.py:404
  0.5 12.3 %collective-permute-start.4 = (bf16[1,2048,512]{2,1,0:T(8,128)(2,1)}, bf16[1,2048,512]{2,1,0:T(8,128)(2,1)}, u32[]{:S(2)}, u32[]{:S(2)}) collective-permute-start(bf16[1,2048,512]{2,1,0:T(8,128)(2,1)} %refs_1_.1), channel_id=1, source_target_pairs={{0,1},{1,0},{2,3},{3,2},{4,5},{5,4},{6,7},{7,6},{8,9},{9,8},{10,11... | collective-permute-start | bytes 6291464 | tf_op jit(solution)/shard_map/ppermute | solution.py:404
  0.5 12.2 %collective-permute-start.5 = (bf16[1,512,2048]{2,1,0:T(8,128)(2,1)}, bf16[1,512,2048]{2,1,0:T(8,128)(2,1)}, u32[]{:S(2)}, u32[]{:S(2)}) collective-permute-start(bf16[1,512,2048]{2,1,0:T(8,128)(2,1)} %refs_2_.1), channel_id=1, source_target_pairs={{0,1},{1,0},{2,3},{3,2},{4,5},{5,4},{6,7},{7,6},{8,9},{9,8},{10,11... | collective-permute-start | bytes 6291464 | tf_op jit(solution)/shard_map/ppermute | solution.py:404
  8.1 12.0 %collective-permute-start.1 = (bf16[64,2176]{1,0:T(8,128)(2,1)S(1)}, bf16[64,2176]{1,0:T(8,128)(2,1)S(1)}, u32[]{:S(2)}, u32[]{:S(2)}) collective-permute-start(bf16[64,2176]{1,0:T(8,128)(2,1)S(1)} %get-tuple-element.87.refs_0_), channel_id=1, source_target_pairs={{0,8},{2,10},{4,12},{6,14},{8,16},{10,18},{12,20},{14,22},{16,24},... | collective-permute-start | bytes 835592 | tf_op jit(solution)/shard_map/ppermute | solution.py:421
  11.1 9.0 %collective-permute-start.2 = (bf16[64,2176]{1,0:T(8,128)(2,1)S(1)}, bf16[64,2176]{1,0:T(8,128)(2,1)S(1)}, u32[]{:S(2)}, u32[]{:S(2)}) collective-permute-start(bf16[64,2176]{1,0:T(8,128)(2,1)S(1)} %get-tuple-element.87.refs_0_), channel_id=1, source_target_pairs={{0,2},{1,5},{2,0},{3,7},{4,6},{5,1},{6,4},{7,3},{8,10},{9,13},{10,... | collective-permute-start | bytes 835592 | tf_op jit(solution)/shard_map/ppermute | solution.py:417
  20.1 9.5 %collective-permute-start.6 = (bf16[64,2176]{1,0:T(8,128)(2,1)S(1)}, bf16[64,2176]{1,0:T(8,128)(2,1)S(1)}, u32[]{:S(2)}, u32[]{:S(2)}) collective-permute-start(bf16[64,2176]{1,0:T(8,128)(2,1)S(1)} %collective-permute-done.1.refs_0_), channel_id=1, source_target_pairs={{0,2},{1,5},{2,0},{3,7},{4,6},{5,1},{6,4},{7,3},{8,10},{9,13},{10,... | collective-permute-start | bytes 835592 | tf_op jit(solution)/shard_map/ppermute | solution.py:417
  21.6 9.5 %collective-permute-start.7 = (bf16[64,2176]{1,0:T(8,128)(2,1)S(1)}, bf16[64,2176]{1,0:T(8,128)(2,1)S(1)}, u32[]{:S(2)}, u32[]{:S(2)}) collective-permute-start(bf16[64,2176]{1,0:T(8,128)(2,1)S(1)} %collective-permute-done.1.refs_0_), channel_id=1, source_target_pairs={{0,8},{2,10},{4,12},{6,14},{8,16},{10,18},{12,20},{14,22},{16,24},... | collective-permute-start | bytes 835592 | tf_op jit(solution)/shard_map/ppermute | solution.py:421
  21.7 11.6 %collective-permute-start.10 = (bf16[128,2176]{1,0:T(8,128)(2,1)S(1)}, bf16[128,2176]{1,0:T(8,128)(2,1)S(1)}, u32[]{:S(2)}, u32[]{:S(2)}) collective-permute-start(bf16[128,2176]{1,0:T(8,128)(2,1)S(1)} %pad_maximum_fusion), channel_id=1, source_target_pairs={{0,4},{1,3},{2,6},{3,1},{4,0},{5,7},{6,2},{7,5},{8,12},{9,11},{10,... | collective-permute-start | bytes 1671176 | tf_op jit(solution)/shard_map/ppermute | solution.py:417
  31.1 9.6 %collective-permute-start.8 = (bf16[64,2176]{1,0:T(8,128)(2,1)S(1)}, bf16[64,2176]{1,0:T(8,128)(2,1)S(1)}, u32[]{:S(2)}, u32[]{:S(2)}) collective-permute-start(bf16[64,2176]{1,0:T(8,128)(2,1)S(1)} %collective-permute-done.7.refs_0_), channel_id=1, source_target_pairs={{0,2},{1,5},{2,0},{3,7},{4,6},{5,1},{6,4},{7,3},{8,10},{9,13},{10,... | collective-permute-start | bytes 835592 | tf_op jit(solution)/shard_map/ppermute | solution.py:417
  32.6 8.3 %collective-permute-start.9 = (bf16[64,2176]{1,0:T(8,128)(2,1)S(1)}, bf16[64,2176]{1,0:T(8,128)(2,1)S(1)}, u32[]{:S(2)}, u32[]{:S(2)}) collective-permute-start(bf16[64,2176]{1,0:T(8,128)(2,1)S(1)} %collective-permute-done.7.refs_0_), channel_id=1, source_target_pairs={{0,8},{2,10},{4,12},{6,14},{8,16},{10,18},{12,20},{14,22},{16,24},... | collective-permute-start | bytes 835592 | tf_op jit(solution)/shard_map/ppermute | solution.py:421
  32.6 12.5 %collective-permute-start.12 = (bf16[128,2176]{1,0:T(8,128)(2,1)S(1)}, bf16[128,2176]{1,0:T(8,128)(2,1)S(1)}, u32[]{:S(2)}, u32[]{:S(2)}) collective-permute-start(bf16[128,2176]{1,0:T(8,128)(2,1)S(1)} %pad_maximum_fusion.1), channel_id=1, source_target_pairs={{0,4},{1,3},{2,6},{3,1},{4,0},{5,7},{6,2},{7,5},{8,12},{9,11},{10,... | collective-permute-start | bytes 1671176 | tf_op jit(solution)/shard_map/ppermute | solution.py:417
  40.9 9.5 %collective-permute-start.11 = (bf16[64,2176]{1,0:T(8,128)(2,1)S(1)}, bf16[64,2176]{1,0:T(8,128)(2,1)S(1)}, u32[]{:S(2)}, u32[]{:S(2)}) collective-permute-start(bf16[64,2176]{1,0:T(8,128)(2,1)S(1)} %collective-permute-done.9.refs_0_), channel_id=1, source_target_pairs={{0,2},{1,5},{2,0},{3,7},{4,6},{5,1},{6,4},{7,3},{8,10},{9,13},{10,... | collective-permute-start | bytes 835592 | tf_op jit(solution)/shard_map/ppermute | solution.py:417
  42.3 11.5 %collective-permute-start.13 = (bf16[128,2176]{1,0:T(8,128)(2,1)S(1)}, bf16[128,2176]{1,0:T(8,128)(2,1)S(1)}, u32[]{:S(2)}, u32[]{:S(2)}) collective-permute-start(bf16[128,2176]{1,0:T(8,128)(2,1)S(1)} %pad_maximum_fusion.2), channel_id=1, source_target_pairs={{0,4},{1,3},{2,6},{3,1},{4,0},{5,7},{6,2},{7,5},{8,12},{9,11},{10,... | collective-permute-start | bytes 1671176 | tf_op jit(solution)/shard_map/ppermute | solution.py:417
  50.5 10.9 %collective-permute-start.14 = (bf16[128,2176]{1,0:T(8,128)(2,1)S(1)}, bf16[128,2176]{1,0:T(8,128)(2,1)S(1)}, u32[]{:S(2)}, u32[]{:S(2)}) collective-permute-start(bf16[128,2176]{1,0:T(8,128)(2,1)S(1)} %pad_maximum_fusion.3), channel_id=1, source_target_pairs={{0,4},{1,3},{2,6},{3,1},{4,0},{5,7},{6,2},{7,5},{8,12},{9,11},{10,... | collective-permute-start | bytes 1671176 | tf_op jit(solution)/shard_map/ppermute | solution.py:417
  51.6 14.2 %collective-permute-start.16 = (bf16[128,2048]{1,0:T(8,128)(2,1)S(1)}, bf16[128,2048]{1,0:T(8,128)(2,1)S(1)}, u32[]{:S(2)}, u32[]{:S(2)}) collective-permute-start(bf16[128,2048]{1,0:T(8,128)(2,1)S(1)} %get-tuple-element.133), channel_id=1, source_target_pairs={{0,24},{2,26},{4,28},{6,30},{8,0},{10,2},{12,4},{14,6},{16,8},{18,... | collective-permute-start | bytes 1572872 | tf_op jit(solution)/shard_map/ppermute | solution.py:421
  60.0 12.8 %collective-permute-start.19 = (bf16[128,2048]{1,0:T(8,128)(2,1)S(1)}, bf16[128,2048]{1,0:T(8,128)(2,1)S(1)}, u32[]{:S(2)}, u32[]{:S(2)}) collective-permute-start(bf16[128,2048]{1,0:T(8,128)(2,1)S(1)} %get-tuple-element.138), channel_id=1, source_target_pairs={{0,24},{2,26},{4,28},{6,30},{8,0},{10,2},{12,4},{14,6},{16,8},{18,... | collective-permute-start | bytes 1572872 | tf_op jit(solution)/shard_map/ppermute | solution.py:421
  60.0 9.1 %collective-permute-start.18 = (bf16[64,2048]{1,0:T(8,128)(2,1)S(1)}, bf16[64,2048]{1,0:T(8,128)(2,1)S(1)}, u32[]{:S(2)}, u32[]{:S(2)}) collective-permute-start(bf16[64,2048]{1,0:T(8,128)(2,1)S(1)} %get-tuple-element.137), channel_id=1, source_target_pairs={{0,4},{1,3},{2,6},{3,1},{4,0},{5,7},{6,2},{7,5},{8,12},{9,11},{10,... | collective-permute-start | bytes 786440 | tf_op jit(solution)/shard_map/ppermute | solution.py:417
  65.9 9.0 %collective-permute-start.17 = (bf16[64,2048]{1,0:T(8,128)(2,1)S(1)}, bf16[64,2048]{1,0:T(8,128)(2,1)S(1)}, u32[]{:S(2)}, u32[]{:S(2)}) collective-permute-start(bf16[64,2048]{1,0:T(8,128)(2,1)S(1)} %add_convert_fusion.8), channel_id=1, source_target_pairs={{0,2},{1,5},{2,0},{3,7},{4,6},{5,1},{6,4},{7,3},{8,10},{9,13},{10,... | collective-permute-start | bytes 786440 | tf_op jit(solution)/shard_map/ppermute | solution.py:417
  66.5 8.4 %collective-permute-start.20 = (bf16[64,2048]{1,0:T(8,128)(2,1)S(1)}, bf16[64,2048]{1,0:T(8,128)(2,1)S(1)}, u32[]{:S(2)}, u32[]{:S(2)}) collective-permute-start(bf16[64,2048]{1,0:T(8,128)(2,1)S(1)} %get-tuple-element.139), channel_id=1, source_target_pairs={{0,4},{1,3},{2,6},{3,1},{4,0},{5,7},{6,2},{7,5},{8,12},{9,11},{10,... | collective-permute-start | bytes 786440 | tf_op jit(solution)/shard_map/ppermute | solution.py:417
  67.7 11.4 %collective-permute-start.22 = (bf16[64,2048]{1,0:T(8,128)(2,1)S(1)}, bf16[64,2048]{1,0:T(8,128)(2,1)S(1)}, u32[]{:S(2)}, u32[]{:S(2)}) collective-permute-start(bf16[64,2048]{1,0:T(8,128)(2,1)S(1)} %get-tuple-element.143), channel_id=1, source_target_pairs={{0,4},{1,3},{2,6},{3,1},{4,0},{5,7},{6,2},{7,5},{8,12},{9,11},{10,... | collective-permute-start | bytes 786440 | tf_op jit(solution)/shard_map/ppermute | solution.py:417
  75.0 8.4 %collective-permute-start.23 = (bf16[64,2048]{1,0:T(8,128)(2,1)S(1)}, bf16[64,2048]{1,0:T(8,128)(2,1)S(1)}, u32[]{:S(2)}, u32[]{:S(2)}) collective-permute-start(bf16[64,2048]{1,0:T(8,128)(2,1)S(1)} %add_convert_fusion.6), channel_id=1, source_target_pairs={{0,8},{2,10},{4,12},{6,14},{8,16},{10,18},{12,20},{14,22},{16,24},... | collective-permute-start | bytes 786440 | tf_op jit(solution)/shard_map/ppermute | solution.py:421
  76.0 7.7 %collective-permute-start.21 = (bf16[64,2048]{1,0:T(8,128)(2,1)S(1)}, bf16[64,2048]{1,0:T(8,128)(2,1)S(1)}, u32[]{:S(2)}, u32[]{:S(2)}) collective-permute-start(bf16[64,2048]{1,0:T(8,128)(2,1)S(1)} %add_convert_fusion.7), channel_id=1, source_target_pairs={{0,2},{1,5},{2,0},{3,7},{4,6},{5,1},{6,4},{7,3},{8,10},{9,13},{10,... | collective-permute-start | bytes 786440 | tf_op jit(solution)/shard_map/ppermute | solution.py:417
  78.8 10.2 %collective-permute-start.25 = (bf16[64,2048]{1,0:T(8,128)(2,1)S(1)}, bf16[64,2048]{1,0:T(8,128)(2,1)S(1)}, u32[]{:S(2)}, u32[]{:S(2)}) collective-permute-start(bf16[64,2048]{1,0:T(8,128)(2,1)S(1)} %get-tuple-element.163), channel_id=1, source_target_pairs={{0,4},{1,3},{2,6},{3,1},{4,0},{5,7},{6,2},{7,5},{8,12},{9,11},{10,... | collective-permute-start | bytes 786440 | tf_op jit(solution)/shard_map/ppermute | solution.py:417
  83.9 8.2 %collective-permute-start.27 = (bf16[64,2048]{1,0:T(8,128)(2,1)S(1)}, bf16[64,2048]{1,0:T(8,128)(2,1)S(1)}, u32[]{:S(2)}, u32[]{:S(2)}) collective-permute-start(bf16[64,2048]{1,0:T(8,128)(2,1)S(1)} %add_convert_fusion), channel_id=1, source_target_pairs={{0,8},{2,10},{4,12},{6,14},{8,16},{10,18},{12,20},{14,22},{16,24},... | collective-permute-start | bytes 786440 | tf_op jit(solution)/shard_map/ppermute | solution.py:421
  (4 other events, 25.0 us)

commit v9 on v8

--- a/solution.py
+++ b/solution.py
@@ -253,9 +253,8 @@
     pieces = len(spans)
     rows_in = refs[:pieces]
     gates, ups, downs = (refs[pieces + 2 * i : pieces + 2 + 2 * i] for i in range(3))
-    outs = refs[pieces + 6 : -2]
-    rows, total = refs[-2:]
-    width = total.shape[1]
+    outs, rows = refs[pieces + 6 : -1], refs[-1]
+    width = outs[0].shape[1]
     at = 0
     for ref, (start, size) in zip(rows_in, spans):
         rows[at : at + size] = ref[start : start + size]
@@ -263,27 +262,23 @@
     table = rows[:, width:].astype(F32)
     column = lax.broadcasted_iota(jnp.int32, table.shape, 1)
     block = rows[:, :width]
-    hidden = gates[0].shape[2]
-    tile = min(256, hidden)
+    acts = []
     for e in range(2):
         index = where_ref[e]
         chosen = (column == index) | (column == index + experts)
         weight = jnp.sum(jnp.where(chosen, table, 0.0), axis=1, keepdims=True)
-        for c in range(0, hidden, tile):
-            span = slice(c, c + tile)
-            gate = _dot(block, gates[e][0, :, span])
-            up = _dot(block, ups[e][0, :, span])
-            act = (jax.nn.silu(gate) * up * weight).astype(BF16)
-            added = _dot(act, downs[e][0, span, :])
-            if e == 0 and c == 0:
-                total[...] = added
-            else:
-                total[...] += added
-    at = 0
-    for out in outs:
-        size = out.shape[0]
-        out[...] = total[at : at + size].astype(BF16)
-        at += size
+        gate = _dot(block, gates[e][0])
+        up = _dot(block, ups[e][0])
+        acts.append((jax.nn.silu(gate) * up * weight).astype(BF16))
+    tile = min(512, width)
+    for c in range(0, width, tile):
+        cols = slice(c, c + tile)
+        made = _dot(acts[0], downs[0][0, :, cols]) + _dot(acts[1], downs[1][0, :, cols])
+        at = 0
+        for out in outs:
+            size = out.shape[0]
+            out[:, cols] = made[at : at + size].astype(BF16)
+            at += size
 
 
 def hold_kernel(count, where_ref, *refs):
@@ -342,7 +337,7 @@
         out_shape=tuple(jax.ShapeDtypeStruct((size, width), BF16) for size in out_rows),
         in_specs=[pl.BlockSpec(memory_space=pltpu.SMEM)] + [vmem] * (len(spans) + 6),
         out_specs=[vmem] * len(out_rows),
-        scratch_shapes=[pltpu.VMEM((count, padded), BF16), pltpu.VMEM((count, width), F32)],
+        scratch_shapes=[pltpu.VMEM((count, padded), BF16)],
         compiler_params=pltpu.CompilerParams(vmem_limit_bytes=24 * 1024 * 1024),
         cost_estimate=pl.CostEstimate(flops=STEP_FLOPS, bytes_accessed=0, transcendentals=0),
     )(where, *arrays, *weights)

time: 93.2 us -> 93 us (level)
  waiting for transfers between devices: 34.6 us -> 35.8 us
    ppermute x7, waiting for transfers between devices: 14.9 us -> 15.8 us  [shifted(): return lambda a: lax.ppermute(a, 'wide', pairs)]
    pallas_call x4, Pallas kernels: 17.4 us -> 16.5 us  [plane_experts(): pl.pallas_call(functools.partial(experts_kernel, spans, experts), out_sha...]
  transfers between devices with their start and end apart: 28 -> 28, of which waited for: 15 -> 15; matrix products, arithmetic and copies ran while one was open for 1% -> 1% of each run, Pallas kernels for 30% -> 29%
where the time goes in v9:
time: 93 us; the launch traced here: 92.8 us
  waiting for transfers between devices  35.8 us (38%)
  starting transfers between devices  28.5 us (31%)
  Pallas kernels  27.5 us (30%)
    ppermute x17, starting transfers between devices, across(): return lambda a: lax.ppermute(a, ('wide', 'narrow'), pairs)  20.9 us
    ppermute x17, waiting for transfers between devices, across(): return lambda a: lax.ppermute(a, ('wide', 'narrow'), pairs)  17.8 us
    pallas_call x4, Pallas kernels, plane_experts(): pl.pallas_call(functools.partial(experts_kernel, spans, experts), out_sha...  16.5 us
    ppermute x7, waiting for transfers between devices, shifted(): return lambda a: lax.ppermute(a, 'wide', pairs)  15.8 us
    ppermute x7, starting transfers between devices, shifted(): return lambda a: lax.ppermute(a, 'wide', pairs)  6.49 us
    pallas_call x1, Pallas kernels, hold_weights(): pl.pallas_call(functools.partial(hold_kernel, count), out_shape=[jax.Shap...  5.29 us
    pallas_call x1, Pallas kernels, attention(): pl.pallas_call(functools.partial(attention_kernel, experts), out_shape=(j...  4.64 us
    ppermute x1, waiting for transfers between devices, on_device(): received = lax.ppermute(outgoing, 'narrow', swap)  2.18 us
  transfers between devices with their start and end apart: 28, of which 15 were waited for; matrix products, arithmetic and copies ran while one was open for 1% of the time, Pallas kernels for 29%

profile of v9, /device:TPU:0, one launch (start us, length us, event | category | flops | bytes accessed | tf_op | source)
XLA Modules:
  0.0 92.8 jit_solution(13423381755767921927)
XLA Ops:
  1.0 4.6 %shard_map.145 = (bf16[64,2048]{1,0:T(8,128)(2,1)S(1)}, f32[64,2048]{1,0:T(8,128)S(1)}, bf16[64,128]{1,0:T(8,128)(2,1)S(1)}, f32[1,2048]{1,0:T(1,128)S(1)}) custom-call(s32[1]{0:T(128)} %bitcast.core_ref, s32[8]{0:T(128)} %draft_len_ref.1, s32[8]{0:T(128)} %cache_len_ref.1, s32[10,64]{1,0:T(8,128)} %bitcast.6, f32[10,64]{1,0:T(8,128)} %bitcast.7, ...), custom_call_target="tpu_custom_call" | custom-call | flops 671088640 | bytes 6291456 | tf_op jit(solution)/shard_map/pallas_call | solution.py:179
  5.7 2.2 %collective-permute-done.received_ref = bf16[64,2048]{1,0:T(8,128)(2,1)S(1)} collective-permute-done((bf16[64,2048]{1,0:T(8,128)(2,1)S(1)}, bf16[64,2048]{1,0:T(8,128)(2,1)S(1)}, u32[]{:S(2)}, u32[]{:S(2)}) %collective-permute-start) | collective-permute-done | bytes 262176 | tf_op jit(solution)/shard_map/ppermute | solution.py:405
  8.1 3.0 %collective-permute-start.1 = (bf16[64,2176]{1,0:T(8,128)(2,1)S(1)}, bf16[64,2176]{1,0:T(8,128)(2,1)S(1)}, u32[]{:S(2)}, u32[]{:S(2)}) collective-permute-start(bf16[64,2176]{1,0:T(8,128)(2,1)S(1)} %get-tuple-element.87.refs_0_), channel_id=1, source_target_pairs={{0,8},{2,10},{4,12},{6,14},{8,16},{10,18},{12,20},{14,22},{16,24},... | collective-permute-start | bytes 835592 | tf_op jit(solution)/shard_map/ppermute | solution.py:416
  12.7 5.3 %shard_map.147 = (s32[2]{0:T(128)S(1)}, bf16[1,2048,512]{2,1,0:T(8,128)(2,1)S(1)}, bf16[1,2048,512]{2,1,0:T(8,128)(2,1)S(1)}, bf16[1,512,2048]{2,1,0:T(8,128)(2,...) custom-call(s32[2]{0:T(128)S(1)} %pad_add_fusion.where_ref, ...), custom_call_target="tpu_custom_call" | custom-call | flops 200000000 | tf_op jit(solution)/shard_map/pallas_call | solution.py:302
  18.0 2.1 %collective-permute-done.1.refs_0_ = bf16[64,2176]{1,0:T(8,128)(2,1)S(1)} collective-permute-done((bf16[64,2176]{1,0:T(8,128)(2,1)S(1)}, bf16[64,2176]{1,0:T(8,128)(2,1)S(1)}, u32[]{:S(2)}, u32[]{:S(2)}) %collective-permute-start.1) | collective-permute-done | bytes 278560 | tf_op jit(solution)/shard_map/ppermute | solution.py:416
  20.1 1.5 %collective-permute-start.6 = (bf16[64,2176]{1,0:T(8,128)(2,1)S(1)}, bf16[64,2176]{1,0:T(8,128)(2,1)S(1)}, u32[]{:S(2)}, u32[]{:S(2)}) collective-permute-start(bf16[64,2176]{1,0:T(8,128)(2,1)S(1)} %collective-permute-done.1.refs_0_), channel_id=1, source_target_pairs={{0,2},{1,5},{2,0},{3,7},{4,6},{5,1},{6,4},{7,3},{8,10},{9,13},{10,... | collective-permute-start | bytes 835592 | tf_op jit(solution)/shard_map/ppermute | solution.py:412
  21.7 1.6 %collective-permute-start.10 = (bf16[128,2176]{1,0:T(8,128)(2,1)S(1)}, bf16[128,2176]{1,0:T(8,128)(2,1)S(1)}, u32[]{:S(2)}, u32[]{:S(2)}) collective-permute-start(bf16[128,2176]{1,0:T(8,128)(2,1)S(1)} %pad_maximum_fusion), channel_id=1, source_target_pairs={{0,4},{1,3},{2,6},{3,1},{4,0},{5,7},{6,2},{7,5},{8,12},{9,11},{10,... | collective-permute-start | bytes 1671176 | tf_op jit(solution)/shard_map/ppermute | solution.py:412
  23.3 6.4 %collective-permute-done.6.refs_1_ = bf16[64,2176]{1,0:T(8,128)(2,1)S(1)} collective-permute-done((bf16[64,2176]{1,0:T(8,128)(2,1)S(1)}, bf16[64,2176]{1,0:T(8,128)(2,1)S(1)}, u32[]{:S(2)}, u32[]{:S(2)}) %collective-permute-start.6) | collective-permute-done | bytes 278560 | tf_op jit(solution)/shard_map/ppermute | solution.py:412
  31.1 1.5 %collective-permute-start.8 = (bf16[64,2176]{1,0:T(8,128)(2,1)S(1)}, bf16[64,2176]{1,0:T(8,128)(2,1)S(1)}, u32[]{:S(2)}, u32[]{:S(2)}) collective-permute-start(bf16[64,2176]{1,0:T(8,128)(2,1)S(1)} %collective-permute-done.7.refs_0_), channel_id=1, source_target_pairs={{0,2},{1,5},{2,0},{3,7},{4,6},{5,1},{6,4},{7,3},{8,10},{9,13},{10,... | collective-permute-start | bytes 835592 | tf_op jit(solution)/shard_map/ppermute | solution.py:412
  33.2 4.1 %shard_map.150 = (bf16[64,2048]{1,0:T(8,128)(2,1)S(1)}, bf16[64,2048]{1,0:T(8,128)(2,1)S(1)}, bf16[64,2048]{1,0:T(8,128)(2,1)S(1)}, bf16[64,2048]{1,0:T(8,128)(2,1)S(1)}) custom-call(s32[2]{0:T(128)S(1)} %get-tuple-element.99.where_ref, bf16[64,2176]{1,0:T(8,128)(2,1)S(1)} %get-tuple-element.87.refs_0_, bf16[64,2176]{1,0:T(8,128)(2,1)S(1)} %collective-permute-done.2.refs_1_, ...), custom_call_target="tpu_custom_call" | custom-call | flops 200000000 | tf_op jit(solution)/shard_map/pallas_call | solution.py:335
  37.3 3.4 %collective-permute-done.8.refs_1_ = bf16[64,2176]{1,0:T(8,128)(2,1)S(1)} collective-permute-done((bf16[64,2176]{1,0:T(8,128)(2,1)S(1)}, bf16[64,2176]{1,0:T(8,128)(2,1)S(1)}, u32[]{:S(2)}, u32[]{:S(2)}) %collective-permute-start.8) | collective-permute-done | bytes 278560 | tf_op jit(solution)/shard_map/ppermute | solution.py:412
  42.3 1.8 %collective-permute-start.13 = (bf16[128,2176]{1,0:T(8,128)(2,1)S(1)}, bf16[128,2176]{1,0:T(8,128)(2,1)S(1)}, u32[]{:S(2)}, u32[]{:S(2)}) collective-permute-start(bf16[128,2176]{1,0:T(8,128)(2,1)S(1)} %pad_maximum_fusion.2), channel_id=1, source_target_pairs={{0,4},{1,3},{2,6},{3,1},{4,0},{5,7},{6,2},{7,5},{8,12},{9,11},{10,... | collective-permute-start | bytes 1671176 | tf_op jit(solution)/shard_map/ppermute | solution.py:412
  45.2 4.1 %shard_map.152 = (bf16[128,2048]{1,0:T(8,128)(2,1)S(1)}, bf16[128,2048]{1,0:T(8,128)(2,1)S(1)}) custom-call(s32[2]{0:T(128)S(1)} %get-tuple-element.99.where_ref, bf16[64,2176]{1,0:T(8,128)(2,1)S(1)} %collective-permute-done.1.refs_0_, bf16[64,2176]{1,0:T(8,128)(2,1)S(1)} %collective-permute-done.6.refs_1_, ...), custom_call_target="tpu_custom_call" | custom-call | flops 200000000 | tf_op jit(solution)/shard_map/pallas_call | solution.py:335
  51.6 1.9 %collective-permute-start.16 = (bf16[128,2048]{1,0:T(8,128)(2,1)S(1)}, bf16[128,2048]{1,0:T(8,128)(2,1)S(1)}, u32[]{:S(2)}, u32[]{:S(2)}) collective-permute-start(bf16[128,2048]{1,0:T(8,128)(2,1)S(1)} %get-tuple-element.133), channel_id=1, source_target_pairs={{0,24},{2,26},{4,28},{6,30},{8,0},{10,2},{12,4},{14,6},{16,8},{18,... | collective-permute-start | bytes 1572872 | tf_op jit(solution)/shard_map/ppermute | solution.py:416
  53.5 4.1 %shard_map.154 = (bf16[64,2048]{1,0:T(8,128)(2,1)S(1)}, bf16[64,2048]{1,0:T(8,128)(2,1)S(1)}, bf16[64,2048]{1,0:T(8,128)(2,1)S(1)}, bf16[64,2048]{1,0:T(8,128)(2,1)S(1)}) custom-call(s32[2]{0:T(128)S(1)} %get-tuple-element.99.where_ref, bf16[64,2176]{1,0:T(8,128)(2,1)S(1)} %collective-permute-done.7.refs_0_, ...), custom_call_target="tpu_custom_call" | custom-call | flops 200000000 | tf_op jit(solution)/shard_map/pallas_call | solution.py:335
  57.7 1.8 %collective-permute-start.15 = (bf16[64,2048]{1,0:T(8,128)(2,1)S(1)}, bf16[64,2048]{1,0:T(8,128)(2,1)S(1)}, u32[]{:S(2)}, u32[]{:S(2)}) collective-permute-start(bf16[64,2048]{1,0:T(8,128)(2,1)S(1)} %get-tuple-element.132), channel_id=1, source_target_pairs={{0,4},{1,3},{2,6},{3,1},{4,0},{5,7},{6,2},{7,5},{8,12},{9,11},{10,... | collective-permute-start | bytes 786440 | tf_op jit(solution)/shard_map/ppermute | solution.py:412
  59.7 1.5 %collective-permute-start.18 = (bf16[64,2048]{1,0:T(8,128)(2,1)S(1)}, bf16[64,2048]{1,0:T(8,128)(2,1)S(1)}, u32[]{:S(2)}, u32[]{:S(2)}) collective-permute-start(bf16[64,2048]{1,0:T(8,128)(2,1)S(1)} %get-tuple-element.137), channel_id=1, source_target_pairs={{0,4},{1,3},{2,6},{3,1},{4,0},{5,7},{6,2},{7,5},{8,12},{9,11},{10,... | collective-permute-start | bytes 786440 | tf_op jit(solution)/shard_map/ppermute | solution.py:412
  61.2 4.1 %shard_map.156 = (bf16[64,2048]{1,0:T(8,128)(2,1)S(1)}, bf16[64,2048]{1,0:T(8,128)(2,1)S(1)}, bf16[64,2048]{1,0:T(8,128)(2,1)S(1)}, bf16[64,2048]{1,0:T(8,128)(2,1)S(1)}) custom-call(s32[2]{0:T(128)S(1)} %get-tuple-element.99.where_ref, bf16[64,2176]{1,0:T(8,128)(2,1)S(1)} %collective-permute-done.9.refs_0_, ...), custom_call_target="tpu_custom_call" | custom-call | flops 200000000 | tf_op jit(solution)/shard_map/pallas_call | solution.py:335
  68.5 4.0 %collective-permute-done.19 = bf16[128,2048]{1,0:T(8,128)(2,1)S(1)} collective-permute-done((bf16[128,2048]{1,0:T(8,128)(2,1)S(1)}, bf16[128,2048]{1,0:T(8,128)(2,1)S(1)}, u32[]{:S(2)}, u32[]{:S(2)}) %collective-permute-start.19) | collective-permute-done | bytes 524320 | tf_op jit(solution)/shard_map/ppermute | solution.py:416
  72.5 1.9 %collective-permute-done.17 = bf16[64,2048]{1,0:T(8,128)(2,1)S(1)} collective-permute-done((bf16[64,2048]{1,0:T(8,128)(2,1)S(1)}, bf16[64,2048]{1,0:T(8,128)(2,1)S(1)}, u32[]{:S(2)}, u32[]{:S(2)}) %collective-permute-start.17) | collective-permute-done | bytes 262176 | tf_op jit(solution)/shard_map/ppermute | solution.py:412
  76.3 1.8 %collective-permute-start.24 = (bf16[64,2048]{1,0:T(8,128)(2,1)S(1)}, bf16[64,2048]{1,0:T(8,128)(2,1)S(1)}, u32[]{:S(2)}, u32[]{:S(2)}) collective-permute-start(bf16[64,2048]{1,0:T(8,128)(2,1)S(1)} %get-tuple-element.164), channel_id=1, source_target_pairs={{0,4},{1,3},{2,6},{3,1},{4,0},{5,7},{6,2},{7,5},{8,12},{9,11},{10,... | collective-permute-start | bytes 786440 | tf_op jit(solution)/shard_map/ppermute | solution.py:412
  78.4 4.5 %collective-permute-done.23 = bf16[64,2048]{1,0:T(8,128)(2,1)S(1)} collective-permute-done((bf16[64,2048]{1,0:T(8,128)(2,1)S(1)}, bf16[64,2048]{1,0:T(8,128)(2,1)S(1)}, u32[]{:S(2)}, u32[]{:S(2)}) %collective-permute-start.23) | collective-permute-done | bytes 262176 | tf_op jit(solution)/shard_map/ppermute | solution.py:416
  85.7 2.7 %collective-permute-done.25.refs_1_ = bf16[64,2048]{1,0:T(8,128)(2,1)S(1)} collective-permute-done((bf16[64,2048]{1,0:T(8,128)(2,1)S(1)}, bf16[64,2048]{1,0:T(8,128)(2,1)S(1)}, u32[]{:S(2)}, u32[]{:S(2)}) %collective-permute-start.25) | collective-permute-done | bytes 262176 | tf_op jit(solution)/shard_map/ppermute | solution.py:412
  88.4 3.6 %collective-permute-done.27.refs_3_ = bf16[64,2048]{1,0:T(8,128)(2,1)S(1)} collective-permute-done((bf16[64,2048]{1,0:T(8,128)(2,1)S(1)}, bf16[64,2048]{1,0:T(8,128)(2,1)S(1)}, u32[]{:S(2)}, u32[]{:S(2)}) %collective-permute-start.27) | collective-permute-done | bytes 262176 | tf_op jit(solution)/shard_map/ppermute | solution.py:416
  (63 shorter events, 19.0 us)
Async XLA Ops:
  0.0 12.7 %collective-permute-start.3 = (bf16[1,2048,512]{2,1,0:T(8,128)(2,1)}, bf16[1,2048,512]{2,1,0:T(8,128)(2,1)S(1)}, u32[]{:S(2)}, u32[]{:S(2)}) collective-permute-start(bf16[1,2048,512]{2,1,0:T(8,128)(2,1)} %refs_0_.1), channel_id=1, source_target_pairs={{0,1},{1,0},{2,3},{3,2},{4,5},{5,4},{6,7},{7,6},{8,9},{9,8},{10,11... | collective-permute-start | bytes 6291464 | tf_op jit(solution)/shard_map/ppermute | solution.py:399
  0.5 12.3 %collective-permute-start.4 = (bf16[1,2048,512]{2,1,0:T(8,128)(2,1)}, bf16[1,2048,512]{2,1,0:T(8,128)(2,1)}, u32[]{:S(2)}, u32[]{:S(2)}) collective-permute-start(bf16[1,2048,512]{2,1,0:T(8,128)(2,1)} %refs_1_.1), channel_id=1, source_target_pairs={{0,1},{1,0},{2,3},{3,2},{4,5},{5,4},{6,7},{7,6},{8,9},{9,8},{10,11... | collective-permute-start | bytes 6291464 | tf_op jit(solution)/shard_map/ppermute | solution.py:399
  0.5 12.2 %collective-permute-start.5 = (bf16[1,512,2048]{2,1,0:T(8,128)(2,1)}, bf16[1,512,2048]{2,1,0:T(8,128)(2,1)}, u32[]{:S(2)}, u32[]{:S(2)}) collective-permute-start(bf16[1,512,2048]{2,1,0:T(8,128)(2,1)} %refs_2_.1), channel_id=1, source_target_pairs={{0,1},{1,0},{2,3},{3,2},{4,5},{5,4},{6,7},{7,6},{8,9},{9,8},{10,11... | collective-permute-start | bytes 6291464 | tf_op jit(solution)/shard_map/ppermute | solution.py:399
  8.1 12.0 %collective-permute-start.1 = (bf16[64,2176]{1,0:T(8,128)(2,1)S(1)}, bf16[64,2176]{1,0:T(8,128)(2,1)S(1)}, u32[]{:S(2)}, u32[]{:S(2)}) collective-permute-start(bf16[64,2176]{1,0:T(8,128)(2,1)S(1)} %get-tuple-element.87.refs_0_), channel_id=1, source_target_pairs={{0,8},{2,10},{4,12},{6,14},{8,16},{10,18},{12,20},{14,22},{16,24},... | collective-permute-start | bytes 835592 | tf_op jit(solution)/shard_map/ppermute | solution.py:416
  11.1 9.0 %collective-permute-start.2 = (bf16[64,2176]{1,0:T(8,128)(2,1)S(1)}, bf16[64,2176]{1,0:T(8,128)(2,1)S(1)}, u32[]{:S(2)}, u32[]{:S(2)}) collective-permute-start(bf16[64,2176]{1,0:T(8,128)(2,1)S(1)} %get-tuple-element.87.refs_0_), channel_id=1, source_target_pairs={{0,2},{1,5},{2,0},{3,7},{4,6},{5,1},{6,4},{7,3},{8,10},{9,13},{10,... | collective-permute-start | bytes 835592 | tf_op jit(solution)/shard_map/ppermute | solution.py:412
  20.1 9.5 %collective-permute-start.6 = (bf16[64,2176]{1,0:T(8,128)(2,1)S(1)}, bf16[64,2176]{1,0:T(8,128)(2,1)S(1)}, u32[]{:S(2)}, u32[]{:S(2)}) collective-permute-start(bf16[64,2176]{1,0:T(8,128)(2,1)S(1)} %collective-permute-done.1.refs_0_), channel_id=1, source_target_pairs={{0,2},{1,5},{2,0},{3,7},{4,6},{5,1},{6,4},{7,3},{8,10},{9,13},{10,... | collective-permute-start | bytes 835592 | tf_op jit(solution)/shard_map/ppermute | solution.py:412
  21.6 9.5 %collective-permute-start.7 = (bf16[64,2176]{1,0:T(8,128)(2,1)S(1)}, bf16[64,2176]{1,0:T(8,128)(2,1)S(1)}, u32[]{:S(2)}, u32[]{:S(2)}) collective-permute-start(bf16[64,2176]{1,0:T(8,128)(2,1)S(1)} %collective-permute-done.1.refs_0_), channel_id=1, source_target_pairs={{0,8},{2,10},{4,12},{6,14},{8,16},{10,18},{12,20},{14,22},{16,24},... | collective-permute-start | bytes 835592 | tf_op jit(solution)/shard_map/ppermute | solution.py:416
  21.7 11.6 %collective-permute-start.10 = (bf16[128,2176]{1,0:T(8,128)(2,1)S(1)}, bf16[128,2176]{1,0:T(8,128)(2,1)S(1)}, u32[]{:S(2)}, u32[]{:S(2)}) collective-permute-start(bf16[128,2176]{1,0:T(8,128)(2,1)S(1)} %pad_maximum_fusion), channel_id=1, source_target_pairs={{0,4},{1,3},{2,6},{3,1},{4,0},{5,7},{6,2},{7,5},{8,12},{9,11},{10,... | collective-permute-start | bytes 1671176 | tf_op jit(solution)/shard_map/ppermute | solution.py:412
  31.1 9.6 %collective-permute-start.8 = (bf16[64,2176]{1,0:T(8,128)(2,1)S(1)}, bf16[64,2176]{1,0:T(8,128)(2,1)S(1)}, u32[]{:S(2)}, u32[]{:S(2)}) collective-permute-start(bf16[64,2176]{1,0:T(8,128)(2,1)S(1)} %collective-permute-done.7.refs_0_), channel_id=1, source_target_pairs={{0,2},{1,5},{2,0},{3,7},{4,6},{5,1},{6,4},{7,3},{8,10},{9,13},{10,... | collective-permute-start | bytes 835592 | tf_op jit(solution)/shard_map/ppermute | solution.py:412
  32.6 8.3 %collective-permute-start.9 = (bf16[64,2176]{1,0:T(8,128)(2,1)S(1)}, bf16[64,2176]{1,0:T(8,128)(2,1)S(1)}, u32[]{:S(2)}, u32[]{:S(2)}) collective-permute-start(bf16[64,2176]{1,0:T(8,128)(2,1)S(1)} %collective-permute-done.7.refs_0_), channel_id=1, source_target_pairs={{0,8},{2,10},{4,12},{6,14},{8,16},{10,18},{12,20},{14,22},{16,24},... | collective-permute-start | bytes 835592 | tf_op jit(solution)/shard_map/ppermute | solution.py:416
  32.6 12.6 %collective-permute-start.12 = (bf16[128,2176]{1,0:T(8,128)(2,1)S(1)}, bf16[128,2176]{1,0:T(8,128)(2,1)S(1)}, u32[]{:S(2)}, u32[]{:S(2)}) collective-permute-start(bf16[128,2176]{1,0:T(8,128)(2,1)S(1)} %pad_maximum_fusion.1), channel_id=1, source_target_pairs={{0,4},{1,3},{2,6},{3,1},{4,0},{5,7},{6,2},{7,5},{8,12},{9,11},{10,... | collective-permute-start | bytes 1671176 | tf_op jit(solution)/shard_map/ppermute | solution.py:412
  40.9 9.5 %collective-permute-start.11 = (bf16[64,2176]{1,0:T(8,128)(2,1)S(1)}, bf16[64,2176]{1,0:T(8,128)(2,1)S(1)}, u32[]{:S(2)}, u32[]{:S(2)}) collective-permute-start(bf16[64,2176]{1,0:T(8,128)(2,1)S(1)} %collective-permute-done.9.refs_0_), channel_id=1, source_target_pairs={{0,2},{1,5},{2,0},{3,7},{4,6},{5,1},{6,4},{7,3},{8,10},{9,13},{10,... | collective-permute-start | bytes 835592 | tf_op jit(solution)/shard_map/ppermute | solution.py:412
  42.3 11.3 %collective-permute-start.13 = (bf16[128,2176]{1,0:T(8,128)(2,1)S(1)}, bf16[128,2176]{1,0:T(8,128)(2,1)S(1)}, u32[]{:S(2)}, u32[]{:S(2)}) collective-permute-start(bf16[128,2176]{1,0:T(8,128)(2,1)S(1)} %pad_maximum_fusion.2), channel_id=1, source_target_pairs={{0,4},{1,3},{2,6},{3,1},{4,0},{5,7},{6,2},{7,5},{8,12},{9,11},{10,... | collective-permute-start | bytes 1671176 | tf_op jit(solution)/shard_map/ppermute | solution.py:412
  50.5 10.7 %collective-permute-start.14 = (bf16[128,2176]{1,0:T(8,128)(2,1)S(1)}, bf16[128,2176]{1,0:T(8,128)(2,1)S(1)}, u32[]{:S(2)}, u32[]{:S(2)}) collective-permute-start(bf16[128,2176]{1,0:T(8,128)(2,1)S(1)} %pad_maximum_fusion.3), channel_id=1, source_target_pairs={{0,4},{1,3},{2,6},{3,1},{4,0},{5,7},{6,2},{7,5},{8,12},{9,11},{10,... | collective-permute-start | bytes 1671176 | tf_op jit(solution)/shard_map/ppermute | solution.py:412
  51.6 13.8 %collective-permute-start.16 = (bf16[128,2048]{1,0:T(8,128)(2,1)S(1)}, bf16[128,2048]{1,0:T(8,128)(2,1)S(1)}, u32[]{:S(2)}, u32[]{:S(2)}) collective-permute-start(bf16[128,2048]{1,0:T(8,128)(2,1)S(1)} %get-tuple-element.133), channel_id=1, source_target_pairs={{0,24},{2,26},{4,28},{6,30},{8,0},{10,2},{12,4},{14,6},{16,8},{18,... | collective-permute-start | bytes 1572872 | tf_op jit(solution)/shard_map/ppermute | solution.py:416
  59.5 13.0 %collective-permute-start.19 = (bf16[128,2048]{1,0:T(8,128)(2,1)S(1)}, bf16[128,2048]{1,0:T(8,128)(2,1)S(1)}, u32[]{:S(2)}, u32[]{:S(2)}) collective-permute-start(bf16[128,2048]{1,0:T(8,128)(2,1)S(1)} %get-tuple-element.138), channel_id=1, source_target_pairs={{0,24},{2,26},{4,28},{6,30},{8,0},{10,2},{12,4},{14,6},{16,8},{18,... | collective-permute-start | bytes 1572872 | tf_op jit(solution)/shard_map/ppermute | solution.py:416
  59.7 8.8 %collective-permute-start.18 = (bf16[64,2048]{1,0:T(8,128)(2,1)S(1)}, bf16[64,2048]{1,0:T(8,128)(2,1)S(1)}, u32[]{:S(2)}, u32[]{:S(2)}) collective-permute-start(bf16[64,2048]{1,0:T(8,128)(2,1)S(1)} %get-tuple-element.137), channel_id=1, source_target_pairs={{0,4},{1,3},{2,6},{3,1},{4,0},{5,7},{6,2},{7,5},{8,12},{9,11},{10,... | collective-permute-start | bytes 786440 | tf_op jit(solution)/shard_map/ppermute | solution.py:412
  65.5 9.0 %collective-permute-start.17 = (bf16[64,2048]{1,0:T(8,128)(2,1)S(1)}, bf16[64,2048]{1,0:T(8,128)(2,1)S(1)}, u32[]{:S(2)}, u32[]{:S(2)}) collective-permute-start(bf16[64,2048]{1,0:T(8,128)(2,1)S(1)} %add_convert_fusion.8), channel_id=1, source_target_pairs={{0,2},{1,5},{2,0},{3,7},{4,6},{5,1},{6,4},{7,3},{8,10},{9,13},{10,... | collective-permute-start | bytes 786440 | tf_op jit(solution)/shard_map/ppermute | solution.py:412
  66.1 8.4 %collective-permute-start.20 = (bf16[64,2048]{1,0:T(8,128)(2,1)S(1)}, bf16[64,2048]{1,0:T(8,128)(2,1)S(1)}, u32[]{:S(2)}, u32[]{:S(2)}) collective-permute-start(bf16[64,2048]{1,0:T(8,128)(2,1)S(1)} %get-tuple-element.139), channel_id=1, source_target_pairs={{0,4},{1,3},{2,6},{3,1},{4,0},{5,7},{6,2},{7,5},{8,12},{9,11},{10,... | collective-permute-start | bytes 786440 | tf_op jit(solution)/shard_map/ppermute | solution.py:412
  67.5 10.9 %collective-permute-start.22 = (bf16[64,2048]{1,0:T(8,128)(2,1)S(1)}, bf16[64,2048]{1,0:T(8,128)(2,1)S(1)}, u32[]{:S(2)}, u32[]{:S(2)}) collective-permute-start(bf16[64,2048]{1,0:T(8,128)(2,1)S(1)} %get-tuple-element.143), channel_id=1, source_target_pairs={{0,4},{1,3},{2,6},{3,1},{4,0},{5,7},{6,2},{7,5},{8,12},{9,11},{10,... | collective-permute-start | bytes 786440 | tf_op jit(solution)/shard_map/ppermute | solution.py:412
  74.6 8.4 %collective-permute-start.23 = (bf16[64,2048]{1,0:T(8,128)(2,1)S(1)}, bf16[64,2048]{1,0:T(8,128)(2,1)S(1)}, u32[]{:S(2)}, u32[]{:S(2)}) collective-permute-start(bf16[64,2048]{1,0:T(8,128)(2,1)S(1)} %add_convert_fusion.6), channel_id=1, source_target_pairs={{0,8},{2,10},{4,12},{6,14},{8,16},{10,18},{12,20},{14,22},{16,24},... | collective-permute-start | bytes 786440 | tf_op jit(solution)/shard_map/ppermute | solution.py:416
  75.6 8.0 %collective-permute-start.21 = (bf16[64,2048]{1,0:T(8,128)(2,1)S(1)}, bf16[64,2048]{1,0:T(8,128)(2,1)S(1)}, u32[]{:S(2)}, u32[]{:S(2)}) collective-permute-start(bf16[64,2048]{1,0:T(8,128)(2,1)S(1)} %add_convert_fusion.7), channel_id=1, source_target_pairs={{0,2},{1,5},{2,0},{3,7},{4,6},{5,1},{6,4},{7,3},{8,10},{9,13},{10,... | collective-permute-start | bytes 786440 | tf_op jit(solution)/shard_map/ppermute | solution.py:412
  78.2 10.2 %collective-permute-start.25 = (bf16[64,2048]{1,0:T(8,128)(2,1)S(1)}, bf16[64,2048]{1,0:T(8,128)(2,1)S(1)}, u32[]{:S(2)}, u32[]{:S(2)}) collective-permute-start(bf16[64,2048]{1,0:T(8,128)(2,1)S(1)} %get-tuple-element.163), channel_id=1, source_target_pairs={{0,4},{1,3},{2,6},{3,1},{4,0},{5,7},{6,2},{7,5},{8,12},{9,11},{10,... | collective-permute-start | bytes 786440 | tf_op jit(solution)/shard_map/ppermute | solution.py:412
  83.7 8.2 %collective-permute-start.27 = (bf16[64,2048]{1,0:T(8,128)(2,1)S(1)}, bf16[64,2048]{1,0:T(8,128)(2,1)S(1)}, u32[]{:S(2)}, u32[]{:S(2)}) collective-permute-start(bf16[64,2048]{1,0:T(8,128)(2,1)S(1)} %add_convert_fusion), channel_id=1, source_target_pairs={{0,8},{2,10},{4,12},{6,14},{8,16},{10,18},{12,20},{14,22},{16,24},... | collective-permute-start | bytes 786440 | tf_op jit(solution)/shard_map/ppermute | solution.py:416
  (4 other events, 25.5 us)

commit v10 on v9

--- a/solution.py
+++ b/solution.py
@@ -10,7 +10,7 @@
 
 BF16 = jnp.bfloat16
 F32 = jnp.float32
-LOWEST = -1e30
+LOWEST = -math.inf
 STEP_FLOPS = 200_000_000
 
 
@@ -96,15 +96,6 @@
 
     for copy in groups[0]:
         copy.wait()
-    row = lax.broadcasted_iota(jnp.int32, table_ref.shape[::-1], 0)
-    table = jnp.zeros(row.shape, F32)
-    for k in range(i_buf.shape[0]):
-        index = i_buf[k : k + 1, :]
-        weight = r_buf[k : k + 1, :]
-        high = weight.astype(BF16).astype(F32)
-        table = jnp.where(row == index, high, table)
-        table = jnp.where(row == index + experts, weight - high, table)
-    table_ref[...] = table.T.astype(BF16)
     scale = 1.0 / math.sqrt(head_size)
     stacked = heads * drafts
     slot = lax.broadcasted_iota(jnp.int32, (stacked, context_len), 1)
@@ -138,6 +129,15 @@
             draft_probs, axis=-1, keepdims=True
         )
         probs.append((cache_probs.astype(BF16), draft_probs.astype(BF16), denominator))
+    row = lax.broadcasted_iota(jnp.int32, table_ref.shape[::-1], 0)
+    table = jnp.zeros(row.shape, F32)
+    for k in range(i_buf.shape[0]):
+        index = i_buf[k : k + 1, :]
+        weight = r_buf[k : k + 1, :]
+        high = weight.astype(BF16).astype(F32)
+        table = jnp.where(row == index, high, table)
+        table = jnp.where(row == index + experts, weight - high, table)
+    table_ref[...] = table.T.astype(BF16)
     for copy in groups[1]:
         copy.wait()
     for r in range(reqs_all):

time: 93 us -> 93 us (level)
  no operation moved by 1% of the time
where the time goes in v10:
time: 93 us; the launch traced here: 92.8 us
  waiting for transfers between devices  35.8 us (38%)
  starting transfers between devices  28.5 us (31%)
  Pallas kernels  27.5 us (30%)
    ppermute x17, starting transfers between devices, across(): return lambda a: lax.ppermute(a, ('wide', 'narrow'), pairs)  20.9 us
    ppermute x17, waiting for transfers between devices, across(): return lambda a: lax.ppermute(a, ('wide', 'narrow'), pairs)  17.8 us
    pallas_call x4, Pallas kernels, plane_experts(): pl.pallas_call(functools.partial(experts_kernel, spans, experts), out_sha...  16.5 us
    ppermute x7, waiting for transfers between devices, shifted(): return lambda a: lax.ppermute(a, 'wide', pairs)  15.8 us
    ppermute x7, starting transfers between devices, shifted(): return lambda a: lax.ppermute(a, 'wide', pairs)  6.49 us
    pallas_call x1, Pallas kernels, hold_weights(): pl.pallas_call(functools.partial(hold_kernel, count), out_shape=[jax.Shap...  5.29 us
    pallas_call x1, Pallas kernels, attention(): pl.pallas_call(functools.partial(attention_kernel, experts), out_shape=(j...  4.64 us
    ppermute x1, waiting for transfers between devices, on_device(): received = lax.ppermute(outgoing, 'narrow', swap)  2.18 us
  transfers between devices with their start and end apart: 28, of which 15 were waited for; matrix products, arithmetic and copies ran while one was open for 1% of the time, Pallas kernels for 29%

profile of v10, /device:TPU:0, one launch (start us, length us, event | category | flops | bytes accessed | tf_op | source)
XLA Modules:
  0.0 92.8 jit_solution(17410496607017154069)
XLA Ops:
  1.0 4.6 %shard_map.145 = (bf16[64,2048]{1,0:T(8,128)(2,1)S(1)}, f32[64,2048]{1,0:T(8,128)S(1)}, bf16[64,128]{1,0:T(8,128)(2,1)S(1)}, f32[1,2048]{1,0:T(1,128)S(1)}) custom-call(s32[1]{0:T(128)} %bitcast.core_ref, s32[8]{0:T(128)} %draft_len_ref.1, s32[8]{0:T(128)} %cache_len_ref.1, s32[10,64]{1,0:T(8,128)} %bitcast.6, f32[10,64]{1,0:T(8,128)} %bitcast.7, ...), custom_call_target="tpu_custom_call" | custom-call | flops 671088640 | bytes 6291456 | tf_op jit(solution)/shard_map/pallas_call | solution.py:179
  5.7 2.2 %collective-permute-done.received_ref = bf16[64,2048]{1,0:T(8,128)(2,1)S(1)} collective-permute-done((bf16[64,2048]{1,0:T(8,128)(2,1)S(1)}, bf16[64,2048]{1,0:T(8,128)(2,1)S(1)}, u32[]{:S(2)}, u32[]{:S(2)}) %collective-permute-start) | collective-permute-done | bytes 262176 | tf_op jit(solution)/shard_map/ppermute | solution.py:405
  8.1 3.0 %collective-permute-start.1 = (bf16[64,2176]{1,0:T(8,128)(2,1)S(1)}, bf16[64,2176]{1,0:T(8,128)(2,1)S(1)}, u32[]{:S(2)}, u32[]{:S(2)}) collective-permute-start(bf16[64,2176]{1,0:T(8,128)(2,1)S(1)} %get-tuple-element.87.refs_0_), channel_id=1, source_target_pairs={{0,8},{2,10},{4,12},{6,14},{8,16},{10,18},{12,20},{14,22},{16,24},... | collective-permute-start | bytes 835592 | tf_op jit(solution)/shard_map/ppermute | solution.py:416
  12.7 5.3 %shard_map.147 = (s32[2]{0:T(128)S(1)}, bf16[1,2048,512]{2,1,0:T(8,128)(2,1)S(1)}, bf16[1,2048,512]{2,1,0:T(8,128)(2,1)S(1)}, bf16[1,512,2048]{2,1,0:T(8,128)(2,...) custom-call(s32[2]{0:T(128)S(1)} %pad_add_fusion.where_ref, ...), custom_call_target="tpu_custom_call" | custom-call | flops 200000000 | tf_op jit(solution)/shard_map/pallas_call | solution.py:302
  18.0 2.1 %collective-permute-done.1.refs_0_ = bf16[64,2176]{1,0:T(8,128)(2,1)S(1)} collective-permute-done((bf16[64,2176]{1,0:T(8,128)(2,1)S(1)}, bf16[64,2176]{1,0:T(8,128)(2,1)S(1)}, u32[]{:S(2)}, u32[]{:S(2)}) %collective-permute-start.1) | collective-permute-done | bytes 278560 | tf_op jit(solution)/shard_map/ppermute | solution.py:416
  20.1 1.5 %collective-permute-start.6 = (bf16[64,2176]{1,0:T(8,128)(2,1)S(1)}, bf16[64,2176]{1,0:T(8,128)(2,1)S(1)}, u32[]{:S(2)}, u32[]{:S(2)}) collective-permute-start(bf16[64,2176]{1,0:T(8,128)(2,1)S(1)} %collective-permute-done.1.refs_0_), channel_id=1, source_target_pairs={{0,2},{1,5},{2,0},{3,7},{4,6},{5,1},{6,4},{7,3},{8,10},{9,13},{10,... | collective-permute-start | bytes 835592 | tf_op jit(solution)/shard_map/ppermute | solution.py:412
  21.7 1.6 %collective-permute-start.10 = (bf16[128,2176]{1,0:T(8,128)(2,1)S(1)}, bf16[128,2176]{1,0:T(8,128)(2,1)S(1)}, u32[]{:S(2)}, u32[]{:S(2)}) collective-permute-start(bf16[128,2176]{1,0:T(8,128)(2,1)S(1)} %pad_maximum_fusion), channel_id=1, source_target_pairs={{0,4},{1,3},{2,6},{3,1},{4,0},{5,7},{6,2},{7,5},{8,12},{9,11},{10,... | collective-permute-start | bytes 1671176 | tf_op jit(solution)/shard_map/ppermute | solution.py:412
  23.3 6.4 %collective-permute-done.6.refs_1_ = bf16[64,2176]{1,0:T(8,128)(2,1)S(1)} collective-permute-done((bf16[64,2176]{1,0:T(8,128)(2,1)S(1)}, bf16[64,2176]{1,0:T(8,128)(2,1)S(1)}, u32[]{:S(2)}, u32[]{:S(2)}) %collective-permute-start.6) | collective-permute-done | bytes 278560 | tf_op jit(solution)/shard_map/ppermute | solution.py:412
  31.1 1.5 %collective-permute-start.8 = (bf16[64,2176]{1,0:T(8,128)(2,1)S(1)}, bf16[64,2176]{1,0:T(8,128)(2,1)S(1)}, u32[]{:S(2)}, u32[]{:S(2)}) collective-permute-start(bf16[64,2176]{1,0:T(8,128)(2,1)S(1)} %collective-permute-done.7.refs_0_), channel_id=1, source_target_pairs={{0,2},{1,5},{2,0},{3,7},{4,6},{5,1},{6,4},{7,3},{8,10},{9,13},{10,... | collective-permute-start | bytes 835592 | tf_op jit(solution)/shard_map/ppermute | solution.py:412
  33.2 4.1 %shard_map.150 = (bf16[64,2048]{1,0:T(8,128)(2,1)S(1)}, bf16[64,2048]{1,0:T(8,128)(2,1)S(1)}, bf16[64,2048]{1,0:T(8,128)(2,1)S(1)}, bf16[64,2048]{1,0:T(8,128)(2,1)S(1)}) custom-call(s32[2]{0:T(128)S(1)} %get-tuple-element.99.where_ref, bf16[64,2176]{1,0:T(8,128)(2,1)S(1)} %get-tuple-element.87.refs_0_, bf16[64,2176]{1,0:T(8,128)(2,1)S(1)} %collective-permute-done.2.refs_1_, ...), custom_call_target="tpu_custom_call" | custom-call | flops 200000000 | tf_op jit(solution)/shard_map/pallas_call | solution.py:335
  37.3 3.4 %collective-permute-done.8.refs_1_ = bf16[64,2176]{1,0:T(8,128)(2,1)S(1)} collective-permute-done((bf16[64,2176]{1,0:T(8,128)(2,1)S(1)}, bf16[64,2176]{1,0:T(8,128)(2,1)S(1)}, u32[]{:S(2)}, u32[]{:S(2)}) %collective-permute-start.8) | collective-permute-done | bytes 278560 | tf_op jit(solution)/shard_map/ppermute | solution.py:412
  42.3 1.8 %collective-permute-start.13 = (bf16[128,2176]{1,0:T(8,128)(2,1)S(1)}, bf16[128,2176]{1,0:T(8,128)(2,1)S(1)}, u32[]{:S(2)}, u32[]{:S(2)}) collective-permute-start(bf16[128,2176]{1,0:T(8,128)(2,1)S(1)} %pad_maximum_fusion.2), channel_id=1, source_target_pairs={{0,4},{1,3},{2,6},{3,1},{4,0},{5,7},{6,2},{7,5},{8,12},{9,11},{10,... | collective-permute-start | bytes 1671176 | tf_op jit(solution)/shard_map/ppermute | solution.py:412
  45.2 4.1 %shard_map.152 = (bf16[128,2048]{1,0:T(8,128)(2,1)S(1)}, bf16[128,2048]{1,0:T(8,128)(2,1)S(1)}) custom-call(s32[2]{0:T(128)S(1)} %get-tuple-element.99.where_ref, bf16[64,2176]{1,0:T(8,128)(2,1)S(1)} %collective-permute-done.1.refs_0_, bf16[64,2176]{1,0:T(8,128)(2,1)S(1)} %collective-permute-done.6.refs_1_, ...), custom_call_target="tpu_custom_call" | custom-call | flops 200000000 | tf_op jit(solution)/shard_map/pallas_call | solution.py:335
  51.6 1.9 %collective-permute-start.16 = (bf16[128,2048]{1,0:T(8,128)(2,1)S(1)}, bf16[128,2048]{1,0:T(8,128)(2,1)S(1)}, u32[]{:S(2)}, u32[]{:S(2)}) collective-permute-start(bf16[128,2048]{1,0:T(8,128)(2,1)S(1)} %get-tuple-element.133), channel_id=1, source_target_pairs={{0,24},{2,26},{4,28},{6,30},{8,0},{10,2},{12,4},{14,6},{16,8},{18,... | collective-permute-start | bytes 1572872 | tf_op jit(solution)/shard_map/ppermute | solution.py:416
  53.5 4.1 %shard_map.154 = (bf16[64,2048]{1,0:T(8,128)(2,1)S(1)}, bf16[64,2048]{1,0:T(8,128)(2,1)S(1)}, bf16[64,2048]{1,0:T(8,128)(2,1)S(1)}, bf16[64,2048]{1,0:T(8,128)(2,1)S(1)}) custom-call(s32[2]{0:T(128)S(1)} %get-tuple-element.99.where_ref, bf16[64,2176]{1,0:T(8,128)(2,1)S(1)} %collective-permute-done.7.refs_0_, ...), custom_call_target="tpu_custom_call" | custom-call | flops 200000000 | tf_op jit(solution)/shard_map/pallas_call | solution.py:335
  57.7 1.8 %collective-permute-start.15 = (bf16[64,2048]{1,0:T(8,128)(2,1)S(1)}, bf16[64,2048]{1,0:T(8,128)(2,1)S(1)}, u32[]{:S(2)}, u32[]{:S(2)}) collective-permute-start(bf16[64,2048]{1,0:T(8,128)(2,1)S(1)} %get-tuple-element.132), channel_id=1, source_target_pairs={{0,4},{1,3},{2,6},{3,1},{4,0},{5,7},{6,2},{7,5},{8,12},{9,11},{10,... | collective-permute-start | bytes 786440 | tf_op jit(solution)/shard_map/ppermute | solution.py:412
  59.7 1.5 %collective-permute-start.18 = (bf16[64,2048]{1,0:T(8,128)(2,1)S(1)}, bf16[64,2048]{1,0:T(8,128)(2,1)S(1)}, u32[]{:S(2)}, u32[]{:S(2)}) collective-permute-start(bf16[64,2048]{1,0:T(8,128)(2,1)S(1)} %get-tuple-element.137), channel_id=1, source_target_pairs={{0,4},{1,3},{2,6},{3,1},{4,0},{5,7},{6,2},{7,5},{8,12},{9,11},{10,... | collective-permute-start | bytes 786440 | tf_op jit(solution)/shard_map/ppermute | solution.py:412
  61.2 4.1 %shard_map.156 = (bf16[64,2048]{1,0:T(8,128)(2,1)S(1)}, bf16[64,2048]{1,0:T(8,128)(2,1)S(1)}, bf16[64,2048]{1,0:T(8,128)(2,1)S(1)}, bf16[64,2048]{1,0:T(8,128)(2,1)S(1)}) custom-call(s32[2]{0:T(128)S(1)} %get-tuple-element.99.where_ref, bf16[64,2176]{1,0:T(8,128)(2,1)S(1)} %collective-permute-done.9.refs_0_, ...), custom_call_target="tpu_custom_call" | custom-call | flops 200000000 | tf_op jit(solution)/shard_map/pallas_call | solution.py:335
  68.5 4.0 %collective-permute-done.19 = bf16[128,2048]{1,0:T(8,128)(2,1)S(1)} collective-permute-done((bf16[128,2048]{1,0:T(8,128)(2,1)S(1)}, bf16[128,2048]{1,0:T(8,128)(2,1)S(1)}, u32[]{:S(2)}, u32[]{:S(2)}) %collective-permute-start.19) | collective-permute-done | bytes 524320 | tf_op jit(solution)/shard_map/ppermute | solution.py:416
  72.5 1.9 %collective-permute-done.17 = bf16[64,2048]{1,0:T(8,128)(2,1)S(1)} collective-permute-done((bf16[64,2048]{1,0:T(8,128)(2,1)S(1)}, bf16[64,2048]{1,0:T(8,128)(2,1)S(1)}, u32[]{:S(2)}, u32[]{:S(2)}) %collective-permute-start.17) | collective-permute-done | bytes 262176 | tf_op jit(solution)/shard_map/ppermute | solution.py:412
  76.3 1.8 %collective-permute-start.24 = (bf16[64,2048]{1,0:T(8,128)(2,1)S(1)}, bf16[64,2048]{1,0:T(8,128)(2,1)S(1)}, u32[]{:S(2)}, u32[]{:S(2)}) collective-permute-start(bf16[64,2048]{1,0:T(8,128)(2,1)S(1)} %get-tuple-element.164), channel_id=1, source_target_pairs={{0,4},{1,3},{2,6},{3,1},{4,0},{5,7},{6,2},{7,5},{8,12},{9,11},{10,... | collective-permute-start | bytes 786440 | tf_op jit(solution)/shard_map/ppermute | solution.py:412
  78.4 4.5 %collective-permute-done.23 = bf16[64,2048]{1,0:T(8,128)(2,1)S(1)} collective-permute-done((bf16[64,2048]{1,0:T(8,128)(2,1)S(1)}, bf16[64,2048]{1,0:T(8,128)(2,1)S(1)}, u32[]{:S(2)}, u32[]{:S(2)}) %collective-permute-start.23) | collective-permute-done | bytes 262176 | tf_op jit(solution)/shard_map/ppermute | solution.py:416
  85.7 2.7 %collective-permute-done.25.refs_1_ = bf16[64,2048]{1,0:T(8,128)(2,1)S(1)} collective-permute-done((bf16[64,2048]{1,0:T(8,128)(2,1)S(1)}, bf16[64,2048]{1,0:T(8,128)(2,1)S(1)}, u32[]{:S(2)}, u32[]{:S(2)}) %collective-permute-start.25) | collective-permute-done | bytes 262176 | tf_op jit(solution)/shard_map/ppermute | solution.py:412
  88.4 3.6 %collective-permute-done.27.refs_3_ = bf16[64,2048]{1,0:T(8,128)(2,1)S(1)} collective-permute-done((bf16[64,2048]{1,0:T(8,128)(2,1)S(1)}, bf16[64,2048]{1,0:T(8,128)(2,1)S(1)}, u32[]{:S(2)}, u32[]{:S(2)}) %collective-permute-start.27) | collective-permute-done | bytes 262176 | tf_op jit(solution)/shard_map/ppermute | solution.py:416
  (63 shorter events, 19.0 us)
Async XLA Ops:
  0.0 12.7 %collective-permute-start.3 = (bf16[1,2048,512]{2,1,0:T(8,128)(2,1)}, bf16[1,2048,512]{2,1,0:T(8,128)(2,1)S(1)}, u32[]{:S(2)}, u32[]{:S(2)}) collective-permute-start(bf16[1,2048,512]{2,1,0:T(8,128)(2,1)} %refs_0_.1), channel_id=1, source_target_pairs={{0,1},{1,0},{2,3},{3,2},{4,5},{5,4},{6,7},{7,6},{8,9},{9,8},{10,11... | collective-permute-start | bytes 6291464 | tf_op jit(solution)/shard_map/ppermute | solution.py:399
  0.5 12.3 %collective-permute-start.4 = (bf16[1,2048,512]{2,1,0:T(8,128)(2,1)}, bf16[1,2048,512]{2,1,0:T(8,128)(2,1)}, u32[]{:S(2)}, u32[]{:S(2)}) collective-permute-start(bf16[1,2048,512]{2,1,0:T(8,128)(2,1)} %refs_1_.1), channel_id=1, source_target_pairs={{0,1},{1,0},{2,3},{3,2},{4,5},{5,4},{6,7},{7,6},{8,9},{9,8},{10,11... | collective-permute-start | bytes 6291464 | tf_op jit(solution)/shard_map/ppermute | solution.py:399
  0.5 12.2 %collective-permute-start.5 = (bf16[1,512,2048]{2,1,0:T(8,128)(2,1)}, bf16[1,512,2048]{2,1,0:T(8,128)(2,1)}, u32[]{:S(2)}, u32[]{:S(2)}) collective-permute-start(bf16[1,512,2048]{2,1,0:T(8,128)(2,1)} %refs_2_.1), channel_id=1, source_target_pairs={{0,1},{1,0},{2,3},{3,2},{4,5},{5,4},{6,7},{7,6},{8,9},{9,8},{10,11... | collective-permute-start | bytes 6291464 | tf_op jit(solution)/shard_map/ppermute | solution.py:399
  8.1 12.0 %collective-permute-start.1 = (bf16[64,2176]{1,0:T(8,128)(2,1)S(1)}, bf16[64,2176]{1,0:T(8,128)(2,1)S(1)}, u32[]{:S(2)}, u32[]{:S(2)}) collective-permute-start(bf16[64,2176]{1,0:T(8,128)(2,1)S(1)} %get-tuple-element.87.refs_0_), channel_id=1, source_target_pairs={{0,8},{2,10},{4,12},{6,14},{8,16},{10,18},{12,20},{14,22},{16,24},... | collective-permute-start | bytes 835592 | tf_op jit(solution)/shard_map/ppermute | solution.py:416
  11.1 9.0 %collective-permute-start.2 = (bf16[64,2176]{1,0:T(8,128)(2,1)S(1)}, bf16[64,2176]{1,0:T(8,128)(2,1)S(1)}, u32[]{:S(2)}, u32[]{:S(2)}) collective-permute-start(bf16[64,2176]{1,0:T(8,128)(2,1)S(1)} %get-tuple-element.87.refs_0_), channel_id=1, source_target_pairs={{0,2},{1,5},{2,0},{3,7},{4,6},{5,1},{6,4},{7,3},{8,10},{9,13},{10,... | collective-permute-start | bytes 835592 | tf_op jit(solution)/shard_map/ppermute | solution.py:412
  20.1 9.5 %collective-permute-start.6 = (bf16[64,2176]{1,0:T(8,128)(2,1)S(1)}, bf16[64,2176]{1,0:T(8,128)(2,1)S(1)}, u32[]{:S(2)}, u32[]{:S(2)}) collective-permute-start(bf16[64,2176]{1,0:T(8,128)(2,1)S(1)} %collective-permute-done.1.refs_0_), channel_id=1, source_target_pairs={{0,2},{1,5},{2,0},{3,7},{4,6},{5,1},{6,4},{7,3},{8,10},{9,13},{10,... | collective-permute-start | bytes 835592 | tf_op jit(solution)/shard_map/ppermute | solution.py:412
  21.6 9.5 %collective-permute-start.7 = (bf16[64,2176]{1,0:T(8,128)(2,1)S(1)}, bf16[64,2176]{1,0:T(8,128)(2,1)S(1)}, u32[]{:S(2)}, u32[]{:S(2)}) collective-permute-start(bf16[64,2176]{1,0:T(8,128)(2,1)S(1)} %collective-permute-done.1.refs_0_), channel_id=1, source_target_pairs={{0,8},{2,10},{4,12},{6,14},{8,16},{10,18},{12,20},{14,22},{16,24},... | collective-permute-start | bytes 835592 | tf_op jit(solution)/shard_map/ppermute | solution.py:416
  21.7 11.6 %collective-permute-start.10 = (bf16[128,2176]{1,0:T(8,128)(2,1)S(1)}, bf16[128,2176]{1,0:T(8,128)(2,1)S(1)}, u32[]{:S(2)}, u32[]{:S(2)}) collective-permute-start(bf16[128,2176]{1,0:T(8,128)(2,1)S(1)} %pad_maximum_fusion), channel_id=1, source_target_pairs={{0,4},{1,3},{2,6},{3,1},{4,0},{5,7},{6,2},{7,5},{8,12},{9,11},{10,... | collective-permute-start | bytes 1671176 | tf_op jit(solution)/shard_map/ppermute | solution.py:412
  31.1 9.6 %collective-permute-start.8 = (bf16[64,2176]{1,0:T(8,128)(2,1)S(1)}, bf16[64,2176]{1,0:T(8,128)(2,1)S(1)}, u32[]{:S(2)}, u32[]{:S(2)}) collective-permute-start(bf16[64,2176]{1,0:T(8,128)(2,1)S(1)} %collective-permute-done.7.refs_0_), channel_id=1, source_target_pairs={{0,2},{1,5},{2,0},{3,7},{4,6},{5,1},{6,4},{7,3},{8,10},{9,13},{10,... | collective-permute-start | bytes 835592 | tf_op jit(solution)/shard_map/ppermute | solution.py:412
  32.6 8.3 %collective-permute-start.9 = (bf16[64,2176]{1,0:T(8,128)(2,1)S(1)}, bf16[64,2176]{1,0:T(8,128)(2,1)S(1)}, u32[]{:S(2)}, u32[]{:S(2)}) collective-permute-start(bf16[64,2176]{1,0:T(8,128)(2,1)S(1)} %collective-permute-done.7.refs_0_), channel_id=1, source_target_pairs={{0,8},{2,10},{4,12},{6,14},{8,16},{10,18},{12,20},{14,22},{16,24},... | collective-permute-start | bytes 835592 | tf_op jit(solution)/shard_map/ppermute | solution.py:416
  32.6 12.6 %collective-permute-start.12 = (bf16[128,2176]{1,0:T(8,128)(2,1)S(1)}, bf16[128,2176]{1,0:T(8,128)(2,1)S(1)}, u32[]{:S(2)}, u32[]{:S(2)}) collective-permute-start(bf16[128,2176]{1,0:T(8,128)(2,1)S(1)} %pad_maximum_fusion.1), channel_id=1, source_target_pairs={{0,4},{1,3},{2,6},{3,1},{4,0},{5,7},{6,2},{7,5},{8,12},{9,11},{10,... | collective-permute-start | bytes 1671176 | tf_op jit(solution)/shard_map/ppermute | solution.py:412
  40.9 9.5 %collective-permute-start.11 = (bf16[64,2176]{1,0:T(8,128)(2,1)S(1)}, bf16[64,2176]{1,0:T(8,128)(2,1)S(1)}, u32[]{:S(2)}, u32[]{:S(2)}) collective-permute-start(bf16[64,2176]{1,0:T(8,128)(2,1)S(1)} %collective-permute-done.9.refs_0_), channel_id=1, source_target_pairs={{0,2},{1,5},{2,0},{3,7},{4,6},{5,1},{6,4},{7,3},{8,10},{9,13},{10,... | collective-permute-start | bytes 835592 | tf_op jit(solution)/shard_map/ppermute | solution.py:412
  42.3 11.3 %collective-permute-start.13 = (bf16[128,2176]{1,0:T(8,128)(2,1)S(1)}, bf16[128,2176]{1,0:T(8,128)(2,1)S(1)}, u32[]{:S(2)}, u32[]{:S(2)}) collective-permute-start(bf16[128,2176]{1,0:T(8,128)(2,1)S(1)} %pad_maximum_fusion.2), channel_id=1, source_target_pairs={{0,4},{1,3},{2,6},{3,1},{4,0},{5,7},{6,2},{7,5},{8,12},{9,11},{10,... | collective-permute-start | bytes 1671176 | tf_op jit(solution)/shard_map/ppermute | solution.py:412
  50.5 10.7 %collective-permute-start.14 = (bf16[128,2176]{1,0:T(8,128)(2,1)S(1)}, bf16[128,2176]{1,0:T(8,128)(2,1)S(1)}, u32[]{:S(2)}, u32[]{:S(2)}) collective-permute-start(bf16[128,2176]{1,0:T(8,128)(2,1)S(1)} %pad_maximum_fusion.3), channel_id=1, source_target_pairs={{0,4},{1,3},{2,6},{3,1},{4,0},{5,7},{6,2},{7,5},{8,12},{9,11},{10,... | collective-permute-start | bytes 1671176 | tf_op jit(solution)/shard_map/ppermute | solution.py:412
  51.6 13.8 %collective-permute-start.16 = (bf16[128,2048]{1,0:T(8,128)(2,1)S(1)}, bf16[128,2048]{1,0:T(8,128)(2,1)S(1)}, u32[]{:S(2)}, u32[]{:S(2)}) collective-permute-start(bf16[128,2048]{1,0:T(8,128)(2,1)S(1)} %get-tuple-element.133), channel_id=1, source_target_pairs={{0,24},{2,26},{4,28},{6,30},{8,0},{10,2},{12,4},{14,6},{16,8},{18,... | collective-permute-start | bytes 1572872 | tf_op jit(solution)/shard_map/ppermute | solution.py:416
  59.5 13.0 %collective-permute-start.19 = (bf16[128,2048]{1,0:T(8,128)(2,1)S(1)}, bf16[128,2048]{1,0:T(8,128)(2,1)S(1)}, u32[]{:S(2)}, u32[]{:S(2)}) collective-permute-start(bf16[128,2048]{1,0:T(8,128)(2,1)S(1)} %get-tuple-element.138), channel_id=1, source_target_pairs={{0,24},{2,26},{4,28},{6,30},{8,0},{10,2},{12,4},{14,6},{16,8},{18,... | collective-permute-start | bytes 1572872 | tf_op jit(solution)/shard_map/ppermute | solution.py:416
  59.7 8.8 %collective-permute-start.18 = (bf16[64,2048]{1,0:T(8,128)(2,1)S(1)}, bf16[64,2048]{1,0:T(8,128)(2,1)S(1)}, u32[]{:S(2)}, u32[]{:S(2)}) collective-permute-start(bf16[64,2048]{1,0:T(8,128)(2,1)S(1)} %get-tuple-element.137), channel_id=1, source_target_pairs={{0,4},{1,3},{2,6},{3,1},{4,0},{5,7},{6,2},{7,5},{8,12},{9,11},{10,... | collective-permute-start | bytes 786440 | tf_op jit(solution)/shard_map/ppermute | solution.py:412
  65.5 9.0 %collective-permute-start.17 = (bf16[64,2048]{1,0:T(8,128)(2,1)S(1)}, bf16[64,2048]{1,0:T(8,128)(2,1)S(1)}, u32[]{:S(2)}, u32[]{:S(2)}) collective-permute-start(bf16[64,2048]{1,0:T(8,128)(2,1)S(1)} %add_convert_fusion.8), channel_id=1, source_target_pairs={{0,2},{1,5},{2,0},{3,7},{4,6},{5,1},{6,4},{7,3},{8,10},{9,13},{10,... | collective-permute-start | bytes 786440 | tf_op jit(solution)/shard_map/ppermute | solution.py:412
  66.1 8.4 %collective-permute-start.20 = (bf16[64,2048]{1,0:T(8,128)(2,1)S(1)}, bf16[64,2048]{1,0:T(8,128)(2,1)S(1)}, u32[]{:S(2)}, u32[]{:S(2)}) collective-permute-start(bf16[64,2048]{1,0:T(8,128)(2,1)S(1)} %get-tuple-element.139), channel_id=1, source_target_pairs={{0,4},{1,3},{2,6},{3,1},{4,0},{5,7},{6,2},{7,5},{8,12},{9,11},{10,... | collective-permute-start | bytes 786440 | tf_op jit(solution)/shard_map/ppermute | solution.py:412
  67.5 10.9 %collective-permute-start.22 = (bf16[64,2048]{1,0:T(8,128)(2,1)S(1)}, bf16[64,2048]{1,0:T(8,128)(2,1)S(1)}, u32[]{:S(2)}, u32[]{:S(2)}) collective-permute-start(bf16[64,2048]{1,0:T(8,128)(2,1)S(1)} %get-tuple-element.143), channel_id=1, source_target_pairs={{0,4},{1,3},{2,6},{3,1},{4,0},{5,7},{6,2},{7,5},{8,12},{9,11},{10,... | collective-permute-start | bytes 786440 | tf_op jit(solution)/shard_map/ppermute | solution.py:412
  74.6 8.4 %collective-permute-start.23 = (bf16[64,2048]{1,0:T(8,128)(2,1)S(1)}, bf16[64,2048]{1,0:T(8,128)(2,1)S(1)}, u32[]{:S(2)}, u32[]{:S(2)}) collective-permute-start(bf16[64,2048]{1,0:T(8,128)(2,1)S(1)} %add_convert_fusion.6), channel_id=1, source_target_pairs={{0,8},{2,10},{4,12},{6,14},{8,16},{10,18},{12,20},{14,22},{16,24},... | collective-permute-start | bytes 786440 | tf_op jit(solution)/shard_map/ppermute | solution.py:416
  75.6 8.0 %collective-permute-start.21 = (bf16[64,2048]{1,0:T(8,128)(2,1)S(1)}, bf16[64,2048]{1,0:T(8,128)(2,1)S(1)}, u32[]{:S(2)}, u32[]{:S(2)}) collective-permute-start(bf16[64,2048]{1,0:T(8,128)(2,1)S(1)} %add_convert_fusion.7), channel_id=1, source_target_pairs={{0,2},{1,5},{2,0},{3,7},{4,6},{5,1},{6,4},{7,3},{8,10},{9,13},{10,... | collective-permute-start | bytes 786440 | tf_op jit(solution)/shard_map/ppermute | solution.py:412
  78.2 10.2 %collective-permute-start.25 = (bf16[64,2048]{1,0:T(8,128)(2,1)S(1)}, bf16[64,2048]{1,0:T(8,128)(2,1)S(1)}, u32[]{:S(2)}, u32[]{:S(2)}) collective-permute-start(bf16[64,2048]{1,0:T(8,128)(2,1)S(1)} %get-tuple-element.163), channel_id=1, source_target_pairs={{0,4},{1,3},{2,6},{3,1},{4,0},{5,7},{6,2},{7,5},{8,12},{9,11},{10,... | collective-permute-start | bytes 786440 | tf_op jit(solution)/shard_map/ppermute | solution.py:412
  83.7 8.2 %collective-permute-start.27 = (bf16[64,2048]{1,0:T(8,128)(2,1)S(1)}, bf16[64,2048]{1,0:T(8,128)(2,1)S(1)}, u32[]{:S(2)}, u32[]{:S(2)}) collective-permute-start(bf16[64,2048]{1,0:T(8,128)(2,1)S(1)} %add_convert_fusion), channel_id=1, source_target_pairs={{0,8},{2,10},{4,12},{6,14},{8,16},{10,18},{12,20},{14,22},{16,24},... | collective-permute-start | bytes 786440 | tf_op jit(solution)/shard_map/ppermute | solution.py:416
  (4 other events, 25.5 us)

commit v11 on v10

--- a/solution.py
+++ b/solution.py
@@ -63,7 +63,7 @@
     rows, reqs = rows_all // 2, reqs_all // 2
     drafts = rows // reqs
     heads = q_buf.shape[1] // head_size
-    groups = [[], [], [], []]
+    groups = [[], [], [], [], [], [], []]
 
     def fetch(group, source, target):
         at = sum(len(g) for g in groups)
@@ -79,23 +79,21 @@
         half = 1 - core if i == 0 else core
         return pl.ds(half * reqs, reqs)
 
-    fetch(0, ids_in, i_buf)
-    fetch(0, weights_in, r_buf)
     for i in range(2):
         here = pl.ds(i * rows, rows)
-        fetch(0, queries.at[half_rows(i)], q_buf.at[here])
-        fetch(0, cache_keys.at[half_reqs(i)], k_buf.at[pl.ds(i * reqs, reqs)])
-        fetch(0, draft_kv.at[:, half_rows(i)], d_buf.at[:, here])
+        fetch(i, queries.at[half_rows(i)], q_buf.at[here])
+        fetch(i, cache_keys.at[half_reqs(i)], k_buf.at[pl.ds(i * reqs, reqs)])
+        fetch(i, draft_kv.at[:, half_rows(i)], d_buf.at[:, here])
+    fetch(6, ids_in, i_buf)
+    fetch(6, weights_in, r_buf)
     for i in range(2):
         here = pl.ds(i * rows, rows)
-        fetch(1, cache_values.at[half_reqs(i)], v_buf.at[pl.ds(i * reqs, reqs)])
-        fetch(1, out_gate.at[half_rows(i)], g_buf.at[here])
+        fetch(4 + i, cache_values.at[half_reqs(i)], v_buf.at[pl.ds(i * reqs, reqs)])
+        fetch(4 + i, out_gate.at[half_rows(i)], g_buf.at[here])
     fetch(2, o_weight, w_buf)
     fetch(3, hidden_in, h_buf)
     fetch(3, gain_in, gain_ref)
 
-    for copy in groups[0]:
-        copy.wait()
     scale = 1.0 / math.sqrt(head_size)
     stacked = heads * drafts
     slot = lax.broadcasted_iota(jnp.int32, (stacked, context_len), 1)
@@ -109,6 +107,9 @@
         lens.append((cache_len_ref[place], draft_len_ref[place]))
     probs = []
     for r in range(reqs_all):
+        if r % reqs == 0:
+            for copy in groups[r // reqs]:
+                copy.wait()
         span = slice(r * drafts, (r + 1) * drafts)
         query = jnp.concatenate(
             [q_buf[span, h * head_size : (h + 1) * head_size] for h in range(heads)], axis=0
@@ -129,6 +130,8 @@
             draft_probs, axis=-1, keepdims=True
         )
         probs.append((cache_probs.astype(BF16), draft_probs.astype(BF16), denominator))
+    for copy in groups[6]:
+        copy.wait()
     row = lax.broadcasted_iota(jnp.int32, table_ref.shape[::-1], 0)
     table = jnp.zeros(row.shape, F32)
     for k in range(i_buf.shape[0]):
@@ -138,9 +141,10 @@
         table = jnp.where(row == index, high, table)
         table = jnp.where(row == index + experts, weight - high, table)
     table_ref[...] = table.T.astype(BF16)
-    for copy in groups[1]:
-        copy.wait()
     for r in range(reqs_all):
+        if r % reqs == 0:
+            for copy in groups[4 + r // reqs]:
+                copy.wait()
         span = slice(r * drafts, (r + 1) * drafts)
         cache_probs, draft_probs, denominator = probs[r]
         context = _dot(cache_probs, v_buf[r]) + _dot(draft_probs, d_buf[1, span])

time: 93 us -> 93 us (level)
  no operation moved by 1% of the time
where the time goes in v11:
time: 93 us; the launch traced here: 92.8 us
  waiting for transfers between devices  35.8 us (38%)
  starting transfers between devices  28.5 us (31%)
  Pallas kernels  27.5 us (30%)
    ppermute x17, starting transfers between devices, across(): return lambda a: lax.ppermute(a, ('wide', 'narrow'), pairs)  20.9 us
    ppermute x17, waiting for transfers between devices, across(): return lambda a: lax.ppermute(a, ('wide', 'narrow'), pairs)  17.8 us
    pallas_call x4, Pallas kernels, plane_experts(): pl.pallas_call(functools.partial(experts_kernel, spans, experts), out_sha...  16.5 us
    ppermute x7, waiting for transfers between devices, shifted(): return lambda a: lax.ppermute(a, 'wide', pairs)  15.8 us
    ppermute x7, starting transfers between devices, shifted(): return lambda a: lax.ppermute(a, 'wide', pairs)  6.49 us
    pallas_call x1, Pallas kernels, hold_weights(): pl.pallas_call(functools.partial(hold_kernel, count), out_shape=[jax.Shap...  5.29 us
    pallas_call x1, Pallas kernels, attention(): pl.pallas_call(functools.partial(attention_kernel, experts), out_shape=(j...  4.64 us
    ppermute x1, waiting for transfers between devices, on_device(): received = lax.ppermute(outgoing, 'narrow', swap)  2.17 us
  transfers between devices with their start and end apart: 28, of which 15 were waited for; matrix products, arithmetic and copies ran while one was open for 1% of the time, Pallas kernels for 29%

profile of v11, /device:TPU:0, one launch (start us, length us, event | category | flops | bytes accessed | tf_op | source)
XLA Modules:
  0.0 92.8 jit_solution(6259326912414159163)
XLA Ops:
  1.0 4.6 %shard_map.145 = (bf16[64,2048]{1,0:T(8,128)(2,1)S(1)}, f32[64,2048]{1,0:T(8,128)S(1)}, bf16[64,128]{1,0:T(8,128)(2,1)S(1)}, f32[1,2048]{1,0:T(1,128)S(1)}) custom-call(s32[1]{0:T(128)} %bitcast.core_ref, s32[8]{0:T(128)} %draft_len_ref.1, s32[8]{0:T(128)} %cache_len_ref.1, s32[10,64]{1,0:T(8,128)} %bitcast.6, f32[10,64]{1,0:T(8,128)} %bitcast.7, ...), custom_call_target="tpu_custom_call" | custom-call | flops 671088640 | bytes 6291456 | tf_op jit(solution)/shard_map/pallas_call | solution.py:183
  5.7 2.2 %collective-permute-done.received_ref = bf16[64,2048]{1,0:T(8,128)(2,1)S(1)} collective-permute-done((bf16[64,2048]{1,0:T(8,128)(2,1)S(1)}, bf16[64,2048]{1,0:T(8,128)(2,1)S(1)}, u32[]{:S(2)}, u32[]{:S(2)}) %collective-permute-start) | collective-permute-done | bytes 262176 | tf_op jit(solution)/shard_map/ppermute | solution.py:409
  8.1 3.0 %collective-permute-start.1 = (bf16[64,2176]{1,0:T(8,128)(2,1)S(1)}, bf16[64,2176]{1,0:T(8,128)(2,1)S(1)}, u32[]{:S(2)}, u32[]{:S(2)}) collective-permute-start(bf16[64,2176]{1,0:T(8,128)(2,1)S(1)} %get-tuple-element.87.refs_0_), channel_id=1, source_target_pairs={{0,8},{2,10},{4,12},{6,14},{8,16},{10,18},{12,20},{14,22},{16,24},... | collective-permute-start | bytes 835592 | tf_op jit(solution)/shard_map/ppermute | solution.py:420
  12.7 5.3 %shard_map.147 = (s32[2]{0:T(128)S(1)}, bf16[1,2048,512]{2,1,0:T(8,128)(2,1)S(1)}, bf16[1,2048,512]{2,1,0:T(8,128)(2,1)S(1)}, bf16[1,512,2048]{2,1,0:T(8,128)(2,...) custom-call(s32[2]{0:T(128)S(1)} %pad_add_fusion.where_ref, ...), custom_call_target="tpu_custom_call" | custom-call | flops 200000000 | tf_op jit(solution)/shard_map/pallas_call | solution.py:306
  18.0 2.1 %collective-permute-done.1.refs_0_ = bf16[64,2176]{1,0:T(8,128)(2,1)S(1)} collective-permute-done((bf16[64,2176]{1,0:T(8,128)(2,1)S(1)}, bf16[64,2176]{1,0:T(8,128)(2,1)S(1)}, u32[]{:S(2)}, u32[]{:S(2)}) %collective-permute-start.1) | collective-permute-done | bytes 278560 | tf_op jit(solution)/shard_map/ppermute | solution.py:420
  20.1 1.5 %collective-permute-start.6 = (bf16[64,2176]{1,0:T(8,128)(2,1)S(1)}, bf16[64,2176]{1,0:T(8,128)(2,1)S(1)}, u32[]{:S(2)}, u32[]{:S(2)}) collective-permute-start(bf16[64,2176]{1,0:T(8,128)(2,1)S(1)} %collective-permute-done.1.refs_0_), channel_id=1, source_target_pairs={{0,2},{1,5},{2,0},{3,7},{4,6},{5,1},{6,4},{7,3},{8,10},{9,13},{10,... | collective-permute-start | bytes 835592 | tf_op jit(solution)/shard_map/ppermute | solution.py:416
  21.7 1.6 %collective-permute-start.10 = (bf16[128,2176]{1,0:T(8,128)(2,1)S(1)}, bf16[128,2176]{1,0:T(8,128)(2,1)S(1)}, u32[]{:S(2)}, u32[]{:S(2)}) collective-permute-start(bf16[128,2176]{1,0:T(8,128)(2,1)S(1)} %pad_maximum_fusion), channel_id=1, source_target_pairs={{0,4},{1,3},{2,6},{3,1},{4,0},{5,7},{6,2},{7,5},{8,12},{9,11},{10,... | collective-permute-start | bytes 1671176 | tf_op jit(solution)/shard_map/ppermute | solution.py:416
  23.3 6.4 %collective-permute-done.6.refs_1_ = bf16[64,2176]{1,0:T(8,128)(2,1)S(1)} collective-permute-done((bf16[64,2176]{1,0:T(8,128)(2,1)S(1)}, bf16[64,2176]{1,0:T(8,128)(2,1)S(1)}, u32[]{:S(2)}, u32[]{:S(2)}) %collective-permute-start.6) | collective-permute-done | bytes 278560 | tf_op jit(solution)/shard_map/ppermute | solution.py:416
  31.1 1.5 %collective-permute-start.8 = (bf16[64,2176]{1,0:T(8,128)(2,1)S(1)}, bf16[64,2176]{1,0:T(8,128)(2,1)S(1)}, u32[]{:S(2)}, u32[]{:S(2)}) collective-permute-start(bf16[64,2176]{1,0:T(8,128)(2,1)S(1)} %collective-permute-done.7.refs_0_), channel_id=1, source_target_pairs={{0,2},{1,5},{2,0},{3,7},{4,6},{5,1},{6,4},{7,3},{8,10},{9,13},{10,... | collective-permute-start | bytes 835592 | tf_op jit(solution)/shard_map/ppermute | solution.py:416
  33.2 4.1 %shard_map.150 = (bf16[64,2048]{1,0:T(8,128)(2,1)S(1)}, bf16[64,2048]{1,0:T(8,128)(2,1)S(1)}, bf16[64,2048]{1,0:T(8,128)(2,1)S(1)}, bf16[64,2048]{1,0:T(8,128)(2,1)S(1)}) custom-call(s32[2]{0:T(128)S(1)} %get-tuple-element.99.where_ref, bf16[64,2176]{1,0:T(8,128)(2,1)S(1)} %get-tuple-element.87.refs_0_, bf16[64,2176]{1,0:T(8,128)(2,1)S(1)} %collective-permute-done.2.refs_1_, ...), custom_call_target="tpu_custom_call" | custom-call | flops 200000000 | tf_op jit(solution)/shard_map/pallas_call | solution.py:339
  37.3 3.4 %collective-permute-done.8.refs_1_ = bf16[64,2176]{1,0:T(8,128)(2,1)S(1)} collective-permute-done((bf16[64,2176]{1,0:T(8,128)(2,1)S(1)}, bf16[64,2176]{1,0:T(8,128)(2,1)S(1)}, u32[]{:S(2)}, u32[]{:S(2)}) %collective-permute-start.8) | collective-permute-done | bytes 278560 | tf_op jit(solution)/shard_map/ppermute | solution.py:416
  42.3 1.8 %collective-permute-start.13 = (bf16[128,2176]{1,0:T(8,128)(2,1)S(1)}, bf16[128,2176]{1,0:T(8,128)(2,1)S(1)}, u32[]{:S(2)}, u32[]{:S(2)}) collective-permute-start(bf16[128,2176]{1,0:T(8,128)(2,1)S(1)} %pad_maximum_fusion.2), channel_id=1, source_target_pairs={{0,4},{1,3},{2,6},{3,1},{4,0},{5,7},{6,2},{7,5},{8,12},{9,11},{10,... | collective-permute-start | bytes 1671176 | tf_op jit(solution)/shard_map/ppermute | solution.py:416
  45.2 4.1 %shard_map.152 = (bf16[128,2048]{1,0:T(8,128)(2,1)S(1)}, bf16[128,2048]{1,0:T(8,128)(2,1)S(1)}) custom-call(s32[2]{0:T(128)S(1)} %get-tuple-element.99.where_ref, bf16[64,2176]{1,0:T(8,128)(2,1)S(1)} %collective-permute-done.1.refs_0_, bf16[64,2176]{1,0:T(8,128)(2,1)S(1)} %collective-permute-done.6.refs_1_, ...), custom_call_target="tpu_custom_call" | custom-call | flops 200000000 | tf_op jit(solution)/shard_map/pallas_call | solution.py:339
  51.6 1.9 %collective-permute-start.16 = (bf16[128,2048]{1,0:T(8,128)(2,1)S(1)}, bf16[128,2048]{1,0:T(8,128)(2,1)S(1)}, u32[]{:S(2)}, u32[]{:S(2)}) collective-permute-start(bf16[128,2048]{1,0:T(8,128)(2,1)S(1)} %get-tuple-element.133), channel_id=1, source_target_pairs={{0,24},{2,26},{4,28},{6,30},{8,0},{10,2},{12,4},{14,6},{16,8},{18,... | collective-permute-start | bytes 1572872 | tf_op jit(solution)/shard_map/ppermute | solution.py:420
  53.5 4.1 %shard_map.154 = (bf16[64,2048]{1,0:T(8,128)(2,1)S(1)}, bf16[64,2048]{1,0:T(8,128)(2,1)S(1)}, bf16[64,2048]{1,0:T(8,128)(2,1)S(1)}, bf16[64,2048]{1,0:T(8,128)(2,1)S(1)}) custom-call(s32[2]{0:T(128)S(1)} %get-tuple-element.99.where_ref, bf16[64,2176]{1,0:T(8,128)(2,1)S(1)} %collective-permute-done.7.refs_0_, ...), custom_call_target="tpu_custom_call" | custom-call | flops 200000000 | tf_op jit(solution)/shard_map/pallas_call | solution.py:339
  57.7 1.8 %collective-permute-start.15 = (bf16[64,2048]{1,0:T(8,128)(2,1)S(1)}, bf16[64,2048]{1,0:T(8,128)(2,1)S(1)}, u32[]{:S(2)}, u32[]{:S(2)}) collective-permute-start(bf16[64,2048]{1,0:T(8,128)(2,1)S(1)} %get-tuple-element.132), channel_id=1, source_target_pairs={{0,4},{1,3},{2,6},{3,1},{4,0},{5,7},{6,2},{7,5},{8,12},{9,11},{10,... | collective-permute-start | bytes 786440 | tf_op jit(solution)/shard_map/ppermute | solution.py:416
  59.7 1.5 %collective-permute-start.18 = (bf16[64,2048]{1,0:T(8,128)(2,1)S(1)}, bf16[64,2048]{1,0:T(8,128)(2,1)S(1)}, u32[]{:S(2)}, u32[]{:S(2)}) collective-permute-start(bf16[64,2048]{1,0:T(8,128)(2,1)S(1)} %get-tuple-element.137), channel_id=1, source_target_pairs={{0,4},{1,3},{2,6},{3,1},{4,0},{5,7},{6,2},{7,5},{8,12},{9,11},{10,... | collective-permute-start | bytes 786440 | tf_op jit(solution)/shard_map/ppermute | solution.py:416
  61.2 4.1 %shard_map.156 = (bf16[64,2048]{1,0:T(8,128)(2,1)S(1)}, bf16[64,2048]{1,0:T(8,128)(2,1)S(1)}, bf16[64,2048]{1,0:T(8,128)(2,1)S(1)}, bf16[64,2048]{1,0:T(8,128)(2,1)S(1)}) custom-call(s32[2]{0:T(128)S(1)} %get-tuple-element.99.where_ref, bf16[64,2176]{1,0:T(8,128)(2,1)S(1)} %collective-permute-done.9.refs_0_, ...), custom_call_target="tpu_custom_call" | custom-call | flops 200000000 | tf_op jit(solution)/shard_map/pallas_call | solution.py:339
  68.5 4.0 %collective-permute-done.19 = bf16[128,2048]{1,0:T(8,128)(2,1)S(1)} collective-permute-done((bf16[128,2048]{1,0:T(8,128)(2,1)S(1)}, bf16[128,2048]{1,0:T(8,128)(2,1)S(1)}, u32[]{:S(2)}, u32[]{:S(2)}) %collective-permute-start.19) | collective-permute-done | bytes 524320 | tf_op jit(solution)/shard_map/ppermute | solution.py:420
  72.5 1.9 %collective-permute-done.17 = bf16[64,2048]{1,0:T(8,128)(2,1)S(1)} collective-permute-done((bf16[64,2048]{1,0:T(8,128)(2,1)S(1)}, bf16[64,2048]{1,0:T(8,128)(2,1)S(1)}, u32[]{:S(2)}, u32[]{:S(2)}) %collective-permute-start.17) | collective-permute-done | bytes 262176 | tf_op jit(solution)/shard_map/ppermute | solution.py:416
  76.3 1.8 %collective-permute-start.24 = (bf16[64,2048]{1,0:T(8,128)(2,1)S(1)}, bf16[64,2048]{1,0:T(8,128)(2,1)S(1)}, u32[]{:S(2)}, u32[]{:S(2)}) collective-permute-start(bf16[64,2048]{1,0:T(8,128)(2,1)S(1)} %get-tuple-element.164), channel_id=1, source_target_pairs={{0,4},{1,3},{2,6},{3,1},{4,0},{5,7},{6,2},{7,5},{8,12},{9,11},{10,... | collective-permute-start | bytes 786440 | tf_op jit(solution)/shard_map/ppermute | solution.py:416
  78.4 4.5 %collective-permute-done.23 = bf16[64,2048]{1,0:T(8,128)(2,1)S(1)} collective-permute-done((bf16[64,2048]{1,0:T(8,128)(2,1)S(1)}, bf16[64,2048]{1,0:T(8,128)(2,1)S(1)}, u32[]{:S(2)}, u32[]{:S(2)}) %collective-permute-start.23) | collective-permute-done | bytes 262176 | tf_op jit(solution)/shard_map/ppermute | solution.py:420
  85.7 2.7 %collective-permute-done.25.refs_1_ = bf16[64,2048]{1,0:T(8,128)(2,1)S(1)} collective-permute-done((bf16[64,2048]{1,0:T(8,128)(2,1)S(1)}, bf16[64,2048]{1,0:T(8,128)(2,1)S(1)}, u32[]{:S(2)}, u32[]{:S(2)}) %collective-permute-start.25) | collective-permute-done | bytes 262176 | tf_op jit(solution)/shard_map/ppermute | solution.py:416
  88.4 3.6 %collective-permute-done.27.refs_3_ = bf16[64,2048]{1,0:T(8,128)(2,1)S(1)} collective-permute-done((bf16[64,2048]{1,0:T(8,128)(2,1)S(1)}, bf16[64,2048]{1,0:T(8,128)(2,1)S(1)}, u32[]{:S(2)}, u32[]{:S(2)}) %collective-permute-start.27) | collective-permute-done | bytes 262176 | tf_op jit(solution)/shard_map/ppermute | solution.py:420
  (63 shorter events, 19.0 us)
Async XLA Ops:
  0.0 12.7 %collective-permute-start.3 = (bf16[1,2048,512]{2,1,0:T(8,128)(2,1)}, bf16[1,2048,512]{2,1,0:T(8,128)(2,1)S(1)}, u32[]{:S(2)}, u32[]{:S(2)}) collective-permute-start(bf16[1,2048,512]{2,1,0:T(8,128)(2,1)} %refs_0_.1), channel_id=1, source_target_pairs={{0,1},{1,0},{2,3},{3,2},{4,5},{5,4},{6,7},{7,6},{8,9},{9,8},{10,11... | collective-permute-start | bytes 6291464 | tf_op jit(solution)/shard_map/ppermute | solution.py:403
  0.5 12.3 %collective-permute-start.4 = (bf16[1,2048,512]{2,1,0:T(8,128)(2,1)}, bf16[1,2048,512]{2,1,0:T(8,128)(2,1)}, u32[]{:S(2)}, u32[]{:S(2)}) collective-permute-start(bf16[1,2048,512]{2,1,0:T(8,128)(2,1)} %refs_1_.1), channel_id=1, source_target_pairs={{0,1},{1,0},{2,3},{3,2},{4,5},{5,4},{6,7},{7,6},{8,9},{9,8},{10,11... | collective-permute-start | bytes 6291464 | tf_op jit(solution)/shard_map/ppermute | solution.py:403
  0.5 12.2 %collective-permute-start.5 = (bf16[1,512,2048]{2,1,0:T(8,128)(2,1)}, bf16[1,512,2048]{2,1,0:T(8,128)(2,1)}, u32[]{:S(2)}, u32[]{:S(2)}) collective-permute-start(bf16[1,512,2048]{2,1,0:T(8,128)(2,1)} %refs_2_.1), channel_id=1, source_target_pairs={{0,1},{1,0},{2,3},{3,2},{4,5},{5,4},{6,7},{7,6},{8,9},{9,8},{10,11... | collective-permute-start | bytes 6291464 | tf_op jit(solution)/shard_map/ppermute | solution.py:403
  8.1 12.0 %collective-permute-start.1 = (bf16[64,2176]{1,0:T(8,128)(2,1)S(1)}, bf16[64,2176]{1,0:T(8,128)(2,1)S(1)}, u32[]{:S(2)}, u32[]{:S(2)}) collective-permute-start(bf16[64,2176]{1,0:T(8,128)(2,1)S(1)} %get-tuple-element.87.refs_0_), channel_id=1, source_target_pairs={{0,8},{2,10},{4,12},{6,14},{8,16},{10,18},{12,20},{14,22},{16,24},... | collective-permute-start | bytes 835592 | tf_op jit(solution)/shard_map/ppermute | solution.py:420
  11.1 9.0 %collective-permute-start.2 = (bf16[64,2176]{1,0:T(8,128)(2,1)S(1)}, bf16[64,2176]{1,0:T(8,128)(2,1)S(1)}, u32[]{:S(2)}, u32[]{:S(2)}) collective-permute-start(bf16[64,2176]{1,0:T(8,128)(2,1)S(1)} %get-tuple-element.87.refs_0_), channel_id=1, source_target_pairs={{0,2},{1,5},{2,0},{3,7},{4,6},{5,1},{6,4},{7,3},{8,10},{9,13},{10,... | collective-permute-start | bytes 835592 | tf_op jit(solution)/shard_map/ppermute | solution.py:416
  20.1 9.5 %collective-permute-start.6 = (bf16[64,2176]{1,0:T(8,128)(2,1)S(1)}, bf16[64,2176]{1,0:T(8,128)(2,1)S(1)}, u32[]{:S(2)}, u32[]{:S(2)}) collective-permute-start(bf16[64,2176]{1,0:T(8,128)(2,1)S(1)} %collective-permute-done.1.refs_0_), channel_id=1, source_target_pairs={{0,2},{1,5},{2,0},{3,7},{4,6},{5,1},{6,4},{7,3},{8,10},{9,13},{10,... | collective-permute-start | bytes 835592 | tf_op jit(solution)/shard_map/ppermute | solution.py:416
  21.6 9.5 %collective-permute-start.7 = (bf16[64,2176]{1,0:T(8,128)(2,1)S(1)}, bf16[64,2176]{1,0:T(8,128)(2,1)S(1)}, u32[]{:S(2)}, u32[]{:S(2)}) collective-permute-start(bf16[64,2176]{1,0:T(8,128)(2,1)S(1)} %collective-permute-done.1.refs_0_), channel_id=1, source_target_pairs={{0,8},{2,10},{4,12},{6,14},{8,16},{10,18},{12,20},{14,22},{16,24},... | collective-permute-start | bytes 835592 | tf_op jit(solution)/shard_map/ppermute | solution.py:420
  21.7 11.6 %collective-permute-start.10 = (bf16[128,2176]{1,0:T(8,128)(2,1)S(1)}, bf16[128,2176]{1,0:T(8,128)(2,1)S(1)}, u32[]{:S(2)}, u32[]{:S(2)}) collective-permute-start(bf16[128,2176]{1,0:T(8,128)(2,1)S(1)} %pad_maximum_fusion), channel_id=1, source_target_pairs={{0,4},{1,3},{2,6},{3,1},{4,0},{5,7},{6,2},{7,5},{8,12},{9,11},{10,... | collective-permute-start | bytes 1671176 | tf_op jit(solution)/shard_map/ppermute | solution.py:416
  31.1 9.6 %collective-permute-start.8 = (bf16[64,2176]{1,0:T(8,128)(2,1)S(1)}, bf16[64,2176]{1,0:T(8,128)(2,1)S(1)}, u32[]{:S(2)}, u32[]{:S(2)}) collective-permute-start(bf16[64,2176]{1,0:T(8,128)(2,1)S(1)} %collective-permute-done.7.refs_0_), channel_id=1, source_target_pairs={{0,2},{1,5},{2,0},{3,7},{4,6},{5,1},{6,4},{7,3},{8,10},{9,13},{10,... | collective-permute-start | bytes 835592 | tf_op jit(solution)/shard_map/ppermute | solution.py:416
  32.6 8.3 %collective-permute-start.9 = (bf16[64,2176]{1,0:T(8,128)(2,1)S(1)}, bf16[64,2176]{1,0:T(8,128)(2,1)S(1)}, u32[]{:S(2)}, u32[]{:S(2)}) collective-permute-start(bf16[64,2176]{1,0:T(8,128)(2,1)S(1)} %collective-permute-done.7.refs_0_), channel_id=1, source_target_pairs={{0,8},{2,10},{4,12},{6,14},{8,16},{10,18},{12,20},{14,22},{16,24},... | collective-permute-start | bytes 835592 | tf_op jit(solution)/shard_map/ppermute | solution.py:420
  32.6 12.6 %collective-permute-start.12 = (bf16[128,2176]{1,0:T(8,128)(2,1)S(1)}, bf16[128,2176]{1,0:T(8,128)(2,1)S(1)}, u32[]{:S(2)}, u32[]{:S(2)}) collective-permute-start(bf16[128,2176]{1,0:T(8,128)(2,1)S(1)} %pad_maximum_fusion.1), channel_id=1, source_target_pairs={{0,4},{1,3},{2,6},{3,1},{4,0},{5,7},{6,2},{7,5},{8,12},{9,11},{10,... | collective-permute-start | bytes 1671176 | tf_op jit(solution)/shard_map/ppermute | solution.py:416
  40.9 9.5 %collective-permute-start.11 = (bf16[64,2176]{1,0:T(8,128)(2,1)S(1)}, bf16[64,2176]{1,0:T(8,128)(2,1)S(1)}, u32[]{:S(2)}, u32[]{:S(2)}) collective-permute-start(bf16[64,2176]{1,0:T(8,128)(2,1)S(1)} %collective-permute-done.9.refs_0_), channel_id=1, source_target_pairs={{0,2},{1,5},{2,0},{3,7},{4,6},{5,1},{6,4},{7,3},{8,10},{9,13},{10,... | collective-permute-start | bytes 835592 | tf_op jit(solution)/shard_map/ppermute | solution.py:416
  42.3 11.3 %collective-permute-start.13 = (bf16[128,2176]{1,0:T(8,128)(2,1)S(1)}, bf16[128,2176]{1,0:T(8,128)(2,1)S(1)}, u32[]{:S(2)}, u32[]{:S(2)}) collective-permute-start(bf16[128,2176]{1,0:T(8,128)(2,1)S(1)} %pad_maximum_fusion.2), channel_id=1, source_target_pairs={{0,4},{1,3},{2,6},{3,1},{4,0},{5,7},{6,2},{7,5},{8,12},{9,11},{10,... | collective-permute-start | bytes 1671176 | tf_op jit(solution)/shard_map/ppermute | solution.py:416
  50.5 10.7 %collective-permute-start.14 = (bf16[128,2176]{1,0:T(8,128)(2,1)S(1)}, bf16[128,2176]{1,0:T(8,128)(2,1)S(1)}, u32[]{:S(2)}, u32[]{:S(2)}) collective-permute-start(bf16[128,2176]{1,0:T(8,128)(2,1)S(1)} %pad_maximum_fusion.3), channel_id=1, source_target_pairs={{0,4},{1,3},{2,6},{3,1},{4,0},{5,7},{6,2},{7,5},{8,12},{9,11},{10,... | collective-permute-start | bytes 1671176 | tf_op jit(solution)/shard_map/ppermute | solution.py:416
  51.6 13.8 %collective-permute-start.16 = (bf16[128,2048]{1,0:T(8,128)(2,1)S(1)}, bf16[128,2048]{1,0:T(8,128)(2,1)S(1)}, u32[]{:S(2)}, u32[]{:S(2)}) collective-permute-start(bf16[128,2048]{1,0:T(8,128)(2,1)S(1)} %get-tuple-element.133), channel_id=1, source_target_pairs={{0,24},{2,26},{4,28},{6,30},{8,0},{10,2},{12,4},{14,6},{16,8},{18,... | collective-permute-start | bytes 1572872 | tf_op jit(solution)/shard_map/ppermute | solution.py:420
  59.5 13.0 %collective-permute-start.19 = (bf16[128,2048]{1,0:T(8,128)(2,1)S(1)}, bf16[128,2048]{1,0:T(8,128)(2,1)S(1)}, u32[]{:S(2)}, u32[]{:S(2)}) collective-permute-start(bf16[128,2048]{1,0:T(8,128)(2,1)S(1)} %get-tuple-element.138), channel_id=1, source_target_pairs={{0,24},{2,26},{4,28},{6,30},{8,0},{10,2},{12,4},{14,6},{16,8},{18,... | collective-permute-start | bytes 1572872 | tf_op jit(solution)/shard_map/ppermute | solution.py:420
  59.7 8.8 %collective-permute-start.18 = (bf16[64,2048]{1,0:T(8,128)(2,1)S(1)}, bf16[64,2048]{1,0:T(8,128)(2,1)S(1)}, u32[]{:S(2)}, u32[]{:S(2)}) collective-permute-start(bf16[64,2048]{1,0:T(8,128)(2,1)S(1)} %get-tuple-element.137), channel_id=1, source_target_pairs={{0,4},{1,3},{2,6},{3,1},{4,0},{5,7},{6,2},{7,5},{8,12},{9,11},{10,... | collective-permute-start | bytes 786440 | tf_op jit(solution)/shard_map/ppermute | solution.py:416
  65.5 9.0 %collective-permute-start.17 = (bf16[64,2048]{1,0:T(8,128)(2,1)S(1)}, bf16[64,2048]{1,0:T(8,128)(2,1)S(1)}, u32[]{:S(2)}, u32[]{:S(2)}) collective-permute-start(bf16[64,2048]{1,0:T(8,128)(2,1)S(1)} %add_convert_fusion.8), channel_id=1, source_target_pairs={{0,2},{1,5},{2,0},{3,7},{4,6},{5,1},{6,4},{7,3},{8,10},{9,13},{10,... | collective-permute-start | bytes 786440 | tf_op jit(solution)/shard_map/ppermute | solution.py:416
  66.1 8.4 %collective-permute-start.20 = (bf16[64,2048]{1,0:T(8,128)(2,1)S(1)}, bf16[64,2048]{1,0:T(8,128)(2,1)S(1)}, u32[]{:S(2)}, u32[]{:S(2)}) collective-permute-start(bf16[64,2048]{1,0:T(8,128)(2,1)S(1)} %get-tuple-element.139), channel_id=1, source_target_pairs={{0,4},{1,3},{2,6},{3,1},{4,0},{5,7},{6,2},{7,5},{8,12},{9,11},{10,... | collective-permute-start | bytes 786440 | tf_op jit(solution)/shard_map/ppermute | solution.py:416
  67.5 10.9 %collective-permute-start.22 = (bf16[64,2048]{1,0:T(8,128)(2,1)S(1)}, bf16[64,2048]{1,0:T(8,128)(2,1)S(1)}, u32[]{:S(2)}, u32[]{:S(2)}) collective-permute-start(bf16[64,2048]{1,0:T(8,128)(2,1)S(1)} %get-tuple-element.143), channel_id=1, source_target_pairs={{0,4},{1,3},{2,6},{3,1},{4,0},{5,7},{6,2},{7,5},{8,12},{9,11},{10,... | collective-permute-start | bytes 786440 | tf_op jit(solution)/shard_map/ppermute | solution.py:416
  74.6 8.4 %collective-permute-start.23 = (bf16[64,2048]{1,0:T(8,128)(2,1)S(1)}, bf16[64,2048]{1,0:T(8,128)(2,1)S(1)}, u32[]{:S(2)}, u32[]{:S(2)}) collective-permute-start(bf16[64,2048]{1,0:T(8,128)(2,1)S(1)} %add_convert_fusion.6), channel_id=1, source_target_pairs={{0,8},{2,10},{4,12},{6,14},{8,16},{10,18},{12,20},{14,22},{16,24},... | collective-permute-start | bytes 786440 | tf_op jit(solution)/shard_map/ppermute | solution.py:420
  75.6 8.0 %collective-permute-start.21 = (bf16[64,2048]{1,0:T(8,128)(2,1)S(1)}, bf16[64,2048]{1,0:T(8,128)(2,1)S(1)}, u32[]{:S(2)}, u32[]{:S(2)}) collective-permute-start(bf16[64,2048]{1,0:T(8,128)(2,1)S(1)} %add_convert_fusion.7), channel_id=1, source_target_pairs={{0,2},{1,5},{2,0},{3,7},{4,6},{5,1},{6,4},{7,3},{8,10},{9,13},{10,... | collective-permute-start | bytes 786440 | tf_op jit(solution)/shard_map/ppermute | solution.py:416
  78.2 10.2 %collective-permute-start.25 = (bf16[64,2048]{1,0:T(8,128)(2,1)S(1)}, bf16[64,2048]{1,0:T(8,128)(2,1)S(1)}, u32[]{:S(2)}, u32[]{:S(2)}) collective-permute-start(bf16[64,2048]{1,0:T(8,128)(2,1)S(1)} %get-tuple-element.163), channel_id=1, source_target_pairs={{0,4},{1,3},{2,6},{3,1},{4,0},{5,7},{6,2},{7,5},{8,12},{9,11},{10,... | collective-permute-start | bytes 786440 | tf_op jit(solution)/shard_map/ppermute | solution.py:416
  83.7 8.2 %collective-permute-start.27 = (bf16[64,2048]{1,0:T(8,128)(2,1)S(1)}, bf16[64,2048]{1,0:T(8,128)(2,1)S(1)}, u32[]{:S(2)}, u32[]{:S(2)}) collective-permute-start(bf16[64,2048]{1,0:T(8,128)(2,1)S(1)} %add_convert_fusion), channel_id=1, source_target_pairs={{0,8},{2,10},{4,12},{6,14},{8,16},{10,18},{12,20},{14,22},{16,24},... | collective-permute-start | bytes 786440 | tf_op jit(solution)/shard_map/ppermute | solution.py:420
  (4 other events, 25.5 us)

commit v12 on v10

--- a/solution.py
+++ b/solution.py
@@ -343,18 +343,33 @@
     )(where, *arrays, *weights)
 
 
-def final_kernel(token_ref, residual_ref, *refs):
-    out_ref = refs[-1]
-    mix = refs[0][...].astype(F32)
-    for ref in refs[1:-1]:
-        mix = mix + ref[...].astype(F32)
-    out_ref[...] = (residual_ref[...] + mix).astype(BF16)
+def final_kernel(tiles, token_ref, residual_ref, *refs):
+    pieces, out_ref, made, sems = refs[:-3], refs[-3], refs[-2], refs[-1]
+    size = residual_ref.shape[0] // tiles
+    copies = []
+    for t in range(tiles):
+        span = slice(t * size, (t + 1) * size)
+        mix = pieces[0][span].astype(F32)
+        for ref in pieces[1:]:
+            mix = mix + ref[span].astype(F32)
+        made[span] = (residual_ref[span] + mix).astype(BF16)
+        rows = pl.ds(t * size, size)
+        copy = pltpu.make_async_copy(made.at[rows], out_ref.at[rows], sems.at[t])
+        copy.start()
+        copies.append(copy)
+    for copy in copies:
+        copy.wait()
 
 
 def final_sum(token, residual, pieces):
+    tiles = max(1, residual.shape[0] // 16)
+    vmem = pl.BlockSpec(memory_space=pltpu.VMEM)
     return pl.pallas_call(
-        final_kernel,
+        functools.partial(final_kernel, tiles),
         out_shape=jax.ShapeDtypeStruct(residual.shape, BF16),
+        in_specs=[vmem] * (2 + len(pieces)),
+        out_specs=pl.BlockSpec(memory_space=pl.ANY),
+        scratch_shapes=[pltpu.VMEM(residual.shape, BF16), pltpu.SemaphoreType.DMA((tiles,))],
         compiler_params=pltpu.CompilerParams(vmem_limit_bytes=16 * 1024 * 1024),
     )(token, residual, *pieces)
 

time: 93 us -> 93.1 us (level)
  no operation moved by 1% of the time
where the time goes in v12:
time: 93.1 us; the launch traced here: 92.9 us
  waiting for transfers between devices  35.8 us (38%)
  starting transfers between devices  28.5 us (31%)
  Pallas kernels  27.5 us (30%)
    ppermute x17, starting transfers between devices, across(): return lambda a: lax.ppermute(a, ('wide', 'narrow'), pairs)  20.9 us
    ppermute x17, waiting for transfers between devices, across(): return lambda a: lax.ppermute(a, ('wide', 'narrow'), pairs)  17.8 us
    pallas_call x4, Pallas kernels, plane_experts(): pl.pallas_call(functools.partial(experts_kernel, spans, experts), out_sha...  16.5 us
    ppermute x7, waiting for transfers between devices, shifted(): return lambda a: lax.ppermute(a, 'wide', pairs)  15.8 us
    ppermute x7, starting transfers between devices, shifted(): return lambda a: lax.ppermute(a, 'wide', pairs)  6.49 us
    pallas_call x1, Pallas kernels, hold_weights(): pl.pallas_call(functools.partial(hold_kernel, count), out_shape=[jax.Shap...  5.29 us
    pallas_call x1, Pallas kernels, attention(): pl.pallas_call(functools.partial(attention_kernel, experts), out_shape=(j...  4.64 us
    ppermute x1, waiting for transfers between devices, on_device(): received = lax.ppermute(outgoing, 'narrow', swap)  2.18 us
  transfers between devices with their start and end apart: 28, of which 15 were waited for; matrix products, arithmetic and copies ran while one was open for 1% of the time, Pallas kernels for 29%

profile of v12, /device:TPU:0, one launch (start us, length us, event | category | flops | bytes accessed | tf_op | source)
XLA Modules:
  0.0 92.9 jit_solution(18180263452445560404)
XLA Ops:
  1.0 4.6 %shard_map.145 = (bf16[64,2048]{1,0:T(8,128)(2,1)S(1)}, f32[64,2048]{1,0:T(8,128)S(1)}, bf16[64,128]{1,0:T(8,128)(2,1)S(1)}, f32[1,2048]{1,0:T(1,128)S(1)}) custom-call(s32[1]{0:T(128)} %bitcast.core_ref, s32[8]{0:T(128)} %draft_len_ref.1, s32[8]{0:T(128)} %cache_len_ref.1, s32[10,64]{1,0:T(8,128)} %bitcast.6, f32[10,64]{1,0:T(8,128)} %bitcast.7, ...), custom_call_target="tpu_custom_call" | custom-call | flops 671088640 | bytes 6291456 | tf_op jit(solution)/shard_map/pallas_call | solution.py:179
  5.7 2.2 %collective-permute-done.received_ref = bf16[64,2048]{1,0:T(8,128)(2,1)S(1)} collective-permute-done((bf16[64,2048]{1,0:T(8,128)(2,1)S(1)}, bf16[64,2048]{1,0:T(8,128)(2,1)S(1)}, u32[]{:S(2)}, u32[]{:S(2)}) %collective-permute-start) | collective-permute-done | bytes 262176 | tf_op jit(solution)/shard_map/ppermute | solution.py:420
  8.1 3.0 %collective-permute-start.1 = (bf16[64,2176]{1,0:T(8,128)(2,1)S(1)}, bf16[64,2176]{1,0:T(8,128)(2,1)S(1)}, u32[]{:S(2)}, u32[]{:S(2)}) collective-permute-start(bf16[64,2176]{1,0:T(8,128)(2,1)S(1)} %get-tuple-element.87.refs_0_), channel_id=1, source_target_pairs={{0,8},{2,10},{4,12},{6,14},{8,16},{10,18},{12,20},{14,22},{16,24},... | collective-permute-start | bytes 835592 | tf_op jit(solution)/shard_map/ppermute | solution.py:431
  11.1 1.5 %collective-permute-start.2 = (bf16[64,2176]{1,0:T(8,128)(2,1)S(1)}, bf16[64,2176]{1,0:T(8,128)(2,1)S(1)}, u32[]{:S(2)}, u32[]{:S(2)}) collective-permute-start(bf16[64,2176]{1,0:T(8,128)(2,1)S(1)} %get-tuple-element.87.refs_0_), channel_id=1, source_target_pairs={{0,2},{1,5},{2,0},{3,7},{4,6},{5,1},{6,4},{7,3},{8,10},{9,13},{10,... | collective-permute-start | bytes 835592 | tf_op jit(solution)/shard_map/ppermute | solution.py:427
  12.7 5.3 %shard_map.147 = (s32[2]{0:T(128)S(1)}, bf16[1,2048,512]{2,1,0:T(8,128)(2,1)S(1)}, bf16[1,2048,512]{2,1,0:T(8,128)(2,1)S(1)}, bf16[1,512,2048]{2,1,0:T(8,128)(2,...) custom-call(s32[2]{0:T(128)S(1)} %pad_add_fusion.where_ref, ...), custom_call_target="tpu_custom_call" | custom-call | flops 200000000 | tf_op jit(solution)/shard_map/pallas_call | solution.py:302
  18.0 2.1 %collective-permute-done.1.refs_0_ = bf16[64,2176]{1,0:T(8,128)(2,1)S(1)} collective-permute-done((bf16[64,2176]{1,0:T(8,128)(2,1)S(1)}, bf16[64,2176]{1,0:T(8,128)(2,1)S(1)}, u32[]{:S(2)}, u32[]{:S(2)}) %collective-permute-start.1) | collective-permute-done | bytes 278560 | tf_op jit(solution)/shard_map/ppermute | solution.py:431
  20.1 1.5 %collective-permute-start.6 = (bf16[64,2176]{1,0:T(8,128)(2,1)S(1)}, bf16[64,2176]{1,0:T(8,128)(2,1)S(1)}, u32[]{:S(2)}, u32[]{:S(2)}) collective-permute-start(bf16[64,2176]{1,0:T(8,128)(2,1)S(1)} %collective-permute-done.1.refs_0_), channel_id=1, source_target_pairs={{0,2},{1,5},{2,0},{3,7},{4,6},{5,1},{6,4},{7,3},{8,10},{9,13},{10,... | collective-permute-start | bytes 835592 | tf_op jit(solution)/shard_map/ppermute | solution.py:427
  21.7 1.6 %collective-permute-start.10 = (bf16[128,2176]{1,0:T(8,128)(2,1)S(1)}, bf16[128,2176]{1,0:T(8,128)(2,1)S(1)}, u32[]{:S(2)}, u32[]{:S(2)}) collective-permute-start(bf16[128,2176]{1,0:T(8,128)(2,1)S(1)} %pad_maximum_fusion), channel_id=1, source_target_pairs={{0,4},{1,3},{2,6},{3,1},{4,0},{5,7},{6,2},{7,5},{8,12},{9,11},{10,... | collective-permute-start | bytes 1671176 | tf_op jit(solution)/shard_map/ppermute | solution.py:427
  23.3 6.4 %collective-permute-done.6.refs_1_ = bf16[64,2176]{1,0:T(8,128)(2,1)S(1)} collective-permute-done((bf16[64,2176]{1,0:T(8,128)(2,1)S(1)}, bf16[64,2176]{1,0:T(8,128)(2,1)S(1)}, u32[]{:S(2)}, u32[]{:S(2)}) %collective-permute-start.6) | collective-permute-done | bytes 278560 | tf_op jit(solution)/shard_map/ppermute | solution.py:427
  33.2 4.1 %shard_map.150 = (bf16[64,2048]{1,0:T(8,128)(2,1)S(1)}, bf16[64,2048]{1,0:T(8,128)(2,1)S(1)}, bf16[64,2048]{1,0:T(8,128)(2,1)S(1)}, bf16[64,2048]{1,0:T(8,128)(2,1)S(1)}) custom-call(s32[2]{0:T(128)S(1)} %get-tuple-element.99.where_ref, bf16[64,2176]{1,0:T(8,128)(2,1)S(1)} %get-tuple-element.87.refs_0_, bf16[64,2176]{1,0:T(8,128)(2,1)S(1)} %collective-permute-done.2.refs_1_, ...), custom_call_target="tpu_custom_call" | custom-call | flops 200000000 | tf_op jit(solution)/shard_map/pallas_call | solution.py:335
  37.3 3.4 %collective-permute-done.8.refs_1_ = bf16[64,2176]{1,0:T(8,128)(2,1)S(1)} collective-permute-done((bf16[64,2176]{1,0:T(8,128)(2,1)S(1)}, bf16[64,2176]{1,0:T(8,128)(2,1)S(1)}, u32[]{:S(2)}, u32[]{:S(2)}) %collective-permute-start.8) | collective-permute-done | bytes 278560 | tf_op jit(solution)/shard_map/ppermute | solution.py:427
  42.3 1.8 %collective-permute-start.13 = (bf16[128,2176]{1,0:T(8,128)(2,1)S(1)}, bf16[128,2176]{1,0:T(8,128)(2,1)S(1)}, u32[]{:S(2)}, u32[]{:S(2)}) collective-permute-start(bf16[128,2176]{1,0:T(8,128)(2,1)S(1)} %pad_maximum_fusion.2), channel_id=1, source_target_pairs={{0,4},{1,3},{2,6},{3,1},{4,0},{5,7},{6,2},{7,5},{8,12},{9,11},{10,... | collective-permute-start | bytes 1671176 | tf_op jit(solution)/shard_map/ppermute | solution.py:427
  45.2 4.1 %shard_map.152 = (bf16[128,2048]{1,0:T(8,128)(2,1)S(1)}, bf16[128,2048]{1,0:T(8,128)(2,1)S(1)}) custom-call(s32[2]{0:T(128)S(1)} %get-tuple-element.99.where_ref, bf16[64,2176]{1,0:T(8,128)(2,1)S(1)} %collective-permute-done.1.refs_0_, bf16[64,2176]{1,0:T(8,128)(2,1)S(1)} %collective-permute-done.6.refs_1_, ...), custom_call_target="tpu_custom_call" | custom-call | flops 200000000 | tf_op jit(solution)/shard_map/pallas_call | solution.py:335
  51.6 1.9 %collective-permute-start.16 = (bf16[128,2048]{1,0:T(8,128)(2,1)S(1)}, bf16[128,2048]{1,0:T(8,128)(2,1)S(1)}, u32[]{:S(2)}, u32[]{:S(2)}) collective-permute-start(bf16[128,2048]{1,0:T(8,128)(2,1)S(1)} %get-tuple-element.133), channel_id=1, source_target_pairs={{0,24},{2,26},{4,28},{6,30},{8,0},{10,2},{12,4},{14,6},{16,8},{18,... | collective-permute-start | bytes 1572872 | tf_op jit(solution)/shard_map/ppermute | solution.py:431
  53.5 4.1 %shard_map.154 = (bf16[64,2048]{1,0:T(8,128)(2,1)S(1)}, bf16[64,2048]{1,0:T(8,128)(2,1)S(1)}, bf16[64,2048]{1,0:T(8,128)(2,1)S(1)}, bf16[64,2048]{1,0:T(8,128)(2,1)S(1)}) custom-call(s32[2]{0:T(128)S(1)} %get-tuple-element.99.where_ref, bf16[64,2176]{1,0:T(8,128)(2,1)S(1)} %collective-permute-done.7.refs_0_, ...), custom_call_target="tpu_custom_call" | custom-call | flops 200000000 | tf_op jit(solution)/shard_map/pallas_call | solution.py:335
  57.7 1.8 %collective-permute-start.15 = (bf16[64,2048]{1,0:T(8,128)(2,1)S(1)}, bf16[64,2048]{1,0:T(8,128)(2,1)S(1)}, u32[]{:S(2)}, u32[]{:S(2)}) collective-permute-start(bf16[64,2048]{1,0:T(8,128)(2,1)S(1)} %get-tuple-element.132), channel_id=1, source_target_pairs={{0,4},{1,3},{2,6},{3,1},{4,0},{5,7},{6,2},{7,5},{8,12},{9,11},{10,... | collective-permute-start | bytes 786440 | tf_op jit(solution)/shard_map/ppermute | solution.py:427
  59.7 1.5 %collective-permute-start.18 = (bf16[64,2048]{1,0:T(8,128)(2,1)S(1)}, bf16[64,2048]{1,0:T(8,128)(2,1)S(1)}, u32[]{:S(2)}, u32[]{:S(2)}) collective-permute-start(bf16[64,2048]{1,0:T(8,128)(2,1)S(1)} %get-tuple-element.137), channel_id=1, source_target_pairs={{0,4},{1,3},{2,6},{3,1},{4,0},{5,7},{6,2},{7,5},{8,12},{9,11},{10,... | collective-permute-start | bytes 786440 | tf_op jit(solution)/shard_map/ppermute | solution.py:427
  61.2 4.1 %shard_map.156 = (bf16[64,2048]{1,0:T(8,128)(2,1)S(1)}, bf16[64,2048]{1,0:T(8,128)(2,1)S(1)}, bf16[64,2048]{1,0:T(8,128)(2,1)S(1)}, bf16[64,2048]{1,0:T(8,128)(2,1)S(1)}) custom-call(s32[2]{0:T(128)S(1)} %get-tuple-element.99.where_ref, bf16[64,2176]{1,0:T(8,128)(2,1)S(1)} %collective-permute-done.9.refs_0_, ...), custom_call_target="tpu_custom_call" | custom-call | flops 200000000 | tf_op jit(solution)/shard_map/pallas_call | solution.py:335
  68.5 4.0 %collective-permute-done.19 = bf16[128,2048]{1,0:T(8,128)(2,1)S(1)} collective-permute-done((bf16[128,2048]{1,0:T(8,128)(2,1)S(1)}, bf16[128,2048]{1,0:T(8,128)(2,1)S(1)}, u32[]{:S(2)}, u32[]{:S(2)}) %collective-permute-start.19) | collective-permute-done | bytes 524320 | tf_op jit(solution)/shard_map/ppermute | solution.py:431
  72.5 1.9 %collective-permute-done.17 = bf16[64,2048]{1,0:T(8,128)(2,1)S(1)} collective-permute-done((bf16[64,2048]{1,0:T(8,128)(2,1)S(1)}, bf16[64,2048]{1,0:T(8,128)(2,1)S(1)}, u32[]{:S(2)}, u32[]{:S(2)}) %collective-permute-start.17) | collective-permute-done | bytes 262176 | tf_op jit(solution)/shard_map/ppermute | solution.py:427
  76.3 1.8 %collective-permute-start.24 = (bf16[64,2048]{1,0:T(8,128)(2,1)S(1)}, bf16[64,2048]{1,0:T(8,128)(2,1)S(1)}, u32[]{:S(2)}, u32[]{:S(2)}) collective-permute-start(bf16[64,2048]{1,0:T(8,128)(2,1)S(1)} %get-tuple-element.164), channel_id=1, source_target_pairs={{0,4},{1,3},{2,6},{3,1},{4,0},{5,7},{6,2},{7,5},{8,12},{9,11},{10,... | collective-permute-start | bytes 786440 | tf_op jit(solution)/shard_map/ppermute | solution.py:427
  78.4 4.5 %collective-permute-done.23 = bf16[64,2048]{1,0:T(8,128)(2,1)S(1)} collective-permute-done((bf16[64,2048]{1,0:T(8,128)(2,1)S(1)}, bf16[64,2048]{1,0:T(8,128)(2,1)S(1)}, u32[]{:S(2)}, u32[]{:S(2)}) %collective-permute-start.23) | collective-permute-done | bytes 262176 | tf_op jit(solution)/shard_map/ppermute | solution.py:431
  85.7 2.7 %collective-permute-done.25.refs_1_ = bf16[64,2048]{1,0:T(8,128)(2,1)S(1)} collective-permute-done((bf16[64,2048]{1,0:T(8,128)(2,1)S(1)}, bf16[64,2048]{1,0:T(8,128)(2,1)S(1)}, u32[]{:S(2)}, u32[]{:S(2)}) %collective-permute-start.25) | collective-permute-done | bytes 262176 | tf_op jit(solution)/shard_map/ppermute | solution.py:427
  88.4 3.6 %collective-permute-done.27.refs_3_ = bf16[64,2048]{1,0:T(8,128)(2,1)S(1)} collective-permute-done((bf16[64,2048]{1,0:T(8,128)(2,1)S(1)}, bf16[64,2048]{1,0:T(8,128)(2,1)S(1)}, u32[]{:S(2)}, u32[]{:S(2)}) %collective-permute-start.27) | collective-permute-done | bytes 262176 | tf_op jit(solution)/shard_map/ppermute | solution.py:431
  (63 shorter events, 19.0 us)
Async XLA Ops:
  0.0 12.7 %collective-permute-start.3 = (bf16[1,2048,512]{2,1,0:T(8,128)(2,1)}, bf16[1,2048,512]{2,1,0:T(8,128)(2,1)S(1)}, u32[]{:S(2)}, u32[]{:S(2)}) collective-permute-start(bf16[1,2048,512]{2,1,0:T(8,128)(2,1)} %refs_0_.1), channel_id=1, source_target_pairs={{0,1},{1,0},{2,3},{3,2},{4,5},{5,4},{6,7},{7,6},{8,9},{9,8},{10,11... | collective-permute-start | bytes 6291464 | tf_op jit(solution)/shard_map/ppermute | solution.py:414
  0.5 12.3 %collective-permute-start.4 = (bf16[1,2048,512]{2,1,0:T(8,128)(2,1)}, bf16[1,2048,512]{2,1,0:T(8,128)(2,1)}, u32[]{:S(2)}, u32[]{:S(2)}) collective-permute-start(bf16[1,2048,512]{2,1,0:T(8,128)(2,1)} %refs_1_.1), channel_id=1, source_target_pairs={{0,1},{1,0},{2,3},{3,2},{4,5},{5,4},{6,7},{7,6},{8,9},{9,8},{10,11... | collective-permute-start | bytes 6291464 | tf_op jit(solution)/shard_map/ppermute | solution.py:414
  0.5 12.2 %collective-permute-start.5 = (bf16[1,512,2048]{2,1,0:T(8,128)(2,1)}, bf16[1,512,2048]{2,1,0:T(8,128)(2,1)}, u32[]{:S(2)}, u32[]{:S(2)}) collective-permute-start(bf16[1,512,2048]{2,1,0:T(8,128)(2,1)} %refs_2_.1), channel_id=1, source_target_pairs={{0,1},{1,0},{2,3},{3,2},{4,5},{5,4},{6,7},{7,6},{8,9},{9,8},{10,11... | collective-permute-start | bytes 6291464 | tf_op jit(solution)/shard_map/ppermute | solution.py:414
  8.1 12.0 %collective-permute-start.1 = (bf16[64,2176]{1,0:T(8,128)(2,1)S(1)}, bf16[64,2176]{1,0:T(8,128)(2,1)S(1)}, u32[]{:S(2)}, u32[]{:S(2)}) collective-permute-start(bf16[64,2176]{1,0:T(8,128)(2,1)S(1)} %get-tuple-element.87.refs_0_), channel_id=1, source_target_pairs={{0,8},{2,10},{4,12},{6,14},{8,16},{10,18},{12,20},{14,22},{16,24},... | collective-permute-start | bytes 835592 | tf_op jit(solution)/shard_map/ppermute | solution.py:431
  11.1 9.0 %collective-permute-start.2 = (bf16[64,2176]{1,0:T(8,128)(2,1)S(1)}, bf16[64,2176]{1,0:T(8,128)(2,1)S(1)}, u32[]{:S(2)}, u32[]{:S(2)}) collective-permute-start(bf16[64,2176]{1,0:T(8,128)(2,1)S(1)} %get-tuple-element.87.refs_0_), channel_id=1, source_target_pairs={{0,2},{1,5},{2,0},{3,7},{4,6},{5,1},{6,4},{7,3},{8,10},{9,13},{10,... | collective-permute-start | bytes 835592 | tf_op jit(solution)/shard_map/ppermute | solution.py:427
  20.1 9.5 %collective-permute-start.6 = (bf16[64,2176]{1,0:T(8,128)(2,1)S(1)}, bf16[64,2176]{1,0:T(8,128)(2,1)S(1)}, u32[]{:S(2)}, u32[]{:S(2)}) collective-permute-start(bf16[64,2176]{1,0:T(8,128)(2,1)S(1)} %collective-permute-done.1.refs_0_), channel_id=1, source_target_pairs={{0,2},{1,5},{2,0},{3,7},{4,6},{5,1},{6,4},{7,3},{8,10},{9,13},{10,... | collective-permute-start | bytes 835592 | tf_op jit(solution)/shard_map/ppermute | solution.py:427
  21.6 9.5 %collective-permute-start.7 = (bf16[64,2176]{1,0:T(8,128)(2,1)S(1)}, bf16[64,2176]{1,0:T(8,128)(2,1)S(1)}, u32[]{:S(2)}, u32[]{:S(2)}) collective-permute-start(bf16[64,2176]{1,0:T(8,128)(2,1)S(1)} %collective-permute-done.1.refs_0_), channel_id=1, source_target_pairs={{0,8},{2,10},{4,12},{6,14},{8,16},{10,18},{12,20},{14,22},{16,24},... | collective-permute-start | bytes 835592 | tf_op jit(solution)/shard_map/ppermute | solution.py:431
  21.7 11.6 %collective-permute-start.10 = (bf16[128,2176]{1,0:T(8,128)(2,1)S(1)}, bf16[128,2176]{1,0:T(8,128)(2,1)S(1)}, u32[]{:S(2)}, u32[]{:S(2)}) collective-permute-start(bf16[128,2176]{1,0:T(8,128)(2,1)S(1)} %pad_maximum_fusion), channel_id=1, source_target_pairs={{0,4},{1,3},{2,6},{3,1},{4,0},{5,7},{6,2},{7,5},{8,12},{9,11},{10,... | collective-permute-start | bytes 1671176 | tf_op jit(solution)/shard_map/ppermute | solution.py:427
  31.1 9.6 %collective-permute-start.8 = (bf16[64,2176]{1,0:T(8,128)(2,1)S(1)}, bf16[64,2176]{1,0:T(8,128)(2,1)S(1)}, u32[]{:S(2)}, u32[]{:S(2)}) collective-permute-start(bf16[64,2176]{1,0:T(8,128)(2,1)S(1)} %collective-permute-done.7.refs_0_), channel_id=1, source_target_pairs={{0,2},{1,5},{2,0},{3,7},{4,6},{5,1},{6,4},{7,3},{8,10},{9,13},{10,... | collective-permute-start | bytes 835592 | tf_op jit(solution)/shard_map/ppermute | solution.py:427
  32.6 8.3 %collective-permute-start.9 = (bf16[64,2176]{1,0:T(8,128)(2,1)S(1)}, bf16[64,2176]{1,0:T(8,128)(2,1)S(1)}, u32[]{:S(2)}, u32[]{:S(2)}) collective-permute-start(bf16[64,2176]{1,0:T(8,128)(2,1)S(1)} %collective-permute-done.7.refs_0_), channel_id=1, source_target_pairs={{0,8},{2,10},{4,12},{6,14},{8,16},{10,18},{12,20},{14,22},{16,24},... | collective-permute-start | bytes 835592 | tf_op jit(solution)/shard_map/ppermute | solution.py:431
  32.6 12.6 %collective-permute-start.12 = (bf16[128,2176]{1,0:T(8,128)(2,1)S(1)}, bf16[128,2176]{1,0:T(8,128)(2,1)S(1)}, u32[]{:S(2)}, u32[]{:S(2)}) collective-permute-start(bf16[128,2176]{1,0:T(8,128)(2,1)S(1)} %pad_maximum_fusion.1), channel_id=1, source_target_pairs={{0,4},{1,3},{2,6},{3,1},{4,0},{5,7},{6,2},{7,5},{8,12},{9,11},{10,... | collective-permute-start | bytes 1671176 | tf_op jit(solution)/shard_map/ppermute | solution.py:427
  40.9 9.5 %collective-permute-start.11 = (bf16[64,2176]{1,0:T(8,128)(2,1)S(1)}, bf16[64,2176]{1,0:T(8,128)(2,1)S(1)}, u32[]{:S(2)}, u32[]{:S(2)}) collective-permute-start(bf16[64,2176]{1,0:T(8,128)(2,1)S(1)} %collective-permute-done.9.refs_0_), channel_id=1, source_target_pairs={{0,2},{1,5},{2,0},{3,7},{4,6},{5,1},{6,4},{7,3},{8,10},{9,13},{10,... | collective-permute-start | bytes 835592 | tf_op jit(solution)/shard_map/ppermute | solution.py:427
  42.3 11.3 %collective-permute-start.13 = (bf16[128,2176]{1,0:T(8,128)(2,1)S(1)}, bf16[128,2176]{1,0:T(8,128)(2,1)S(1)}, u32[]{:S(2)}, u32[]{:S(2)}) collective-permute-start(bf16[128,2176]{1,0:T(8,128)(2,1)S(1)} %pad_maximum_fusion.2), channel_id=1, source_target_pairs={{0,4},{1,3},{2,6},{3,1},{4,0},{5,7},{6,2},{7,5},{8,12},{9,11},{10,... | collective-permute-start | bytes 1671176 | tf_op jit(solution)/shard_map/ppermute | solution.py:427
  50.5 10.7 %collective-permute-start.14 = (bf16[128,2176]{1,0:T(8,128)(2,1)S(1)}, bf16[128,2176]{1,0:T(8,128)(2,1)S(1)}, u32[]{:S(2)}, u32[]{:S(2)}) collective-permute-start(bf16[128,2176]{1,0:T(8,128)(2,1)S(1)} %pad_maximum_fusion.3), channel_id=1, source_target_pairs={{0,4},{1,3},{2,6},{3,1},{4,0},{5,7},{6,2},{7,5},{8,12},{9,11},{10,... | collective-permute-start | bytes 1671176 | tf_op jit(solution)/shard_map/ppermute | solution.py:427
  51.6 13.8 %collective-permute-start.16 = (bf16[128,2048]{1,0:T(8,128)(2,1)S(1)}, bf16[128,2048]{1,0:T(8,128)(2,1)S(1)}, u32[]{:S(2)}, u32[]{:S(2)}) collective-permute-start(bf16[128,2048]{1,0:T(8,128)(2,1)S(1)} %get-tuple-element.133), channel_id=1, source_target_pairs={{0,24},{2,26},{4,28},{6,30},{8,0},{10,2},{12,4},{14,6},{16,8},{18,... | collective-permute-start | bytes 1572872 | tf_op jit(solution)/shard_map/ppermute | solution.py:431
  59.5 13.0 %collective-permute-start.19 = (bf16[128,2048]{1,0:T(8,128)(2,1)S(1)}, bf16[128,2048]{1,0:T(8,128)(2,1)S(1)}, u32[]{:S(2)}, u32[]{:S(2)}) collective-permute-start(bf16[128,2048]{1,0:T(8,128)(2,1)S(1)} %get-tuple-element.138), channel_id=1, source_target_pairs={{0,24},{2,26},{4,28},{6,30},{8,0},{10,2},{12,4},{14,6},{16,8},{18,... | collective-permute-start | bytes 1572872 | tf_op jit(solution)/shard_map/ppermute | solution.py:431
  59.7 8.8 %collective-permute-start.18 = (bf16[64,2048]{1,0:T(8,128)(2,1)S(1)}, bf16[64,2048]{1,0:T(8,128)(2,1)S(1)}, u32[]{:S(2)}, u32[]{:S(2)}) collective-permute-start(bf16[64,2048]{1,0:T(8,128)(2,1)S(1)} %get-tuple-element.137), channel_id=1, source_target_pairs={{0,4},{1,3},{2,6},{3,1},{4,0},{5,7},{6,2},{7,5},{8,12},{9,11},{10,... | collective-permute-start | bytes 786440 | tf_op jit(solution)/shard_map/ppermute | solution.py:427
  65.5 9.0 %collective-permute-start.17 = (bf16[64,2048]{1,0:T(8,128)(2,1)S(1)}, bf16[64,2048]{1,0:T(8,128)(2,1)S(1)}, u32[]{:S(2)}, u32[]{:S(2)}) collective-permute-start(bf16[64,2048]{1,0:T(8,128)(2,1)S(1)} %add_convert_fusion.8), channel_id=1, source_target_pairs={{0,2},{1,5},{2,0},{3,7},{4,6},{5,1},{6,4},{7,3},{8,10},{9,13},{10,... | collective-permute-start | bytes 786440 | tf_op jit(solution)/shard_map/ppermute | solution.py:427
  66.1 8.4 %collective-permute-start.20 = (bf16[64,2048]{1,0:T(8,128)(2,1)S(1)}, bf16[64,2048]{1,0:T(8,128)(2,1)S(1)}, u32[]{:S(2)}, u32[]{:S(2)}) collective-permute-start(bf16[64,2048]{1,0:T(8,128)(2,1)S(1)} %get-tuple-element.139), channel_id=1, source_target_pairs={{0,4},{1,3},{2,6},{3,1},{4,0},{5,7},{6,2},{7,5},{8,12},{9,11},{10,... | collective-permute-start | bytes 786440 | tf_op jit(solution)/shard_map/ppermute | solution.py:427
  67.5 10.9 %collective-permute-start.22 = (bf16[64,2048]{1,0:T(8,128)(2,1)S(1)}, bf16[64,2048]{1,0:T(8,128)(2,1)S(1)}, u32[]{:S(2)}, u32[]{:S(2)}) collective-permute-start(bf16[64,2048]{1,0:T(8,128)(2,1)S(1)} %get-tuple-element.143), channel_id=1, source_target_pairs={{0,4},{1,3},{2,6},{3,1},{4,0},{5,7},{6,2},{7,5},{8,12},{9,11},{10,... | collective-permute-start | bytes 786440 | tf_op jit(solution)/shard_map/ppermute | solution.py:427
  74.6 8.4 %collective-permute-start.23 = (bf16[64,2048]{1,0:T(8,128)(2,1)S(1)}, bf16[64,2048]{1,0:T(8,128)(2,1)S(1)}, u32[]{:S(2)}, u32[]{:S(2)}) collective-permute-start(bf16[64,2048]{1,0:T(8,128)(2,1)S(1)} %add_convert_fusion.6), channel_id=1, source_target_pairs={{0,8},{2,10},{4,12},{6,14},{8,16},{10,18},{12,20},{14,22},{16,24},... | collective-permute-start | bytes 786440 | tf_op jit(solution)/shard_map/ppermute | solution.py:431
  75.6 8.0 %collective-permute-start.21 = (bf16[64,2048]{1,0:T(8,128)(2,1)S(1)}, bf16[64,2048]{1,0:T(8,128)(2,1)S(1)}, u32[]{:S(2)}, u32[]{:S(2)}) collective-permute-start(bf16[64,2048]{1,0:T(8,128)(2,1)S(1)} %add_convert_fusion.7), channel_id=1, source_target_pairs={{0,2},{1,5},{2,0},{3,7},{4,6},{5,1},{6,4},{7,3},{8,10},{9,13},{10,... | collective-permute-start | bytes 786440 | tf_op jit(solution)/shard_map/ppermute | solution.py:427
  78.2 10.2 %collective-permute-start.25 = (bf16[64,2048]{1,0:T(8,128)(2,1)S(1)}, bf16[64,2048]{1,0:T(8,128)(2,1)S(1)}, u32[]{:S(2)}, u32[]{:S(2)}) collective-permute-start(bf16[64,2048]{1,0:T(8,128)(2,1)S(1)} %get-tuple-element.163), channel_id=1, source_target_pairs={{0,4},{1,3},{2,6},{3,1},{4,0},{5,7},{6,2},{7,5},{8,12},{9,11},{10,... | collective-permute-start | bytes 786440 | tf_op jit(solution)/shard_map/ppermute | solution.py:427
  83.7 8.2 %collective-permute-start.27 = (bf16[64,2048]{1,0:T(8,128)(2,1)S(1)}, bf16[64,2048]{1,0:T(8,128)(2,1)S(1)}, u32[]{:S(2)}, u32[]{:S(2)}) collective-permute-start(bf16[64,2048]{1,0:T(8,128)(2,1)S(1)} %add_convert_fusion), channel_id=1, source_target_pairs={{0,8},{2,10},{4,12},{6,14},{8,16},{10,18},{12,20},{14,22},{16,24},... | collective-permute-start | bytes 786440 | tf_op jit(solution)/shard_map/ppermute | solution.py:431
  (4 other events, 25.5 us)
